TPU v7x, 32 devices: a whole 2x2x4 slice. The times are simulated.
32 devices in a mesh: groups: 2 (over y), tm: 4 (over z), head: 2 (over x), sub: 2 (over core).
Axes of the slice: x: 2, y: 2, z: 4, core: 2. Of those that a mesh axis runs over, the one named last changes fastest.
Arguments:
- queries: bfloat16 [4096, 4096], P(('groups', 'tm'), ('head', 'sub')), parts along dimension 0, may hold values from -6 to 6
- keys: bfloat16 [4096, 4096], P(('groups', 'tm'), ('head', 'sub')), parts along dimension 0, may hold values from -6 to 6
- values: bfloat16 [4096, 4096], P(('groups', 'tm'), ('head', 'sub')), parts along dimension 0, may hold values from -16 to 16
- band_blocks: int32 [4, 4, 2], replicated, may hold values from 0 to 4, as said below
Outputs:
- attended: bfloat16 [4096, 4096], P(('groups', 'tm'), ('head', 'sub')), parts along dimension 0
There are 2 independent parts, one for each index of `groups`. A program takes and returns all parts, laid end to end along the dimension named above; an argument that names none is the same for every part. Nothing has to cross between parts.
Inputs may be any that keep to these rules, and one draw needn't show every extreme that they name: band_blocks[f, g] lists in rising order blocks of frame g; the slots after the listed ones hold 4. For d = |f - g| of 2 or more the list is o + k * 2 * 2 ** (floor(log2 d) - 1), k = 0, 1, ..., while below 4, for some offset o below that stride; for d of 1 or 0 the list is empty. So frames two or three apart list exactly 2 blocks and frames four or more apart at most one, in slot 0.
All inputs are finite; a program needn't handle non-finite values.
Results may differ from a plain program's by a relative error of at most 0.0032.
Values may be sent and summed in bfloat16 or wider, within the bound.
No kernel may reach another device: no remote copies, remote signals or barrier semaphores. Data moves between devices by JAX's collectives and lax.ppermute only.
A program may use at most 64 MiB of HBM per device.

v0:
```python
import jax
import jax.numpy as jnp
from jax import lax
from jax.sharding import PartitionSpec as P

HD = 128
BLOCK = 128


masked_fill = -1e30


def padded(block, sides, width):
    for axis, dim in sides:
        count = lax.axis_size(axis)
        forward = [(i, i + 1) for i in range(count - 1)]
        backward = [(target, source) for source, target in forward]
        low = lax.ppermute(
            lax.slice_in_dim(block, block.shape[dim] - width, None, axis=dim), axis, forward
        )
        high = lax.ppermute(lax.slice_in_dim(block, 0, width, axis=dim), axis, backward)
        block = jnp.concatenate([low, block, high], axis=dim)
    return block


def shards(queries, keys, values, band_blocks):
    frame_rows, columns = queries.shape
    frames = lax.axis_size("tm")
    current = lax.axis_index("tm")
    half_rows = frame_rows // 2
    frame_blocks = frame_rows // BLOCK
    capacity = band_blocks.shape[2]
    heads_dev = columns // HD
    paired = jnp.stack([keys, values], 0)
    near_kv = padded(paired, (("tm", 1),), half_rows)
    position = jnp.arange(2 * frame_rows)
    near_ok = ((position >= half_rows) | (current > 0)) & (
        (position < half_rows + frame_rows) | (current < frames - 1)
    )
    kv_blocks = jnp.concatenate(
        [
            paired.reshape(2, frame_blocks, BLOCK, columns),
            jnp.zeros((2, 1, BLOCK, columns), jnp.bfloat16),
        ],
        1,
    )
    outgoing = lax.dynamic_index_in_dim(band_blocks, current, 1, keepdims=False)
    incoming = lax.dynamic_index_in_dim(band_blocks, current, 0, keepdims=False)
    outbound = jnp.take(kv_blocks, outgoing, axis=1)
    arrived = lax.all_to_all(outbound, "tm", split_axis=1, concat_axis=1, tiled=True)
    far_kv = arrived.reshape(2, frames * capacity * BLOCK, columns)
    far_ok = jnp.repeat((incoming != frame_blocks).reshape(-1), BLOCK)
    all_kv = jnp.concatenate([near_kv, far_kv], 1)
    visible = jnp.concatenate([near_ok, far_ok], 0)
    inv_root = HD ** (-0.5)

    def per_head(head_at):
        start = head_at * HD
        query_head = lax.dynamic_slice_in_dim(queries, start, HD, 1)
        key_head = lax.dynamic_slice_in_dim(all_kv[0], start, HD, 1)
        value_head = lax.dynamic_slice_in_dim(all_kv[1], start, HD, 1)
        scores = (
            lax.dot_general(
                query_head, key_head, (((1,), (1,)), ((), ())), preferred_element_type=jnp.float32
            )
            * inv_root
        )
        scores = jnp.where(visible[None, :], scores, masked_fill)
        row_max = jnp.max(scores, axis=1, keepdims=True)
        powers = jnp.exp(scores - row_max)
        row_sum = jnp.sum(powers, axis=1, keepdims=True)
        mixed_sum = jnp.dot(
            powers.astype(jnp.bfloat16), value_head, preferred_element_type=jnp.float32
        )
        return (mixed_sum / row_sum).astype(jnp.bfloat16)

    result = lax.map(per_head, jnp.arange(heads_dev, dtype=jnp.int32))
    return jnp.transpose(result, (1, 0, 2)).reshape(frame_rows, columns)


def solution(mesh):
    placed = (
        P(("groups", "tm"), ("head", "sub")),
        P(("groups", "tm"), ("head", "sub")),
        P(("groups", "tm"), ("head", "sub")),
        P(),
    )
    return jax.shard_map(
        shards,
        mesh=mesh,
        in_specs=placed,
        out_specs=P(("groups", "tm"), ("head", "sub")),
        check_vma=False,
    )
```

profile of v0, /device:TPU:10, one launch (start us, length us, event | category | flops | bytes accessed | tf_op | source)
XLA Modules:
  0.0 215.4 jit_solution(11706469682283165903)
XLA Ops:
  1.2 1.9 fusion.30
  3.1 2.8 %gather_fusion = bf16[8,2,128,1024]{3,2,1,0:T(8,128)(2,1)} fusion(bf16[2,5,128,1024]{3,2,1,0:T(8,128)(2,1)S(1)} %fusion.30, s32[1024]{0:T(1024)S(1)} %pad_clamp_fusion), kind=kCustom, calls=%fused_computation | custom fusion | bytes 8388640 | tf_op jit(solution)/shard_map/jit(_take)/gather | solution.py:49
  5.8 2.7 %select_bitcast_fusion = bf16[2,4,2,128,1024]{4,3,0,2,1:T(8,128)(2,1)S(1)} fusion(bf16[4,2,2,128,1024]{4,3,2,1,0:T(8,128)(2,1)} %bitcast.43, pred[4,2]{1,0:T(4,128)(4,1)S(1)} %copy.27), kind=kLoop, calls=%fused_computation.26 | loop fusion | flops 2097152 | bytes 8388616 | tf_op jit(solution)/shard_map/jit(_take)/select_n | solution.py:49
  8.5 2.4 %copy.30 = bf16[2,4,2,128,1024]{4,3,2,0,1:T(8,128)(2,1)} copy(bf16[2,4,2,128,1024]{4,3,0,2,1:T(8,128)(2,1)S(1)} %select_bitcast_fusion) | data formatting | bytes 8388608 | tf_op jit(solution)/shard_map/jit(_take)/select_n | solution.py:49
  10.9 5.4 %all-to-all-start = ((bf16[2,4,2,128,1024]{4,3,2,0,1:T(8,128)(2,1)}), bf16[2,4,2,128,1024]{4,3,2,0,1:T(8,128)(2,1)}, u32[]{:S(2)}, u32[]{:S(2)}) async-start(bf16[2,4,2,128,1024]{4,3,2,0,1:T(8,128)(2,1)} %copy.30), calls=%async_computation | async-start | bytes 8388608 | tf_op jit(solution)/shard_map/all_to_all | solution.py:50
  17.8 3.4 %collective-permute-start = (bf16[2,256,1024]{2,1,0:T(8,128)(2,1)}, bf16[2,256,1024]{2,1,0:T(8,128)(2,1)S(1)}, u32[]{:S(2)}, u32[]{:S(2)}) collective-permute-start(bf16[2,256,1024]{2,1,0:T(8,128)(2,1)} %get-tuple-element.54), channel_id=1, source_target_pairs={{0,4},{4,8},{8,12},{1,5},{5,9},{9,13},{2,6},{6,10},{10,14},{3,7},{... | collective-permute-start | bytes 3145736 | tf_op jit(solution)/shard_map/ppermute | solution.py:18
  21.2 2.5 %collective-permute-start.1 = (bf16[2,256,1024]{2,1,0:T(8,128)(2,1)}, bf16[2,256,1024]{2,1,0:T(8,128)(2,1)}, u32[]{:S(2)}, u32[]{:S(2)}) collective-permute-start(bf16[2,256,1024]{2,1,0:T(8,128)(2,1)} %get-tuple-element.55), channel_id=1, source_target_pairs={{4,0},{8,4},{12,8},{5,1},{9,5},{13,9},{6,2},{10,6},{14,10},{7,3},{... | collective-permute-start | bytes 3145736 | tf_op jit(solution)/shard_map/ppermute | solution.py:21
  24.7 82.9 %all-to-all-done = bf16[2,4,2,128,1024]{4,3,2,0,1:T(8,128)(2,1)} async-done(((bf16[2,4,2,128,1024]{4,3,2,0,1:T(8,128)(2,1)}), bf16[2,4,2,128,1024]{4,3,2,0,1:T(8,128)(2,1)}, u32[]{:S(2)}, u32[]{:S(2)}) %all-to-all-start) | async-done | bytes 4194336 | tf_op jit(solution)/shard_map/all_to_all | solution.py:50
  107.6 2.6 %copy.31 = bf16[2,4,2,128,1024]{4,3,2,1,0:T(8,128)(2,1)S(1)} copy(bf16[2,4,2,128,1024]{4,3,2,0,1:T(8,128)(2,1)} %all-to-all-done) | data formatting | bytes 8388608 | tf_op jit(solution)/shard_map/all_to_all | solution.py:50
  110.3 18.6 %collective-permute-done = bf16[2,256,1024]{2,1,0:T(8,128)(2,1)S(1)} collective-permute-done((bf16[2,256,1024]{2,1,0:T(8,128)(2,1)}, bf16[2,256,1024]{2,1,0:T(8,128)(2,1)S(1)}, u32[]{:S(2)}, u32[]{:S(2)}) %collective-permute-start) | collective-permute-done | bytes 1048608 | tf_op jit(solution)/shard_map/ppermute | solution.py:18
  128.9 1.9 collective-permute-done.1
  130.8 5.4 %pad_maximum_fusion = bf16[2,2048,1024]{2,1,0:T(8,128)(2,1)} fusion(bf16[2,1024,1024]{2,1,0:T(8,128)(2,1)S(1)} %bitcast.44, bf16[2,256,1024]{2,1,0:T(8,128)(2,1)} %collective-permute-done.1, bf16[1,512,1024]{2,1,0:T(8,128)(2,1)S(1)} %bitcast.47, bf16[1,512,1024]{2,1,0:T(8,128)(2,1)S(1)} %bitcast.50, bf16[2,256,1024]{2,1,0:T(8,128)(2,1)S(1)} %collective-permute-done), kind=kLoop, calls=%fused_computation.22 | loop fusion | flops 41943040 | bytes 16777216 | tf_op jit(solution)/shard_map/concatenate | solution.py:53
  136.2 76.9 %while.10 = (s32[]{:T(128)}, bf16[8,512,128]{2,1,0:T(8,128)(2,1)}, pred[2048]{0:T(1024)(128)(4,1)S(1)}, s32[8]{0:T(128)S(1)}, bf16[512,1024]{1,0:T(8,128)(2,1)},...) while((s32[]{:T(128)}, bf16[8,512,128]{2,1,0:T(8,128)(2,1)}, ...), condition=%wide.region_3.4_spmd, body=%wide.region_0.3_spmd.sunk | while | flops 548535296 | bytes 30688928 | solution.py:77
  137.4 3.9 %fusion.45 = (bf16[1,2048,1024]{2,1,0:T(8,128)(2,1)S(1)}, bf16[1,2048,1024]{2,1,0:T(8,128)(2,1)S(1)}) fusion(bf16[2,2048,1024]{2,1,0:T(8,128)(2,1)} %get-tuple-element.126), kind=kLoop, calls=%fused_computation.46.clone.1 | loop fusion | bytes 16777216 | tf_op jit(solution)/shard_map/while/body/eval_jaxpr/slice | solution.py:61
  141.3 1.8 fusion.46
  147.0 3.9 %fusion.45 = (bf16[1,2048,1024]{2,1,0:T(8,128)(2,1)S(1)}, bf16[1,2048,1024]{2,1,0:T(8,128)(2,1)S(1)}) fusion(bf16[2,2048,1024]{2,1,0:T(8,128)(2,1)} %get-tuple-element.126), kind=kLoop, calls=%fused_computation.46.clone.1 | loop fusion | bytes 16777216 | tf_op jit(solution)/shard_map/while/body/eval_jaxpr/slice | solution.py:61
  150.9 1.8 fusion.46
  156.6 3.9 %fusion.45 = (bf16[1,2048,1024]{2,1,0:T(8,128)(2,1)S(1)}, bf16[1,2048,1024]{2,1,0:T(8,128)(2,1)S(1)}) fusion(bf16[2,2048,1024]{2,1,0:T(8,128)(2,1)} %get-tuple-element.126), kind=kLoop, calls=%fused_computation.46.clone.1 | loop fusion | bytes 16777216 | tf_op jit(solution)/shard_map/while/body/eval_jaxpr/slice | solution.py:61
  160.6 1.8 fusion.46
  166.2 3.9 %fusion.45 = (bf16[1,2048,1024]{2,1,0:T(8,128)(2,1)S(1)}, bf16[1,2048,1024]{2,1,0:T(8,128)(2,1)S(1)}) fusion(bf16[2,2048,1024]{2,1,0:T(8,128)(2,1)} %get-tuple-element.126), kind=kLoop, calls=%fused_computation.46.clone.1 | loop fusion | bytes 16777216 | tf_op jit(solution)/shard_map/while/body/eval_jaxpr/slice | solution.py:61
  170.2 1.8 fusion.46
  172.9 1.7 fusion.48
  175.8 3.9 %fusion.45 = (bf16[1,2048,1024]{2,1,0:T(8,128)(2,1)S(1)}, bf16[1,2048,1024]{2,1,0:T(8,128)(2,1)S(1)}) fusion(bf16[2,2048,1024]{2,1,0:T(8,128)(2,1)} %get-tuple-element.126), kind=kLoop, calls=%fused_computation.46.clone.1 | loop fusion | bytes 16777216 | tf_op jit(solution)/shard_map/while/body/eval_jaxpr/slice | solution.py:61
  179.8 1.8 fusion.46
  185.4 3.9 %fusion.45 = (bf16[1,2048,1024]{2,1,0:T(8,128)(2,1)S(1)}, bf16[1,2048,1024]{2,1,0:T(8,128)(2,1)S(1)}) fusion(bf16[2,2048,1024]{2,1,0:T(8,128)(2,1)} %get-tuple-element.126), kind=kLoop, calls=%fused_computation.46.clone.1 | loop fusion | bytes 16777216 | tf_op jit(solution)/shard_map/while/body/eval_jaxpr/slice | solution.py:61
  189.4 1.8 fusion.46
  195.0 3.9 %fusion.45 = (bf16[1,2048,1024]{2,1,0:T(8,128)(2,1)S(1)}, bf16[1,2048,1024]{2,1,0:T(8,128)(2,1)S(1)}) fusion(bf16[2,2048,1024]{2,1,0:T(8,128)(2,1)} %get-tuple-element.126), kind=kLoop, calls=%fused_computation.46.clone.1 | loop fusion | bytes 16777216 | tf_op jit(solution)/shard_map/while/body/eval_jaxpr/slice | solution.py:61
  199.0 1.8 fusion.46
  201.7 1.7 fusion.48
  204.6 3.9 %fusion.45 = (bf16[1,2048,1024]{2,1,0:T(8,128)(2,1)S(1)}, bf16[1,2048,1024]{2,1,0:T(8,128)(2,1)S(1)}) fusion(bf16[2,2048,1024]{2,1,0:T(8,128)(2,1)} %get-tuple-element.126), kind=kLoop, calls=%fused_computation.46.clone.1 | loop fusion | bytes 16777216 | tf_op jit(solution)/shard_map/while/body/eval_jaxpr/slice | solution.py:61
  208.6 1.8 fusion.46
  213.0 2.4 %copy_bitcast_fusion = bf16[512,1024]{1,0:T(8,128)(2,1)} fusion(bf16[8,512,128]{2,1,0:T(8,128)(2,1)} %get-tuple-element.37), kind=kLoop, calls=%fused_computation.31 | loop fusion | bytes 2097152 | tf_op jit(solution)/shard_map/reshape | solution.py:78
  (43 shorter events, 26.0 us)
Async XLA Ops:
  10.9 5.5 %copy-start = (bf16[512,1024]{1,0:T(8,128)(2,1)S(1)}, bf16[512,1024]{1,0:T(8,128)(2,1)}, u32[]{:S(2)}) copy-start(bf16[512,1024]{1,0:T(8,128)(2,1)} %param.8) | copy-start | bytes 3145732
  10.9 5.5 %copy-start.1 = (bf16[512,1024]{1,0:T(8,128)(2,1)S(1)}, bf16[512,1024]{1,0:T(8,128)(2,1)}, u32[]{:S(2)}) copy-start(bf16[512,1024]{1,0:T(8,128)(2,1)} %param.7) | copy-start | bytes 3145732
  10.9 96.8 %all-to-all-start = ((bf16[2,4,2,128,1024]{4,3,2,0,1:T(8,128)(2,1)}), bf16[2,4,2,128,1024]{4,3,2,0,1:T(8,128)(2,1)}, u32[]{:S(2)}, u32[]{:S(2)}) async-start(bf16[2,4,2,128,1024]{4,3,2,0,1:T(8,128)(2,1)} %copy.30), calls=%async_computation | async-start | bytes 8388608 | tf_op jit(solution)/shard_map/all_to_all | solution.py:50
  17.8 111.0 %collective-permute-start = (bf16[2,256,1024]{2,1,0:T(8,128)(2,1)}, bf16[2,256,1024]{2,1,0:T(8,128)(2,1)S(1)}, u32[]{:S(2)}, u32[]{:S(2)}) collective-permute-start(bf16[2,256,1024]{2,1,0:T(8,128)(2,1)} %get-tuple-element.54), channel_id=1, source_target_pairs={{0,4},{4,8},{8,12},{1,5},{5,9},{9,13},{2,6},{6,10},{10,14},{3,7},{... | collective-permute-start | bytes 3145736 | tf_op jit(solution)/shard_map/ppermute | solution.py:18
  21.2 109.6 %collective-permute-start.1 = (bf16[2,256,1024]{2,1,0:T(8,128)(2,1)}, bf16[2,256,1024]{2,1,0:T(8,128)(2,1)}, u32[]{:S(2)}, u32[]{:S(2)}) collective-permute-start(bf16[2,256,1024]{2,1,0:T(8,128)(2,1)} %get-tuple-element.55), channel_id=1, source_target_pairs={{4,0},{8,4},{12,8},{5,1},{9,5},{13,9},{6,2},{10,6},{14,10},{7,3},{... | collective-permute-start | bytes 3145736 | tf_op jit(solution)/shard_map/ppermute | solution.py:21
where the time goes:
time: 216 us; the launch traced here: 215 us
  waiting for transfers between devices  103 us (48%)
  local copies, waits for them, and re-layouts  47.7 us (22%)
  matrix products  27.8 us (13%)
  other arithmetic  19.7 us (9%)
  starting transfers between devices  11.3 us (5%)
  loops' own time  5.33 us (2%)
    all_to_all x1, waiting for transfers between devices, shards(): lax.all_to_all(outbound, 'tm', split_axis=1, concat_axis=1, tiled=True)  82.9 us
    slice x8, local copies, waits for them, and re-layouts, per_head(): value_head = lax.dynamic_slice_in_dim(all_kv[1], start, HD, 1)  31.5 us
    ppermute x1, waiting for transfers between devices, padded(): lax.ppermute(lax.slice_in_dim(block, block.shape[dim] - width, None, axis...  18.6 us
    dot_general x8, matrix products, per_head(): lax.dot_general(query_head, key_head, (((1,), (1,)), ((), ())), preferred...  14.3 us
    dot_general x8, matrix products, per_head(): jnp.dot(powers.astype(jnp.bfloat16), value_head, preferred_element_type=j...  13.5 us
    reduce_sum x8, other arithmetic, per_head(): row_sum = jnp.sum(powers, axis=1, keepdims=True)  7.58 us
    all_to_all x1, starting transfers between devices, shards(): lax.all_to_all(outbound, 'tm', split_axis=1, concat_axis=1, tiled=True)  5.45 us
    concatenate x1, other arithmetic, shards(): all_kv = jnp.concatenate([near_kv, far_kv], 1)  5.35 us
  transfers between devices with their start and end apart: 3, of which 3 were waited for; matrix products, arithmetic and copies ran while one was open for 2% of the time, Pallas kernels for 0%

commit v1 on v0

--- a/solution.py
+++ b/solution.py
@@ -1,11 +1,15 @@
+import functools
+
 import jax
 import jax.numpy as jnp
 from jax import lax
+from jax.experimental import pallas as pl
+from jax.experimental.pallas import tpu as pltpu
 from jax.sharding import PartitionSpec as P
 
 HD = 128
 BLOCK = 128
-
+LOG2E = 1.4426950408889634
 
 masked_fill = -1e30
 
@@ -23,7 +27,7 @@
     return block
 
 
-def shards(queries, keys, values, band_blocks):
+def any_frames(queries, keys, values, band_blocks):
     frame_rows, columns = queries.shape
     frames = lax.axis_size("tm")
     current = lax.axis_index("tm")
@@ -78,6 +82,205 @@
     return jnp.transpose(result, (1, 0, 2)).reshape(frame_rows, columns)
 
 
+def run_copies(copies):
+    for copy in copies:
+        copy.start()
+    for copy in copies:
+        copy.wait()
+
+
+def pick_kernel(groups, width, bands, keys, values, extra, *rest):
+    direct, sems = rest[:groups], rest[groups]
+    frame = lax.axis_index("tm")
+    inner = (frame == 1) | (frame == 2)
+
+    @pl.when(inner)
+    def _():
+        block = jnp.where(frame == 1, bands[3, 1, 0], bands[0, 2, 1])
+        run_copies(
+            [
+                pltpu.make_async_copy(src.at[pl.ds(block * BLOCK, BLOCK)], extra.at[kv], sems.at[kv])
+                for kv, src in enumerate((keys, values))
+            ]
+        )
+
+    @pl.when(jnp.logical_not(inner))
+    def _():
+        other = 3 - frame
+        copies = []
+        for g in range(groups):
+            for kv, src in enumerate((keys, values)):
+                for slot in range(2):
+                    block = bands[other, frame, slot]
+                    copies.append(
+                        pltpu.make_async_copy(
+                            src.at[pl.ds(block * BLOCK, BLOCK), pl.ds(g * width, width)],
+                            direct[g].at[kv, pl.ds(slot * BLOCK, BLOCK)],
+                            sems.at[len(copies)],
+                        )
+                    )
+        run_copies(copies)
+
+
+def relay_kernel(groups, width, bands, keys, values, low, high, extra, *rest):
+    relayed, sems = rest[:groups], rest[groups]
+    frame = lax.axis_index("tm")
+
+    def hand_on(source, picked):
+        copies = []
+        for g in range(groups):
+            for kv in range(2):
+                cols = pl.ds(g * width, width)
+                copies.append(
+                    pltpu.make_async_copy(
+                        source.at[kv, pl.ds(picked * BLOCK, BLOCK), cols],
+                        relayed[g].at[kv, pl.ds(0, BLOCK)],
+                        sems.at[len(copies)],
+                    )
+                )
+                copies.append(
+                    pltpu.make_async_copy(
+                        extra.at[kv, :, cols],
+                        relayed[g].at[kv, pl.ds(BLOCK, BLOCK)],
+                        sems.at[len(copies)],
+                    )
+                )
+        run_copies(copies)
+
+    @pl.when(frame == 1)
+    def _():
+        hand_on(high, bands[0, 2, 0])
+
+    @pl.when(frame == 2)
+    def _():
+        hand_on(low, bands[3, 1, 1] - 2)
+
+    @pl.when((frame == 0) | (frame == 3))
+    def _():
+        other = jnp.where(frame == 0, 2, 1)
+        copies = []
+        for g in range(groups):
+            for kv, src in enumerate((keys, values)):
+                for slot in range(2):
+                    block = bands[other, frame, slot]
+                    copies.append(
+                        pltpu.make_async_copy(
+                            src.at[pl.ds(block * BLOCK, BLOCK), pl.ds(g * width, width)],
+                            relayed[g].at[kv, pl.ds(slot * BLOCK, BLOCK)],
+                            sems.at[len(copies)],
+                        )
+                    )
+        run_copies(copies)
+
+
+def attend_kernel(chunk, queries, keys, values, low, high, relayed, direct, *rest):
+    out = rest[-1]
+    frame = lax.axis_index("tm")
+    first = frame == 0
+    edge = first | (frame == 3)
+
+    def all_rows(own, kv):
+        return jnp.concatenate(
+            [
+                own[...],
+                jnp.where(first, high[kv], low[kv]),
+                jnp.where(edge, direct[kv], high[kv]),
+                relayed[kv],
+            ],
+            0,
+        )
+
+    key_rows = all_rows(keys, 0)
+    value_rows = all_rows(values, 1)
+    rate = LOG2E * HD ** (-0.5)
+    for start in range(0, queries.shape[0], chunk):
+        scores = lax.dot_general(
+            queries[pl.ds(start, chunk)],
+            key_rows,
+            (((1,), (1,)), ((), ())),
+            preferred_element_type=jnp.float32,
+        )
+        row_max = jnp.max(scores, axis=1, keepdims=True)
+        powers = jnp.exp2((scores - row_max) * rate)
+        row_sum = jnp.sum(powers, axis=1, keepdims=True)
+        mixed = jnp.dot(powers.astype(jnp.bfloat16), value_rows, preferred_element_type=jnp.float32)
+        out[pl.ds(start, chunk)] = (mixed / row_sum).astype(jnp.bfloat16)
+
+
+def four_frames(queries, keys, values, band_blocks):
+    rows, columns = queries.shape
+    half = rows // 2
+    heads = columns // HD
+    groups = 4 if heads % 4 == 0 else 1
+    width = columns // groups
+    group_heads = heads // groups
+    anywhere = pl.BlockSpec(memory_space=pl.ANY)
+    scalars = pl.BlockSpec(memory_space=pltpu.SMEM)
+
+    low = lax.ppermute(
+        jnp.stack([keys[half:], values[half:]], 0), "tm", [(0, 1), (1, 2), (2, 3)]
+    )
+    high = lax.ppermute(
+        jnp.stack([keys[:half], values[:half]], 0), "tm", [(1, 0), (2, 1), (3, 2)]
+    )
+    pair = jax.ShapeDtypeStruct((2, 2 * BLOCK, width), jnp.bfloat16)
+    extra, *direct = pl.pallas_call(
+        functools.partial(pick_kernel, groups, width),
+        out_shape=[jax.ShapeDtypeStruct((2, BLOCK, columns), jnp.bfloat16)] + [pair] * groups,
+        in_specs=[scalars, anywhere, anywhere],
+        out_specs=[anywhere] * (1 + groups),
+        scratch_shapes=[pltpu.SemaphoreType.DMA((4 * groups,))],
+        name="pick_blocks",
+    )(band_blocks, keys, values)
+    extra = lax.ppermute(extra, "tm", [(1, 2), (2, 1)])
+    direct = [lax.ppermute(part, "tm", [(0, 3), (3, 0)]) for part in direct]
+    relayed = pl.pallas_call(
+        functools.partial(relay_kernel, groups, width),
+        out_shape=[pair] * groups,
+        in_specs=[scalars] + [anywhere] * 5,
+        out_specs=[anywhere] * groups,
+        scratch_shapes=[pltpu.SemaphoreType.DMA((4 * groups,))],
+        name="relay_blocks",
+    )(band_blocks, keys, values, low, high, extra)
+    relayed = [lax.ppermute(part, "tm", [(0, 2), (3, 1), (2, 3), (1, 0)]) for part in relayed]
+
+    result = None
+    for g in range(groups):
+        own = pl.BlockSpec((rows, HD), lambda h, g=g: (0, g * group_heads + h))
+        near = pl.BlockSpec((2, half, HD), lambda h, g=g: (0, 0, g * group_heads + h))
+        far = pl.BlockSpec((2, half, HD), lambda h: (0, 0, h))
+        in_specs = [own, own, own, near, near, far, far]
+        operands = [queries, keys, values, low, high, relayed[g], direct[g]]
+        aliases = {}
+        if result is not None:
+            aliases = {len(operands): 0}
+            in_specs.append(anywhere)
+            operands.append(result)
+        seen = rows + 3 * half
+        result = pl.pallas_call(
+            functools.partial(attend_kernel, rows // 2),
+            grid=(group_heads,),
+            out_shape=jax.ShapeDtypeStruct(queries.shape, queries.dtype),
+            in_specs=in_specs,
+            out_specs=own,
+            input_output_aliases=aliases,
+            compiler_params=pltpu.CompilerParams(vmem_limit_bytes=32 << 20),
+            cost_estimate=pl.CostEstimate(
+                flops=4 * group_heads * rows * seen * HD,
+                bytes_accessed=2 * width * (2 * rows + 2 * (rows + 4 * half)),
+                transcendentals=group_heads * rows * seen,
+            ),
+            name=f"attend_{g}",
+        )(*operands)
+    return result
+
+
+def shards(queries, keys, values, band_blocks):
+    if lax.axis_size("tm") == 4 and queries.shape[0] == 4 * BLOCK and band_blocks.shape[2] == 2:
+        return four_frames(queries, keys, values, band_blocks)
+    return any_frames(queries, keys, values, band_blocks)
+
+
 def solution(mesh):
     placed = (
         P(("groups", "tm"), ("head", "sub")),

time: 216 us -> 131 us (0.61)
  the two profiles are of different devices: /device:TPU:10 before, /device:TPU:0 now
where the time goes in v1:
time: 131 us
  Pallas kernels  85.6 us (65%)
  starting transfers between devices  28.7 us (22%)
  waiting for transfers between devices  7.42 us (6%)
  local copies, waits for them, and re-layouts  6.59 us (5%)
  other arithmetic  2.14 us (2%)
    pallas_call x1, Pallas kernels, four_frames(): pl.pallas_call(functools.partial(relay_kernel, groups, width), out_shape=...  33.9 us
    pallas_call x1, Pallas kernels, four_frames(): pl.pallas_call(functools.partial(pick_kernel, groups, width), out_shape=[...  33.8 us
    pallas_call x4, Pallas kernels, four_frames(): pl.pallas_call(functools.partial(attend_kernel, rows // 2), grid=(group_h...  17.9 us
    ppermute x4, starting transfers between devices, four_frames(): direct = [lax.ppermute(part, 'tm', [(0, 3), (3, 0)]) for part in direct]  17.2 us
    ppermute x4, waiting for transfers between devices, four_frames(): lax.ppermute(part, 'tm', [(0, 2), (3, 1), (2, 3), (1, 0)])  7.41 us
    ppermute x1, starting transfers between devices, four_frames(): lax.ppermute(jnp.stack([keys[half:], values[half:]], 0), 'tm', [(0, 1), (...  4.98 us
    unnamed x15, local copies, waits for them, and re-layouts  4.9 us
    ppermute x4, starting transfers between devices, four_frames(): lax.ppermute(part, 'tm', [(0, 2), (3, 1), (2, 3), (1, 0)])  4.54 us
  transfers between devices with their start and end apart: 11, of which 2 were waited for; matrix products, arithmetic and copies ran while one was open for 1% of the time, Pallas kernels for 62%

profile of v1, /device:TPU:0, one launch (start us, length us, event | category | flops | bytes accessed | tf_op | source)
XLA Modules:
  0.0 130.7 jit_solution(853442757201718282)
XLA Ops:
  0.0 1.7 %slice_bitcast_fusion = (bf16[1,256,1024]{2,1,0:T(8,128)(2,1)S(1)}, bf16[1,256,1024]{2,1,0:T(8,128)(2,1)S(1)}, bf16[1,256,1024]{2,1,0:T(8,128)(2,1)S(1)}, bf16[1,256,1024]{2,1,0:T(8,128)(2,1)S(1)}) fusion(bf16[512,1024]{1,0:T(8,128)(2,1)} %values.11, bf16[512,1024]{1,0:T(8,128)(2,1)} %keys.11), kind=kLoop, calls=%fused_computation.2 | loop fusion | bytes 4194304 | tf_op jit(solution)/shard_map/stack | solution.py:224
  1.7 1.1 pad_maximum_fusion
  2.8 5.0 %collective-permute-start = (bf16[2,256,1024]{2,1,0:T(8,128)(2,1)}, bf16[2,256,1024]{2,1,0:T(8,128)(2,1)S(1)}, u32[]{:S(2)}, u32[]{:S(2)}) collective-permute-start(bf16[2,256,1024]{2,1,0:T(8,128)(2,1)} %pad_maximum_fusion), channel_id=1, source_target_pairs={{0,4},{4,8},{8,12},{1,5},{5,9},{9,13},{2,6},{6,10},{10,14},{3,7},{... | collective-permute-start | bytes 3145736 | tf_op jit(solution)/shard_map/ppermute | solution.py:220
  7.7 0.0 copy-start.6
  7.8 1.1 pad_maximum_fusion.1
  8.8 1.3 collective-permute-start.1
  10.1 0.7 copy.9.bands
  10.8 33.8 %pick_blocks.1 = (bf16[2,128,1024]{2,1,0:T(8,128)(2,1)}, bf16[2,256,256]{2,1,0:T(8,128)(2,1)}, bf16[2,256,256]{2,1,0:T(8,128)(2,1)}, bf16[2,256,256]{2,1,0:T(8,128)(2,1)}, bf16[2,256,256]{2,1,0:T(8,128)(2,1)}) custom-call(s32[4,4,2]{2,1,0:T(4,128)} %copy.9.bands, bf16[512,1024]{1,0:T(8,128)(2,1)} %keys.11, bf16[512,1024]{1,0:T(8,128)(2,1)} %values.11), custom_call_target="tpu_custom_call" | custom-call | tf_op jit(solution)/shard_map/pick_blocks/pallas_call | solution.py:227
  44.7 0.7 collective-permute-start.2
  45.4 7.5 %collective-permute-start.8 = (bf16[2,256,256]{2,1,0:T(8,128)(2,1)}, bf16[2,256,256]{2,1,0:T(8,128)(2,1)S(1)}, u32[]{:S(2)}, u32[]{:S(2)}) collective-permute-start(bf16[2,256,256]{2,1,0:T(8,128)(2,1)} %get-tuple-element.20), channel_id=1, source_target_pairs={{0,12},{12,0},{1,13},{13,1},{2,14},{14,2},{3,15},{15,3},{16,28},{2... | collective-permute-start | bytes 786440 | tf_op jit(solution)/shard_map/ppermute | solution.py:236
  52.9 0.0 copy-start
  52.9 0.0 copy-start.1
  52.9 2.1 %collective-permute-start.10 = (bf16[2,256,256]{2,1,0:T(8,128)(2,1)}, bf16[2,256,256]{2,1,0:T(8,128)(2,1)}, u32[]{:S(2)}, u32[]{:S(2)}) collective-permute-start(bf16[2,256,256]{2,1,0:T(8,128)(2,1)} %get-tuple-element.22), channel_id=1, source_target_pairs={{0,12},{12,0},{1,13},{13,1},{2,14},{14,2},{3,15},{15,3},{16,28},{2... | collective-permute-start | bytes 786440 | tf_op jit(solution)/shard_map/ppermute | solution.py:236
  54.9 0.0 collective-permute-done.2.extra
  55.0 0.8 copy-done.5
  55.8 1.0 copy-done.2
  56.7 33.9 %relay_blocks.1 = (bf16[2,256,256]{2,1,0:T(8,128)(2,1)}, bf16[2,256,256]{2,1,0:T(8,128)(2,1)}, bf16[2,256,256]{2,1,0:T(8,128)(2,1)}, bf16[2,256,256]{2,1,0:T(8,128)(2,1)}) custom-call(s32[4,4,2]{2,1,0:T(4,128)} %copy.9.bands, bf16[512,1024]{1,0:T(8,128)(2,1)} %keys.11, bf16[512,1024]{1,0:T(8,128)(2,1)} %values.11, bf16[2,256,1024]{2,1,0:T(8,128)(2,1)} %copy-done.2, ...), custom_call_target="tpu_custom_call" | custom-call | tf_op jit(solution)/shard_map/relay_blocks/pallas_call | solution.py:237
  90.6 0.1 collective-permute-start.9
  90.7 4.4 %collective-permute-start.7 = (bf16[2,256,256]{2,1,0:T(8,128)(2,1)}, bf16[2,256,256]{2,1,0:T(8,128)(2,1)S(1)}, u32[]{:S(2)}, u32[]{:S(2)}) collective-permute-start(bf16[2,256,256]{2,1,0:T(8,128)(2,1)} %get-tuple-element.19), channel_id=1, source_target_pairs={{0,8},{12,4},{8,12},{4,0},{1,9},{13,5},{9,13},{5,1},{2,10},{14,6},... | collective-permute-start | bytes 786440 | tf_op jit(solution)/shard_map/ppermute | solution.py:245
  95.1 1.9 %collective-permute-start.6 = (bf16[2,256,256]{2,1,0:T(8,128)(2,1)}, bf16[2,256,256]{2,1,0:T(8,128)(2,1)S(1)}, u32[]{:S(2)}, u32[]{:S(2)}) collective-permute-start(bf16[2,256,256]{2,1,0:T(8,128)(2,1)} %get-tuple-element.18), channel_id=1, source_target_pairs={{0,12},{12,0},{1,13},{13,1},{2,14},{14,2},{3,15},{15,3},{16,28},{2... | collective-permute-start | bytes 786440 | tf_op jit(solution)/shard_map/ppermute | solution.py:236
  97.0 0.1 collective-permute-start.5
  97.1 5.7 %collective-permute-start.4 = (bf16[2,256,256]{2,1,0:T(8,128)(2,1)}, bf16[2,256,256]{2,1,0:T(8,128)(2,1)S(1)}, u32[]{:S(2)}, u32[]{:S(2)}) collective-permute-start(bf16[2,256,256]{2,1,0:T(8,128)(2,1)} %get-tuple-element.16), channel_id=1, source_target_pairs={{0,12},{12,0},{1,13},{13,1},{2,14},{14,2},{3,15},{15,3},{16,28},{2... | collective-permute-start | bytes 786440 | tf_op jit(solution)/shard_map/ppermute | solution.py:236
  102.8 0.1 collective-permute-start.3
  102.9 0.0 copy-start.3
  102.9 1.2 copy-done.3
  104.1 1.2 copy-done.4
  105.4 4.5 %attend_0.1.rest_0_ = bf16[512,1024]{1,0:T(8,128)(2,1)} custom-call(bf16[512,1024]{1,0:T(8,128)(2,1)S(1)} %copy-done.4, bf16[512,1024]{1,0:T(8,128)(2,1)S(1)} %copy-done, bf16[512,1024]{1,0:T(8,128)(2,1)S(1)} %copy-done.1, bf16[2,256,1024]{2,1,0:T(8,128)(2,1)S(1)} %copy-done.3, bf16[2,256,1024]{2,1,0:T(8,128)(2,1)} %collective-permute-done.1.high, ...), custom_call_target="tpu_custom_call" | custom-call | flops 671088640 | bytes 2097152 | tf_op jit(solution)/shard_map/attend_0/pallas_call | solution.py:260
  109.9 4.5 %attend_1.1.rest_0_ = bf16[512,1024]{1,0:T(8,128)(2,1)} custom-call(bf16[512,1024]{1,0:T(8,128)(2,1)S(1)} %copy-done.4, bf16[512,1024]{1,0:T(8,128)(2,1)S(1)} %copy-done, bf16[512,1024]{1,0:T(8,128)(2,1)S(1)} %copy-done.1, bf16[2,256,1024]{2,1,0:T(8,128)(2,1)S(1)} %copy-done.3, ...), custom_call_target="tpu_custom_call", output_to_operand_aliasing={{}: (7, {})} | custom-call | flops 671088640 | bytes 2097152 | tf_op jit(solution)/shard_map/attend_1/pallas_call | solution.py:260
  114.3 6.4 %collective-permute-done.5.relayed = bf16[2,256,256]{2,1,0:T(8,128)(2,1)S(1)} collective-permute-done((bf16[2,256,256]{2,1,0:T(8,128)(2,1)}, bf16[2,256,256]{2,1,0:T(8,128)(2,1)S(1)}, u32[]{:S(2)}, u32[]{:S(2)}) %collective-permute-start.5) | collective-permute-done | bytes 262176 | tf_op jit(solution)/shard_map/ppermute | solution.py:245
  120.7 4.5 %attend_2.1.rest_0_ = bf16[512,1024]{1,0:T(8,128)(2,1)} custom-call(bf16[512,1024]{1,0:T(8,128)(2,1)S(1)} %copy-done.4, bf16[512,1024]{1,0:T(8,128)(2,1)S(1)} %copy-done, bf16[512,1024]{1,0:T(8,128)(2,1)S(1)} %copy-done.1, bf16[2,256,1024]{2,1,0:T(8,128)(2,1)S(1)} %copy-done.3, ...), custom_call_target="tpu_custom_call", output_to_operand_aliasing={{}: (7, {})} | custom-call | flops 671088640 | bytes 2097152 | tf_op jit(solution)/shard_map/attend_2/pallas_call | solution.py:260
  125.2 1.0 collective-permute-done.3.relayed
  126.2 4.5 %attend_3.1 = bf16[512,1024]{1,0:T(8,128)(2,1)} custom-call(bf16[512,1024]{1,0:T(8,128)(2,1)S(1)} %copy-done.4, bf16[512,1024]{1,0:T(8,128)(2,1)S(1)} %copy-done, bf16[512,1024]{1,0:T(8,128)(2,1)S(1)} %copy-done.1, bf16[2,256,1024]{2,1,0:T(8,128)(2,1)S(1)} %copy-done.3, ...), custom_call_target="tpu_custom_call", output_to_operand_aliasing={{}: (7, {})} | custom-call | flops 671088640 | bytes 2097152 | tf_op jit(solution)/shard_map/attend_3/pallas_call | solution.py:260
  (14 shorter events, 0.0 us)
Async XLA Ops:
  2.8 52.2 %collective-permute-start = (bf16[2,256,1024]{2,1,0:T(8,128)(2,1)}, bf16[2,256,1024]{2,1,0:T(8,128)(2,1)S(1)}, u32[]{:S(2)}, u32[]{:S(2)}) collective-permute-start(bf16[2,256,1024]{2,1,0:T(8,128)(2,1)} %pad_maximum_fusion), channel_id=1, source_target_pairs={{0,4},{4,8},{8,12},{1,5},{5,9},{9,13},{2,6},{6,10},{10,14},{3,7},{... | collective-permute-start | bytes 3145736 | tf_op jit(solution)/shard_map/ppermute | solution.py:220
  7.7 2.4 %copy-start.6 = (s32[4,4,2]{1,2,0:T(2,128)S(1)}, s32[4,4,2]{1,2,0:T(2,128)}, u32[]{:S(2)}) copy-start(s32[4,4,2]{1,2,0:T(2,128)} %param.7) | copy-start | bytes 388
  8.8 46.9 %collective-permute-start.1 = (bf16[2,256,1024]{2,1,0:T(8,128)(2,1)}, bf16[2,256,1024]{2,1,0:T(8,128)(2,1)}, u32[]{:S(2)}, u32[]{:S(2)}) collective-permute-start(bf16[2,256,1024]{2,1,0:T(8,128)(2,1)} %pad_maximum_fusion.1), channel_id=1, source_target_pairs={{4,0},{8,4},{12,8},{5,1},{9,5},{13,9},{6,2},{10,6},{14,10},{7,3},{... | collective-permute-start | bytes 3145736 | tf_op jit(solution)/shard_map/ppermute | solution.py:223
  44.7 10.3 %collective-permute-start.2 = (bf16[2,128,1024]{2,1,0:T(8,128)(2,1)}, bf16[2,128,1024]{2,1,0:T(8,128)(2,1)S(1)}, u32[]{:S(2)}, u32[]{:S(2)}) collective-permute-start(bf16[2,128,1024]{2,1,0:T(8,128)(2,1)} %get-tuple-element.14), channel_id=1, source_target_pairs={{4,8},{8,4},{5,9},{9,5},{6,10},{10,6},{7,11},{11,7},{20,24},{24,20... | collective-permute-start | bytes 1572872 | tf_op jit(solution)/shard_map/ppermute | solution.py:235
  45.4 51.6 %collective-permute-start.8 = (bf16[2,256,256]{2,1,0:T(8,128)(2,1)}, bf16[2,256,256]{2,1,0:T(8,128)(2,1)S(1)}, u32[]{:S(2)}, u32[]{:S(2)}) collective-permute-start(bf16[2,256,256]{2,1,0:T(8,128)(2,1)} %get-tuple-element.20), channel_id=1, source_target_pairs={{0,12},{12,0},{1,13},{13,1},{2,14},{14,2},{3,15},{15,3},{16,28},{2... | collective-permute-start | bytes 786440 | tf_op jit(solution)/shard_map/ppermute | solution.py:236
  52.9 50.0 %copy-start = (bf16[512,1024]{1,0:T(8,128)(2,1)S(1)}, bf16[512,1024]{1,0:T(8,128)(2,1)}, u32[]{:S(2)}) copy-start(bf16[512,1024]{1,0:T(8,128)(2,1)} %keys.11) | copy-start | bytes 3145732
  52.9 50.0 %copy-start.1 = (bf16[512,1024]{1,0:T(8,128)(2,1)S(1)}, bf16[512,1024]{1,0:T(8,128)(2,1)}, u32[]{:S(2)}) copy-start(bf16[512,1024]{1,0:T(8,128)(2,1)} %values.11) | copy-start | bytes 3145732
  52.9 44.2 %collective-permute-start.10 = (bf16[2,256,256]{2,1,0:T(8,128)(2,1)}, bf16[2,256,256]{2,1,0:T(8,128)(2,1)}, u32[]{:S(2)}, u32[]{:S(2)}) collective-permute-start(bf16[2,256,256]{2,1,0:T(8,128)(2,1)} %get-tuple-element.22), channel_id=1, source_target_pairs={{0,12},{12,0},{1,13},{13,1},{2,14},{14,2},{3,15},{15,3},{16,28},{2... | collective-permute-start | bytes 786440 | tf_op jit(solution)/shard_map/ppermute | solution.py:236
  55.0 0.8 copy-start.5
  55.7 1.0 copy-start.2
  90.6 12.2 %collective-permute-start.9 = (bf16[2,256,256]{2,1,0:T(8,128)(2,1)}, bf16[2,256,256]{2,1,0:T(8,128)(2,1)S(1)}, u32[]{:S(2)}, u32[]{:S(2)}) collective-permute-start(bf16[2,256,256]{2,1,0:T(8,128)(2,1)} %get-tuple-element.21), channel_id=1, source_target_pairs={{0,8},{12,4},{8,12},{4,0},{1,9},{13,5},{9,13},{5,1},{2,10},{14,6},... | collective-permute-start | bytes 786440 | tf_op jit(solution)/shard_map/ppermute | solution.py:245
  90.7 19.2 %collective-permute-start.7 = (bf16[2,256,256]{2,1,0:T(8,128)(2,1)}, bf16[2,256,256]{2,1,0:T(8,128)(2,1)S(1)}, u32[]{:S(2)}, u32[]{:S(2)}) collective-permute-start(bf16[2,256,256]{2,1,0:T(8,128)(2,1)} %get-tuple-element.19), channel_id=1, source_target_pairs={{0,8},{12,4},{8,12},{4,0},{1,9},{13,5},{9,13},{5,1},{2,10},{14,6},... | collective-permute-start | bytes 786440 | tf_op jit(solution)/shard_map/ppermute | solution.py:245
  95.1 19.3 %collective-permute-start.6 = (bf16[2,256,256]{2,1,0:T(8,128)(2,1)}, bf16[2,256,256]{2,1,0:T(8,128)(2,1)S(1)}, u32[]{:S(2)}, u32[]{:S(2)}) collective-permute-start(bf16[2,256,256]{2,1,0:T(8,128)(2,1)} %get-tuple-element.18), channel_id=1, source_target_pairs={{0,12},{12,0},{1,13},{13,1},{2,14},{14,2},{3,15},{15,3},{16,28},{2... | collective-permute-start | bytes 786440 | tf_op jit(solution)/shard_map/ppermute | solution.py:236
  97.0 23.7 %collective-permute-start.5 = (bf16[2,256,256]{2,1,0:T(8,128)(2,1)}, bf16[2,256,256]{2,1,0:T(8,128)(2,1)S(1)}, u32[]{:S(2)}, u32[]{:S(2)}) collective-permute-start(bf16[2,256,256]{2,1,0:T(8,128)(2,1)} %get-tuple-element.17), channel_id=1, source_target_pairs={{0,8},{12,4},{8,12},{4,0},{1,9},{13,5},{9,13},{5,1},{2,10},{14,6},... | collective-permute-start | bytes 786440 | tf_op jit(solution)/shard_map/ppermute | solution.py:245
  97.1 28.1 %collective-permute-start.4 = (bf16[2,256,256]{2,1,0:T(8,128)(2,1)}, bf16[2,256,256]{2,1,0:T(8,128)(2,1)S(1)}, u32[]{:S(2)}, u32[]{:S(2)}) collective-permute-start(bf16[2,256,256]{2,1,0:T(8,128)(2,1)} %get-tuple-element.16), channel_id=1, source_target_pairs={{0,12},{12,0},{1,13},{13,1},{2,14},{14,2},{3,15},{15,3},{16,28},{2... | collective-permute-start | bytes 786440 | tf_op jit(solution)/shard_map/ppermute | solution.py:236
  102.8 23.4 %collective-permute-start.3 = (bf16[2,256,256]{2,1,0:T(8,128)(2,1)}, bf16[2,256,256]{2,1,0:T(8,128)(2,1)S(1)}, u32[]{:S(2)}, u32[]{:S(2)}) collective-permute-start(bf16[2,256,256]{2,1,0:T(8,128)(2,1)} %get-tuple-element.15), channel_id=1, source_target_pairs={{0,8},{12,4},{8,12},{4,0},{1,9},{13,5},{9,13},{5,1},{2,10},{14,6},... | collective-permute-start | bytes 786440 | tf_op jit(solution)/shard_map/ppermute | solution.py:245
  102.9 1.2 copy-start.3
  104.1 1.2 copy-start.4

commit v2 on v1

--- a/solution.py
+++ b/solution.py
@@ -82,95 +82,53 @@
     return jnp.transpose(result, (1, 0, 2)).reshape(frame_rows, columns)
 
 
-def run_copies(copies):
-    for copy in copies:
-        copy.start()
-    for copy in copies:
-        copy.wait()
-
-
-def pick_kernel(groups, width, bands, keys, values, extra, *rest):
-    direct, sems = rest[:groups], rest[groups]
+def pick_kernel(groups, width, bands, keys, values, extra, edge, *direct):
     frame = lax.axis_index("tm")
     inner = (frame == 1) | (frame == 2)
 
     @pl.when(inner)
     def _():
         block = jnp.where(frame == 1, bands[3, 1, 0], bands[0, 2, 1])
-        run_copies(
-            [
-                pltpu.make_async_copy(src.at[pl.ds(block * BLOCK, BLOCK)], extra.at[kv], sems.at[kv])
-                for kv, src in enumerate((keys, values))
-            ]
-        )
+        rows = pl.ds(pl.multiple_of(block * BLOCK, BLOCK), BLOCK)
+        extra[0] = keys[rows]
+        extra[1] = values[rows]
 
     @pl.when(jnp.logical_not(inner))
     def _():
-        other = 3 - frame
-        copies = []
+        for slot in range(2):
+            to = pl.ds(slot * BLOCK, BLOCK)
+            near = bands[jnp.where(frame == 0, 2, 1), frame, slot]
+            far = bands[3 - frame, frame, slot]
+            near_rows = pl.ds(pl.multiple_of(near * BLOCK, BLOCK), BLOCK)
+            far_rows = pl.ds(pl.multiple_of(far * BLOCK, BLOCK), BLOCK)
+            for kv, source in enumerate((keys, values)):
+                edge[kv, to] = source[near_rows]
+                for g in range(groups):
+                    direct[g][kv, to] = source[far_rows, pl.ds(g * width, width)]
+
+
+def relay_kernel(groups, width, bands, edge, low, high, extra, *relayed):
+    frame = lax.axis_index("tm")
+
+    def hand_on(source, picked):
+        rows = pl.ds(pl.multiple_of(picked * BLOCK, BLOCK), BLOCK)
         for g in range(groups):
-            for kv, src in enumerate((keys, values)):
-                for slot in range(2):
-                    block = bands[other, frame, slot]
-                    copies.append(
-                        pltpu.make_async_copy(
-                            src.at[pl.ds(block * BLOCK, BLOCK), pl.ds(g * width, width)],
-                            direct[g].at[kv, pl.ds(slot * BLOCK, BLOCK)],
-                            sems.at[len(copies)],
-                        )
-                    )
-        run_copies(copies)
-
-
-def relay_kernel(groups, width, bands, keys, values, low, high, extra, *rest):
-    relayed, sems = rest[:groups], rest[groups]
-    frame = lax.axis_index("tm")
-
-    def hand_on(source, picked):
-        copies = []
+            cols = pl.ds(g * width, width)
+            relayed[g][:, pl.ds(0, BLOCK)] = source[:, rows, cols]
+            relayed[g][:, pl.ds(BLOCK, BLOCK)] = extra[:, :, cols]
+
+    @pl.when(frame == 1)
+    def _():
+        hand_on(high, bands[0, 2, 0])
+
+    @pl.when(frame == 2)
+    def _():
+        hand_on(low, bands[3, 1, 1] - 2)
+
+    @pl.when((frame == 0) | (frame == 3))
+    def _():
         for g in range(groups):
-            for kv in range(2):
-                cols = pl.ds(g * width, width)
-                copies.append(
-                    pltpu.make_async_copy(
-                        source.at[kv, pl.ds(picked * BLOCK, BLOCK), cols],
-                        relayed[g].at[kv, pl.ds(0, BLOCK)],
-                        sems.at[len(copies)],
-                    )
-                )
-                copies.append(
-                    pltpu.make_async_copy(
-                        extra.at[kv, :, cols],
-                        relayed[g].at[kv, pl.ds(BLOCK, BLOCK)],
-                        sems.at[len(copies)],
-                    )
-                )
-        run_copies(copies)
-
-    @pl.when(frame == 1)
-    def _():
-        hand_on(high, bands[0, 2, 0])
-
-    @pl.when(frame == 2)
-    def _():
-        hand_on(low, bands[3, 1, 1] - 2)
-
-    @pl.when((frame == 0) | (frame == 3))
-    def _():
-        other = jnp.where(frame == 0, 2, 1)
-        copies = []
-        for g in range(groups):
-            for kv, src in enumerate((keys, values)):
-                for slot in range(2):
-                    block = bands[other, frame, slot]
-                    copies.append(
-                        pltpu.make_async_copy(
-                            src.at[pl.ds(block * BLOCK, BLOCK), pl.ds(g * width, width)],
-                            relayed[g].at[kv, pl.ds(slot * BLOCK, BLOCK)],
-                            sems.at[len(copies)],
-                        )
-                    )
-        run_copies(copies)
+            relayed[g][...] = edge[:, :, pl.ds(g * width, width)]
 
 
 def attend_kernel(chunk, queries, keys, values, low, high, relayed, direct, *rest):
@@ -215,6 +173,7 @@
     width = columns // groups
     group_heads = heads // groups
     anywhere = pl.BlockSpec(memory_space=pl.ANY)
+    local = pl.BlockSpec(memory_space=pltpu.VMEM)
     scalars = pl.BlockSpec(memory_space=pltpu.SMEM)
 
     low = lax.ppermute(
@@ -224,12 +183,16 @@
         jnp.stack([keys[:half], values[:half]], 0), "tm", [(1, 0), (2, 1), (3, 2)]
     )
     pair = jax.ShapeDtypeStruct((2, 2 * BLOCK, width), jnp.bfloat16)
-    extra, *direct = pl.pallas_call(
+    extra, edge, *direct = pl.pallas_call(
         functools.partial(pick_kernel, groups, width),
-        out_shape=[jax.ShapeDtypeStruct((2, BLOCK, columns), jnp.bfloat16)] + [pair] * groups,
-        in_specs=[scalars, anywhere, anywhere],
-        out_specs=[anywhere] * (1 + groups),
-        scratch_shapes=[pltpu.SemaphoreType.DMA((4 * groups,))],
+        out_shape=[
+            jax.ShapeDtypeStruct((2, BLOCK, columns), jnp.bfloat16),
+            jax.ShapeDtypeStruct((2, 2 * BLOCK, columns), jnp.bfloat16),
+        ]
+        + [pair] * groups,
+        in_specs=[scalars, local, local],
+        out_specs=[local] * (2 + groups),
+        compiler_params=pltpu.CompilerParams(vmem_limit_bytes=32 << 20),
         name="pick_blocks",
     )(band_blocks, keys, values)
     extra = lax.ppermute(extra, "tm", [(1, 2), (2, 1)])
@@ -237,11 +200,11 @@
     relayed = pl.pallas_call(
         functools.partial(relay_kernel, groups, width),
         out_shape=[pair] * groups,
-        in_specs=[scalars] + [anywhere] * 5,
-        out_specs=[anywhere] * groups,
-        scratch_shapes=[pltpu.SemaphoreType.DMA((4 * groups,))],
+        in_specs=[scalars] + [local] * 4,
+        out_specs=[local] * groups,
+        compiler_params=pltpu.CompilerParams(vmem_limit_bytes=32 << 20),
         name="relay_blocks",
-    )(band_blocks, keys, values, low, high, extra)
+    )(band_blocks, edge, low, high, extra)
     relayed = [lax.ppermute(part, "tm", [(0, 2), (3, 1), (2, 3), (1, 0)]) for part in relayed]
 
     result = None

time: 131 us -> 99.2 us (0.76)
  Pallas kernels: 85.6 us -> 20 us
  starting transfers between devices: 28.7 us -> 49 us
  waiting for transfers between devices: 7.42 us -> 25.6 us
  local copies, waits for them, and re-layouts: 6.59 us -> 1.86 us
    pallas_call x1, Pallas kernels: 33.8 us -> 0.83 us  [four_frames(): pl.pallas_call(functools.partial(pick_kernel, groups, width), out_shape=[...]
    pallas_call x1, Pallas kernels: 33.9 us -> 1.41 us  [four_frames(): pl.pallas_call(functools.partial(relay_kernel, groups, width), out_shape=...]
    ppermute x4, starting transfers between devices: 4.54 us -> 24.9 us  [four_frames(): lax.ppermute(part, 'tm', [(0, 2), (3, 1), (2, 3), (1, 0)])]
    ppermute x1, waiting for transfers between devices: 0.01 us -> 10.3 us  [four_frames(): lax.ppermute(jnp.stack([keys[half:], values[half:]], 0), 'tm', [(0, 1), (...]
    unnamed x15 -> x9, local copies, waits for them, and re-layouts: 4.9 us -> 0.13 us
    ppermute x1, waiting for transfers between devices: 0.01 us -> 4.13 us  [four_frames(): lax.ppermute(jnp.stack([keys[:half], values[:half]], 0), 'tm', [(1, 0), (...]
    ppermute x4, waiting for transfers between devices: 0.01 us -> 2.26 us  [four_frames(): direct = [lax.ppermute(part, 'tm', [(0, 3), (3, 0)]) for part in direct]]
    ppermute x4, waiting for transfers between devices: 7.41 us -> 8.93 us  [four_frames(): lax.ppermute(part, 'tm', [(0, 2), (3, 1), (2, 3), (1, 0)])]
  transfers between devices with their start and end apart: 11 -> 11, of which waited for: 2 -> 8; matrix products, arithmetic and copies ran while one was open for 1% -> 1% of each run, Pallas kernels for 62% -> 16%
where the time goes in v2:
time: 99.2 us; the launch traced here: 98.8 us
  starting transfers between devices  49 us (49%)
  waiting for transfers between devices  25.6 us (26%)
  Pallas kernels  20 us (20%)
  other arithmetic  2.14 us (2%)
  local copies, waits for them, and re-layouts  1.86 us (2%)
    ppermute x4, starting transfers between devices, four_frames(): lax.ppermute(part, 'tm', [(0, 2), (3, 1), (2, 3), (1, 0)])  24.9 us
    pallas_call x4, Pallas kernels, four_frames(): pl.pallas_call(functools.partial(attend_kernel, rows // 2), grid=(group_h...  17.8 us
    ppermute x4, starting transfers between devices, four_frames(): direct = [lax.ppermute(part, 'tm', [(0, 3), (3, 0)]) for part in direct]  17.1 us
    ppermute x1, waiting for transfers between devices, four_frames(): lax.ppermute(jnp.stack([keys[half:], values[half:]], 0), 'tm', [(0, 1), (...  10.3 us
    ppermute x4, waiting for transfers between devices, four_frames(): lax.ppermute(part, 'tm', [(0, 2), (3, 1), (2, 3), (1, 0)])  8.93 us
    ppermute x1, starting transfers between devices, four_frames(): lax.ppermute(jnp.stack([keys[half:], values[half:]], 0), 'tm', [(0, 1), (...  4.98 us
    ppermute x1, waiting for transfers between devices, four_frames(): lax.ppermute(jnp.stack([keys[:half], values[:half]], 0), 'tm', [(1, 0), (...  4.13 us
    ppermute x4, waiting for transfers between devices, four_frames(): direct = [lax.ppermute(part, 'tm', [(0, 3), (3, 0)]) for part in direct]  2.26 us
  transfers between devices with their start and end apart: 11, of which 8 were waited for; matrix products, arithmetic and copies ran while one was open for 1% of the time, Pallas kernels for 16%

profile of v2, /device:TPU:0, one launch (start us, length us, event | category | flops | bytes accessed | tf_op | source)
XLA Modules:
  0.0 98.8 jit_solution(3434988869023325450)
XLA Ops:
  0.0 1.7 %slice_bitcast_fusion = (bf16[1,256,1024]{2,1,0:T(8,128)(2,1)S(1)}, bf16[1,256,1024]{2,1,0:T(8,128)(2,1)S(1)}, bf16[1,256,1024]{2,1,0:T(8,128)(2,1)S(1)}, bf16[1,256,1024]{2,1,0:T(8,128)(2,1)S(1)}) fusion(bf16[512,1024]{1,0:T(8,128)(2,1)} %values.9, bf16[512,1024]{1,0:T(8,128)(2,1)} %keys.9), kind=kLoop, calls=%fused_computation.2 | loop fusion | bytes 4194304 | tf_op jit(solution)/shard_map/stack | solution.py:183
  1.7 0.0 copy-start.3
  1.8 1.1 %pad_maximum_fusion = bf16[2,256,1024]{2,1,0:T(8,128)(2,1)} fusion(bf16[1,256,1024]{2,1,0:T(8,128)(2,1)S(1)} %get-tuple-element.28, bf16[1,256,1024]{2,1,0:T(8,128)(2,1)S(1)} %get-tuple-element.29), kind=kLoop, calls=%fused_computation | loop fusion | flops 524288 | bytes 2097152 | tf_op jit(solution)/shard_map/stack | solution.py:180
  2.8 5.0 %collective-permute-start = (bf16[2,256,1024]{2,1,0:T(8,128)(2,1)}, bf16[2,256,1024]{2,1,0:T(8,128)(2,1)S(1)}, u32[]{:S(2)}, u32[]{:S(2)}) collective-permute-start(bf16[2,256,1024]{2,1,0:T(8,128)(2,1)} %pad_maximum_fusion), channel_id=1, source_target_pairs={{0,4},{4,8},{8,12},{1,5},{5,9},{9,13},{2,6},{6,10},{10,14},{3,7},{... | collective-permute-start | bytes 3145736 | tf_op jit(solution)/shard_map/ppermute | solution.py:179
  7.8 0.0 copy-start
  7.8 0.0 copy-start.1
  7.8 1.1 %pad_maximum_fusion.1 = bf16[2,256,1024]{2,1,0:T(8,128)(2,1)} fusion(bf16[1,256,1024]{2,1,0:T(8,128)(2,1)S(1)} %get-tuple-element.27, bf16[1,256,1024]{2,1,0:T(8,128)(2,1)S(1)} %get-tuple-element.30), kind=kLoop, calls=%fused_computation.1 | loop fusion | flops 524288 | bytes 2097152 | tf_op jit(solution)/shard_map/stack | solution.py:183
  8.9 1.3 %collective-permute-start.1 = (bf16[2,256,1024]{2,1,0:T(8,128)(2,1)}, bf16[2,256,1024]{2,1,0:T(8,128)(2,1)}, u32[]{:S(2)}, u32[]{:S(2)}) collective-permute-start(bf16[2,256,1024]{2,1,0:T(8,128)(2,1)} %pad_maximum_fusion.1), channel_id=1, source_target_pairs={{4,0},{8,4},{12,8},{5,1},{9,5},{13,9},{6,2},{10,6},{14,10},{7,3},{... | collective-permute-start | bytes 3145736 | tf_op jit(solution)/shard_map/ppermute | solution.py:182
  10.2 0.1 copy.9.bands
  10.3 0.8 pick_blocks.1
  11.2 0.7 collective-permute-start.2
  11.9 7.5 %collective-permute-start.8 = (bf16[2,256,256]{2,1,0:T(8,128)(2,1)S(1)}, bf16[2,256,256]{2,1,0:T(8,128)(2,1)S(1)}, u32[]{:S(2)}, u32[]{:S(2)}) collective-permute-start(bf16[2,256,256]{2,1,0:T(8,128)(2,1)S(1)} %get-tuple-element.22), channel_id=1, source_target_pairs={{0,12},{12,0},{1,13},{13,1},{2,14},{14,2},{3,15},{15,3},{16,28},{2... | collective-permute-start | bytes 786440 | tf_op jit(solution)/shard_map/ppermute | solution.py:199
  19.4 1.9 %collective-permute-start.10 = (bf16[2,256,256]{2,1,0:T(8,128)(2,1)S(1)}, bf16[2,256,256]{2,1,0:T(8,128)(2,1)S(1)}, u32[]{:S(2)}, u32[]{:S(2)}) collective-permute-start(bf16[2,256,256]{2,1,0:T(8,128)(2,1)S(1)} %get-tuple-element.24), channel_id=1, source_target_pairs={{0,12},{12,0},{1,13},{13,1},{2,14},{14,2},{3,15},{15,3},{16,28},{2... | collective-permute-start | bytes 786440 | tf_op jit(solution)/shard_map/ppermute | solution.py:199
  21.3 10.3 %collective-permute-done.low = bf16[2,256,1024]{2,1,0:T(8,128)(2,1)S(1)} collective-permute-done((bf16[2,256,1024]{2,1,0:T(8,128)(2,1)}, bf16[2,256,1024]{2,1,0:T(8,128)(2,1)S(1)}, u32[]{:S(2)}, u32[]{:S(2)}) %collective-permute-start) | collective-permute-done | bytes 1048608 | tf_op jit(solution)/shard_map/ppermute | solution.py:179
  31.6 4.1 %collective-permute-done.1.high = bf16[2,256,1024]{2,1,0:T(8,128)(2,1)} collective-permute-done((bf16[2,256,1024]{2,1,0:T(8,128)(2,1)}, bf16[2,256,1024]{2,1,0:T(8,128)(2,1)}, u32[]{:S(2)}, u32[]{:S(2)}) %collective-permute-start.1) | collective-permute-done | bytes 1048608 | tf_op jit(solution)/shard_map/ppermute | solution.py:182
  35.7 1.4 %relay_blocks.1 = (bf16[2,256,256]{2,1,0:T(8,128)(2,1)S(1)}, bf16[2,256,256]{2,1,0:T(8,128)(2,1)S(1)}, bf16[2,256,256]{2,1,0:T(8,128)(2,1)S(1)}, bf16[2,256,256]{2,1,0:T(8,128)(2,1)S(1)}) custom-call(s32[4,4,2]{2,1,0:T(4,128)S(1)} %copy.9.bands, bf16[2,256,1024]{2,1,0:T(8,128)(2,1)S(1)} %get-tuple-element.15.edge, ...), custom_call_target="tpu_custom_call" | custom-call | tf_op jit(solution)/shard_map/relay_blocks/pallas_call | solution.py:200
  37.1 22.9 %collective-permute-start.9 = (bf16[2,256,256]{2,1,0:T(8,128)(2,1)S(1)}, bf16[2,256,256]{2,1,0:T(8,128)(2,1)S(1)}, u32[]{:S(2)}, u32[]{:S(2)}) collective-permute-start(bf16[2,256,256]{2,1,0:T(8,128)(2,1)S(1)} %get-tuple-element.23), channel_id=1, source_target_pairs={{0,8},{12,4},{8,12},{4,0},{1,9},{13,5},{9,13},{5,1},{2,10},{14,6},... | collective-permute-start | bytes 786440 | tf_op jit(solution)/shard_map/ppermute | solution.py:208
  60.1 0.1 collective-permute-start.7
  60.1 5.3 %collective-permute-start.6 = (bf16[2,256,256]{2,1,0:T(8,128)(2,1)S(1)}, bf16[2,256,256]{2,1,0:T(8,128)(2,1)S(1)}, u32[]{:S(2)}, u32[]{:S(2)}) collective-permute-start(bf16[2,256,256]{2,1,0:T(8,128)(2,1)S(1)} %get-tuple-element.20), channel_id=1, source_target_pairs={{0,12},{12,0},{1,13},{13,1},{2,14},{14,2},{3,15},{15,3},{16,28},{2... | collective-permute-start | bytes 786440 | tf_op jit(solution)/shard_map/ppermute | solution.py:199
  65.4 0.1 collective-permute-start.5
  65.5 2.3 %collective-permute-start.4 = (bf16[2,256,256]{2,1,0:T(8,128)(2,1)S(1)}, bf16[2,256,256]{2,1,0:T(8,128)(2,1)S(1)}, u32[]{:S(2)}, u32[]{:S(2)}) collective-permute-start(bf16[2,256,256]{2,1,0:T(8,128)(2,1)S(1)} %get-tuple-element.18), channel_id=1, source_target_pairs={{0,12},{12,0},{1,13},{13,1},{2,14},{14,2},{3,15},{15,3},{16,28},{2... | collective-permute-start | bytes 786440 | tf_op jit(solution)/shard_map/ppermute | solution.py:199
  67.9 0.4 collective-permute-done.9.relayed
  68.3 1.9 %collective-permute-start.3 = (bf16[2,256,256]{2,1,0:T(8,128)(2,1)S(1)}, bf16[2,256,256]{2,1,0:T(8,128)(2,1)S(1)}, u32[]{:S(2)}, u32[]{:S(2)}) collective-permute-start(bf16[2,256,256]{2,1,0:T(8,128)(2,1)S(1)} %get-tuple-element.17), channel_id=1, source_target_pairs={{0,8},{12,4},{8,12},{4,0},{1,9},{13,5},{9,13},{5,1},{2,10},{14,6},... | collective-permute-start | bytes 786440 | tf_op jit(solution)/shard_map/ppermute | solution.py:208
  70.2 4.4 %attend_0.1.rest_0_ = bf16[512,1024]{1,0:T(8,128)(2,1)} custom-call(bf16[512,1024]{1,0:T(8,128)(2,1)S(1)} %copy-done.2, bf16[512,1024]{1,0:T(8,128)(2,1)S(1)} %copy-done, bf16[512,1024]{1,0:T(8,128)(2,1)S(1)} %copy-done.1, bf16[2,256,1024]{2,1,0:T(8,128)(2,1)S(1)} %collective-permute-done.low, bf16[2,256,1024]{2,1,0:T(8,128)(2,1)} %collective-permute-done.1.high, ...), custom_call_target="tpu_custom_call" | custom-call | flops 671088640 | bytes 2097152 | tf_op jit(solution)/shard_map/attend_0/pallas_call | solution.py:223
  74.7 1.7 %collective-permute-done.7.relayed = bf16[2,256,256]{2,1,0:T(8,128)(2,1)S(1)} collective-permute-done((bf16[2,256,256]{2,1,0:T(8,128)(2,1)S(1)}, bf16[2,256,256]{2,1,0:T(8,128)(2,1)S(1)}, u32[]{:S(2)}, u32[]{:S(2)}) %collective-permute-start.7) | collective-permute-done | bytes 262176 | tf_op jit(solution)/shard_map/ppermute | solution.py:208
  76.3 4.5 %attend_1.1.rest_0_ = bf16[512,1024]{1,0:T(8,128)(2,1)} custom-call(bf16[512,1024]{1,0:T(8,128)(2,1)S(1)} %copy-done.2, bf16[512,1024]{1,0:T(8,128)(2,1)S(1)} %copy-done, bf16[512,1024]{1,0:T(8,128)(2,1)S(1)} %copy-done.1, bf16[2,256,1024]{2,1,0:T(8,128)(2,1)S(1)} %collective-permute-done.low, ...), custom_call_target="tpu_custom_call", output_to_operand_aliasing={{}: (7, {})} | custom-call | flops 671088640 | bytes 2097152 | tf_op jit(solution)/shard_map/attend_1/pallas_call | solution.py:223
  80.8 1.1 %collective-permute-done.6.direct = bf16[2,256,256]{2,1,0:T(8,128)(2,1)S(1)} collective-permute-done((bf16[2,256,256]{2,1,0:T(8,128)(2,1)S(1)}, bf16[2,256,256]{2,1,0:T(8,128)(2,1)S(1)}, u32[]{:S(2)}, u32[]{:S(2)}) %collective-permute-start.6) | collective-permute-done | bytes 262176 | tf_op jit(solution)/shard_map/ppermute | solution.py:199
  81.9 5.7 %collective-permute-done.5.relayed = bf16[2,256,256]{2,1,0:T(8,128)(2,1)S(1)} collective-permute-done((bf16[2,256,256]{2,1,0:T(8,128)(2,1)S(1)}, bf16[2,256,256]{2,1,0:T(8,128)(2,1)S(1)}, u32[]{:S(2)}, u32[]{:S(2)}) %collective-permute-start.5) | collective-permute-done | bytes 262176 | tf_op jit(solution)/shard_map/ppermute | solution.py:208
  87.6 4.4 %attend_2.1.rest_0_ = bf16[512,1024]{1,0:T(8,128)(2,1)} custom-call(bf16[512,1024]{1,0:T(8,128)(2,1)S(1)} %copy-done.2, bf16[512,1024]{1,0:T(8,128)(2,1)S(1)} %copy-done, bf16[512,1024]{1,0:T(8,128)(2,1)S(1)} %copy-done.1, bf16[2,256,1024]{2,1,0:T(8,128)(2,1)S(1)} %collective-permute-done.low, ...), custom_call_target="tpu_custom_call", output_to_operand_aliasing={{}: (7, {})} | custom-call | flops 671088640 | bytes 2097152 | tf_op jit(solution)/shard_map/attend_2/pallas_call | solution.py:223
  92.0 1.1 %collective-permute-done.4.direct = bf16[2,256,256]{2,1,0:T(8,128)(2,1)S(1)} collective-permute-done((bf16[2,256,256]{2,1,0:T(8,128)(2,1)S(1)}, bf16[2,256,256]{2,1,0:T(8,128)(2,1)S(1)}, u32[]{:S(2)}, u32[]{:S(2)}) %collective-permute-start.4) | collective-permute-done | bytes 262176 | tf_op jit(solution)/shard_map/ppermute | solution.py:199
  93.1 1.2 %collective-permute-done.3.relayed = bf16[2,256,256]{2,1,0:T(8,128)(2,1)S(1)} collective-permute-done((bf16[2,256,256]{2,1,0:T(8,128)(2,1)S(1)}, bf16[2,256,256]{2,1,0:T(8,128)(2,1)S(1)}, u32[]{:S(2)}, u32[]{:S(2)}) %collective-permute-start.3) | collective-permute-done | bytes 262176 | tf_op jit(solution)/shard_map/ppermute | solution.py:208
  94.3 4.5 %attend_3.1 = bf16[512,1024]{1,0:T(8,128)(2,1)} custom-call(bf16[512,1024]{1,0:T(8,128)(2,1)S(1)} %copy-done.2, bf16[512,1024]{1,0:T(8,128)(2,1)S(1)} %copy-done, bf16[512,1024]{1,0:T(8,128)(2,1)S(1)} %copy-done.1, bf16[2,256,1024]{2,1,0:T(8,128)(2,1)S(1)} %collective-permute-done.low, ...), custom_call_target="tpu_custom_call", output_to_operand_aliasing={{}: (7, {})} | custom-call | flops 671088640 | bytes 2097152 | tf_op jit(solution)/shard_map/attend_3/pallas_call | solution.py:223
  (8 shorter events, 0.0 us)
Async XLA Ops:
  1.7 8.5 %copy-start.3 = (s32[4,4,2]{1,2,0:T(2,128)S(1)}, s32[4,4,2]{1,2,0:T(2,128)}, u32[]{:S(2)}) copy-start(s32[4,4,2]{1,2,0:T(2,128)} %param.7) | copy-start | bytes 388
  2.8 28.8 %collective-permute-start = (bf16[2,256,1024]{2,1,0:T(8,128)(2,1)}, bf16[2,256,1024]{2,1,0:T(8,128)(2,1)S(1)}, u32[]{:S(2)}, u32[]{:S(2)}) collective-permute-start(bf16[2,256,1024]{2,1,0:T(8,128)(2,1)} %pad_maximum_fusion), channel_id=1, source_target_pairs={{0,4},{4,8},{8,12},{1,5},{5,9},{9,13},{2,6},{6,10},{10,14},{3,7},{... | collective-permute-start | bytes 3145736 | tf_op jit(solution)/shard_map/ppermute | solution.py:179
  7.8 2.5 %copy-start = (bf16[512,1024]{1,0:T(8,128)(2,1)S(1)}, bf16[512,1024]{1,0:T(8,128)(2,1)}, u32[]{:S(2)}) copy-start(bf16[512,1024]{1,0:T(8,128)(2,1)} %keys.9) | copy-start | bytes 3145732
  7.8 2.5 %copy-start.1 = (bf16[512,1024]{1,0:T(8,128)(2,1)S(1)}, bf16[512,1024]{1,0:T(8,128)(2,1)}, u32[]{:S(2)}) copy-start(bf16[512,1024]{1,0:T(8,128)(2,1)} %values.9) | copy-start | bytes 3145732
  8.9 26.8 %collective-permute-start.1 = (bf16[2,256,1024]{2,1,0:T(8,128)(2,1)}, bf16[2,256,1024]{2,1,0:T(8,128)(2,1)}, u32[]{:S(2)}, u32[]{:S(2)}) collective-permute-start(bf16[2,256,1024]{2,1,0:T(8,128)(2,1)} %pad_maximum_fusion.1), channel_id=1, source_target_pairs={{4,0},{8,4},{12,8},{5,1},{9,5},{13,9},{6,2},{10,6},{14,10},{7,3},{... | collective-permute-start | bytes 3145736 | tf_op jit(solution)/shard_map/ppermute | solution.py:182
  11.2 10.1 %collective-permute-start.2 = (bf16[2,128,1024]{2,1,0:T(8,128)(2,1)S(1)}, bf16[2,128,1024]{2,1,0:T(8,128)(2,1)S(1)}, u32[]{:S(2)}, u32[]{:S(2)}) collective-permute-start(bf16[2,128,1024]{2,1,0:T(8,128)(2,1)S(1)} %get-tuple-element.16), channel_id=1, source_target_pairs={{4,8},{8,4},{5,9},{9,5},{6,10},{10,6},{7,11},{11,7},{20,24},{24,20... | collective-permute-start | bytes 1572872 | tf_op jit(solution)/shard_map/ppermute | solution.py:198
  11.9 53.6 %collective-permute-start.8 = (bf16[2,256,256]{2,1,0:T(8,128)(2,1)S(1)}, bf16[2,256,256]{2,1,0:T(8,128)(2,1)S(1)}, u32[]{:S(2)}, u32[]{:S(2)}) collective-permute-start(bf16[2,256,256]{2,1,0:T(8,128)(2,1)S(1)} %get-tuple-element.22), channel_id=1, source_target_pairs={{0,12},{12,0},{1,13},{13,1},{2,14},{14,2},{3,15},{15,3},{16,28},{2... | collective-permute-start | bytes 786440 | tf_op jit(solution)/shard_map/ppermute | solution.py:199
  19.4 46.1 %collective-permute-start.10 = (bf16[2,256,256]{2,1,0:T(8,128)(2,1)S(1)}, bf16[2,256,256]{2,1,0:T(8,128)(2,1)S(1)}, u32[]{:S(2)}, u32[]{:S(2)}) collective-permute-start(bf16[2,256,256]{2,1,0:T(8,128)(2,1)S(1)} %get-tuple-element.24), channel_id=1, source_target_pairs={{0,12},{12,0},{1,13},{13,1},{2,14},{14,2},{3,15},{15,3},{16,28},{2... | collective-permute-start | bytes 786440 | tf_op jit(solution)/shard_map/ppermute | solution.py:199
  35.7 34.5 %copy-start.2 = (bf16[512,1024]{1,0:T(8,128)(2,1)S(1)}, bf16[512,1024]{1,0:T(8,128)(2,1)}, u32[]{:S(2)}) copy-start(bf16[512,1024]{1,0:T(8,128)(2,1)} %queries.7) | copy-start | bytes 3145732
  37.1 31.2 %collective-permute-start.9 = (bf16[2,256,256]{2,1,0:T(8,128)(2,1)S(1)}, bf16[2,256,256]{2,1,0:T(8,128)(2,1)S(1)}, u32[]{:S(2)}, u32[]{:S(2)}) collective-permute-start(bf16[2,256,256]{2,1,0:T(8,128)(2,1)S(1)} %get-tuple-element.23), channel_id=1, source_target_pairs={{0,8},{12,4},{8,12},{4,0},{1,9},{13,5},{9,13},{5,1},{2,10},{14,6},... | collective-permute-start | bytes 786440 | tf_op jit(solution)/shard_map/ppermute | solution.py:208
  60.1 16.3 %collective-permute-start.7 = (bf16[2,256,256]{2,1,0:T(8,128)(2,1)S(1)}, bf16[2,256,256]{2,1,0:T(8,128)(2,1)S(1)}, u32[]{:S(2)}, u32[]{:S(2)}) collective-permute-start(bf16[2,256,256]{2,1,0:T(8,128)(2,1)S(1)} %get-tuple-element.21), channel_id=1, source_target_pairs={{0,8},{12,4},{8,12},{4,0},{1,9},{13,5},{9,13},{5,1},{2,10},{14,6},... | collective-permute-start | bytes 786440 | tf_op jit(solution)/shard_map/ppermute | solution.py:208
  60.1 21.8 %collective-permute-start.6 = (bf16[2,256,256]{2,1,0:T(8,128)(2,1)S(1)}, bf16[2,256,256]{2,1,0:T(8,128)(2,1)S(1)}, u32[]{:S(2)}, u32[]{:S(2)}) collective-permute-start(bf16[2,256,256]{2,1,0:T(8,128)(2,1)S(1)} %get-tuple-element.20), channel_id=1, source_target_pairs={{0,12},{12,0},{1,13},{13,1},{2,14},{14,2},{3,15},{15,3},{16,28},{2... | collective-permute-start | bytes 786440 | tf_op jit(solution)/shard_map/ppermute | solution.py:199
  65.4 22.1 %collective-permute-start.5 = (bf16[2,256,256]{2,1,0:T(8,128)(2,1)S(1)}, bf16[2,256,256]{2,1,0:T(8,128)(2,1)S(1)}, u32[]{:S(2)}, u32[]{:S(2)}) collective-permute-start(bf16[2,256,256]{2,1,0:T(8,128)(2,1)S(1)} %get-tuple-element.19), channel_id=1, source_target_pairs={{0,8},{12,4},{8,12},{4,0},{1,9},{13,5},{9,13},{5,1},{2,10},{14,6},... | collective-permute-start | bytes 786440 | tf_op jit(solution)/shard_map/ppermute | solution.py:208
  65.5 27.6 %collective-permute-start.4 = (bf16[2,256,256]{2,1,0:T(8,128)(2,1)S(1)}, bf16[2,256,256]{2,1,0:T(8,128)(2,1)S(1)}, u32[]{:S(2)}, u32[]{:S(2)}) collective-permute-start(bf16[2,256,256]{2,1,0:T(8,128)(2,1)S(1)} %get-tuple-element.18), channel_id=1, source_target_pairs={{0,12},{12,0},{1,13},{13,1},{2,14},{14,2},{3,15},{15,3},{16,28},{2... | collective-permute-start | bytes 786440 | tf_op jit(solution)/shard_map/ppermute | solution.py:199
  68.3 26.0 %collective-permute-start.3 = (bf16[2,256,256]{2,1,0:T(8,128)(2,1)S(1)}, bf16[2,256,256]{2,1,0:T(8,128)(2,1)S(1)}, u32[]{:S(2)}, u32[]{:S(2)}) collective-permute-start(bf16[2,256,256]{2,1,0:T(8,128)(2,1)S(1)} %get-tuple-element.17), channel_id=1, source_target_pairs={{0,8},{12,4},{8,12},{4,0},{1,9},{13,5},{9,13},{5,1},{2,10},{14,6},... | collective-permute-start | bytes 786440 | tf_op jit(solution)/shard_map/ppermute | solution.py:208

commit v3 on v2

--- a/solution.py
+++ b/solution.py
@@ -82,7 +82,19 @@
     return jnp.transpose(result, (1, 0, 2)).reshape(frame_rows, columns)
 
 
-def pick_kernel(groups, width, bands, keys, values, extra, edge, *direct):
+def near_kernel(half, keys, values, up, down, sems):
+    copies = [
+        pltpu.make_async_copy(source.at[pl.ds(start, half)], target.at[kv], sems.at[way, kv])
+        for way, (target, start) in enumerate(((up, half), (down, 0)))
+        for kv, source in enumerate((keys, values))
+    ]
+    for copy in copies:
+        copy.start()
+    for copy in copies:
+        copy.wait()
+
+
+def pick_kernel(cuts, bands, keys, values, extra, *far):
     frame = lax.axis_index("tm")
     inner = (frame == 1) | (frame == 2)
 
@@ -95,27 +107,25 @@
 
     @pl.when(jnp.logical_not(inner))
     def _():
-        for slot in range(2):
-            to = pl.ds(slot * BLOCK, BLOCK)
-            near = bands[jnp.where(frame == 0, 2, 1), frame, slot]
-            far = bands[3 - frame, frame, slot]
-            near_rows = pl.ds(pl.multiple_of(near * BLOCK, BLOCK), BLOCK)
-            far_rows = pl.ds(pl.multiple_of(far * BLOCK, BLOCK), BLOCK)
-            for kv, source in enumerate((keys, values)):
-                edge[kv, to] = source[near_rows]
-                for g in range(groups):
-                    direct[g][kv, to] = source[far_rows, pl.ds(g * width, width)]
-
-
-def relay_kernel(groups, width, bands, edge, low, high, extra, *relayed):
+        for target, parts in enumerate((far[: len(cuts)], far[len(cuts) :])):
+            reader = jnp.where(frame == 0, 2 + target, 1 - target)
+            for slot in range(2):
+                block = bands[reader, frame, slot]
+                rows = pl.ds(pl.multiple_of(block * BLOCK, BLOCK), BLOCK)
+                for part, (first, size) in zip(parts, cuts):
+                    for kv, source in enumerate((keys, values)):
+                        part[kv, pl.ds(slot * BLOCK, BLOCK)] = source[rows, pl.ds(first, size)]
+
+
+def relay_kernel(cuts, bands, low, high, extra, *relayed):
     frame = lax.axis_index("tm")
 
     def hand_on(source, picked):
         rows = pl.ds(pl.multiple_of(picked * BLOCK, BLOCK), BLOCK)
-        for g in range(groups):
-            cols = pl.ds(g * width, width)
-            relayed[g][:, pl.ds(0, BLOCK)] = source[:, rows, cols]
-            relayed[g][:, pl.ds(BLOCK, BLOCK)] = extra[:, :, cols]
+        for part, (first, size) in zip(relayed, cuts):
+            cols = pl.ds(first, size)
+            part[:, pl.ds(0, BLOCK)] = source[:, rows, cols]
+            part[:, pl.ds(BLOCK, BLOCK)] = extra[:, :, cols]
 
     @pl.when(frame == 1)
     def _():
@@ -125,13 +135,8 @@
     def _():
         hand_on(low, bands[3, 1, 1] - 2)
 
-    @pl.when((frame == 0) | (frame == 3))
-    def _():
-        for g in range(groups):
-            relayed[g][...] = edge[:, :, pl.ds(g * width, width)]
-
-
-def attend_kernel(chunk, queries, keys, values, low, high, relayed, direct, *rest):
+
+def attend_kernel(chunk, queries, keys, values, low, high, relayed, crossed, direct, *rest):
     out = rest[-1]
     frame = lax.axis_index("tm")
     first = frame == 0
@@ -143,7 +148,7 @@
                 own[...],
                 jnp.where(first, high[kv], low[kv]),
                 jnp.where(edge, direct[kv], high[kv]),
-                relayed[kv],
+                jnp.where(edge, relayed[kv], crossed[kv]),
             ],
             0,
         )
@@ -169,51 +174,58 @@
     rows, columns = queries.shape
     half = rows // 2
     heads = columns // HD
-    groups = 4 if heads % 4 == 0 else 1
-    width = columns // groups
-    group_heads = heads // groups
+    last = heads // 4
+    cuts = ((0, (heads - last) * HD), ((heads - last) * HD, last * HD)) if last else ((0, columns),)
     anywhere = pl.BlockSpec(memory_space=pl.ANY)
     local = pl.BlockSpec(memory_space=pltpu.VMEM)
     scalars = pl.BlockSpec(memory_space=pltpu.SMEM)
-
-    low = lax.ppermute(
-        jnp.stack([keys[half:], values[half:]], 0), "tm", [(0, 1), (1, 2), (2, 3)]
-    )
-    high = lax.ppermute(
-        jnp.stack([keys[:half], values[:half]], 0), "tm", [(1, 0), (2, 1), (3, 2)]
-    )
-    pair = jax.ShapeDtypeStruct((2, 2 * BLOCK, width), jnp.bfloat16)
-    extra, edge, *direct = pl.pallas_call(
-        functools.partial(pick_kernel, groups, width),
-        out_shape=[
-            jax.ShapeDtypeStruct((2, BLOCK, columns), jnp.bfloat16),
-            jax.ShapeDtypeStruct((2, 2 * BLOCK, columns), jnp.bfloat16),
-        ]
-        + [pair] * groups,
+    roomy = pltpu.CompilerParams(vmem_limit_bytes=32 << 20)
+
+    def send(array, pairs):
+        return lax.ppermute(array, "tm", pairs)
+
+    near = jax.ShapeDtypeStruct((2, half, columns), jnp.bfloat16)
+    up, down = pl.pallas_call(
+        functools.partial(near_kernel, half),
+        out_shape=[near] * 2,
+        in_specs=[pl.BlockSpec(memory_space=pltpu.HBM)] * 2,
+        out_specs=[local] * 2,
+        scratch_shapes=[pltpu.SemaphoreType.DMA((2, 2))],
+        compiler_params=roomy,
+        name="near_halves",
+    )(keys, values)
+    low = send(up, [(0, 1), (1, 2), (2, 3)])
+    high = send(down, [(1, 0), (2, 1), (3, 2)])
+    parts = [jax.ShapeDtypeStruct((2, half, size), jnp.bfloat16) for _, size in cuts]
+    extra, *far = pl.pallas_call(
+        functools.partial(pick_kernel, cuts),
+        out_shape=[jax.ShapeDtypeStruct((2, BLOCK, columns), jnp.bfloat16)] + parts + parts,
         in_specs=[scalars, local, local],
-        out_specs=[local] * (2 + groups),
-        compiler_params=pltpu.CompilerParams(vmem_limit_bytes=32 << 20),
+        out_specs=[local] * (1 + 2 * len(cuts)),
+        compiler_params=roomy,
         name="pick_blocks",
     )(band_blocks, keys, values)
-    extra = lax.ppermute(extra, "tm", [(1, 2), (2, 1)])
-    direct = [lax.ppermute(part, "tm", [(0, 3), (3, 0)]) for part in direct]
+    extra = send(extra, [(1, 2), (2, 1)])
+    crossed = [send(part, [(0, 2), (3, 1)]) for part in far[: len(cuts)]]
+    direct = [send(part, [(0, 3), (3, 0)]) for part in far[len(cuts) :]]
     relayed = pl.pallas_call(
-        functools.partial(relay_kernel, groups, width),
-        out_shape=[pair] * groups,
-        in_specs=[scalars] + [local] * 4,
-        out_specs=[local] * groups,
-        compiler_params=pltpu.CompilerParams(vmem_limit_bytes=32 << 20),
+        functools.partial(relay_kernel, cuts),
+        out_shape=parts,
+        in_specs=[scalars] + [local] * 3,
+        out_specs=[local] * len(cuts),
+        compiler_params=roomy,
         name="relay_blocks",
-    )(band_blocks, edge, low, high, extra)
-    relayed = [lax.ppermute(part, "tm", [(0, 2), (3, 1), (2, 3), (1, 0)]) for part in relayed]
+    )(band_blocks, low, high, extra)
+    relayed = [send(part, [(2, 3), (1, 0)]) for part in relayed]
 
     result = None
-    for g in range(groups):
-        own = pl.BlockSpec((rows, HD), lambda h, g=g: (0, g * group_heads + h))
-        near = pl.BlockSpec((2, half, HD), lambda h, g=g: (0, 0, g * group_heads + h))
-        far = pl.BlockSpec((2, half, HD), lambda h: (0, 0, h))
-        in_specs = [own, own, own, near, near, far, far]
-        operands = [queries, keys, values, low, high, relayed[g], direct[g]]
+    for g, (first, size) in enumerate(cuts):
+        skip = first // HD
+        own = pl.BlockSpec((rows, HD), lambda h, skip=skip: (0, skip + h))
+        beside = pl.BlockSpec((2, half, HD), lambda h, skip=skip: (0, 0, skip + h))
+        away = pl.BlockSpec((2, half, HD), lambda h: (0, 0, h))
+        in_specs = [own] * 3 + [beside] * 2 + [away] * 3
+        operands = [queries, keys, values, low, high, relayed[g], crossed[g], direct[g]]
         aliases = {}
         if result is not None:
             aliases = {len(operands): 0}
@@ -222,16 +234,16 @@
         seen = rows + 3 * half
         result = pl.pallas_call(
             functools.partial(attend_kernel, rows // 2),
-            grid=(group_heads,),
+            grid=(size // HD,),
             out_shape=jax.ShapeDtypeStruct(queries.shape, queries.dtype),
             in_specs=in_specs,
             out_specs=own,
             input_output_aliases=aliases,
-            compiler_params=pltpu.CompilerParams(vmem_limit_bytes=32 << 20),
+            compiler_params=roomy,
             cost_estimate=pl.CostEstimate(
-                flops=4 * group_heads * rows * seen * HD,
-                bytes_accessed=2 * width * (2 * rows + 2 * (rows + 4 * half)),
-                transcendentals=group_heads * rows * seen,
+                flops=4 * size * rows * seen,
+                bytes_accessed=2 * size * (2 * rows + 2 * (rows + 5 * half)),
+                transcendentals=size // HD * rows * seen,
             ),
             name=f"attend_{g}",
         )(*operands)

time: 99.2 us -> 125 us (1.26)
  starting transfers between devices: 49 us -> 73.9 us
  waiting for transfers between devices: 25.6 us -> 28 us
  other arithmetic: 2.14 us -> 0 us
  local copies, waits for them, and re-layouts: 1.86 us -> 3.26 us
    ppermute x11 -> x9, starting transfers between devices: 49 us -> 73.9 us  [send(): return lax.ppermute(array, 'tm', pairs)]
    unnamed x9 -> x11, local copies, waits for them, and re-layouts: 0.13 us -> 3.26 us
    ppermute x11 -> x9, waiting for transfers between devices: 25.6 us -> 28 us  [send(): return lax.ppermute(array, 'tm', pairs)]
    another operation x2 -> x0, other arithmetic: 2.14 us -> none  [the longest x1 1.08 us: four_frames(): jnp.stack([keys[:half], values[:half]], 0)]
    another operation x1 -> x0, local copies, waits for them, and re-layouts: 1.73 us -> none  [four_frames(): jnp.stack([keys[:half], values[:half]], 0)]
    pallas_call x6 -> x5, Pallas kernels: 20 us -> 18.8 us  [the longest x2 15.3 us: four_frames(): pl.pallas_call(functools.partial(attend_kernel, rows // 2), grid=(size //...]
  transfers between devices with their start and end apart: 11 -> 9, of which waited for: 8 -> 3; matrix products, arithmetic and copies ran while one was open for 1% -> 1% of each run, Pallas kernels for 16% -> 10%
where the time goes in v3:
time: 125 us; the launch traced here: 124 us
  starting transfers between devices  73.9 us (59%)
  waiting for transfers between devices  28 us (22%)
  Pallas kernels  18.8 us (15%)
  local copies, waits for them, and re-layouts  3.26 us (3%)
    ppermute x9, starting transfers between devices, send(): return lax.ppermute(array, 'tm', pairs)  73.9 us
    ppermute x9, waiting for transfers between devices, send(): return lax.ppermute(array, 'tm', pairs)  28 us
    pallas_call x2, Pallas kernels, four_frames(): pl.pallas_call(functools.partial(attend_kernel, rows // 2), grid=(size //...  15.3 us
    unnamed x11, local copies, waits for them, and re-layouts  3.26 us
  transfers between devices with their start and end apart: 9, of which 3 were waited for; matrix products, arithmetic and copies ran while one was open for 1% of the time, Pallas kernels for 10%

profile of v3, /device:TPU:0, one launch (start us, length us, event | category | flops | bytes accessed | tf_op | source)
XLA Modules:
  0.0 124.1 jit_solution(17832623889759318238)
XLA Ops:
  0.0 0.0 copy-start
  0.0 1.2 copy-done
  1.2 0.0 copy-start.2
  1.2 1.2 copy-done.2
  2.5 1.5 %near_halves.1 = (bf16[2,256,1024]{2,1,0:T(8,128)(2,1)}, bf16[2,256,1024]{2,1,0:T(8,128)(2,1)}) custom-call(bf16[512,1024]{1,0:T(8,128)(2,1)S(1)} %copy-done, bf16[512,1024]{1,0:T(8,128)(2,1)S(1)} %copy-done.2), custom_call_target="tpu_custom_call" | custom-call | tf_op jit(solution)/shard_map/near_halves/pallas_call | solution.py:188
  4.0 5.0 %collective-permute-start = (bf16[2,256,1024]{2,1,0:T(8,128)(2,1)}, bf16[2,256,1024]{2,1,0:T(8,128)(2,1)S(1)}, u32[]{:S(2)}, u32[]{:S(2)}) collective-permute-start(bf16[2,256,1024]{2,1,0:T(8,128)(2,1)} %get-tuple-element.14), channel_id=1, source_target_pairs={{0,4},{4,8},{8,12},{1,5},{5,9},{9,13},{2,6},{6,10},{10,14},{3,7},{... | collective-permute-start | bytes 3145736 | tf_op jit(solution)/shard_map/ppermute | solution.py:185
  9.0 1.3 %collective-permute-start.1 = (bf16[2,256,1024]{2,1,0:T(8,128)(2,1)}, bf16[2,256,1024]{2,1,0:T(8,128)(2,1)}, u32[]{:S(2)}, u32[]{:S(2)}) collective-permute-start(bf16[2,256,1024]{2,1,0:T(8,128)(2,1)} %get-tuple-element.15), channel_id=1, source_target_pairs={{4,0},{8,4},{12,8},{5,1},{9,5},{13,9},{6,2},{10,6},{14,10},{7,3},{... | collective-permute-start | bytes 3145736 | tf_op jit(solution)/shard_map/ppermute | solution.py:185
  10.3 0.8 copy.7.bands
  11.1 0.0 copy-done.1
  11.1 0.0 copy-done.3
  11.1 0.8 pick_blocks.1
  11.9 0.7 collective-permute-start.2
  12.6 7.2 %collective-permute-start.7 = (bf16[2,256,768]{2,1,0:T(8,128)(2,1)S(1)}, bf16[2,256,768]{2,1,0:T(8,128)(2,1)S(1)}, u32[]{:S(2)}, u32[]{:S(2)}) collective-permute-start(bf16[2,256,768]{2,1,0:T(8,128)(2,1)S(1)} %get-tuple-element.21), channel_id=1, source_target_pairs={{0,8},{12,4},{1,9},{13,5},{2,10},{14,6},{3,11},{15,7},{16,24},{28,... | collective-permute-start | bytes 2359304 | tf_op jit(solution)/shard_map/ppermute | solution.py:185
  19.8 0.0 copy-start.4
  19.8 4.5 %collective-permute-start.8 = (bf16[2,256,768]{2,1,0:T(8,128)(2,1)S(1)}, bf16[2,256,768]{2,1,0:T(8,128)(2,1)S(1)}, u32[]{:S(2)}, u32[]{:S(2)}) collective-permute-start(bf16[2,256,768]{2,1,0:T(8,128)(2,1)S(1)} %get-tuple-element.22), channel_id=1, source_target_pairs={{0,12},{12,0},{1,13},{13,1},{2,14},{14,2},{3,15},{15,3},{16,28},{2... | collective-permute-start | bytes 2359304 | tf_op jit(solution)/shard_map/ppermute | solution.py:185
  24.3 0.0 collective-permute-done.2.extra
  24.3 8.5 %collective-permute-done.low = bf16[2,256,1024]{2,1,0:T(8,128)(2,1)S(1)} collective-permute-done((bf16[2,256,1024]{2,1,0:T(8,128)(2,1)}, bf16[2,256,1024]{2,1,0:T(8,128)(2,1)S(1)}, u32[]{:S(2)}, u32[]{:S(2)}) %collective-permute-start) | collective-permute-done | bytes 1048608 | tf_op jit(solution)/shard_map/ppermute | solution.py:185
  32.8 3.0 %collective-permute-done.1.high = bf16[2,256,1024]{2,1,0:T(8,128)(2,1)} collective-permute-done((bf16[2,256,1024]{2,1,0:T(8,128)(2,1)}, bf16[2,256,1024]{2,1,0:T(8,128)(2,1)}, u32[]{:S(2)}, u32[]{:S(2)}) %collective-permute-start.1) | collective-permute-done | bytes 1048608 | tf_op jit(solution)/shard_map/ppermute | solution.py:185
  35.8 1.3 %relay_blocks.1 = (bf16[2,256,768]{2,1,0:T(8,128)(2,1)S(1)}, bf16[2,256,256]{2,1,0:T(8,128)(2,1)S(1)}) custom-call(s32[4,4,2]{2,1,0:T(4,128)S(1)} %copy.7.bands, bf16[2,256,1024]{2,1,0:T(8,128)(2,1)S(1)} %collective-permute-done.low, bf16[2,256,1024]{2,1,0:T(8,128)(2,1)} %collective-permute-done.1.high, bf16[2,128,1024]{2,1,0:T(8,128)(2,1)S(1)} %collective-permute-done.2.extra), custom_call_target="tpu_custom_call" | custom-call | tf_op jit(solution)/shard_map/relay_blocks/pallas_call | solution.py:211
  37.1 1.3 %collective-permute-start.6 = (bf16[2,256,768]{2,1,0:T(8,128)(2,1)S(1)}, bf16[2,256,768]{2,1,0:T(8,128)(2,1)S(1)}, u32[]{:S(2)}, u32[]{:S(2)}) collective-permute-start(bf16[2,256,768]{2,1,0:T(8,128)(2,1)S(1)} %get-tuple-element.20), channel_id=1, source_target_pairs={{8,12},{4,0},{9,13},{5,1},{10,14},{6,2},{11,15},{7,3},{24,28},{20,... | collective-permute-start | bytes 2359304 | tf_op jit(solution)/shard_map/ppermute | solution.py:185
  38.4 47.4 %collective-permute-start.4 = (bf16[2,256,256]{2,1,0:T(8,128)(2,1)S(1)}, bf16[2,256,256]{2,1,0:T(8,128)(2,1)S(1)}, u32[]{:S(2)}, u32[]{:S(2)}) collective-permute-start(bf16[2,256,256]{2,1,0:T(8,128)(2,1)S(1)} %get-tuple-element.18), channel_id=1, source_target_pairs={{0,8},{12,4},{1,9},{13,5},{2,10},{14,6},{3,11},{15,7},{16,24},{28,... | collective-permute-start | bytes 786440 | tf_op jit(solution)/shard_map/ppermute | solution.py:185
  85.8 5.3 %collective-permute-start.5 = (bf16[2,256,256]{2,1,0:T(8,128)(2,1)S(1)}, bf16[2,256,256]{2,1,0:T(8,128)(2,1)S(1)}, u32[]{:S(2)}, u32[]{:S(2)}) collective-permute-start(bf16[2,256,256]{2,1,0:T(8,128)(2,1)S(1)} %get-tuple-element.19), channel_id=1, source_target_pairs={{0,12},{12,0},{1,13},{13,1},{2,14},{14,2},{3,15},{15,3},{16,28},{2... | collective-permute-start | bytes 786440 | tf_op jit(solution)/shard_map/ppermute | solution.py:185
  91.1 0.0 collective-permute-done.7.crossed
  91.1 1.3 %collective-permute-start.3 = (bf16[2,256,256]{2,1,0:T(8,128)(2,1)S(1)}, bf16[2,256,256]{2,1,0:T(8,128)(2,1)S(1)}, u32[]{:S(2)}, u32[]{:S(2)}) collective-permute-start(bf16[2,256,256]{2,1,0:T(8,128)(2,1)S(1)} %get-tuple-element.17), channel_id=1, source_target_pairs={{8,12},{4,0},{9,13},{5,1},{10,14},{6,2},{11,15},{7,3},{24,28},{20,... | collective-permute-start | bytes 786440 | tf_op jit(solution)/shard_map/ppermute | solution.py:185
  92.4 0.0 collective-permute-done.8.direct
  92.4 16.5 %collective-permute-done.6.relayed = bf16[2,256,768]{2,1,0:T(8,128)(2,1)S(1)} collective-permute-done((bf16[2,256,768]{2,1,0:T(8,128)(2,1)S(1)}, bf16[2,256,768]{2,1,0:T(8,128)(2,1)S(1)}, u32[]{:S(2)}, u32[]{:S(2)}) %collective-permute-start.6) | collective-permute-done | bytes 786464 | tf_op jit(solution)/shard_map/ppermute | solution.py:185
  108.8 0.0 copy-done.4
  108.9 10.8 %attend_0.1.rest_0_ = bf16[512,1024]{1,0:T(8,128)(2,1)} custom-call(bf16[512,1024]{1,0:T(8,128)(2,1)S(1)} %copy-done.4, bf16[512,1024]{1,0:T(8,128)(2,1)S(1)} %copy-done.1, bf16[512,1024]{1,0:T(8,128)(2,1)S(1)} %copy-done.3, bf16[2,256,1024]{2,1,0:T(8,128)(2,1)S(1)} %collective-permute-done.low, bf16[2,256,1024]{2,1,0:T(8,128)(2,1)} %collective-permute-done.1.high, ...), custom_call_target="tpu_custom_call" | custom-call | flops 2013265920 | bytes 7077888 | tf_op jit(solution)/shard_map/attend_0/pallas_call | solution.py:235
  119.6 0.0 collective-permute-done.4.crossed
  119.6 0.0 collective-permute-done.5.direct
  119.6 0.0 collective-permute-done.3.relayed
  119.7 4.5 %attend_1.1 = bf16[512,1024]{1,0:T(8,128)(2,1)} custom-call(bf16[512,1024]{1,0:T(8,128)(2,1)S(1)} %copy-done.4, bf16[512,1024]{1,0:T(8,128)(2,1)S(1)} %copy-done.1, bf16[512,1024]{1,0:T(8,128)(2,1)S(1)} %copy-done.3, bf16[2,256,1024]{2,1,0:T(8,128)(2,1)S(1)} %collective-permute-done.low, ...), custom_call_target="tpu_custom_call", output_to_operand_aliasing={{}: (8, {})} | custom-call | flops 671088640 | bytes 2359296 | tf_op jit(solution)/shard_map/attend_1/pallas_call | solution.py:235
  (2 shorter events, 0.0 us)
Async XLA Ops:
  0.0 1.2 copy-start
  1.2 1.2 copy-start.2
  2.5 8.6 %copy-start.1 = (bf16[512,1024]{1,0:T(8,128)(2,1)S(1)}, bf16[512,1024]{1,0:T(8,128)(2,1)}, u32[]{:S(2)}) copy-start(bf16[512,1024]{1,0:T(8,128)(2,1)} %keys.7) | copy-start | bytes 3145732
  2.5 8.6 %copy-start.3 = (bf16[512,1024]{1,0:T(8,128)(2,1)S(1)}, bf16[512,1024]{1,0:T(8,128)(2,1)}, u32[]{:S(2)}) copy-start(bf16[512,1024]{1,0:T(8,128)(2,1)} %values.7) | copy-start | bytes 3145732
  4.0 28.8 %collective-permute-start = (bf16[2,256,1024]{2,1,0:T(8,128)(2,1)}, bf16[2,256,1024]{2,1,0:T(8,128)(2,1)S(1)}, u32[]{:S(2)}, u32[]{:S(2)}) collective-permute-start(bf16[2,256,1024]{2,1,0:T(8,128)(2,1)} %get-tuple-element.14), channel_id=1, source_target_pairs={{0,4},{4,8},{8,12},{1,5},{5,9},{9,13},{2,6},{6,10},{10,14},{3,7},{... | collective-permute-start | bytes 3145736 | tf_op jit(solution)/shard_map/ppermute | solution.py:185
  9.0 26.8 %collective-permute-start.1 = (bf16[2,256,1024]{2,1,0:T(8,128)(2,1)}, bf16[2,256,1024]{2,1,0:T(8,128)(2,1)}, u32[]{:S(2)}, u32[]{:S(2)}) collective-permute-start(bf16[2,256,1024]{2,1,0:T(8,128)(2,1)} %get-tuple-element.15), channel_id=1, source_target_pairs={{4,0},{8,4},{12,8},{5,1},{9,5},{13,9},{6,2},{10,6},{14,10},{7,3},{... | collective-permute-start | bytes 3145736 | tf_op jit(solution)/shard_map/ppermute | solution.py:185
  11.9 12.3 %collective-permute-start.2 = (bf16[2,128,1024]{2,1,0:T(8,128)(2,1)S(1)}, bf16[2,128,1024]{2,1,0:T(8,128)(2,1)S(1)}, u32[]{:S(2)}, u32[]{:S(2)}) collective-permute-start(bf16[2,128,1024]{2,1,0:T(8,128)(2,1)S(1)} %get-tuple-element.16), channel_id=1, source_target_pairs={{4,8},{8,4},{5,9},{9,5},{6,10},{10,6},{7,11},{11,7},{20,24},{24,20... | collective-permute-start | bytes 1572872 | tf_op jit(solution)/shard_map/ppermute | solution.py:185
  12.6 78.4 %collective-permute-start.7 = (bf16[2,256,768]{2,1,0:T(8,128)(2,1)S(1)}, bf16[2,256,768]{2,1,0:T(8,128)(2,1)S(1)}, u32[]{:S(2)}, u32[]{:S(2)}) collective-permute-start(bf16[2,256,768]{2,1,0:T(8,128)(2,1)S(1)} %get-tuple-element.21), channel_id=1, source_target_pairs={{0,8},{12,4},{1,9},{13,5},{2,10},{14,6},{3,11},{15,7},{16,24},{28,... | collective-permute-start | bytes 2359304 | tf_op jit(solution)/shard_map/ppermute | solution.py:185
  19.8 89.1 %copy-start.4 = (bf16[512,1024]{1,0:T(8,128)(2,1)S(1)}, bf16[512,1024]{1,0:T(8,128)(2,1)}, u32[]{:S(2)}) copy-start(bf16[512,1024]{1,0:T(8,128)(2,1)} %queries.3) | copy-start | bytes 3145732
  19.8 72.6 %collective-permute-start.8 = (bf16[2,256,768]{2,1,0:T(8,128)(2,1)S(1)}, bf16[2,256,768]{2,1,0:T(8,128)(2,1)S(1)}, u32[]{:S(2)}, u32[]{:S(2)}) collective-permute-start(bf16[2,256,768]{2,1,0:T(8,128)(2,1)S(1)} %get-tuple-element.22), channel_id=1, source_target_pairs={{0,12},{12,0},{1,13},{13,1},{2,14},{14,2},{3,15},{15,3},{16,28},{2... | collective-permute-start | bytes 2359304 | tf_op jit(solution)/shard_map/ppermute | solution.py:185
  37.1 71.8 %collective-permute-start.6 = (bf16[2,256,768]{2,1,0:T(8,128)(2,1)S(1)}, bf16[2,256,768]{2,1,0:T(8,128)(2,1)S(1)}, u32[]{:S(2)}, u32[]{:S(2)}) collective-permute-start(bf16[2,256,768]{2,1,0:T(8,128)(2,1)S(1)} %get-tuple-element.20), channel_id=1, source_target_pairs={{8,12},{4,0},{9,13},{5,1},{10,14},{6,2},{11,15},{7,3},{24,28},{20,... | collective-permute-start | bytes 2359304 | tf_op jit(solution)/shard_map/ppermute | solution.py:185
  38.4 81.3 %collective-permute-start.4 = (bf16[2,256,256]{2,1,0:T(8,128)(2,1)S(1)}, bf16[2,256,256]{2,1,0:T(8,128)(2,1)S(1)}, u32[]{:S(2)}, u32[]{:S(2)}) collective-permute-start(bf16[2,256,256]{2,1,0:T(8,128)(2,1)S(1)} %get-tuple-element.18), channel_id=1, source_target_pairs={{0,8},{12,4},{1,9},{13,5},{2,10},{14,6},{3,11},{15,7},{16,24},{28,... | collective-permute-start | bytes 786440 | tf_op jit(solution)/shard_map/ppermute | solution.py:185
  85.8 33.9 %collective-permute-start.5 = (bf16[2,256,256]{2,1,0:T(8,128)(2,1)S(1)}, bf16[2,256,256]{2,1,0:T(8,128)(2,1)S(1)}, u32[]{:S(2)}, u32[]{:S(2)}) collective-permute-start(bf16[2,256,256]{2,1,0:T(8,128)(2,1)S(1)} %get-tuple-element.19), channel_id=1, source_target_pairs={{0,12},{12,0},{1,13},{13,1},{2,14},{14,2},{3,15},{15,3},{16,28},{2... | collective-permute-start | bytes 786440 | tf_op jit(solution)/shard_map/ppermute | solution.py:185
  91.1 28.6 %collective-permute-start.3 = (bf16[2,256,256]{2,1,0:T(8,128)(2,1)S(1)}, bf16[2,256,256]{2,1,0:T(8,128)(2,1)S(1)}, u32[]{:S(2)}, u32[]{:S(2)}) collective-permute-start(bf16[2,256,256]{2,1,0:T(8,128)(2,1)S(1)} %get-tuple-element.17), channel_id=1, source_target_pairs={{8,12},{4,0},{9,13},{5,1},{10,14},{6,2},{11,15},{7,3},{24,28},{20,... | collective-permute-start | bytes 786440 | tf_op jit(solution)/shard_map/ppermute | solution.py:185

commit v4 on v0

--- a/solution.py
+++ b/solution.py
@@ -1,11 +1,15 @@
+import functools
+
 import jax
 import jax.numpy as jnp
 from jax import lax
+from jax.experimental import pallas as pl
+from jax.experimental.pallas import tpu as pltpu
 from jax.sharding import PartitionSpec as P
 
 HD = 128
 BLOCK = 128
-
+LOG2E = 1.4426950408889634
 
 masked_fill = -1e30
 
@@ -23,7 +27,7 @@
     return block
 
 
-def shards(queries, keys, values, band_blocks):
+def any_frames(queries, keys, values, band_blocks):
     frame_rows, columns = queries.shape
     frames = lax.axis_size("tm")
     current = lax.axis_index("tm")
@@ -78,6 +82,232 @@
     return jnp.transpose(result, (1, 0, 2)).reshape(frame_rows, columns)
 
 
+def run_copies(pairs, sems):
+    copies = [
+        pltpu.make_async_copy(source, target, sems.at[at])
+        for at, (source, target) in enumerate(pairs)
+    ]
+    for copy in copies:
+        copy.start()
+    for copy in copies:
+        copy.wait()
+
+
+def rows_of(block):
+    return pl.ds(pl.multiple_of(block * BLOCK, BLOCK), BLOCK)
+
+
+def stage_near_kernel(half, bands, keys, values, inner, beside, sems):
+    frame = lax.axis_index("tm")
+    rows = pl.ds(pl.multiple_of(lax.rem(frame + 1, 2) * half, half), half)
+    near = [
+        pltpu.make_async_copy(source.at[rows], beside.at[kv], sems.at[kv])
+        for kv, source in enumerate((keys, values))
+    ]
+
+    @pl.when((frame == 1) | (frame == 2))
+    def _():
+        facing = pl.ds(pl.multiple_of((2 - frame) * half, half), half)
+        missing = rows_of(jnp.where(frame == 1, bands[3, 0, 1], bands[0, 1, 2]))
+        pairs = []
+        for kv, source in enumerate((keys, values)):
+            pairs.append((source.at[facing], inner.at[kv, pl.ds(0, half)]))
+            pairs.append((source.at[missing], inner.at[kv, pl.ds(half, BLOCK)]))
+        for copy in near:
+            copy.start()
+        run_copies(pairs, sems.at[pl.ds(2, 4)])
+
+    @pl.when((frame == 0) | (frame == 3))
+    def _():
+        for copy in near:
+            copy.start()
+
+    for copy in near:
+        copy.wait()
+
+
+def stage_far_kernel(cuts, bands, keys, values, direct, *rest):
+    crossed, sems = rest[:-1], rest[-1]
+    frame = lax.axis_index("tm")
+
+    @pl.when((frame == 0) | (frame == 3))
+    def _():
+        reader = jnp.where(frame == 0, 2, 1)
+        pairs = []
+        for slot in range(2):
+            to = pl.ds(slot * BLOCK, BLOCK)
+            for kv, source in enumerate((keys, values)):
+                rows = rows_of(bands[3 - frame, slot, frame])
+                pairs.append((source.at[rows], direct.at[kv, to]))
+                rows = rows_of(bands[reader, slot, frame])
+                for part, (first, size) in zip(crossed, cuts):
+                    pairs.append((source.at[rows, pl.ds(first, size)], part.at[kv, to]))
+        run_copies(pairs, sems)
+
+
+def relay_kernel(half, cuts, bands, inner, *relayed):
+    frame = lax.axis_index("tm")
+
+    @pl.when((frame == 1) | (frame == 2))
+    def _():
+        rows = rows_of(jnp.where(frame == 1, bands[0, 0, 2], bands[3, 1, 1] - 2))
+        for part, (first, size) in zip(relayed, cuts):
+            cols = pl.ds(first, size)
+            part[:, pl.ds(0, BLOCK)] = inner[:, rows, cols]
+            part[:, pl.ds(BLOCK, BLOCK)] = inner[:, pl.ds(half, BLOCK), cols]
+
+
+def attend_kernel(
+    chunk, first, size, queries, keys, values, beside, inner, direct, relayed, crossed, *rest
+):
+    out, mixed_out, sems = rest[-3:]
+    frame = lax.axis_index("tm")
+    edge = (frame == 0) | (frame == 3)
+    rate = LOG2E * HD ** (-0.5)
+    rows = queries.shape[0]
+    half = rows // 2
+    heads = range(size // HD)
+
+    def pieces(head, own, kv):
+        here, there = pl.ds(first + head * HD, HD), pl.ds(head * HD, HD)
+        return [
+            own[:, here],
+            beside[kv, :, here],
+            jnp.where(edge, direct[kv, :, here], inner[kv, pl.ds(0, half), here]),
+            jnp.where(edge, relayed[kv, :, there], crossed[kv, :, there]),
+        ]
+
+    def score(head, start):
+        rows_q = queries[pl.ds(start, chunk), pl.ds(first + head * HD, HD)]
+        return [
+            lax.dot_general(
+                rows_q, piece, (((1,), (1,)), ((), ())), preferred_element_type=jnp.float32
+            )
+            for piece in pieces(head, keys, 0)
+        ]
+
+    def finish(head, start, scores):
+        row_max = functools.reduce(
+            jnp.maximum, [jnp.max(part, axis=1, keepdims=True) for part in scores]
+        )
+        powers = [jnp.exp2((part - row_max) * rate) for part in scores]
+        row_sum = sum(jnp.sum(part, axis=1, keepdims=True) for part in powers)
+        mixed = sum(
+            jnp.dot(part.astype(jnp.bfloat16), piece, preferred_element_type=jnp.float32)
+            for part, piece in zip(powers, pieces(head, values, 1))
+        )
+        mixed_out[head, pl.ds(start, chunk)] = (mixed / row_sum).astype(jnp.bfloat16)
+
+    units = [(head, start) for head in heads for start in range(0, rows, chunk)]
+    copies = []
+    scores = score(*units[0])
+    for unit, following in zip(units, units[1:] + [None]):
+        ahead = score(*following) if following else None
+        finish(*unit, scores)
+        scores = ahead
+        head, start = unit
+        if start + chunk == rows:
+            copies.append(
+                pltpu.make_async_copy(
+                    mixed_out.at[head], out.at[:, pl.ds(first + head * HD, HD)], sems.at[head]
+                )
+            )
+            copies[-1].start()
+    for copy in copies:
+        copy.wait()
+
+
+def four_frames(queries, keys, values, band_blocks):
+    rows, columns = queries.shape
+    half = rows // 2
+    heads = columns // HD
+    last = heads // 4
+    cuts = [(0, heads - 2 * last), (heads - 2 * last, last), (heads - last, last)]
+    cuts = [(first * HD, size * HD) for first, size in cuts if size]
+    anywhere = pl.BlockSpec(memory_space=pl.ANY)
+    local = pl.BlockSpec(memory_space=pltpu.VMEM)
+    scalars = pl.BlockSpec(memory_space=pltpu.SMEM)
+    roomy = pltpu.CompilerParams(vmem_limit_bytes=32 << 20)
+
+    def send(array, pairs):
+        return lax.ppermute(array, "tm", pairs)
+
+    bands = jnp.transpose(band_blocks, (0, 2, 1))
+    facing = jax.ShapeDtypeStruct((2, half, columns), jnp.bfloat16)
+    more = jax.ShapeDtypeStruct((2, half + BLOCK, columns), jnp.bfloat16)
+    parts = [jax.ShapeDtypeStruct((2, half, size), jnp.bfloat16) for _, size in cuts]
+
+    def stage(kernel, shapes, copies, name):
+        return pl.pallas_call(
+            kernel,
+            out_shape=shapes,
+            in_specs=[scalars, anywhere, anywhere],
+            out_specs=[local] * len(shapes),
+            scratch_shapes=[pltpu.SemaphoreType.DMA((copies,))],
+            compiler_params=pltpu.CompilerParams(vmem_limit_bytes=60 << 20),
+            name=name,
+        )(bands, keys, values)
+
+    inner, beside = stage(
+        functools.partial(stage_near_kernel, half), [more, facing], 6, "stage_near"
+    )
+    direct, *crossed = stage(
+        functools.partial(stage_far_kernel, cuts),
+        [facing] + parts,
+        4 * (1 + len(cuts)),
+        "stage_far",
+    )
+    inner = send(inner, [(1, 2), (2, 1)])
+    beside = send(beside, [(0, 1), (1, 0), (2, 3), (3, 2)])
+    direct = send(direct, [(0, 3), (3, 0)])
+    crossed = [send(part, [(0, 2), (3, 1)]) for part in crossed]
+    relayed = pl.pallas_call(
+        functools.partial(relay_kernel, half, cuts),
+        out_shape=parts,
+        in_specs=[scalars, local],
+        out_specs=[local] * len(cuts),
+        compiler_params=roomy,
+        name="relay",
+    )(bands, inner)
+    relayed = [send(part, [(2, 3), (1, 0)]) for part in relayed]
+
+    result = None
+    seen = rows + 3 * half
+    for g, (first, size) in enumerate(cuts):
+        operands = [queries, keys, values, beside, inner, direct, relayed[g], crossed[g]]
+        in_specs = [local] * len(operands)
+        aliases = {}
+        if result is not None:
+            aliases = {len(operands): 0}
+            in_specs.append(anywhere)
+            operands.append(result)
+        result = pl.pallas_call(
+            functools.partial(attend_kernel, rows // 2, first, size),
+            out_shape=jax.ShapeDtypeStruct(queries.shape, queries.dtype),
+            in_specs=in_specs,
+            out_specs=anywhere,
+            input_output_aliases=aliases,
+            scratch_shapes=[
+                pltpu.VMEM((size // HD, rows, HD), jnp.bfloat16),
+                pltpu.SemaphoreType.DMA((size // HD,)),
+            ],
+            compiler_params=roomy,
+            cost_estimate=pl.CostEstimate(
+                flops=4 * size * rows * seen,
+                bytes_accessed=2 * size * (2 * rows + 2 * (rows + 4 * half)),
+                transcendentals=size // HD * rows * seen,
+            ),
+            name=f"attend_{g}",
+        )(*operands)
+    return result
+
+
+def shards(queries, keys, values, band_blocks):
+    if lax.axis_size("tm") == 4 and queries.shape[0] == 4 * BLOCK and band_blocks.shape[2] == 2:
+        return four_frames(queries, keys, values, band_blocks)
+    return any_frames(queries, keys, values, band_blocks)
+
+
 def solution(mesh):
     placed = (
         P(("groups", "tm"), ("head", "sub")),

time: 216 us -> 107 us (0.50)
  the two profiles are of different devices: /device:TPU:10 before, /device:TPU:0 now
where the time goes in v4:
time: 107 us; the launch traced here: 106 us
  starting transfers between devices  83.1 us (78%)
  Pallas kernels  19.1 us (18%)
  waiting for transfers between devices  3.91 us (4%)
    ppermute x9, starting transfers between devices, send(): return lax.ppermute(array, 'tm', pairs)  83.1 us
    pallas_call x3, Pallas kernels, four_frames(): pl.pallas_call(functools.partial(attend_kernel, rows // 2, first, size),...  11.2 us
    pallas_call x2, Pallas kernels, stage(): pl.pallas_call(kernel, out_shape=shapes, in_specs=[scalars, anywhere, any...  7.21 us
    ppermute x9, waiting for transfers between devices, send(): return lax.ppermute(array, 'tm', pairs)  3.91 us
  transfers between devices with their start and end apart: 9, of which 3 were waited for; matrix products, arithmetic and copies ran while one was open for 0% of the time, Pallas kernels for 12%

profile of v4, /device:TPU:0, one launch (start us, length us, event | category | flops | bytes accessed | tf_op | source)
XLA Modules:
  0.0 106.3 jit_solution(4225876216653750629)
XLA Ops:
  0.0 3.5 %stage_near.1 = (bf16[2,384,1024]{2,1,0:T(8,128)(2,1)}, bf16[2,256,1024]{2,1,0:T(8,128)(2,1)}) custom-call(s32[4,2,4]{2,1,0:T(2,128)} %bitcast.1, bf16[512,1024]{1,0:T(8,128)(2,1)} %keys.9, bf16[512,1024]{1,0:T(8,128)(2,1)} %values.9), custom_call_target="tpu_custom_call" | custom-call | tf_op jit(solution)/shard_map/stage_near/pallas_call | solution.py:241
  3.5 0.0 copy-start.3
  3.5 0.0 copy-start
  3.5 0.0 copy-start.1
  3.5 0.9 collective-permute-start.1
  4.4 3.7 %stage_far.1 = (bf16[2,256,1024]{2,1,0:T(8,128)(2,1)}, bf16[2,256,512]{2,1,0:T(8,128)(2,1)}, bf16[2,256,256]{2,1,0:T(8,128)(2,1)}, bf16[2,256,256]{2,1,0:T(8,128)(2,1)}) custom-call(s32[4,2,4]{2,1,0:T(2,128)} %bitcast.2, bf16[512,1024]{1,0:T(8,128)(2,1)} %keys.9, bf16[512,1024]{1,0:T(8,128)(2,1)} %values.9), custom_call_target="tpu_custom_call" | custom-call | tf_op jit(solution)/shard_map/stage_far/pallas_call | solution.py:241
  8.2 0.0 copy-start.5
  8.2 0.0 copy-start.2
  8.2 7.1 %collective-permute-start.2 = (bf16[2,256,1024]{2,1,0:T(8,128)(2,1)}, bf16[2,256,1024]{2,1,0:T(8,128)(2,1)S(1)}, u32[]{:S(2)}, u32[]{:S(2)}) collective-permute-start(bf16[2,256,1024]{2,1,0:T(8,128)(2,1)} %get-tuple-element.16), channel_id=1, source_target_pairs={{0,12},{12,0},{1,13},{13,1},{2,14},{14,2},{3,15},{15,3},{16,28},{2... | collective-permute-start | bytes 3145736 | tf_op jit(solution)/shard_map/ppermute | solution.py:233
  15.3 0.1 collective-permute-start
  15.3 2.5 %collective-permute-start.8 = (bf16[2,256,512]{2,1,0:T(8,128)(2,1)}, bf16[2,256,512]{2,1,0:T(8,128)(2,1)S(1)}, u32[]{:S(2)}, u32[]{:S(2)}) collective-permute-start(bf16[2,256,512]{2,1,0:T(8,128)(2,1)} %get-tuple-element.22), channel_id=1, source_target_pairs={{0,8},{12,4},{1,9},{13,5},{2,10},{14,6},{3,11},{15,7},{16,24},{28,... | collective-permute-start | bytes 1572872 | tf_op jit(solution)/shard_map/ppermute | solution.py:233
  17.8 0.0 collective-permute-done.1.inner
  17.9 0.0 copy-done.3
  17.9 0.6 relay.1
  18.5 1.3 %collective-permute-start.7 = (bf16[2,256,512]{2,1,0:T(8,128)(2,1)S(1)}, bf16[2,256,512]{2,1,0:T(8,128)(2,1)S(1)}, u32[]{:S(2)}, u32[]{:S(2)}) collective-permute-start(bf16[2,256,512]{2,1,0:T(8,128)(2,1)S(1)} %get-tuple-element.21), channel_id=1, source_target_pairs={{8,12},{4,0},{9,13},{5,1},{10,14},{6,2},{11,15},{7,3},{24,28},{20,... | collective-permute-start | bytes 1572872 | tf_op jit(solution)/shard_map/ppermute | solution.py:233
  19.8 64.2 %collective-permute-start.6 = (bf16[2,256,256]{2,1,0:T(8,128)(2,1)S(1)}, bf16[2,256,256]{2,1,0:T(8,128)(2,1)S(1)}, u32[]{:S(2)}, u32[]{:S(2)}) collective-permute-start(bf16[2,256,256]{2,1,0:T(8,128)(2,1)S(1)} %copy-done.5), channel_id=1, source_target_pairs={{0,8},{12,4},{1,9},{13,5},{2,10},{14,6},{3,11},{15,7},{16,24},{28,... | collective-permute-start | bytes 786440 | tf_op jit(solution)/shard_map/ppermute | solution.py:233
  84.1 0.0 collective-permute-done.8.crossed
  84.1 1.3 %collective-permute-start.5 = (bf16[2,256,256]{2,1,0:T(8,128)(2,1)S(1)}, bf16[2,256,256]{2,1,0:T(8,128)(2,1)S(1)}, u32[]{:S(2)}, u32[]{:S(2)}) collective-permute-start(bf16[2,256,256]{2,1,0:T(8,128)(2,1)S(1)} %get-tuple-element.19), channel_id=1, source_target_pairs={{8,12},{4,0},{9,13},{5,1},{10,14},{6,2},{11,15},{7,3},{24,28},{20,... | collective-permute-start | bytes 786440 | tf_op jit(solution)/shard_map/ppermute | solution.py:233
  85.4 0.0 collective-permute-done.2.direct
  85.4 4.5 %collective-permute-start.4 = (bf16[2,256,256]{2,1,0:T(8,128)(2,1)S(1)}, bf16[2,256,256]{2,1,0:T(8,128)(2,1)S(1)}, u32[]{:S(2)}, u32[]{:S(2)}) collective-permute-start(bf16[2,256,256]{2,1,0:T(8,128)(2,1)S(1)} %copy-done.4), channel_id=1, source_target_pairs={{0,8},{12,4},{1,9},{13,5},{2,10},{14,6},{3,11},{15,7},{16,24},{28,... | collective-permute-start | bytes 786440 | tf_op jit(solution)/shard_map/ppermute | solution.py:233
  89.8 0.0 collective-permute-done.beside
  89.9 1.3 %collective-permute-start.3 = (bf16[2,256,256]{2,1,0:T(8,128)(2,1)S(1)}, bf16[2,256,256]{2,1,0:T(8,128)(2,1)S(1)}, u32[]{:S(2)}, u32[]{:S(2)}) collective-permute-start(bf16[2,256,256]{2,1,0:T(8,128)(2,1)S(1)} %get-tuple-element.17), channel_id=1, source_target_pairs={{8,12},{4,0},{9,13},{5,1},{10,14},{6,2},{11,15},{7,3},{24,28},{20,... | collective-permute-start | bytes 786440 | tf_op jit(solution)/shard_map/ppermute | solution.py:233
  91.2 2.7 %collective-permute-done.7.relayed = bf16[2,256,512]{2,1,0:T(8,128)(2,1)S(1)} collective-permute-done((bf16[2,256,512]{2,1,0:T(8,128)(2,1)S(1)}, bf16[2,256,512]{2,1,0:T(8,128)(2,1)S(1)}, u32[]{:S(2)}, u32[]{:S(2)}) %collective-permute-start.7) | collective-permute-done | bytes 524320 | tf_op jit(solution)/shard_map/ppermute | solution.py:233
  93.9 0.0 copy-done
  93.9 0.0 copy-done.2
  93.9 5.2 %attend_0.1.rest_0_ = bf16[512,1024]{1,0:T(8,128)(2,1)} custom-call(bf16[512,1024]{1,0:T(8,128)(2,1)S(1)} %copy-done.2, bf16[512,1024]{1,0:T(8,128)(2,1)S(1)} %copy-done, bf16[512,1024]{1,0:T(8,128)(2,1)S(1)} %copy-done.1, bf16[2,256,1024]{2,1,0:T(8,128)(2,1)S(1)} %collective-permute-done.beside, bf16[2,384,1024]{2,1,0:T(8,128)(2,1)S(1)} %collective-permute-done.1.inner, ...), custom_call_target="tpu_custom_call" | custom-call | flops 1342177280 | bytes 4194304 | tf_op jit(solution)/shard_map/attend_0/pallas_call | solution.py:284
  99.1 0.0 collective-permute-done.6.crossed
  99.1 0.4 collective-permute-done.5.relayed
  99.5 3.0 %attend_1.1.rest_0_ = bf16[512,1024]{1,0:T(8,128)(2,1)} custom-call(bf16[512,1024]{1,0:T(8,128)(2,1)S(1)} %copy-done.2, bf16[512,1024]{1,0:T(8,128)(2,1)S(1)} %copy-done, bf16[512,1024]{1,0:T(8,128)(2,1)S(1)} %copy-done.1, bf16[2,256,1024]{2,1,0:T(8,128)(2,1)S(1)} %collective-permute-done.beside, ...), custom_call_target="tpu_custom_call", output_to_operand_aliasing={{}: (8, {})} | custom-call | flops 671088640 | bytes 2097152 | tf_op jit(solution)/shard_map/attend_1/pallas_call | solution.py:284
  102.5 0.0 collective-permute-done.4.crossed
  102.5 0.8 collective-permute-done.3.relayed
  103.3 3.0 %attend_2.1 = bf16[512,1024]{1,0:T(8,128)(2,1)} custom-call(bf16[512,1024]{1,0:T(8,128)(2,1)S(1)} %copy-done.2, bf16[512,1024]{1,0:T(8,128)(2,1)S(1)} %copy-done, bf16[512,1024]{1,0:T(8,128)(2,1)S(1)} %copy-done.1, bf16[2,256,1024]{2,1,0:T(8,128)(2,1)S(1)} %collective-permute-done.beside, ...), custom_call_target="tpu_custom_call", output_to_operand_aliasing={{}: (8, {})} | custom-call | flops 671088640 | bytes 2097152 | tf_op jit(solution)/shard_map/attend_2/pallas_call | solution.py:284
  (4 shorter events, 0.0 us)
Async XLA Ops:
  3.5 14.4 %copy-start.3 = (s32[4,4,2]{1,2,0:T(2,128)S(1)}, s32[4,4,2]{1,2,0:T(2,128)}, u32[]{:S(2)}) copy-start(s32[4,4,2]{1,2,0:T(2,128)} %param.7) | copy-start | bytes 388
  3.5 90.4 %copy-start = (bf16[512,1024]{1,0:T(8,128)(2,1)S(1)}, bf16[512,1024]{1,0:T(8,128)(2,1)}, u32[]{:S(2)}) copy-start(bf16[512,1024]{1,0:T(8,128)(2,1)} %keys.9) | copy-start | bytes 3145732
  3.5 90.4 %copy-start.1 = (bf16[512,1024]{1,0:T(8,128)(2,1)S(1)}, bf16[512,1024]{1,0:T(8,128)(2,1)}, u32[]{:S(2)}) copy-start(bf16[512,1024]{1,0:T(8,128)(2,1)} %values.9) | copy-start | bytes 3145732
  3.5 14.3 %collective-permute-start.1 = (bf16[2,384,1024]{2,1,0:T(8,128)(2,1)}, bf16[2,384,1024]{2,1,0:T(8,128)(2,1)S(1)}, u32[]{:S(2)}, u32[]{:S(2)}) collective-permute-start(bf16[2,384,1024]{2,1,0:T(8,128)(2,1)} %get-tuple-element.15), channel_id=1, source_target_pairs={{4,8},{8,4},{5,9},{9,5},{6,10},{10,6},{7,11},{11,7},{20,24},{24,20... | collective-permute-start | bytes 4718600 | tf_op jit(solution)/shard_map/ppermute | solution.py:233
  8.2 11.6 %copy-start.5 = (bf16[2,256,256]{2,1,0:T(8,128)(2,1)S(1)}, bf16[2,256,256]{2,1,0:T(8,128)(2,1)}, u32[]{:S(2)}) copy-start(bf16[2,256,256]{2,1,0:T(8,128)(2,1)} %get-tuple-element.20) | copy-start | bytes 786436
  8.2 77.2 %copy-start.4 = (bf16[2,256,256]{2,1,0:T(8,128)(2,1)S(1)}, bf16[2,256,256]{2,1,0:T(8,128)(2,1)}, u32[]{:S(2)}) copy-start(bf16[2,256,256]{2,1,0:T(8,128)(2,1)} %get-tuple-element.18) | copy-start | bytes 786436
  8.2 85.7 %copy-start.2 = (bf16[512,1024]{1,0:T(8,128)(2,1)S(1)}, bf16[512,1024]{1,0:T(8,128)(2,1)}, u32[]{:S(2)}) copy-start(bf16[512,1024]{1,0:T(8,128)(2,1)} %queries.5) | copy-start | bytes 3145732
  8.2 77.2 %collective-permute-start.2 = (bf16[2,256,1024]{2,1,0:T(8,128)(2,1)}, bf16[2,256,1024]{2,1,0:T(8,128)(2,1)S(1)}, u32[]{:S(2)}, u32[]{:S(2)}) collective-permute-start(bf16[2,256,1024]{2,1,0:T(8,128)(2,1)} %get-tuple-element.16), channel_id=1, source_target_pairs={{0,12},{12,0},{1,13},{13,1},{2,14},{14,2},{3,15},{15,3},{16,28},{2... | collective-permute-start | bytes 3145736 | tf_op jit(solution)/shard_map/ppermute | solution.py:233
  15.3 74.6 %collective-permute-start = (bf16[2,256,1024]{2,1,0:T(8,128)(2,1)}, bf16[2,256,1024]{2,1,0:T(8,128)(2,1)S(1)}, u32[]{:S(2)}, u32[]{:S(2)}) collective-permute-start(bf16[2,256,1024]{2,1,0:T(8,128)(2,1)} %get-tuple-element.14), channel_id=1, source_target_pairs={{0,4},{4,0},{8,12},{12,8},{1,5},{5,1},{9,13},{13,9},{2,6},{6,2},{1... | collective-permute-start | bytes 3145736 | tf_op jit(solution)/shard_map/ppermute | solution.py:233
  15.3 68.7 %collective-permute-start.8 = (bf16[2,256,512]{2,1,0:T(8,128)(2,1)}, bf16[2,256,512]{2,1,0:T(8,128)(2,1)S(1)}, u32[]{:S(2)}, u32[]{:S(2)}) collective-permute-start(bf16[2,256,512]{2,1,0:T(8,128)(2,1)} %get-tuple-element.22), channel_id=1, source_target_pairs={{0,8},{12,4},{1,9},{13,5},{2,10},{14,6},{3,11},{15,7},{16,24},{28,... | collective-permute-start | bytes 1572872 | tf_op jit(solution)/shard_map/ppermute | solution.py:233
  18.5 75.4 %collective-permute-start.7 = (bf16[2,256,512]{2,1,0:T(8,128)(2,1)S(1)}, bf16[2,256,512]{2,1,0:T(8,128)(2,1)S(1)}, u32[]{:S(2)}, u32[]{:S(2)}) collective-permute-start(bf16[2,256,512]{2,1,0:T(8,128)(2,1)S(1)} %get-tuple-element.21), channel_id=1, source_target_pairs={{8,12},{4,0},{9,13},{5,1},{10,14},{6,2},{11,15},{7,3},{24,28},{20,... | collective-permute-start | bytes 1572872 | tf_op jit(solution)/shard_map/ppermute | solution.py:233
  19.8 79.3 %collective-permute-start.6 = (bf16[2,256,256]{2,1,0:T(8,128)(2,1)S(1)}, bf16[2,256,256]{2,1,0:T(8,128)(2,1)S(1)}, u32[]{:S(2)}, u32[]{:S(2)}) collective-permute-start(bf16[2,256,256]{2,1,0:T(8,128)(2,1)S(1)} %copy-done.5), channel_id=1, source_target_pairs={{0,8},{12,4},{1,9},{13,5},{2,10},{14,6},{3,11},{15,7},{16,24},{28,... | collective-permute-start | bytes 786440 | tf_op jit(solution)/shard_map/ppermute | solution.py:233
  84.1 15.4 %collective-permute-start.5 = (bf16[2,256,256]{2,1,0:T(8,128)(2,1)S(1)}, bf16[2,256,256]{2,1,0:T(8,128)(2,1)S(1)}, u32[]{:S(2)}, u32[]{:S(2)}) collective-permute-start(bf16[2,256,256]{2,1,0:T(8,128)(2,1)S(1)} %get-tuple-element.19), channel_id=1, source_target_pairs={{8,12},{4,0},{9,13},{5,1},{10,14},{6,2},{11,15},{7,3},{24,28},{20,... | collective-permute-start | bytes 786440 | tf_op jit(solution)/shard_map/ppermute | solution.py:233
  85.4 17.1 %collective-permute-start.4 = (bf16[2,256,256]{2,1,0:T(8,128)(2,1)S(1)}, bf16[2,256,256]{2,1,0:T(8,128)(2,1)S(1)}, u32[]{:S(2)}, u32[]{:S(2)}) collective-permute-start(bf16[2,256,256]{2,1,0:T(8,128)(2,1)S(1)} %copy-done.4), channel_id=1, source_target_pairs={{0,8},{12,4},{1,9},{13,5},{2,10},{14,6},{3,11},{15,7},{16,24},{28,... | collective-permute-start | bytes 786440 | tf_op jit(solution)/shard_map/ppermute | solution.py:233
  89.9 13.5 %collective-permute-start.3 = (bf16[2,256,256]{2,1,0:T(8,128)(2,1)S(1)}, bf16[2,256,256]{2,1,0:T(8,128)(2,1)S(1)}, u32[]{:S(2)}, u32[]{:S(2)}) collective-permute-start(bf16[2,256,256]{2,1,0:T(8,128)(2,1)S(1)} %get-tuple-element.17), channel_id=1, source_target_pairs={{8,12},{4,0},{9,13},{5,1},{10,14},{6,2},{11,15},{7,3},{24,28},{20,... | collective-permute-start | bytes 786440 | tf_op jit(solution)/shard_map/ppermute | solution.py:233

commit v5 on v4

--- a/solution.py
+++ b/solution.py
@@ -97,37 +97,27 @@
     return pl.ds(pl.multiple_of(block * BLOCK, BLOCK), BLOCK)
 
 
-def stage_near_kernel(half, bands, keys, values, inner, beside, sems):
-    frame = lax.axis_index("tm")
-    rows = pl.ds(pl.multiple_of(lax.rem(frame + 1, 2) * half, half), half)
-    near = [
-        pltpu.make_async_copy(source.at[rows], beside.at[kv], sems.at[kv])
-        for kv, source in enumerate((keys, values))
-    ]
+def stage_missing_kernel(bands, keys, values, missing, sems):
+    frame = lax.axis_index("tm")
 
     @pl.when((frame == 1) | (frame == 2))
     def _():
-        facing = pl.ds(pl.multiple_of((2 - frame) * half, half), half)
-        missing = rows_of(jnp.where(frame == 1, bands[3, 0, 1], bands[0, 1, 2]))
-        pairs = []
-        for kv, source in enumerate((keys, values)):
-            pairs.append((source.at[facing], inner.at[kv, pl.ds(0, half)]))
-            pairs.append((source.at[missing], inner.at[kv, pl.ds(half, BLOCK)]))
-        for copy in near:
-            copy.start()
-        run_copies(pairs, sems.at[pl.ds(2, 4)])
-
-    @pl.when((frame == 0) | (frame == 3))
-    def _():
-        for copy in near:
-            copy.start()
-
-    for copy in near:
-        copy.wait()
-
-
-def stage_far_kernel(cuts, bands, keys, values, direct, *rest):
-    crossed, sems = rest[:-1], rest[-1]
+        rows = rows_of(jnp.where(frame == 1, bands[3, 0, 1], bands[0, 1, 2]))
+        run_copies([(keys.at[rows], missing.at[0]), (values.at[rows], missing.at[1])], sems)
+
+
+def stage_near_kernel(half, after, keys, values, inner, beside, sems):
+    frame = lax.axis_index("tm")
+    outer = pl.ds(pl.multiple_of(lax.rem(frame + 1, 2) * half, half), half)
+    facing = pl.ds(pl.multiple_of(lax.rem(frame, 2) * half, half), half)
+    pairs = []
+    for kv, source in enumerate((keys, values)):
+        pairs.append((source.at[facing], inner.at[kv]))
+        pairs.append((source.at[outer], beside.at[kv]))
+    run_copies(pairs, sems)
+
+
+def stage_crossed_kernel(after, bands, keys, values, crossed, sems):
     frame = lax.axis_index("tm")
 
     @pl.when((frame == 0) | (frame == 3))
@@ -135,46 +125,56 @@
         reader = jnp.where(frame == 0, 2, 1)
         pairs = []
         for slot in range(2):
-            to = pl.ds(slot * BLOCK, BLOCK)
+            rows = rows_of(bands[reader, slot, frame])
             for kv, source in enumerate((keys, values)):
-                rows = rows_of(bands[3 - frame, slot, frame])
-                pairs.append((source.at[rows], direct.at[kv, to]))
-                rows = rows_of(bands[reader, slot, frame])
-                for part, (first, size) in zip(crossed, cuts):
-                    pairs.append((source.at[rows, pl.ds(first, size)], part.at[kv, to]))
+                pairs.append((source.at[rows], crossed.at[kv, pl.ds(slot * BLOCK, BLOCK)]))
         run_copies(pairs, sems)
 
 
-def relay_kernel(half, cuts, bands, inner, *relayed):
-    frame = lax.axis_index("tm")
-
-    @pl.when((frame == 1) | (frame == 2))
+def stage_last_kernel(cuts, inner, bands, keys, values, picked, *rest):
+    direct, sems = rest[:-1], rest[-1]
+    frame = lax.axis_index("tm")
+    edge = (frame == 0) | (frame == 3)
+
+    @pl.when(edge)
+    def _():
+        pairs = []
+        for slot in range(2):
+            rows = rows_of(bands[3 - frame, slot, frame])
+            for part, (first, size) in zip(direct, cuts):
+                for kv, source in enumerate((keys, values)):
+                    pairs.append(
+                        (
+                            source.at[rows, pl.ds(first, size)],
+                            part.at[kv, pl.ds(slot * BLOCK, BLOCK)],
+                        )
+                    )
+        run_copies(pairs, sems)
+
+    @pl.when(jnp.logical_not(edge))
     def _():
         rows = rows_of(jnp.where(frame == 1, bands[0, 0, 2], bands[3, 1, 1] - 2))
-        for part, (first, size) in zip(relayed, cuts):
-            cols = pl.ds(first, size)
-            part[:, pl.ds(0, BLOCK)] = inner[:, rows, cols]
-            part[:, pl.ds(BLOCK, BLOCK)] = inner[:, pl.ds(half, BLOCK), cols]
+        run_copies([(inner.at[:, rows], picked)], sems)
 
 
 def attend_kernel(
-    chunk, first, size, queries, keys, values, beside, inner, direct, relayed, crossed, *rest
+    chunk, first, size, queries, keys, values, beside, inner, crossed, lone, picked, direct, *rest
 ):
     out, mixed_out, sems = rest[-3:]
     frame = lax.axis_index("tm")
     edge = (frame == 0) | (frame == 3)
     rate = LOG2E * HD ** (-0.5)
     rows = queries.shape[0]
-    half = rows // 2
     heads = range(size // HD)
 
     def pieces(head, own, kv):
         here, there = pl.ds(first + head * HD, HD), pl.ds(head * HD, HD)
+        relayed = jnp.concatenate([lone[kv, :, here], picked[kv, :, here]], 0)
         return [
             own[:, here],
             beside[kv, :, here],
-            jnp.where(edge, direct[kv, :, here], inner[kv, pl.ds(0, half), here]),
-            jnp.where(edge, relayed[kv, :, there], crossed[kv, :, there]),
+            jnp.where(edge, direct[kv, :, there], inner[kv, :, here]),
+            jnp.where(edge, relayed, crossed[kv, :, here]),
         ]
 
     def score(head, start):
@@ -233,48 +233,53 @@
         return lax.ppermute(array, "tm", pairs)
 
     bands = jnp.transpose(band_blocks, (0, 2, 1))
+    block = jax.ShapeDtypeStruct((2, BLOCK, columns), jnp.bfloat16)
     facing = jax.ShapeDtypeStruct((2, half, columns), jnp.bfloat16)
-    more = jax.ShapeDtypeStruct((2, half + BLOCK, columns), jnp.bfloat16)
     parts = [jax.ShapeDtypeStruct((2, half, size), jnp.bfloat16) for _, size in cuts]
 
-    def stage(kernel, shapes, copies, name):
+    def stage(kernel, shapes, copies, operands, name):
         return pl.pallas_call(
             kernel,
             out_shape=shapes,
-            in_specs=[scalars, anywhere, anywhere],
+            in_specs=[scalars if operand is bands else anywhere for operand in operands],
             out_specs=[local] * len(shapes),
             scratch_shapes=[pltpu.SemaphoreType.DMA((copies,))],
             compiler_params=pltpu.CompilerParams(vmem_limit_bytes=60 << 20),
             name=name,
-        )(bands, keys, values)
-
+        )(*operands)
+
+    (missing,) = stage(
+        stage_missing_kernel, [block], 2, [bands, keys, values], "stage_missing"
+    )
     inner, beside = stage(
-        functools.partial(stage_near_kernel, half), [more, facing], 6, "stage_near"
-    )
-    direct, *crossed = stage(
-        functools.partial(stage_far_kernel, cuts),
-        [facing] + parts,
-        4 * (1 + len(cuts)),
-        "stage_far",
-    )
+        functools.partial(stage_near_kernel, half),
+        [facing, facing],
+        4,
+        [missing, keys, values],
+        "stage_near",
+    )
+    missing = send(missing, [(1, 2), (2, 1)])
+    beside = send(beside, [(0, 1), (1, 0), (2, 3), (3, 2)])
     inner = send(inner, [(1, 2), (2, 1)])
-    beside = send(beside, [(0, 1), (1, 0), (2, 3), (3, 2)])
-    direct = send(direct, [(0, 3), (3, 0)])
-    crossed = [send(part, [(0, 2), (3, 1)]) for part in crossed]
-    relayed = pl.pallas_call(
-        functools.partial(relay_kernel, half, cuts),
-        out_shape=parts,
-        in_specs=[scalars, local],
-        out_specs=[local] * len(cuts),
-        compiler_params=roomy,
-        name="relay",
-    )(bands, inner)
-    relayed = [send(part, [(2, 3), (1, 0)]) for part in relayed]
+    lone = send(missing, [(2, 3), (1, 0)])
+    (crossed,) = stage(
+        stage_crossed_kernel, [facing], 4, [missing, bands, keys, values], "stage_crossed"
+    )
+    crossed = send(crossed, [(0, 2), (3, 1)])
+    picked, *direct = stage(
+        functools.partial(stage_last_kernel, cuts),
+        [block] + parts,
+        4 * len(cuts),
+        [inner, bands, keys, values],
+        "stage_last",
+    )
+    picked = send(picked, [(2, 3), (1, 0)])
+    direct = [send(part, [(0, 3), (3, 0)]) for part in direct]
 
     result = None
     seen = rows + 3 * half
     for g, (first, size) in enumerate(cuts):
-        operands = [queries, keys, values, beside, inner, direct, relayed[g], crossed[g]]
+        operands = [queries, keys, values, beside, inner, crossed, lone, picked, direct[g]]
         in_specs = [local] * len(operands)
         aliases = {}
         if result is not None:

time: 107 us -> 120 us (1.12)
  waiting for transfers between devices: 3.91 us -> 30.5 us
  starting transfers between devices: 83.1 us -> 58.6 us
  Pallas kernels: 19.1 us -> 26.2 us
  local copies, waits for them, and re-layouts: 0.03 us -> 4.22 us
    ppermute x9, waiting for transfers between devices: 3.91 us -> 30.5 us  [send(): return lax.ppermute(array, 'tm', pairs)]
    ppermute x9, starting transfers between devices: 83.1 us -> 58.6 us  [send(): return lax.ppermute(array, 'tm', pairs)]
    pallas_call x3, Pallas kernels: 11.2 us -> 15.4 us  [four_frames(): pl.pallas_call(functools.partial(attend_kernel, rows // 2, first, size),...]
    unnamed x12 -> x14, local copies, waits for them, and re-layouts: 0.03 us -> 4.22 us
    pallas_call x3 -> x4, Pallas kernels: 7.83 us -> 10.7 us  [stage(): pl.pallas_call(kernel, out_shape=shapes, in_specs=[scalars if operand is...]
  transfers between devices with their start and end apart: 9 -> 9, of which waited for: 3 -> 2; matrix products, arithmetic and copies ran while one was open for 0% -> 0% of each run, Pallas kernels for 12% -> 14%
where the time goes in v5:
time: 120 us
  starting transfers between devices  58.6 us (49%)
  waiting for transfers between devices  30.5 us (25%)
  Pallas kernels  26.2 us (22%)
  local copies, waits for them, and re-layouts  4.22 us (4%)
    ppermute x9, starting transfers between devices, send(): return lax.ppermute(array, 'tm', pairs)  58.6 us
    ppermute x9, waiting for transfers between devices, send(): return lax.ppermute(array, 'tm', pairs)  30.5 us
    pallas_call x3, Pallas kernels, four_frames(): pl.pallas_call(functools.partial(attend_kernel, rows // 2, first, size),...  15.4 us
    pallas_call x4, Pallas kernels, stage(): pl.pallas_call(kernel, out_shape=shapes, in_specs=[scalars if operand is...  10.7 us
    unnamed x14, local copies, waits for them, and re-layouts  4.22 us
  transfers between devices with their start and end apart: 9, of which 2 were waited for; matrix products, arithmetic and copies ran while one was open for 0% of the time, Pallas kernels for 14%

profile of v5, /device:TPU:0, one launch (start us, length us, event | category | flops | bytes accessed | tf_op | source)
XLA Modules:
  0.0 119.7 jit_solution(13239898795202472689)
XLA Ops:
  0.0 1.5 %stage_missing.1.after = bf16[2,128,1024]{2,1,0:T(8,128)(2,1)} custom-call(s32[4,2,4]{2,1,0:T(2,128)} %bitcast.1, bf16[512,1024]{1,0:T(8,128)(2,1)} %keys.13, bf16[512,1024]{1,0:T(8,128)(2,1)} %values.13), custom_call_target="tpu_custom_call" | custom-call | tf_op jit(solution)/shard_map/stage_missing/pallas_call | solution.py:241
  1.6 2.9 %stage_near.1 = (bf16[2,256,1024]{2,1,0:T(8,128)(2,1)}, bf16[2,256,1024]{2,1,0:T(8,128)(2,1)}) custom-call(bf16[2,128,1024]{2,1,0:T(8,128)(2,1)} %stage_missing.1.after, bf16[512,1024]{1,0:T(8,128)(2,1)} %keys.13, bf16[512,1024]{1,0:T(8,128)(2,1)} %values.13), custom_call_target="tpu_custom_call" | custom-call | tf_op jit(solution)/shard_map/stage_near/pallas_call | solution.py:241
  4.5 0.7 collective-permute-start.1
  5.2 0.7 collective-permute-start.2
  5.9 8.5 %collective-permute-start = (bf16[2,256,1024]{2,1,0:T(8,128)(2,1)}, bf16[2,256,1024]{2,1,0:T(8,128)(2,1)}, u32[]{:S(2)}, u32[]{:S(2)}) collective-permute-start(bf16[2,256,1024]{2,1,0:T(8,128)(2,1)} %get-tuple-element.11), channel_id=1, source_target_pairs={{0,4},{4,0},{8,12},{12,8},{1,5},{5,1},{9,13},{13,9},{2,6},{6,2},{1... | collective-permute-start | bytes 3145736 | tf_op jit(solution)/shard_map/ppermute | solution.py:233
  14.5 0.0 collective-permute-done.2.after
  14.5 0.8 copy-done.6
  15.3 3.0 %stage_crossed.1 = bf16[2,256,1024]{2,1,0:T(8,128)(2,1)} custom-call(bf16[2,128,1024]{2,1,0:T(8,128)(2,1)} %copy-done.6, s32[4,2,4]{2,1,0:T(2,128)} %bitcast.2, bf16[512,1024]{1,0:T(8,128)(2,1)} %keys.13, bf16[512,1024]{1,0:T(8,128)(2,1)} %values.13), custom_call_target="tpu_custom_call" | custom-call | tf_op jit(solution)/shard_map/stage_crossed/pallas_call | solution.py:241
  18.3 0.0 copy-start
  18.3 0.0 copy-start.1
  18.3 35.2 %collective-permute-start.3 = (bf16[2,256,1024]{2,1,0:T(8,128)(2,1)}, bf16[2,256,1024]{2,1,0:T(8,128)(2,1)}, u32[]{:S(2)}, u32[]{:S(2)}) collective-permute-start(bf16[2,256,1024]{2,1,0:T(8,128)(2,1)} %stage_crossed.1), channel_id=1, source_target_pairs={{0,8},{12,4},{1,9},{13,5},{2,10},{14,6},{3,11},{15,7},{16,24},{28,... | collective-permute-start | bytes 3145736 | tf_op jit(solution)/shard_map/ppermute | solution.py:233
  53.5 1.3 %collective-permute-start.4 = (bf16[2,128,1024]{2,1,0:T(8,128)(2,1)}, bf16[2,128,1024]{2,1,0:T(8,128)(2,1)S(1)}, u32[]{:S(2)}, u32[]{:S(2)}) collective-permute-start(bf16[2,128,1024]{2,1,0:T(8,128)(2,1)} %copy-done.6), channel_id=1, source_target_pairs={{8,12},{4,0},{9,13},{5,1},{10,14},{6,2},{11,15},{7,3},{24,28},{20,... | collective-permute-start | bytes 1572872 | tf_op jit(solution)/shard_map/ppermute | solution.py:233
  54.7 0.0 collective-permute-done.1.inner
  54.8 0.0 copy-start.2
  54.8 1.0 copy-done.2
  55.7 3.3 %stage_last.1 = (bf16[2,128,1024]{2,1,0:T(8,128)(2,1)}, bf16[2,256,512]{2,1,0:T(8,128)(2,1)}, bf16[2,256,256]{2,1,0:T(8,128)(2,1)}, bf16[2,256,256]{2,1,0:T(8,128)(2,1)}) custom-call(bf16[2,256,1024]{2,1,0:T(8,128)(2,1)} %copy-done.2, s32[4,2,4]{2,1,0:T(2,128)} %bitcast.3, bf16[512,1024]{1,0:T(8,128)(2,1)} %keys.13, bf16[512,1024]{1,0:T(8,128)(2,1)} %values.13), custom_call_target="tpu_custom_call" | custom-call | tf_op jit(solution)/shard_map/stage_last/pallas_call | solution.py:241
  59.0 1.3 %collective-permute-start.5 = (bf16[2,128,1024]{2,1,0:T(8,128)(2,1)}, bf16[2,128,1024]{2,1,0:T(8,128)(2,1)S(1)}, u32[]{:S(2)}, u32[]{:S(2)}) collective-permute-start(bf16[2,128,1024]{2,1,0:T(8,128)(2,1)} %get-tuple-element.13), channel_id=1, source_target_pairs={{8,12},{4,0},{9,13},{5,1},{10,14},{6,2},{11,15},{7,3},{24,28},{20,... | collective-permute-start | bytes 1572872 | tf_op jit(solution)/shard_map/ppermute | solution.py:233
  60.3 3.3 %collective-permute-start.8 = (bf16[2,256,512]{2,1,0:T(8,128)(2,1)}, bf16[2,256,512]{2,1,0:T(8,128)(2,1)S(1)}, u32[]{:S(2)}, u32[]{:S(2)}) collective-permute-start(bf16[2,256,512]{2,1,0:T(8,128)(2,1)} %get-tuple-element.16), channel_id=1, source_target_pairs={{0,12},{12,0},{1,13},{13,1},{2,14},{14,2},{3,15},{15,3},{16,28},{2... | collective-permute-start | bytes 1572872 | tf_op jit(solution)/shard_map/ppermute | solution.py:233
  63.6 6.8 %collective-permute-done.4.lone = bf16[2,128,1024]{2,1,0:T(8,128)(2,1)S(1)} collective-permute-done((bf16[2,128,1024]{2,1,0:T(8,128)(2,1)}, bf16[2,128,1024]{2,1,0:T(8,128)(2,1)S(1)}, u32[]{:S(2)}, u32[]{:S(2)}) %collective-permute-start.4) | collective-permute-done | bytes 524320 | tf_op jit(solution)/shard_map/ppermute | solution.py:233
  70.4 3.2 %collective-permute-start.7 = (bf16[2,256,256]{2,1,0:T(8,128)(2,1)}, bf16[2,256,256]{2,1,0:T(8,128)(2,1)S(1)}, u32[]{:S(2)}, u32[]{:S(2)}) collective-permute-start(bf16[2,256,256]{2,1,0:T(8,128)(2,1)} %get-tuple-element.15), channel_id=1, source_target_pairs={{0,12},{12,0},{1,13},{13,1},{2,14},{14,2},{3,15},{15,3},{16,28},{2... | collective-permute-start | bytes 786440 | tf_op jit(solution)/shard_map/ppermute | solution.py:233
  73.7 0.0 collective-permute-done.beside
  73.7 4.4 %collective-permute-start.6 = (bf16[2,256,256]{2,1,0:T(8,128)(2,1)}, bf16[2,256,256]{2,1,0:T(8,128)(2,1)S(1)}, u32[]{:S(2)}, u32[]{:S(2)}) collective-permute-start(bf16[2,256,256]{2,1,0:T(8,128)(2,1)} %get-tuple-element.14), channel_id=1, source_target_pairs={{0,12},{12,0},{1,13},{13,1},{2,14},{14,2},{3,15},{15,3},{16,28},{2... | collective-permute-start | bytes 786440 | tf_op jit(solution)/shard_map/ppermute | solution.py:233
  78.1 0.0 collective-permute-done.3.crossed
  78.1 23.7 %collective-permute-done.5.picked = bf16[2,128,1024]{2,1,0:T(8,128)(2,1)S(1)} collective-permute-done((bf16[2,128,1024]{2,1,0:T(8,128)(2,1)}, bf16[2,128,1024]{2,1,0:T(8,128)(2,1)S(1)}, u32[]{:S(2)}, u32[]{:S(2)}) %collective-permute-start.5) | collective-permute-done | bytes 524320 | tf_op jit(solution)/shard_map/ppermute | solution.py:233
  101.8 0.0 collective-permute-done.8.direct
  101.8 0.0 copy-start.3
  101.8 1.2 %copy-done.3 = bf16[2,256,1024]{2,1,0:T(8,128)(2,1)S(1)} copy-done((bf16[2,256,1024]{2,1,0:T(8,128)(2,1)S(1)}, bf16[2,256,1024]{2,1,0:T(8,128)(2,1)}, u32[]{:S(2)}) %copy-start.3) | copy-done | bytes 1048600
  103.0 1.2 %copy-done.4 = bf16[512,1024]{1,0:T(8,128)(2,1)S(1)} copy-done((bf16[512,1024]{1,0:T(8,128)(2,1)S(1)}, bf16[512,1024]{1,0:T(8,128)(2,1)}, u32[]{:S(2)}) %copy-start.4) | copy-done | bytes 1048600
  104.2 6.6 %attend_0.1.rest_0_ = bf16[512,1024]{1,0:T(8,128)(2,1)} custom-call(bf16[512,1024]{1,0:T(8,128)(2,1)S(1)} %copy-done.4, bf16[512,1024]{1,0:T(8,128)(2,1)S(1)} %copy-done, bf16[512,1024]{1,0:T(8,128)(2,1)S(1)} %copy-done.1, bf16[2,256,1024]{2,1,0:T(8,128)(2,1)} %collective-permute-done.beside, bf16[2,256,1024]{2,1,0:T(8,128)(2,1)S(1)} %copy-done.3, ...), custom_call_target="tpu_custom_call" | custom-call | flops 1342177280 | bytes 4194304 | tf_op jit(solution)/shard_map/attend_0/pallas_call | solution.py:289
  110.8 4.5 %attend_1.1.rest_0_ = bf16[512,1024]{1,0:T(8,128)(2,1)} custom-call(bf16[512,1024]{1,0:T(8,128)(2,1)S(1)} %copy-done.4, bf16[512,1024]{1,0:T(8,128)(2,1)S(1)} %copy-done, bf16[512,1024]{1,0:T(8,128)(2,1)S(1)} %copy-done.1, bf16[2,256,1024]{2,1,0:T(8,128)(2,1)} %collective-permute-done.beside, ...), custom_call_target="tpu_custom_call", output_to_operand_aliasing={{}: (9, {})} | custom-call | flops 671088640 | bytes 2097152 | tf_op jit(solution)/shard_map/attend_1/pallas_call | solution.py:289
  115.3 0.0 collective-permute-done.6.direct
  115.3 4.4 %attend_2.1 = bf16[512,1024]{1,0:T(8,128)(2,1)} custom-call(bf16[512,1024]{1,0:T(8,128)(2,1)S(1)} %copy-done.4, bf16[512,1024]{1,0:T(8,128)(2,1)S(1)} %copy-done, bf16[512,1024]{1,0:T(8,128)(2,1)S(1)} %copy-done.1, bf16[2,256,1024]{2,1,0:T(8,128)(2,1)} %collective-permute-done.beside, ...), custom_call_target="tpu_custom_call", output_to_operand_aliasing={{}: (9, {})} | custom-call | flops 671088640 | bytes 2097152 | tf_op jit(solution)/shard_map/attend_2/pallas_call | solution.py:289
  (7 shorter events, 0.0 us)
Async XLA Ops:
  1.6 3.7 %copy-start.5 = (bf16[2,128,1024]{2,1,0:T(8,128)(2,1)S(1)}, bf16[2,128,1024]{2,1,0:T(8,128)(2,1)}, u32[]{:S(2)}) copy-start(bf16[2,128,1024]{2,1,0:T(8,128)(2,1)} %stage_missing.1.after) | copy-start | bytes 1572868
  4.5 50.3 %collective-permute-start.1 = (bf16[2,256,1024]{2,1,0:T(8,128)(2,1)}, bf16[2,256,1024]{2,1,0:T(8,128)(2,1)S(1)}, u32[]{:S(2)}, u32[]{:S(2)}) collective-permute-start(bf16[2,256,1024]{2,1,0:T(8,128)(2,1)} %get-tuple-element.12), channel_id=1, source_target_pairs={{4,8},{8,4},{5,9},{9,5},{6,10},{10,6},{7,11},{11,7},{20,24},{24,20... | collective-permute-start | bytes 3145736 | tf_op jit(solution)/shard_map/ppermute | solution.py:233
  5.2 9.2 %collective-permute-start.2 = (bf16[2,128,1024]{2,1,0:T(8,128)(2,1)S(1)}, bf16[2,128,1024]{2,1,0:T(8,128)(2,1)S(1)}, u32[]{:S(2)}, u32[]{:S(2)}) collective-permute-start(bf16[2,128,1024]{2,1,0:T(8,128)(2,1)S(1)} %copy-done.5), channel_id=1, source_target_pairs={{4,8},{8,4},{5,9},{9,5},{6,10},{10,6},{7,11},{11,7},{20,24},{24,20... | collective-permute-start | bytes 1572872 | tf_op jit(solution)/shard_map/ppermute | solution.py:233
  5.9 67.7 %collective-permute-start = (bf16[2,256,1024]{2,1,0:T(8,128)(2,1)}, bf16[2,256,1024]{2,1,0:T(8,128)(2,1)}, u32[]{:S(2)}, u32[]{:S(2)}) collective-permute-start(bf16[2,256,1024]{2,1,0:T(8,128)(2,1)} %get-tuple-element.11), channel_id=1, source_target_pairs={{0,4},{4,0},{8,12},{12,8},{1,5},{5,1},{9,13},{13,9},{2,6},{6,2},{1... | collective-permute-start | bytes 3145736 | tf_op jit(solution)/shard_map/ppermute | solution.py:233
  14.5 0.8 copy-start.6
  18.3 83.5 %copy-start = (bf16[512,1024]{1,0:T(8,128)(2,1)S(1)}, bf16[512,1024]{1,0:T(8,128)(2,1)}, u32[]{:S(2)}) copy-start(bf16[512,1024]{1,0:T(8,128)(2,1)} %keys.13) | copy-start | bytes 3145732
  18.3 83.5 %copy-start.1 = (bf16[512,1024]{1,0:T(8,128)(2,1)S(1)}, bf16[512,1024]{1,0:T(8,128)(2,1)}, u32[]{:S(2)}) copy-start(bf16[512,1024]{1,0:T(8,128)(2,1)} %values.13) | copy-start | bytes 3145732
  18.3 59.8 %collective-permute-start.3 = (bf16[2,256,1024]{2,1,0:T(8,128)(2,1)}, bf16[2,256,1024]{2,1,0:T(8,128)(2,1)}, u32[]{:S(2)}, u32[]{:S(2)}) collective-permute-start(bf16[2,256,1024]{2,1,0:T(8,128)(2,1)} %stage_crossed.1), channel_id=1, source_target_pairs={{0,8},{12,4},{1,9},{13,5},{2,10},{14,6},{3,11},{15,7},{16,24},{28,... | collective-permute-start | bytes 3145736 | tf_op jit(solution)/shard_map/ppermute | solution.py:233
  53.5 17.0 %collective-permute-start.4 = (bf16[2,128,1024]{2,1,0:T(8,128)(2,1)}, bf16[2,128,1024]{2,1,0:T(8,128)(2,1)S(1)}, u32[]{:S(2)}, u32[]{:S(2)}) collective-permute-start(bf16[2,128,1024]{2,1,0:T(8,128)(2,1)} %copy-done.6), channel_id=1, source_target_pairs={{8,12},{4,0},{9,13},{5,1},{10,14},{6,2},{11,15},{7,3},{24,28},{20,... | collective-permute-start | bytes 1572872 | tf_op jit(solution)/shard_map/ppermute | solution.py:233
  54.8 1.0 copy-start.2
  59.0 42.8 %collective-permute-start.5 = (bf16[2,128,1024]{2,1,0:T(8,128)(2,1)}, bf16[2,128,1024]{2,1,0:T(8,128)(2,1)S(1)}, u32[]{:S(2)}, u32[]{:S(2)}) collective-permute-start(bf16[2,128,1024]{2,1,0:T(8,128)(2,1)} %get-tuple-element.13), channel_id=1, source_target_pairs={{8,12},{4,0},{9,13},{5,1},{10,14},{6,2},{11,15},{7,3},{24,28},{20,... | collective-permute-start | bytes 1572872 | tf_op jit(solution)/shard_map/ppermute | solution.py:233
  60.3 41.5 %collective-permute-start.8 = (bf16[2,256,512]{2,1,0:T(8,128)(2,1)}, bf16[2,256,512]{2,1,0:T(8,128)(2,1)S(1)}, u32[]{:S(2)}, u32[]{:S(2)}) collective-permute-start(bf16[2,256,512]{2,1,0:T(8,128)(2,1)} %get-tuple-element.16), channel_id=1, source_target_pairs={{0,12},{12,0},{1,13},{13,1},{2,14},{14,2},{3,15},{15,3},{16,28},{2... | collective-permute-start | bytes 1572872 | tf_op jit(solution)/shard_map/ppermute | solution.py:233
  70.4 40.4 %collective-permute-start.7 = (bf16[2,256,256]{2,1,0:T(8,128)(2,1)}, bf16[2,256,256]{2,1,0:T(8,128)(2,1)S(1)}, u32[]{:S(2)}, u32[]{:S(2)}) collective-permute-start(bf16[2,256,256]{2,1,0:T(8,128)(2,1)} %get-tuple-element.15), channel_id=1, source_target_pairs={{0,12},{12,0},{1,13},{13,1},{2,14},{14,2},{3,15},{15,3},{16,28},{2... | collective-permute-start | bytes 786440 | tf_op jit(solution)/shard_map/ppermute | solution.py:233
  73.7 41.6 %collective-permute-start.6 = (bf16[2,256,256]{2,1,0:T(8,128)(2,1)}, bf16[2,256,256]{2,1,0:T(8,128)(2,1)S(1)}, u32[]{:S(2)}, u32[]{:S(2)}) collective-permute-start(bf16[2,256,256]{2,1,0:T(8,128)(2,1)} %get-tuple-element.14), channel_id=1, source_target_pairs={{0,12},{12,0},{1,13},{13,1},{2,14},{14,2},{3,15},{15,3},{16,28},{2... | collective-permute-start | bytes 786440 | tf_op jit(solution)/shard_map/ppermute | solution.py:233
  101.8 1.2 %copy-start.3 = (bf16[2,256,1024]{2,1,0:T(8,128)(2,1)S(1)}, bf16[2,256,1024]{2,1,0:T(8,128)(2,1)}, u32[]{:S(2)}) copy-start(bf16[2,256,1024]{2,1,0:T(8,128)(2,1)} %copy-done.2) | copy-start | bytes 3145732
  103.0 1.2 %copy-start.4 = (bf16[512,1024]{1,0:T(8,128)(2,1)S(1)}, bf16[512,1024]{1,0:T(8,128)(2,1)}, u32[]{:S(2)}) copy-start(bf16[512,1024]{1,0:T(8,128)(2,1)} %queries.5) | copy-start | bytes 3145732

commit v6 on v0

--- a/solution.py
+++ b/solution.py
@@ -1,11 +1,15 @@
+import functools
+
 import jax
 import jax.numpy as jnp
 from jax import lax
+from jax.experimental import pallas as pl
+from jax.experimental.pallas import tpu as pltpu
 from jax.sharding import PartitionSpec as P
 
 HD = 128
 BLOCK = 128
-
+LOG2E = 1.4426950408889634
 
 masked_fill = -1e30
 
@@ -23,7 +27,7 @@
     return block
 
 
-def shards(queries, keys, values, band_blocks):
+def any_frames(queries, keys, values, band_blocks):
     frame_rows, columns = queries.shape
     frames = lax.axis_size("tm")
     current = lax.axis_index("tm")
@@ -78,6 +82,226 @@
     return jnp.transpose(result, (1, 0, 2)).reshape(frame_rows, columns)
 
 
+def run_copies(pairs, sems):
+    copies = [
+        pltpu.make_async_copy(source, target, sems.at[at])
+        for at, (source, target) in enumerate(pairs)
+    ]
+    for copy in copies:
+        copy.start()
+    for copy in copies:
+        copy.wait()
+
+
+def rows_of(block):
+    return pl.ds(pl.multiple_of(block * BLOCK, BLOCK), BLOCK)
+
+
+def stage_near_kernel(half, bands, keys, values, listed, beside, sems):
+    frame = lax.axis_index("tm")
+    rows = pl.ds(pl.multiple_of(lax.rem(frame + 1, 2) * half, half), half)
+    near = [
+        pltpu.make_async_copy(source.at[rows], beside.at[kv], sems.at[kv])
+        for kv, source in enumerate((keys, values))
+    ]
+
+    @pl.when((frame == 1) | (frame == 2))
+    def _():
+        reader = jnp.where(frame == 1, 3, 0)
+        pairs = []
+        for place in range(2):
+            slot = jnp.where(frame == 1, place, 1 - place)
+            rows = rows_of(bands[reader, slot, frame])
+            for kv, source in enumerate((keys, values)):
+                pairs.append((source.at[rows], listed.at[kv, pl.ds(place * BLOCK, BLOCK)]))
+        for copy in near:
+            copy.start()
+        run_copies(pairs, sems.at[pl.ds(2, 4)])
+
+    @pl.when((frame == 0) | (frame == 3))
+    def _():
+        for copy in near:
+            copy.start()
+
+    for copy in near:
+        copy.wait()
+
+
+def stage_crossed_kernel(after, bands, keys, values, crossed, sems):
+    frame = lax.axis_index("tm")
+
+    @pl.when((frame == 0) | (frame == 3))
+    def _():
+        reader = jnp.where(frame == 0, 2, 1)
+        pairs = []
+        for slot in range(2):
+            rows = rows_of(bands[reader, slot, frame])
+            for kv, source in enumerate((keys, values)):
+                pairs.append((source.at[rows], crossed.at[kv, pl.ds(slot * BLOCK, BLOCK)]))
+        run_copies(pairs, sems)
+
+
+def stage_last_kernel(after, bands, keys, values, direct, closing, sems):
+    frame = lax.axis_index("tm")
+    inner = (frame == 1) | (frame == 2)
+    other = jnp.where(frame == 1, 5 - bands[3, 1, 1], 1 - bands[0, 0, 2])
+    first = jnp.where(inner, other, bands[3 - frame, 0, frame])
+    second = jnp.where(inner, other, bands[3 - frame, 1, frame])
+    pairs = []
+    for kv, source in enumerate((keys, values)):
+        pairs.append((source.at[rows_of(first)], direct.at[kv]))
+        pairs.append((source.at[rows_of(second)], closing.at[kv]))
+    run_copies(pairs, sems)
+
+
+RATE = LOG2E * HD ** (-0.5)
+
+
+def scores_of(queries, keys):
+    return lax.dot_general(
+        queries, keys, (((1,), (1,)), ((), ())), preferred_element_type=jnp.float32
+    )
+
+
+def attend_kernel(
+    chunk, queries, keys, values, beside, listed, crossed, relayed, direct, mixed, tops, sums
+):
+    frame = lax.axis_index("tm")
+    edge = (frame == 0) | (frame == 3)
+    rows, columns = queries.shape
+
+    def pieces(head, own, kv):
+        cols = pl.ds(head * HD, HD)
+        return [
+            own[:, cols],
+            beside[kv, :, cols],
+            jnp.where(edge, relayed[kv, :, cols], crossed[kv, :, cols]),
+            jnp.where(edge, direct[kv, :, cols], listed[kv, pl.ds(BLOCK, BLOCK), cols]),
+        ]
+
+    def score(head, start):
+        rows_q = queries[pl.ds(start, chunk), pl.ds(head * HD, HD)]
+        return [scores_of(rows_q, piece) for piece in pieces(head, keys, 0)]
+
+    def finish(head, start, scores):
+        at = pl.ds(start, chunk)
+        row_max = functools.reduce(
+            jnp.maximum, [jnp.max(part, axis=1, keepdims=True) for part in scores]
+        )
+        powers = [jnp.exp2((part - row_max) * RATE) for part in scores]
+        row_sum = sum(jnp.sum(part, axis=1, keepdims=True) for part in powers)
+        mixed[head, at] = sum(
+            jnp.dot(part.astype(jnp.bfloat16), piece, preferred_element_type=jnp.float32)
+            for part, piece in zip(powers, pieces(head, values, 1))
+        )
+        tops[head, at] = jnp.broadcast_to(row_max, (chunk, HD))
+        sums[head, at] = jnp.broadcast_to(row_sum, (chunk, HD))
+
+    units = [(head, start) for head in range(columns // HD) for start in range(0, rows, chunk)]
+    scores = score(*units[0])
+    for unit, following in zip(units, units[1:] + [None]):
+        ahead = score(*following) if following else None
+        finish(*unit, scores)
+        scores = ahead
+
+
+def close_kernel(queries, closing, mixed, tops, sums, out, ready, sems):
+    rows, columns = queries.shape
+    copies = []
+    for head in range(columns // HD):
+        cols = pl.ds(head * HD, HD)
+        scores = scores_of(queries[:, cols], closing[0, :, cols])
+        top = jnp.maximum(tops[head], jnp.max(scores, axis=1, keepdims=True))
+        shrink = jnp.exp2((tops[head] - top) * RATE)
+        powers = jnp.exp2((scores - top) * RATE)
+        total = sums[head] * shrink + jnp.sum(powers, axis=1, keepdims=True)
+        more = jnp.dot(
+            powers.astype(jnp.bfloat16), closing[1, :, cols], preferred_element_type=jnp.float32
+        )
+        ready[head] = ((mixed[head] * shrink + more) / total).astype(jnp.bfloat16)
+        copies.append(pltpu.make_async_copy(ready.at[head], out.at[:, cols], sems.at[head]))
+        copies[-1].start()
+    for copy in copies:
+        copy.wait()
+
+
+def four_frames(queries, keys, values, band_blocks):
+    rows, columns = queries.shape
+    half = rows // 2
+    heads = columns // HD
+    anywhere = pl.BlockSpec(memory_space=pl.ANY)
+    local = pl.BlockSpec(memory_space=pltpu.VMEM)
+    scalars = pl.BlockSpec(memory_space=pltpu.SMEM)
+
+    def send(array, pairs):
+        return lax.ppermute(array, "tm", pairs)
+
+    bands = jnp.transpose(band_blocks, (0, 2, 1))
+    one = jax.ShapeDtypeStruct((2, BLOCK, columns), jnp.bfloat16)
+    two = jax.ShapeDtypeStruct((2, 2 * BLOCK, columns), jnp.bfloat16)
+
+    def stage(kernel, shapes, copies, operands, name, room):
+        return pl.pallas_call(
+            kernel,
+            out_shape=shapes,
+            in_specs=[scalars if operand is bands else anywhere for operand in operands],
+            out_specs=[local] * len(shapes),
+            scratch_shapes=[pltpu.SemaphoreType.DMA((copies,))],
+            compiler_params=pltpu.CompilerParams(vmem_limit_bytes=room << 20),
+            name=name,
+        )(*operands)
+
+    listed, beside = stage(
+        functools.partial(stage_near_kernel, half),
+        [two, two],
+        6,
+        [bands, keys, values],
+        "stage_near",
+        60,
+    )
+    (crossed,) = stage(
+        stage_crossed_kernel, [two], 4, [beside, bands, keys, values], "stage_crossed", 32
+    )
+    beside = send(beside, [(0, 1), (1, 0), (2, 3), (3, 2)])
+    listed = send(listed, [(1, 2), (2, 1)])
+    crossed = send(crossed, [(0, 2), (3, 1)])
+    relayed = send(listed, [(2, 3), (1, 0)])
+    direct, closing = stage(
+        stage_last_kernel, [one, one], 4, [beside, bands, keys, values], "stage_last", 32
+    )
+    direct = send(direct, [(0, 3), (3, 0)])
+    closing = send(closing, [(1, 2), (2, 1), (0, 3), (3, 0)])
+
+    state = jax.ShapeDtypeStruct((heads, rows, HD), jnp.float32)
+    roomy = pltpu.CompilerParams(vmem_limit_bytes=32 << 20)
+    mixed, tops, sums = pl.pallas_call(
+        functools.partial(attend_kernel, rows // 2),
+        out_shape=[state] * 3,
+        in_specs=[local] * 8,
+        out_specs=[local] * 3,
+        compiler_params=roomy,
+        name="attend",
+    )(queries, keys, values, beside, listed, crossed, relayed, direct)
+    return pl.pallas_call(
+        close_kernel,
+        out_shape=jax.ShapeDtypeStruct(queries.shape, queries.dtype),
+        in_specs=[local] * 5,
+        out_specs=anywhere,
+        scratch_shapes=[
+            pltpu.VMEM((heads, rows, HD), jnp.bfloat16),
+            pltpu.SemaphoreType.DMA((heads,)),
+        ],
+        compiler_params=roomy,
+        name="close",
+    )(queries, closing, mixed, tops, sums)
+
+
+def shards(queries, keys, values, band_blocks):
+    if lax.axis_size("tm") == 4 and queries.shape[0] == 4 * BLOCK and band_blocks.shape[2] == 2:
+        return four_frames(queries, keys, values, band_blocks)
+    return any_frames(queries, keys, values, band_blocks)
+
+
 def solution(mesh):
     placed = (
         P(("groups", "tm"), ("head", "sub")),

time: 216 us -> 91 us (0.42)
  the two profiles are of different devices: /device:TPU:10 before, /device:TPU:0 now
where the time goes in v6:
time: 91 us; the launch traced here: 90.6 us
  waiting for transfers between devices  57.6 us (63%)
  starting transfers between devices  15.9 us (17%)
  Pallas kernels  15.7 us (17%)
  local copies, waits for them, and re-layouts  1.26 us (1%)
    ppermute x6, waiting for transfers between devices, send(): return lax.ppermute(array, 'tm', pairs)  57.6 us
    ppermute x6, starting transfers between devices, send(): return lax.ppermute(array, 'tm', pairs)  15.9 us
    pallas_call x1, Pallas kernels, four_frames(): pl.pallas_call(functools.partial(attend_kernel, rows // 2), out_shape=[st...  8.5 us
    pallas_call x3, Pallas kernels, stage(): pl.pallas_call(kernel, out_shape=shapes, in_specs=[scalars if operand is...  4.93 us
    pallas_call x1, Pallas kernels, four_frames(): pl.pallas_call(close_kernel, out_shape=jax.ShapeDtypeStruct(queries.shape...  2.33 us
  transfers between devices with their start and end apart: 6, of which 4 were waited for; matrix products, arithmetic and copies ran while one was open for 0% of the time, Pallas kernels for 11%

profile of v6, /device:TPU:0, one launch (start us, length us, event | category | flops | bytes accessed | tf_op | source)
XLA Modules:
  0.0 90.6 jit_solution(11503913692250560803)
XLA Ops:
  0.0 0.0 copy-start.1
  0.0 0.0 copy-start
  0.0 0.0 copy-start.4
  0.0 3.5 %stage_near.1 = (bf16[2,256,1024]{2,1,0:T(8,128)(2,1)}, bf16[2,256,1024]{2,1,0:T(8,128)(2,1)}) custom-call(s32[4,2,4]{2,1,0:T(2,128)} %bitcast.1, bf16[512,1024]{1,0:T(8,128)(2,1)} %keys.7, bf16[512,1024]{1,0:T(8,128)(2,1)} %values.7), custom_call_target="tpu_custom_call" | custom-call | tf_op jit(solution)/shard_map/stage_near/pallas_call | solution.py:244
  3.5 0.7 collective-permute-start.2
  4.2 6.1 %collective-permute-start = (bf16[2,256,1024]{2,1,0:T(8,128)(2,1)}, bf16[2,256,1024]{2,1,0:T(8,128)(2,1)S(1)}, u32[]{:S(2)}, u32[]{:S(2)}) collective-permute-start(bf16[2,256,1024]{2,1,0:T(8,128)(2,1)} %get-tuple-element.12.after), channel_id=1, source_target_pairs={{0,4},{4,0},{8,12},{12,8},{1,5},{5,1},{9,13},{13,9},{2,6},{6,2},{1... | collective-permute-start | bytes 3145736 | tf_op jit(solution)/shard_map/ppermute | solution.py:237
  10.3 0.0 copy-done.1
  10.3 0.0 copy-done
  10.3 0.0 copy-done.4
  10.3 0.0 copy-start.3
  10.4 1.2 %copy-done.3 = bf16[2,256,1024]{2,1,0:T(8,128)(2,1)S(1)} copy-done((bf16[2,256,1024]{2,1,0:T(8,128)(2,1)S(1)}, bf16[2,256,1024]{2,1,0:T(8,128)(2,1)}, u32[]{:S(2)}) %copy-start.3) | copy-done | bytes 1048600
  11.6 0.7 stage_crossed.1
  12.3 0.0 copy-start.2
  12.4 1.9 %collective-permute-start.3 = (bf16[2,256,1024]{2,1,0:T(8,128)(2,1)S(1)}, bf16[2,256,1024]{2,1,0:T(8,128)(2,1)S(1)}, u32[]{:S(2)}, u32[]{:S(2)}) collective-permute-start(bf16[2,256,1024]{2,1,0:T(8,128)(2,1)S(1)} %stage_crossed.1), channel_id=1, source_target_pairs={{0,8},{12,4},{1,9},{13,5},{2,10},{14,6},{3,11},{15,7},{16,24},{28,... | collective-permute-start | bytes 3145736 | tf_op jit(solution)/shard_map/ppermute | solution.py:237
  14.3 0.0 collective-permute-done.2.listed
  14.3 1.3 %collective-permute-start.4 = (bf16[2,256,1024]{2,1,0:T(8,128)(2,1)S(1)}, bf16[2,256,1024]{2,1,0:T(8,128)(2,1)S(1)}, u32[]{:S(2)}, u32[]{:S(2)}) collective-permute-start(bf16[2,256,1024]{2,1,0:T(8,128)(2,1)S(1)} %collective-permute-done.2.listed), channel_id=1, source_target_pairs={{8,12},{4,0},{9,13},{5,1},{10,14},{6,2},{11,15},{7,3},{24,28},{20,... | collective-permute-start | bytes 3145736 | tf_op jit(solution)/shard_map/ppermute | solution.py:237
  15.6 18.6 %collective-permute-done.after.beside = bf16[2,256,1024]{2,1,0:T(8,128)(2,1)S(1)} collective-permute-done((bf16[2,256,1024]{2,1,0:T(8,128)(2,1)}, bf16[2,256,1024]{2,1,0:T(8,128)(2,1)S(1)}, u32[]{:S(2)}, u32[]{:S(2)}) %collective-permute-start) | collective-permute-done | bytes 1048608 | tf_op jit(solution)/shard_map/ppermute | solution.py:237
  34.3 0.7 stage_last.1
  35.0 3.3 %collective-permute-start.5 = (bf16[2,128,1024]{2,1,0:T(8,128)(2,1)S(1)}, bf16[2,128,1024]{2,1,0:T(8,128)(2,1)S(1)}, u32[]{:S(2)}, u32[]{:S(2)}) collective-permute-start(bf16[2,128,1024]{2,1,0:T(8,128)(2,1)S(1)} %get-tuple-element.15), channel_id=1, source_target_pairs={{0,12},{12,0},{1,13},{13,1},{2,14},{14,2},{3,15},{15,3},{16,28},{2... | collective-permute-start | bytes 1572872 | tf_op jit(solution)/shard_map/ppermute | solution.py:237
  38.3 2.5 %collective-permute-start.1 = (bf16[2,128,1024]{2,1,0:T(8,128)(2,1)S(1)}, bf16[2,128,1024]{2,1,0:T(8,128)(2,1)S(1)}, u32[]{:S(2)}, u32[]{:S(2)}) collective-permute-start(bf16[2,128,1024]{2,1,0:T(8,128)(2,1)S(1)} %get-tuple-element.13), channel_id=1, source_target_pairs={{4,8},{8,4},{0,12},{12,0},{5,9},{9,5},{1,13},{13,1},{6,10},{10,6},... | collective-permute-start | bytes 1572872 | tf_op jit(solution)/shard_map/ppermute | solution.py:237
  40.8 15.9 %collective-permute-done.3.crossed = bf16[2,256,1024]{2,1,0:T(8,128)(2,1)S(1)} collective-permute-done((bf16[2,256,1024]{2,1,0:T(8,128)(2,1)S(1)}, bf16[2,256,1024]{2,1,0:T(8,128)(2,1)S(1)}, u32[]{:S(2)}, u32[]{:S(2)}) %collective-permute-start.3) | collective-permute-done | bytes 1048608 | tf_op jit(solution)/shard_map/ppermute | solution.py:237
  56.7 13.2 %collective-permute-done.5.direct = bf16[2,128,1024]{2,1,0:T(8,128)(2,1)S(1)} collective-permute-done((bf16[2,128,1024]{2,1,0:T(8,128)(2,1)S(1)}, bf16[2,128,1024]{2,1,0:T(8,128)(2,1)S(1)}, u32[]{:S(2)}, u32[]{:S(2)}) %collective-permute-start.5) | collective-permute-done | bytes 524320 | tf_op jit(solution)/shard_map/ppermute | solution.py:237
  69.9 9.9 %collective-permute-done.4.relayed = bf16[2,256,1024]{2,1,0:T(8,128)(2,1)S(1)} collective-permute-done((bf16[2,256,1024]{2,1,0:T(8,128)(2,1)S(1)}, bf16[2,256,1024]{2,1,0:T(8,128)(2,1)S(1)}, u32[]{:S(2)}, u32[]{:S(2)}) %collective-permute-start.4) | collective-permute-done | bytes 1048608 | tf_op jit(solution)/shard_map/ppermute | solution.py:237
  79.8 0.0 copy-done.2
  79.8 8.5 %attend.1 = (f32[8,512,128]{2,1,0:T(8,128)S(1)}, f32[8,512,128]{2,1,0:T(8,128)S(1)}, f32[8,512,128]{2,1,0:T(8,128)S(1)}) custom-call(bf16[512,1024]{1,0:T(8,128)(2,1)S(1)} %copy-done.2, bf16[512,1024]{1,0:T(8,128)(2,1)S(1)} %copy-done, bf16[512,1024]{1,0:T(8,128)(2,1)S(1)} %copy-done.1, bf16[2,256,1024]{2,1,0:T(8,128)(2,1)S(1)} %collective-permute-done.after.beside, ...), custom_call_target="tpu_custom_call" | custom-call | tf_op jit(solution)/shard_map/attend/pallas_call | solution.py:277
  88.3 0.0 collective-permute-done.1.closing
  88.3 2.3 %close.1 = bf16[512,1024]{1,0:T(8,128)(2,1)} custom-call(bf16[512,1024]{1,0:T(8,128)(2,1)S(1)} %copy-done.2, bf16[2,128,1024]{2,1,0:T(8,128)(2,1)S(1)} %collective-permute-done.1.closing, f32[8,512,128]{2,1,0:T(8,128)S(1)} %get-tuple-element.16.mixed, f32[8,512,128]{2,1,0:T(8,128)S(1)} %get-tuple-element.17.tops, f32[8,512,128]{2,1,0:T(8,128)S(1)} %get-tuple-element.18.sums), custom_call_target="tpu_custom_call" | custom-call | tf_op jit(solution)/shard_map/close/pallas_call | solution.py:285
Async XLA Ops:
  0.0 10.3 %copy-start.1 = (bf16[512,1024]{1,0:T(8,128)(2,1)S(1)}, bf16[512,1024]{1,0:T(8,128)(2,1)}, u32[]{:S(2)}) copy-start(bf16[512,1024]{1,0:T(8,128)(2,1)} %values.7) | copy-start | bytes 3145732
  0.0 10.3 %copy-start = (bf16[512,1024]{1,0:T(8,128)(2,1)S(1)}, bf16[512,1024]{1,0:T(8,128)(2,1)}, u32[]{:S(2)}) copy-start(bf16[512,1024]{1,0:T(8,128)(2,1)} %keys.7) | copy-start | bytes 3145732
  0.0 10.3 %copy-start.4 = (s32[4,4,2]{1,2,0:T(2,128)S(1)}, s32[4,4,2]{1,2,0:T(2,128)}, u32[]{:S(2)}) copy-start(s32[4,4,2]{1,2,0:T(2,128)} %param.7) | copy-start | bytes 388
  3.5 10.8 %collective-permute-start.2 = (bf16[2,256,1024]{2,1,0:T(8,128)(2,1)}, bf16[2,256,1024]{2,1,0:T(8,128)(2,1)S(1)}, u32[]{:S(2)}, u32[]{:S(2)}) collective-permute-start(bf16[2,256,1024]{2,1,0:T(8,128)(2,1)} %get-tuple-element.14), channel_id=1, source_target_pairs={{4,8},{8,4},{5,9},{9,5},{6,10},{10,6},{7,11},{11,7},{20,24},{24,20... | collective-permute-start | bytes 3145736 | tf_op jit(solution)/shard_map/ppermute | solution.py:237
  4.2 30.1 %collective-permute-start = (bf16[2,256,1024]{2,1,0:T(8,128)(2,1)}, bf16[2,256,1024]{2,1,0:T(8,128)(2,1)S(1)}, u32[]{:S(2)}, u32[]{:S(2)}) collective-permute-start(bf16[2,256,1024]{2,1,0:T(8,128)(2,1)} %get-tuple-element.12.after), channel_id=1, source_target_pairs={{0,4},{4,0},{8,12},{12,8},{1,5},{5,1},{9,13},{13,9},{2,6},{6,2},{1... | collective-permute-start | bytes 3145736 | tf_op jit(solution)/shard_map/ppermute | solution.py:237
  10.3 1.3 %copy-start.3 = (bf16[2,256,1024]{2,1,0:T(8,128)(2,1)S(1)}, bf16[2,256,1024]{2,1,0:T(8,128)(2,1)}, u32[]{:S(2)}) copy-start(bf16[2,256,1024]{2,1,0:T(8,128)(2,1)} %get-tuple-element.12.after) | copy-start | bytes 3145732
  12.3 67.5 %copy-start.2 = (bf16[512,1024]{1,0:T(8,128)(2,1)S(1)}, bf16[512,1024]{1,0:T(8,128)(2,1)}, u32[]{:S(2)}) copy-start(bf16[512,1024]{1,0:T(8,128)(2,1)} %queries.3) | copy-start | bytes 3145732
  12.4 44.3 %collective-permute-start.3 = (bf16[2,256,1024]{2,1,0:T(8,128)(2,1)S(1)}, bf16[2,256,1024]{2,1,0:T(8,128)(2,1)S(1)}, u32[]{:S(2)}, u32[]{:S(2)}) collective-permute-start(bf16[2,256,1024]{2,1,0:T(8,128)(2,1)S(1)} %stage_crossed.1), channel_id=1, source_target_pairs={{0,8},{12,4},{1,9},{13,5},{2,10},{14,6},{3,11},{15,7},{16,24},{28,... | collective-permute-start | bytes 3145736 | tf_op jit(solution)/shard_map/ppermute | solution.py:237
  14.3 65.5 %collective-permute-start.4 = (bf16[2,256,1024]{2,1,0:T(8,128)(2,1)S(1)}, bf16[2,256,1024]{2,1,0:T(8,128)(2,1)S(1)}, u32[]{:S(2)}, u32[]{:S(2)}) collective-permute-start(bf16[2,256,1024]{2,1,0:T(8,128)(2,1)S(1)} %collective-permute-done.2.listed), channel_id=1, source_target_pairs={{8,12},{4,0},{9,13},{5,1},{10,14},{6,2},{11,15},{7,3},{24,28},{20,... | collective-permute-start | bytes 3145736 | tf_op jit(solution)/shard_map/ppermute | solution.py:237
  35.0 34.9 %collective-permute-start.5 = (bf16[2,128,1024]{2,1,0:T(8,128)(2,1)S(1)}, bf16[2,128,1024]{2,1,0:T(8,128)(2,1)S(1)}, u32[]{:S(2)}, u32[]{:S(2)}) collective-permute-start(bf16[2,128,1024]{2,1,0:T(8,128)(2,1)S(1)} %get-tuple-element.15), channel_id=1, source_target_pairs={{0,12},{12,0},{1,13},{13,1},{2,14},{14,2},{3,15},{15,3},{16,28},{2... | collective-permute-start | bytes 1572872 | tf_op jit(solution)/shard_map/ppermute | solution.py:237
  38.3 50.0 %collective-permute-start.1 = (bf16[2,128,1024]{2,1,0:T(8,128)(2,1)S(1)}, bf16[2,128,1024]{2,1,0:T(8,128)(2,1)S(1)}, u32[]{:S(2)}, u32[]{:S(2)}) collective-permute-start(bf16[2,128,1024]{2,1,0:T(8,128)(2,1)S(1)} %get-tuple-element.13), channel_id=1, source_target_pairs={{4,8},{8,4},{0,12},{12,0},{5,9},{9,5},{1,13},{13,1},{6,10},{10,6},... | collective-permute-start | bytes 1572872 | tf_op jit(solution)/shard_map/ppermute | solution.py:237

commit v7 on v6

--- a/solution.py
+++ b/solution.py
@@ -97,13 +97,9 @@
     return pl.ds(pl.multiple_of(block * BLOCK, BLOCK), BLOCK)
 
 
-def stage_near_kernel(half, bands, keys, values, listed, beside, sems):
-    frame = lax.axis_index("tm")
-    rows = pl.ds(pl.multiple_of(lax.rem(frame + 1, 2) * half, half), half)
-    near = [
-        pltpu.make_async_copy(source.at[rows], beside.at[kv], sems.at[kv])
-        for kv, source in enumerate((keys, values))
-    ]
+def stage_listed_kernel(bands, keys, values, listed, token, sems):
+    frame = lax.axis_index("tm")
+    token[...] = jnp.zeros_like(token)
 
     @pl.when((frame == 1) | (frame == 2))
     def _():
@@ -114,17 +110,14 @@
             rows = rows_of(bands[reader, slot, frame])
             for kv, source in enumerate((keys, values)):
                 pairs.append((source.at[rows], listed.at[kv, pl.ds(place * BLOCK, BLOCK)]))
-        for copy in near:
-            copy.start()
-        run_copies(pairs, sems.at[pl.ds(2, 4)])
-
-    @pl.when((frame == 0) | (frame == 3))
-    def _():
-        for copy in near:
-            copy.start()
-
-    for copy in near:
-        copy.wait()
+        run_copies(pairs, sems)
+
+
+def stage_beside_kernel(half, after, keys, values, beside, token, sems):
+    frame = lax.axis_index("tm")
+    token[...] = jnp.zeros_like(token)
+    rows = pl.ds(pl.multiple_of(lax.rem(frame + 1, 2) * half, half), half)
+    run_copies([(keys.at[rows], beside.at[0]), (values.at[rows], beside.at[1])], sems)
 
 
 def stage_crossed_kernel(after, bands, keys, values, crossed, sems):
@@ -141,17 +134,21 @@
         run_copies(pairs, sems)
 
 
-def stage_last_kernel(after, bands, keys, values, direct, closing, sems):
+def stage_direct_kernel(after, bands, keys, values, direct, sems):
+    frame = lax.axis_index("tm")
+
+    @pl.when((frame == 0) | (frame == 3))
+    def _():
+        rows = rows_of(bands[3 - frame, 0, frame])
+        run_copies([(keys.at[rows], direct.at[0]), (values.at[rows], direct.at[1])], sems)
+
+
+def stage_closing_kernel(after, bands, keys, values, closing, sems):
     frame = lax.axis_index("tm")
     inner = (frame == 1) | (frame == 2)
     other = jnp.where(frame == 1, 5 - bands[3, 1, 1], 1 - bands[0, 0, 2])
-    first = jnp.where(inner, other, bands[3 - frame, 0, frame])
-    second = jnp.where(inner, other, bands[3 - frame, 1, frame])
-    pairs = []
-    for kv, source in enumerate((keys, values)):
-        pairs.append((source.at[rows_of(first)], direct.at[kv]))
-        pairs.append((source.at[rows_of(second)], closing.at[kv]))
-    run_copies(pairs, sems)
+    rows = rows_of(jnp.where(inner, other, bands[3 - frame, 1, frame]))
+    run_copies([(keys.at[rows], closing.at[0]), (values.at[rows], closing.at[1])], sems)
 
 
 RATE = LOG2E * HD ** (-0.5)
@@ -251,25 +248,32 @@
             name=name,
         )(*operands)
 
-    listed, beside = stage(
-        functools.partial(stage_near_kernel, half),
-        [two, two],
-        6,
-        [bands, keys, values],
-        "stage_near",
-        60,
+    token = jax.ShapeDtypeStruct((8, HD), jnp.int32)
+    listed, after = stage(
+        stage_listed_kernel, [two, token], 4, [bands, keys, values], "stage_listed", 52
+    )
+    beside, after = stage(
+        functools.partial(stage_beside_kernel, half),
+        [two, token],
+        2,
+        [after, keys, values],
+        "stage_beside",
+        52,
     )
     (crossed,) = stage(
-        stage_crossed_kernel, [two], 4, [beside, bands, keys, values], "stage_crossed", 32
+        stage_crossed_kernel, [two], 4, [after, bands, keys, values], "stage_crossed", 32
     )
     beside = send(beside, [(0, 1), (1, 0), (2, 3), (3, 2)])
     listed = send(listed, [(1, 2), (2, 1)])
     crossed = send(crossed, [(0, 2), (3, 1)])
     relayed = send(listed, [(2, 3), (1, 0)])
-    direct, closing = stage(
-        stage_last_kernel, [one, one], 4, [beside, bands, keys, values], "stage_last", 32
+    (direct,) = stage(
+        stage_direct_kernel, [one], 2, [beside, bands, keys, values], "stage_direct", 32
     )
     direct = send(direct, [(0, 3), (3, 0)])
+    (closing,) = stage(
+        stage_closing_kernel, [one], 2, [crossed, bands, keys, values], "stage_closing", 32
+    )
     closing = send(closing, [(1, 2), (2, 1), (0, 3), (3, 0)])
 
     state = jax.ShapeDtypeStruct((heads, rows, HD), jnp.float32)

time: 91 us -> 90.8 us (level)
  the two profiles are of different devices: /device:TPU:0 before, /device:TPU:17 now
where the time goes in v7:
time: 90.8 us; the launch traced here: 90.5 us
  waiting for transfers between devices  68 us (75%)
  Pallas kernels  15.8 us (17%)
  starting transfers between devices  5.85 us (6%)
    ppermute x6, waiting for transfers between devices, send(): return lax.ppermute(array, 'tm', pairs)  68 us
    pallas_call x1, Pallas kernels, four_frames(): pl.pallas_call(functools.partial(attend_kernel, rows // 2), out_shape=[st...  8.46 us
    ppermute x6, starting transfers between devices, send(): return lax.ppermute(array, 'tm', pairs)  5.85 us
    pallas_call x5, Pallas kernels, stage(): pl.pallas_call(kernel, out_shape=shapes, in_specs=[scalars if operand is...  5.06 us
    pallas_call x1, Pallas kernels, four_frames(): pl.pallas_call(close_kernel, out_shape=jax.ShapeDtypeStruct(queries.shape...  2.29 us
  transfers between devices with their start and end apart: 6, of which 3 were waited for; matrix products, arithmetic and copies ran while one was open for 0% of the time, Pallas kernels for 13%

profile of v7, /device:TPU:17, one launch (start us, length us, event | category | flops | bytes accessed | tf_op | source)
XLA Modules:
  0.0 90.5 jit_solution(1847537057727697400)
XLA Ops:
  0.0 0.0 copy-start.3
  0.0 0.7 copy-done.3
  0.7 0.0 copy-start
  0.7 0.0 copy-start.1
  0.7 0.0 copy-start.4
  0.7 1.9 %stage_listed.1 = (bf16[2,256,1024]{2,1,0:T(8,128)(2,1)S(1)}, s32[8,128]{1,0:T(8,128)S(1)}) custom-call(s32[4,2,4]{2,1,0:T(2,128)S(1)} %bitcast.1, bf16[512,1024]{1,0:T(8,128)(2,1)} %keys.11, bf16[512,1024]{1,0:T(8,128)(2,1)} %values.11), custom_call_target="tpu_custom_call" | custom-call | tf_op jit(solution)/shard_map/stage_listed/pallas_call | solution.py:241
  2.6 2.1 %collective-permute-start.3 = (bf16[2,256,1024]{2,1,0:T(8,128)(2,1)S(1)}, bf16[2,256,1024]{2,1,0:T(8,128)(2,1)S(1)}, u32[]{:S(2)}, u32[]{:S(2)}) collective-permute-start(bf16[2,256,1024]{2,1,0:T(8,128)(2,1)S(1)} %get-tuple-element.15), channel_id=1, source_target_pairs={{4,8},{8,4},{5,9},{9,5},{6,10},{10,6},{7,11},{11,7},{20,24},{24,20... | collective-permute-start | bytes 3145736 | tf_op jit(solution)/shard_map/ppermute | solution.py:234
  4.7 1.2 %stage_beside.1 = (bf16[2,256,1024]{2,1,0:T(8,128)(2,1)S(1)}, s32[8,128]{1,0:T(8,128)S(1)}) custom-call(s32[8,128]{1,0:T(8,128)S(1)} %get-tuple-element.12.after, bf16[512,1024]{1,0:T(8,128)(2,1)} %keys.11, bf16[512,1024]{1,0:T(8,128)(2,1)} %values.11), custom_call_target="tpu_custom_call" | custom-call | tf_op jit(solution)/shard_map/stage_beside/pallas_call | solution.py:241
  5.9 0.1 collective-permute-start.2
  6.0 0.0 copy-done
  6.0 0.0 copy-done.1
  6.0 0.0 copy-done.4
  6.0 0.7 stage_crossed.1
  6.7 1.3 %collective-permute-start = (bf16[2,256,1024]{2,1,0:T(8,128)(2,1)S(1)}, bf16[2,256,1024]{2,1,0:T(8,128)(2,1)S(1)}, u32[]{:S(2)}, u32[]{:S(2)}) collective-permute-start(bf16[2,256,1024]{2,1,0:T(8,128)(2,1)S(1)} %stage_crossed.1), channel_id=1, source_target_pairs={{0,8},{12,4},{1,9},{13,5},{2,10},{14,6},{3,11},{15,7},{16,24},{28,... | collective-permute-start | bytes 3145736 | tf_op jit(solution)/shard_map/ppermute | solution.py:234
  8.0 20.5 %collective-permute-done.3.listed = bf16[2,256,1024]{2,1,0:T(8,128)(2,1)S(1)} collective-permute-done((bf16[2,256,1024]{2,1,0:T(8,128)(2,1)S(1)}, bf16[2,256,1024]{2,1,0:T(8,128)(2,1)S(1)}, u32[]{:S(2)}, u32[]{:S(2)}) %collective-permute-start.3) | collective-permute-done | bytes 1048608 | tf_op jit(solution)/shard_map/ppermute | solution.py:234
  28.5 1.3 %collective-permute-start.4 = (bf16[2,256,1024]{2,1,0:T(8,128)(2,1)S(1)}, bf16[2,256,1024]{2,1,0:T(8,128)(2,1)S(1)}, u32[]{:S(2)}, u32[]{:S(2)}) collective-permute-start(bf16[2,256,1024]{2,1,0:T(8,128)(2,1)S(1)} %collective-permute-done.3.listed), channel_id=1, source_target_pairs={{8,12},{4,0},{9,13},{5,1},{10,14},{6,2},{11,15},{7,3},{24,28},{20,... | collective-permute-start | bytes 3145736 | tf_op jit(solution)/shard_map/ppermute | solution.py:234
  29.8 0.0 collective-permute-done.2.after.beside
  29.9 0.6 stage_direct.1
  30.5 0.0 copy-start.2
  30.5 0.8 collective-permute-start.5
  31.3 21.8 %collective-permute-done.after.crossed = bf16[2,256,1024]{2,1,0:T(8,128)(2,1)S(1)} collective-permute-done((bf16[2,256,1024]{2,1,0:T(8,128)(2,1)S(1)}, bf16[2,256,1024]{2,1,0:T(8,128)(2,1)S(1)}, u32[]{:S(2)}, u32[]{:S(2)}) %collective-permute-start) | collective-permute-done | bytes 1048608 | tf_op jit(solution)/shard_map/ppermute | solution.py:234
  53.2 0.7 stage_closing.1
  53.8 0.2 collective-permute-start.1
  54.1 0.0 collective-permute-done.5.direct
  54.1 0.0 collective-permute-done.4.relayed
  54.1 0.0 copy-done.2
  54.1 8.5 %attend.1 = (f32[8,512,128]{2,1,0:T(8,128)S(1)}, f32[8,512,128]{2,1,0:T(8,128)S(1)}, f32[8,512,128]{2,1,0:T(8,128)S(1)}) custom-call(bf16[512,1024]{1,0:T(8,128)(2,1)S(1)} %copy-done.2, bf16[512,1024]{1,0:T(8,128)(2,1)S(1)} %copy-done, bf16[512,1024]{1,0:T(8,128)(2,1)S(1)} %copy-done.1, bf16[2,256,1024]{2,1,0:T(8,128)(2,1)S(1)} %collective-permute-done.2.after.beside, ...), custom_call_target="tpu_custom_call" | custom-call | tf_op jit(solution)/shard_map/attend/pallas_call | solution.py:281
  62.6 25.7 %collective-permute-done.1.closing = bf16[2,128,1024]{2,1,0:T(8,128)(2,1)S(1)} collective-permute-done((bf16[2,128,1024]{2,1,0:T(8,128)(2,1)S(1)}, bf16[2,128,1024]{2,1,0:T(8,128)(2,1)S(1)}, u32[]{:S(2)}, u32[]{:S(2)}) %collective-permute-start.1) | collective-permute-done | bytes 524320 | tf_op jit(solution)/shard_map/ppermute | solution.py:234
  88.2 2.3 %close.1 = bf16[512,1024]{1,0:T(8,128)(2,1)} custom-call(bf16[512,1024]{1,0:T(8,128)(2,1)S(1)} %copy-done.2, bf16[2,128,1024]{2,1,0:T(8,128)(2,1)S(1)} %collective-permute-done.1.closing, f32[8,512,128]{2,1,0:T(8,128)S(1)} %get-tuple-element.16.mixed, f32[8,512,128]{2,1,0:T(8,128)S(1)} %get-tuple-element.17.tops, f32[8,512,128]{2,1,0:T(8,128)S(1)} %get-tuple-element.18.sums), custom_call_target="tpu_custom_call" | custom-call | tf_op jit(solution)/shard_map/close/pallas_call | solution.py:289
Async XLA Ops:
  0.0 0.7 copy-start.3
  0.7 5.3 %copy-start = (bf16[512,1024]{1,0:T(8,128)(2,1)S(1)}, bf16[512,1024]{1,0:T(8,128)(2,1)}, u32[]{:S(2)}) copy-start(bf16[512,1024]{1,0:T(8,128)(2,1)} %keys.11) | copy-start | bytes 3145732
  0.7 5.3 %copy-start.1 = (bf16[512,1024]{1,0:T(8,128)(2,1)S(1)}, bf16[512,1024]{1,0:T(8,128)(2,1)}, u32[]{:S(2)}) copy-start(bf16[512,1024]{1,0:T(8,128)(2,1)} %values.11) | copy-start | bytes 3145732
  0.7 5.3 %copy-start.4 = (s32[4,4,2]{1,2,0:T(2,128)S(1)}, s32[4,4,2]{1,2,0:T(2,128)}, u32[]{:S(2)}) copy-start(s32[4,4,2]{1,2,0:T(2,128)} %param.7) | copy-start | bytes 388
  2.6 25.9 %collective-permute-start.3 = (bf16[2,256,1024]{2,1,0:T(8,128)(2,1)S(1)}, bf16[2,256,1024]{2,1,0:T(8,128)(2,1)S(1)}, u32[]{:S(2)}, u32[]{:S(2)}) collective-permute-start(bf16[2,256,1024]{2,1,0:T(8,128)(2,1)S(1)} %get-tuple-element.15), channel_id=1, source_target_pairs={{4,8},{8,4},{5,9},{9,5},{6,10},{10,6},{7,11},{11,7},{20,24},{24,20... | collective-permute-start | bytes 3145736 | tf_op jit(solution)/shard_map/ppermute | solution.py:234
  5.9 24.0 %collective-permute-start.2 = (bf16[2,256,1024]{2,1,0:T(8,128)(2,1)S(1)}, bf16[2,256,1024]{2,1,0:T(8,128)(2,1)S(1)}, u32[]{:S(2)}, u32[]{:S(2)}) collective-permute-start(bf16[2,256,1024]{2,1,0:T(8,128)(2,1)S(1)} %get-tuple-element.14), channel_id=1, source_target_pairs={{0,4},{4,0},{8,12},{12,8},{1,5},{5,1},{9,13},{13,9},{2,6},{6,2},{1... | collective-permute-start | bytes 3145736 | tf_op jit(solution)/shard_map/ppermute | solution.py:234
  6.7 46.5 %collective-permute-start = (bf16[2,256,1024]{2,1,0:T(8,128)(2,1)S(1)}, bf16[2,256,1024]{2,1,0:T(8,128)(2,1)S(1)}, u32[]{:S(2)}, u32[]{:S(2)}) collective-permute-start(bf16[2,256,1024]{2,1,0:T(8,128)(2,1)S(1)} %stage_crossed.1), channel_id=1, source_target_pairs={{0,8},{12,4},{1,9},{13,5},{2,10},{14,6},{3,11},{15,7},{16,24},{28,... | collective-permute-start | bytes 3145736 | tf_op jit(solution)/shard_map/ppermute | solution.py:234
  28.5 25.6 %collective-permute-start.4 = (bf16[2,256,1024]{2,1,0:T(8,128)(2,1)S(1)}, bf16[2,256,1024]{2,1,0:T(8,128)(2,1)S(1)}, u32[]{:S(2)}, u32[]{:S(2)}) collective-permute-start(bf16[2,256,1024]{2,1,0:T(8,128)(2,1)S(1)} %collective-permute-done.3.listed), channel_id=1, source_target_pairs={{8,12},{4,0},{9,13},{5,1},{10,14},{6,2},{11,15},{7,3},{24,28},{20,... | collective-permute-start | bytes 3145736 | tf_op jit(solution)/shard_map/ppermute | solution.py:234
  30.5 23.6 %copy-start.2 = (bf16[512,1024]{1,0:T(8,128)(2,1)S(1)}, bf16[512,1024]{1,0:T(8,128)(2,1)}, u32[]{:S(2)}) copy-start(bf16[512,1024]{1,0:T(8,128)(2,1)} %queries.3) | copy-start | bytes 3145732
  30.5 23.6 %collective-permute-start.5 = (bf16[2,128,1024]{2,1,0:T(8,128)(2,1)S(1)}, bf16[2,128,1024]{2,1,0:T(8,128)(2,1)S(1)}, u32[]{:S(2)}, u32[]{:S(2)}) collective-permute-start(bf16[2,128,1024]{2,1,0:T(8,128)(2,1)S(1)} %stage_direct.1), channel_id=1, source_target_pairs={{0,12},{12,0},{1,13},{13,1},{2,14},{14,2},{3,15},{15,3},{16,28},{2... | collective-permute-start | bytes 1572872 | tf_op jit(solution)/shard_map/ppermute | solution.py:234
  53.8 34.4 %collective-permute-start.1 = (bf16[2,128,1024]{2,1,0:T(8,128)(2,1)S(1)}, bf16[2,128,1024]{2,1,0:T(8,128)(2,1)S(1)}, u32[]{:S(2)}, u32[]{:S(2)}) collective-permute-start(bf16[2,128,1024]{2,1,0:T(8,128)(2,1)S(1)} %stage_closing.1), channel_id=1, source_target_pairs={{4,8},{8,4},{0,12},{12,0},{5,9},{9,5},{1,13},{13,1},{6,10},{10,6},... | collective-permute-start | bytes 1572872 | tf_op jit(solution)/shard_map/ppermute | solution.py:234

commit v8 on v7

--- a/solution.py
+++ b/solution.py
@@ -97,41 +97,32 @@
     return pl.ds(pl.multiple_of(block * BLOCK, BLOCK), BLOCK)
 
 
-def stage_listed_kernel(bands, keys, values, listed, token, sems):
+def stage_first_kernel(bands, keys, values, first, token, sems):
     frame = lax.axis_index("tm")
     token[...] = jnp.zeros_like(token)
-
-    @pl.when((frame == 1) | (frame == 2))
-    def _():
-        reader = jnp.where(frame == 1, 3, 0)
-        pairs = []
-        for place in range(2):
-            slot = jnp.where(frame == 1, place, 1 - place)
-            rows = rows_of(bands[reader, slot, frame])
-            for kv, source in enumerate((keys, values)):
-                pairs.append((source.at[rows], listed.at[kv, pl.ds(place * BLOCK, BLOCK)]))
-        run_copies(pairs, sems)
-
-
-def stage_beside_kernel(half, after, keys, values, beside, token, sems):
-    frame = lax.axis_index("tm")
-    token[...] = jnp.zeros_like(token)
-    rows = pl.ds(pl.multiple_of(lax.rem(frame + 1, 2) * half, half), half)
-    run_copies([(keys.at[rows], beside.at[0]), (values.at[rows], beside.at[1])], sems)
-
-
-def stage_crossed_kernel(after, bands, keys, values, crossed, sems):
-    frame = lax.axis_index("tm")
-
-    @pl.when((frame == 0) | (frame == 3))
-    def _():
-        reader = jnp.where(frame == 0, 2, 1)
-        pairs = []
-        for slot in range(2):
-            rows = rows_of(bands[reader, slot, frame])
-            for kv, source in enumerate((keys, values)):
-                pairs.append((source.at[rows], crossed.at[kv, pl.ds(slot * BLOCK, BLOCK)]))
-        run_copies(pairs, sems)
+    inner = (frame == 1) | (frame == 2)
+    reader = jnp.where(frame == 1, 3, 0)
+    pairs = []
+    for place in range(2):
+        slot = jnp.where(frame == 1, place, 1 - place)
+        facing = jnp.where(frame == 0, 2 + place, place)
+        rows = rows_of(jnp.where(inner, bands[reader, slot, frame], facing))
+        for kv, source in enumerate((keys, values)):
+            pairs.append((source.at[rows], first.at[kv, pl.ds(place * BLOCK, BLOCK)]))
+    run_copies(pairs, sems)
+
+
+def stage_second_kernel(after, bands, keys, values, second, sems):
+    frame = lax.axis_index("tm")
+    inner = (frame == 1) | (frame == 2)
+    reader = jnp.where(frame == 0, 2, 1)
+    pairs = []
+    for place in range(2):
+        facing = jnp.where(frame == 1, place, 2 + place)
+        rows = rows_of(jnp.where(inner, facing, bands[reader, place, frame]))
+        for kv, source in enumerate((keys, values)):
+            pairs.append((source.at[rows], second.at[kv, pl.ds(place * BLOCK, BLOCK)]))
+    run_copies(pairs, sems)
 
 
 def stage_direct_kernel(after, bands, keys, values, direct, sems):
@@ -143,12 +134,20 @@
         run_copies([(keys.at[rows], direct.at[0]), (values.at[rows], direct.at[1])], sems)
 
 
-def stage_closing_kernel(after, bands, keys, values, closing, sems):
+def stage_closing_kernel(cuts, after, bands, keys, values, *rest):
+    closing, sems = rest[:-1], rest[-1]
     frame = lax.axis_index("tm")
     inner = (frame == 1) | (frame == 2)
     other = jnp.where(frame == 1, 5 - bands[3, 1, 1], 1 - bands[0, 0, 2])
     rows = rows_of(jnp.where(inner, other, bands[3 - frame, 1, frame]))
-    run_copies([(keys.at[rows], closing.at[0]), (values.at[rows], closing.at[1])], sems)
+    run_copies(
+        [
+            (source.at[rows, pl.ds(first, size)], part.at[kv])
+            for part, (first, size) in zip(closing, cuts)
+            for kv, source in enumerate((keys, values))
+        ],
+        sems,
+    )
 
 
 RATE = LOG2E * HD ** (-0.5)
@@ -161,7 +160,7 @@
 
 
 def attend_kernel(
-    chunk, queries, keys, values, beside, listed, crossed, relayed, direct, mixed, tops, sums
+    chunk, queries, keys, values, inward, listed, around, relayed, direct, mixed, tops, sums
 ):
     frame = lax.axis_index("tm")
     edge = (frame == 0) | (frame == 3)
@@ -171,8 +170,8 @@
         cols = pl.ds(head * HD, HD)
         return [
             own[:, cols],
-            beside[kv, :, cols],
-            jnp.where(edge, relayed[kv, :, cols], crossed[kv, :, cols]),
+            around[kv, :, cols],
+            jnp.where(edge, relayed[kv, :, cols], inward[kv, :, cols]),
             jnp.where(edge, direct[kv, :, cols], listed[kv, pl.ds(BLOCK, BLOCK), cols]),
         ]
 
@@ -202,21 +201,22 @@
         scores = ahead
 
 
-def close_kernel(queries, closing, mixed, tops, sums, out, ready, sems):
-    rows, columns = queries.shape
+def close_kernel(first, queries, closing, mixed, tops, sums, *rest):
+    out, ready, sems = rest[-3:]
     copies = []
-    for head in range(columns // HD):
-        cols = pl.ds(head * HD, HD)
-        scores = scores_of(queries[:, cols], closing[0, :, cols])
+    for at in range(ready.shape[0]):
+        head = first // HD + at
+        here, there = pl.ds(first + at * HD, HD), pl.ds(at * HD, HD)
+        scores = scores_of(queries[:, here], closing[0, :, there])
         top = jnp.maximum(tops[head], jnp.max(scores, axis=1, keepdims=True))
         shrink = jnp.exp2((tops[head] - top) * RATE)
         powers = jnp.exp2((scores - top) * RATE)
         total = sums[head] * shrink + jnp.sum(powers, axis=1, keepdims=True)
         more = jnp.dot(
-            powers.astype(jnp.bfloat16), closing[1, :, cols], preferred_element_type=jnp.float32
-        )
-        ready[head] = ((mixed[head] * shrink + more) / total).astype(jnp.bfloat16)
-        copies.append(pltpu.make_async_copy(ready.at[head], out.at[:, cols], sems.at[head]))
+            powers.astype(jnp.bfloat16), closing[1, :, there], preferred_element_type=jnp.float32
+        )
+        ready[at] = ((mixed[head] * shrink + more) / total).astype(jnp.bfloat16)
+        copies.append(pltpu.make_async_copy(ready.at[at], out.at[:, here], sems.at[at]))
         copies[-1].start()
     for copy in copies:
         copy.wait()
@@ -249,32 +249,32 @@
         )(*operands)
 
     token = jax.ShapeDtypeStruct((8, HD), jnp.int32)
-    listed, after = stage(
-        stage_listed_kernel, [two, token], 4, [bands, keys, values], "stage_listed", 52
-    )
-    beside, after = stage(
-        functools.partial(stage_beside_kernel, half),
-        [two, token],
-        2,
-        [after, keys, values],
-        "stage_beside",
-        52,
-    )
-    (crossed,) = stage(
-        stage_crossed_kernel, [two], 4, [after, bands, keys, values], "stage_crossed", 32
-    )
-    beside = send(beside, [(0, 1), (1, 0), (2, 3), (3, 2)])
-    listed = send(listed, [(1, 2), (2, 1)])
-    crossed = send(crossed, [(0, 2), (3, 1)])
+    first, after = stage(
+        stage_first_kernel, [two, token], 4, [bands, keys, values], "stage_first", 52
+    )
+    (second,) = stage(
+        stage_second_kernel, [two], 4, [after, bands, keys, values], "stage_second", 32
+    )
+    listed = send(first, [(1, 2), (2, 1)])
+    inward = send(first, [(0, 1), (3, 2)])
+    around = send(second, [(1, 0), (2, 3), (0, 2), (3, 1)])
     relayed = send(listed, [(2, 3), (1, 0)])
     (direct,) = stage(
-        stage_direct_kernel, [one], 2, [beside, bands, keys, values], "stage_direct", 32
+        stage_direct_kernel, [one], 2, [inward, bands, keys, values], "stage_direct", 32
     )
     direct = send(direct, [(0, 3), (3, 0)])
-    (closing,) = stage(
-        stage_closing_kernel, [one], 2, [crossed, bands, keys, values], "stage_closing", 32
-    )
-    closing = send(closing, [(1, 2), (2, 1), (0, 3), (3, 0)])
+    last = heads // 4
+    cuts = [(0, heads - last), (heads - last, last)] if last else [(0, heads)]
+    cuts = [(start * HD, size * HD) for start, size in cuts]
+    closing = stage(
+        functools.partial(stage_closing_kernel, cuts),
+        [jax.ShapeDtypeStruct((2, BLOCK, size), jnp.bfloat16) for _, size in cuts],
+        2 * len(cuts),
+        [around, bands, keys, values],
+        "stage_closing",
+        32,
+    )
+    closing = [send(part, [(1, 2), (2, 1), (0, 3), (3, 0)]) for part in closing]
 
     state = jax.ShapeDtypeStruct((heads, rows, HD), jnp.float32)
     roomy = pltpu.CompilerParams(vmem_limit_bytes=32 << 20)
@@ -285,19 +285,30 @@
         out_specs=[local] * 3,
         compiler_params=roomy,
         name="attend",
-    )(queries, keys, values, beside, listed, crossed, relayed, direct)
-    return pl.pallas_call(
-        close_kernel,
-        out_shape=jax.ShapeDtypeStruct(queries.shape, queries.dtype),
-        in_specs=[local] * 5,
-        out_specs=anywhere,
-        scratch_shapes=[
-            pltpu.VMEM((heads, rows, HD), jnp.bfloat16),
-            pltpu.SemaphoreType.DMA((heads,)),
-        ],
-        compiler_params=roomy,
-        name="close",
-    )(queries, closing, mixed, tops, sums)
+    )(queries, keys, values, inward, listed, around, relayed, direct)
+    result = None
+    for part, (start, size) in zip(closing, cuts):
+        operands = [queries, part, mixed, tops, sums]
+        in_specs = [local] * len(operands)
+        aliases = {}
+        if result is not None:
+            aliases = {len(operands): 0}
+            in_specs.append(anywhere)
+            operands.append(result)
+        result = pl.pallas_call(
+            functools.partial(close_kernel, start),
+            out_shape=jax.ShapeDtypeStruct(queries.shape, queries.dtype),
+            in_specs=in_specs,
+            out_specs=anywhere,
+            input_output_aliases=aliases,
+            scratch_shapes=[
+                pltpu.VMEM((size // HD, rows, HD), jnp.bfloat16),
+                pltpu.SemaphoreType.DMA((size // HD,)),
+            ],
+            compiler_params=roomy,
+            name="close",
+        )(*operands)
+    return result
 
 
 def shards(queries, keys, values, band_blocks):

time: 90.8 us -> 93.1 us (1.025)
  the two profiles are of different devices: /device:TPU:17 before, /device:TPU:0 now
where the time goes in v8:
time: 93.1 us; the launch traced here: 92.9 us
  waiting for transfers between devices  59.2 us (64%)
  starting transfers between devices  17.1 us (18%)
  Pallas kernels  15.5 us (17%)
    ppermute x7, waiting for transfers between devices, send(): return lax.ppermute(array, 'tm', pairs)  59.2 us
    ppermute x7, starting transfers between devices, send(): return lax.ppermute(array, 'tm', pairs)  17.1 us
    pallas_call x1, Pallas kernels, four_frames(): pl.pallas_call(functools.partial(attend_kernel, rows // 2), out_shape=[st...  8.2 us
    pallas_call x4, Pallas kernels, stage(): pl.pallas_call(kernel, out_shape=shapes, in_specs=[scalars if operand is...  3.99 us
    pallas_call x2, Pallas kernels, four_frames(): pl.pallas_call(functools.partial(close_kernel, start), out_shape=jax.Shap...  3.33 us
  transfers between devices with their start and end apart: 7, of which 4 were waited for; matrix products, arithmetic and copies ran while one was open for 0% of the time, Pallas kernels for 13%

profile of v8, /device:TPU:0, one launch (start us, length us, event | category | flops | bytes accessed | tf_op | source)
XLA Modules:
  0.0 92.9 jit_solution(16154383259626785255)
XLA Ops:
  0.0 0.0 copy-start
  0.0 0.0 copy-start.1
  0.0 0.0 copy-start.3
  0.0 0.8 copy-done.3
  0.8 1.8 %stage_first.1 = (bf16[2,256,1024]{2,1,0:T(8,128)(2,1)S(1)}, s32[8,128]{1,0:T(8,128)S(1)}) custom-call(s32[4,2,4]{2,1,0:T(2,128)S(1)} %bitcast.1, bf16[512,1024]{1,0:T(8,128)(2,1)} %keys.9, bf16[512,1024]{1,0:T(8,128)(2,1)} %values.9), custom_call_target="tpu_custom_call" | custom-call | tf_op jit(solution)/shard_map/stage_first/pallas_call | solution.py:241
  2.7 0.7 collective-permute-start.3
  3.4 7.8 %collective-permute-start.2 = (bf16[2,256,1024]{2,1,0:T(8,128)(2,1)S(1)}, bf16[2,256,1024]{2,1,0:T(8,128)(2,1)S(1)}, u32[]{:S(2)}, u32[]{:S(2)}) collective-permute-start(bf16[2,256,1024]{2,1,0:T(8,128)(2,1)S(1)} %get-tuple-element.14), channel_id=1, source_target_pairs={{0,4},{12,8},{1,5},{13,9},{2,6},{14,10},{3,7},{15,11},{16,20},{28,... | collective-permute-start | bytes 3145736 | tf_op jit(solution)/shard_map/ppermute | solution.py:234
  11.2 0.0 copy-done
  11.2 0.0 copy-done.1
  11.2 0.7 stage_second.1
  11.9 0.1 collective-permute-start
  12.0 0.0 collective-permute-done.3.listed
  12.0 1.3 %collective-permute-start.4 = (bf16[2,256,1024]{2,1,0:T(8,128)(2,1)S(1)}, bf16[2,256,1024]{2,1,0:T(8,128)(2,1)S(1)}, u32[]{:S(2)}, u32[]{:S(2)}) collective-permute-start(bf16[2,256,1024]{2,1,0:T(8,128)(2,1)S(1)} %collective-permute-done.3.listed), channel_id=1, source_target_pairs={{8,12},{4,0},{9,13},{5,1},{10,14},{6,2},{11,15},{7,3},{24,28},{20,... | collective-permute-start | bytes 3145736 | tf_op jit(solution)/shard_map/ppermute | solution.py:234
  13.3 21.4 %collective-permute-done.2.after.inward = bf16[2,256,1024]{2,1,0:T(8,128)(2,1)S(1)} collective-permute-done((bf16[2,256,1024]{2,1,0:T(8,128)(2,1)S(1)}, bf16[2,256,1024]{2,1,0:T(8,128)(2,1)S(1)}, u32[]{:S(2)}, u32[]{:S(2)}) %collective-permute-start.2) | collective-permute-done | bytes 1048608 | tf_op jit(solution)/shard_map/ppermute | solution.py:234
  34.7 0.7 stage_direct.1
  35.4 0.0 copy-start.2
  35.4 3.4 %collective-permute-start.5 = (bf16[2,128,1024]{2,1,0:T(8,128)(2,1)S(1)}, bf16[2,128,1024]{2,1,0:T(8,128)(2,1)S(1)}, u32[]{:S(2)}, u32[]{:S(2)}) collective-permute-start(bf16[2,128,1024]{2,1,0:T(8,128)(2,1)S(1)} %stage_direct.1), channel_id=1, source_target_pairs={{0,12},{12,0},{1,13},{13,1},{2,14},{14,2},{3,15},{15,3},{16,28},{2... | collective-permute-start | bytes 1572872 | tf_op jit(solution)/shard_map/ppermute | solution.py:234
  38.8 18.4 %collective-permute-done.after.around = bf16[2,256,1024]{2,1,0:T(8,128)(2,1)S(1)} collective-permute-done((bf16[2,256,1024]{2,1,0:T(8,128)(2,1)S(1)}, bf16[2,256,1024]{2,1,0:T(8,128)(2,1)S(1)}, u32[]{:S(2)}, u32[]{:S(2)}) %collective-permute-start) | collective-permute-done | bytes 1048608 | tf_op jit(solution)/shard_map/ppermute | solution.py:234
  57.2 0.7 stage_closing.1
  57.9 1.4 %collective-permute-start.6 = (bf16[2,128,768]{2,1,0:T(8,128)(2,1)S(1)}, bf16[2,128,768]{2,1,0:T(8,128)(2,1)S(1)}, u32[]{:S(2)}, u32[]{:S(2)}) collective-permute-start(bf16[2,128,768]{2,1,0:T(8,128)(2,1)S(1)} %get-tuple-element.18), channel_id=1, source_target_pairs={{4,8},{8,4},{0,12},{12,0},{5,9},{9,5},{1,13},{13,1},{6,10},{10,6},... | collective-permute-start | bytes 1179656 | tf_op jit(solution)/shard_map/ppermute | solution.py:234
  59.3 2.5 %collective-permute-start.1 = (bf16[2,128,256]{2,1,0:T(8,128)(2,1)S(1)}, bf16[2,128,256]{2,1,0:T(8,128)(2,1)S(1)}, u32[]{:S(2)}, u32[]{:S(2)}) collective-permute-start(bf16[2,128,256]{2,1,0:T(8,128)(2,1)S(1)} %get-tuple-element.13), channel_id=1, source_target_pairs={{4,8},{8,4},{0,12},{12,0},{5,9},{9,5},{1,13},{13,1},{6,10},{10,6},... | collective-permute-start | bytes 393224 | tf_op jit(solution)/shard_map/ppermute | solution.py:234
  61.8 8.6 %collective-permute-done.5.direct = bf16[2,128,1024]{2,1,0:T(8,128)(2,1)S(1)} collective-permute-done((bf16[2,128,1024]{2,1,0:T(8,128)(2,1)S(1)}, bf16[2,128,1024]{2,1,0:T(8,128)(2,1)S(1)}, u32[]{:S(2)}, u32[]{:S(2)}) %collective-permute-start.5) | collective-permute-done | bytes 524320 | tf_op jit(solution)/shard_map/ppermute | solution.py:234
  70.4 10.9 %collective-permute-done.4.relayed = bf16[2,256,1024]{2,1,0:T(8,128)(2,1)S(1)} collective-permute-done((bf16[2,256,1024]{2,1,0:T(8,128)(2,1)S(1)}, bf16[2,256,1024]{2,1,0:T(8,128)(2,1)S(1)}, u32[]{:S(2)}, u32[]{:S(2)}) %collective-permute-start.4) | collective-permute-done | bytes 1048608 | tf_op jit(solution)/shard_map/ppermute | solution.py:234
  81.3 0.0 copy-done.2
  81.3 8.2 %attend.1 = (f32[8,512,128]{2,1,0:T(8,128)S(1)}, f32[8,512,128]{2,1,0:T(8,128)S(1)}, f32[8,512,128]{2,1,0:T(8,128)S(1)}) custom-call(bf16[512,1024]{1,0:T(8,128)(2,1)S(1)} %copy-done.2, bf16[512,1024]{1,0:T(8,128)(2,1)S(1)} %copy-done, bf16[512,1024]{1,0:T(8,128)(2,1)S(1)} %copy-done.1, bf16[2,256,1024]{2,1,0:T(8,128)(2,1)S(1)} %collective-permute-done.2.after.inward, ...), custom_call_target="tpu_custom_call" | custom-call | tf_op jit(solution)/shard_map/attend/pallas_call | solution.py:281
  89.5 0.0 collective-permute-done.6.closing
  89.5 2.0 %close.2.rest_0_ = bf16[512,1024]{1,0:T(8,128)(2,1)} custom-call(bf16[512,1024]{1,0:T(8,128)(2,1)S(1)} %copy-done.2, bf16[2,128,768]{2,1,0:T(8,128)(2,1)S(1)} %collective-permute-done.6.closing, f32[8,512,128]{2,1,0:T(8,128)S(1)} %get-tuple-element.15.mixed, f32[8,512,128]{2,1,0:T(8,128)S(1)} %get-tuple-element.16.tops, ...), custom_call_target="tpu_custom_call" | custom-call | tf_op jit(solution)/shard_map/close/pallas_call | solution.py:298
  91.5 0.0 collective-permute-done.1.closing
  91.5 1.4 %close.3 = bf16[512,1024]{1,0:T(8,128)(2,1)} custom-call(bf16[512,1024]{1,0:T(8,128)(2,1)S(1)} %copy-done.2, bf16[2,128,256]{2,1,0:T(8,128)(2,1)S(1)} %collective-permute-done.1.closing, f32[8,512,128]{2,1,0:T(8,128)S(1)} %get-tuple-element.15.mixed, f32[8,512,128]{2,1,0:T(8,128)S(1)} %get-tuple-element.16.tops, ...), custom_call_target="tpu_custom_call", output_to_operand_aliasing={{}: (5, {})} | custom-call | tf_op jit(solution)/shard_map/close/pallas_call | solution.py:298
Async XLA Ops:
  0.0 11.2 %copy-start = (bf16[512,1024]{1,0:T(8,128)(2,1)S(1)}, bf16[512,1024]{1,0:T(8,128)(2,1)}, u32[]{:S(2)}) copy-start(bf16[512,1024]{1,0:T(8,128)(2,1)} %keys.9) | copy-start | bytes 3145732
  0.0 11.2 %copy-start.1 = (bf16[512,1024]{1,0:T(8,128)(2,1)S(1)}, bf16[512,1024]{1,0:T(8,128)(2,1)}, u32[]{:S(2)}) copy-start(bf16[512,1024]{1,0:T(8,128)(2,1)} %values.9) | copy-start | bytes 3145732
  0.0 0.8 copy-start.3
  2.7 9.3 %collective-permute-start.3 = (bf16[2,256,1024]{2,1,0:T(8,128)(2,1)S(1)}, bf16[2,256,1024]{2,1,0:T(8,128)(2,1)S(1)}, u32[]{:S(2)}, u32[]{:S(2)}) collective-permute-start(bf16[2,256,1024]{2,1,0:T(8,128)(2,1)S(1)} %get-tuple-element.14), channel_id=1, source_target_pairs={{4,8},{8,4},{5,9},{9,5},{6,10},{10,6},{7,11},{11,7},{20,24},{24,20... | collective-permute-start | bytes 3145736 | tf_op jit(solution)/shard_map/ppermute | solution.py:234
  3.4 31.3 %collective-permute-start.2 = (bf16[2,256,1024]{2,1,0:T(8,128)(2,1)S(1)}, bf16[2,256,1024]{2,1,0:T(8,128)(2,1)S(1)}, u32[]{:S(2)}, u32[]{:S(2)}) collective-permute-start(bf16[2,256,1024]{2,1,0:T(8,128)(2,1)S(1)} %get-tuple-element.14), channel_id=1, source_target_pairs={{0,4},{12,8},{1,5},{13,9},{2,6},{14,10},{3,7},{15,11},{16,20},{28,... | collective-permute-start | bytes 3145736 | tf_op jit(solution)/shard_map/ppermute | solution.py:234
  11.9 45.2 %collective-permute-start = (bf16[2,256,1024]{2,1,0:T(8,128)(2,1)S(1)}, bf16[2,256,1024]{2,1,0:T(8,128)(2,1)S(1)}, u32[]{:S(2)}, u32[]{:S(2)}) collective-permute-start(bf16[2,256,1024]{2,1,0:T(8,128)(2,1)S(1)} %stage_second.1), channel_id=1, source_target_pairs={{4,0},{8,12},{0,8},{12,4},{5,1},{9,13},{1,9},{13,5},{6,2},{10,14},... | collective-permute-start | bytes 3145736 | tf_op jit(solution)/shard_map/ppermute | solution.py:234
  12.0 69.3 %collective-permute-start.4 = (bf16[2,256,1024]{2,1,0:T(8,128)(2,1)S(1)}, bf16[2,256,1024]{2,1,0:T(8,128)(2,1)S(1)}, u32[]{:S(2)}, u32[]{:S(2)}) collective-permute-start(bf16[2,256,1024]{2,1,0:T(8,128)(2,1)S(1)} %collective-permute-done.3.listed), channel_id=1, source_target_pairs={{8,12},{4,0},{9,13},{5,1},{10,14},{6,2},{11,15},{7,3},{24,28},{20,... | collective-permute-start | bytes 3145736 | tf_op jit(solution)/shard_map/ppermute | solution.py:234
  35.4 45.9 %copy-start.2 = (bf16[512,1024]{1,0:T(8,128)(2,1)S(1)}, bf16[512,1024]{1,0:T(8,128)(2,1)}, u32[]{:S(2)}) copy-start(bf16[512,1024]{1,0:T(8,128)(2,1)} %queries.5) | copy-start | bytes 3145732
  35.4 35.0 %collective-permute-start.5 = (bf16[2,128,1024]{2,1,0:T(8,128)(2,1)S(1)}, bf16[2,128,1024]{2,1,0:T(8,128)(2,1)S(1)}, u32[]{:S(2)}, u32[]{:S(2)}) collective-permute-start(bf16[2,128,1024]{2,1,0:T(8,128)(2,1)S(1)} %stage_direct.1), channel_id=1, source_target_pairs={{0,12},{12,0},{1,13},{13,1},{2,14},{14,2},{3,15},{15,3},{16,28},{2... | collective-permute-start | bytes 1572872 | tf_op jit(solution)/shard_map/ppermute | solution.py:234
  57.9 31.6 %collective-permute-start.6 = (bf16[2,128,768]{2,1,0:T(8,128)(2,1)S(1)}, bf16[2,128,768]{2,1,0:T(8,128)(2,1)S(1)}, u32[]{:S(2)}, u32[]{:S(2)}) collective-permute-start(bf16[2,128,768]{2,1,0:T(8,128)(2,1)S(1)} %get-tuple-element.18), channel_id=1, source_target_pairs={{4,8},{8,4},{0,12},{12,0},{5,9},{9,5},{1,13},{13,1},{6,10},{10,6},... | collective-permute-start | bytes 1179656 | tf_op jit(solution)/shard_map/ppermute | solution.py:234
  59.3 32.2 %collective-permute-start.1 = (bf16[2,128,256]{2,1,0:T(8,128)(2,1)S(1)}, bf16[2,128,256]{2,1,0:T(8,128)(2,1)S(1)}, u32[]{:S(2)}, u32[]{:S(2)}) collective-permute-start(bf16[2,128,256]{2,1,0:T(8,128)(2,1)S(1)} %get-tuple-element.13), channel_id=1, source_target_pairs={{4,8},{8,4},{0,12},{12,0},{5,9},{9,5},{1,13},{13,1},{6,10},{10,6},... | collective-permute-start | bytes 393224 | tf_op jit(solution)/shard_map/ppermute | solution.py:234

commit v9 on v8

--- a/solution.py
+++ b/solution.py
@@ -97,9 +97,8 @@
     return pl.ds(pl.multiple_of(block * BLOCK, BLOCK), BLOCK)
 
 
-def stage_first_kernel(bands, keys, values, first, token, sems):
-    frame = lax.axis_index("tm")
-    token[...] = jnp.zeros_like(token)
+def stage_first_kernel(bands, keys, values, first, sems):
+    frame = lax.axis_index("tm")
     inner = (frame == 1) | (frame == 2)
     reader = jnp.where(frame == 1, 3, 0)
     pairs = []
@@ -112,17 +111,27 @@
     run_copies(pairs, sems)
 
 
-def stage_second_kernel(after, bands, keys, values, second, sems):
-    frame = lax.axis_index("tm")
-    inner = (frame == 1) | (frame == 2)
-    reader = jnp.where(frame == 0, 2, 1)
-    pairs = []
-    for place in range(2):
-        facing = jnp.where(frame == 1, place, 2 + place)
-        rows = rows_of(jnp.where(inner, facing, bands[reader, place, frame]))
-        for kv, source in enumerate((keys, values)):
-            pairs.append((source.at[rows], second.at[kv, pl.ds(place * BLOCK, BLOCK)]))
-    run_copies(pairs, sems)
+def stage_outward_kernel(half, keys, values, outward, sems):
+    frame = lax.axis_index("tm")
+
+    @pl.when((frame == 1) | (frame == 2))
+    def _():
+        rows = pl.ds(pl.multiple_of((frame - 1) * half, half), half)
+        run_copies([(keys.at[rows], outward.at[0]), (values.at[rows], outward.at[1])], sems)
+
+
+def stage_crossed_kernel(after, bands, keys, values, crossed, sems):
+    frame = lax.axis_index("tm")
+
+    @pl.when((frame == 0) | (frame == 3))
+    def _():
+        reader = jnp.where(frame == 0, 2, 1)
+        pairs = []
+        for slot in range(2):
+            rows = rows_of(bands[reader, slot, frame])
+            for kv, source in enumerate((keys, values)):
+                pairs.append((source.at[rows], crossed.at[kv, pl.ds(slot * BLOCK, BLOCK)]))
+        run_copies(pairs, sems)
 
 
 def stage_direct_kernel(after, bands, keys, values, direct, sems):
@@ -134,7 +143,7 @@
         run_copies([(keys.at[rows], direct.at[0]), (values.at[rows], direct.at[1])], sems)
 
 
-def stage_closing_kernel(cuts, after, bands, keys, values, *rest):
+def stage_closing_kernel(cuts, after, after_too, bands, keys, values, *rest):
     closing, sems = rest[:-1], rest[-1]
     frame = lax.axis_index("tm")
     inner = (frame == 1) | (frame == 2)
@@ -160,7 +169,8 @@
 
 
 def attend_kernel(
-    chunk, queries, keys, values, inward, listed, around, relayed, direct, mixed, tops, sums
+    chunk, queries, keys, values, inward, outward, listed, crossed, relayed, direct,
+    mixed, tops, sums
 ):
     frame = lax.axis_index("tm")
     edge = (frame == 0) | (frame == 3)
@@ -170,8 +180,8 @@
         cols = pl.ds(head * HD, HD)
         return [
             own[:, cols],
-            around[kv, :, cols],
-            jnp.where(edge, relayed[kv, :, cols], inward[kv, :, cols]),
+            jnp.where(edge, outward[kv, :, cols], inward[kv, :, cols]),
+            jnp.where(edge, relayed[kv, :, cols], crossed[kv, :, cols]),
             jnp.where(edge, direct[kv, :, cols], listed[kv, pl.ds(BLOCK, BLOCK), cols]),
         ]
 
@@ -248,19 +258,27 @@
             name=name,
         )(*operands)
 
-    token = jax.ShapeDtypeStruct((8, HD), jnp.int32)
-    first, after = stage(
-        stage_first_kernel, [two, token], 4, [bands, keys, values], "stage_first", 52
-    )
-    (second,) = stage(
-        stage_second_kernel, [two], 4, [after, bands, keys, values], "stage_second", 32
-    )
+    (first,) = stage(
+        stage_first_kernel, [two], 4, [bands, keys, values], "stage_first", 52
+    )
+    inward = send(first, [(0, 1), (3, 2)])
     listed = send(first, [(1, 2), (2, 1)])
-    inward = send(first, [(0, 1), (3, 2)])
-    around = send(second, [(1, 0), (2, 3), (0, 2), (3, 1)])
+    (outward,) = stage(
+        functools.partial(stage_outward_kernel, half),
+        [two],
+        2,
+        [keys, values],
+        "stage_outward",
+        32,
+    )
+    outward = send(outward, [(1, 0), (2, 3)])
+    (crossed,) = stage(
+        stage_crossed_kernel, [two], 4, [inward, bands, keys, values], "stage_crossed", 32
+    )
+    crossed = send(crossed, [(0, 2), (3, 1)])
     relayed = send(listed, [(2, 3), (1, 0)])
     (direct,) = stage(
-        stage_direct_kernel, [one], 2, [inward, bands, keys, values], "stage_direct", 32
+        stage_direct_kernel, [one], 2, [outward, bands, keys, values], "stage_direct", 32
     )
     direct = send(direct, [(0, 3), (3, 0)])
     last = heads // 4
@@ -270,7 +288,7 @@
         functools.partial(stage_closing_kernel, cuts),
         [jax.ShapeDtypeStruct((2, BLOCK, size), jnp.bfloat16) for _, size in cuts],
         2 * len(cuts),
-        [around, bands, keys, values],
+        [crossed, relayed, bands, keys, values],
         "stage_closing",
         32,
     )
@@ -281,11 +299,11 @@
     mixed, tops, sums = pl.pallas_call(
         functools.partial(attend_kernel, rows // 2),
         out_shape=[state] * 3,
-        in_specs=[local] * 8,
+        in_specs=[local] * 9,
         out_specs=[local] * 3,
         compiler_params=roomy,
         name="attend",
-    )(queries, keys, values, inward, listed, around, relayed, direct)
+    )(queries, keys, values, inward, outward, listed, crossed, relayed, direct)
     result = None
     for part, (start, size) in zip(closing, cuts):
         operands = [queries, part, mixed, tops, sums]

time: 93.1 us -> 95.7 us (1.028)
  starting transfers between devices: 17.1 us -> 21 us
  waiting for transfers between devices: 59.2 us -> 57.3 us
    ppermute x7 -> x8, starting transfers between devices: 17.1 us -> 21 us  [send(): return lax.ppermute(array, 'tm', pairs)]
    ppermute x7 -> x8, waiting for transfers between devices: 59.2 us -> 57.3 us  [send(): return lax.ppermute(array, 'tm', pairs)]
    pallas_call x4 -> x5, Pallas kernels: 3.99 us -> 4.03 us  [stage(): pl.pallas_call(kernel, out_shape=shapes, in_specs=[scalars if operand is...]
  transfers between devices with their start and end apart: 7 -> 8, of which waited for: 4 -> 3; matrix products, arithmetic and copies ran while one was open for 0% -> 0% of each run, Pallas kernels for 13% -> 14%
where the time goes in v9:
time: 95.7 us; the launch traced here: 95.4 us
  waiting for transfers between devices  57.3 us (60%)
  starting transfers between devices  21 us (22%)
  Pallas kernels  16.1 us (17%)
    ppermute x8, waiting for transfers between devices, send(): return lax.ppermute(array, 'tm', pairs)  57.3 us
    ppermute x8, starting transfers between devices, send(): return lax.ppermute(array, 'tm', pairs)  21 us
    pallas_call x1, Pallas kernels, four_frames(): pl.pallas_call(functools.partial(attend_kernel, rows // 2), out_shape=[st...  8.76 us
    pallas_call x5, Pallas kernels, stage(): pl.pallas_call(kernel, out_shape=shapes, in_specs=[scalars if operand is...  4.03 us
    pallas_call x2, Pallas kernels, four_frames(): pl.pallas_call(functools.partial(close_kernel, start), out_shape=jax.Shap...  3.35 us
  transfers between devices with their start and end apart: 8, of which 3 were waited for; matrix products, arithmetic and copies ran while one was open for 0% of the time, Pallas kernels for 14%

profile of v9, /device:TPU:0, one launch (start us, length us, event | category | flops | bytes accessed | tf_op | source)
XLA Modules:
  0.0 95.4 jit_solution(9759001585122000842)
XLA Ops:
  0.0 0.0 copy-start
  0.0 0.0 copy-start.1
  0.0 0.0 copy-start.3
  0.0 0.8 copy-done.3
  0.8 1.8 %stage_first.1 = bf16[2,256,1024]{2,1,0:T(8,128)(2,1)S(1)} custom-call(s32[4,2,4]{2,1,0:T(2,128)S(1)} %bitcast.1, bf16[512,1024]{1,0:T(8,128)(2,1)} %keys.11, bf16[512,1024]{1,0:T(8,128)(2,1)} %values.11), custom_call_target="tpu_custom_call" | custom-call | tf_op jit(solution)/shard_map/stage_first/pallas_call | solution.py:251
  2.7 5.0 %collective-permute-start = (bf16[2,256,1024]{2,1,0:T(8,128)(2,1)S(1)}, bf16[2,256,1024]{2,1,0:T(8,128)(2,1)S(1)}, u32[]{:S(2)}, u32[]{:S(2)}) collective-permute-start(bf16[2,256,1024]{2,1,0:T(8,128)(2,1)S(1)} %stage_first.1), channel_id=1, source_target_pairs={{0,4},{12,8},{1,5},{13,9},{2,6},{14,10},{3,7},{15,11},{16,20},{28,... | collective-permute-start | bytes 3145736 | tf_op jit(solution)/shard_map/ppermute | solution.py:244
  7.7 0.7 collective-permute-start.2
  8.4 0.0 copy-done
  8.4 0.0 copy-done.1
  8.5 1.3 %collective-permute-start.5 = (bf16[2,256,1024]{2,1,0:T(8,128)(2,1)S(1)}, bf16[2,256,1024]{2,1,0:T(8,128)(2,1)S(1)}, u32[]{:S(2)}, u32[]{:S(2)}) collective-permute-start(bf16[2,256,1024]{2,1,0:T(8,128)(2,1)S(1)} %stage_outward.1), channel_id=1, source_target_pairs={{4,0},{8,12},{5,1},{9,13},{6,2},{10,14},{7,3},{11,15},{20,16},{24,... | collective-permute-start | bytes 3145736 | tf_op jit(solution)/shard_map/ppermute | solution.py:244
  9.8 20.2 %collective-permute-done.after.inward = bf16[2,256,1024]{2,1,0:T(8,128)(2,1)S(1)} collective-permute-done((bf16[2,256,1024]{2,1,0:T(8,128)(2,1)S(1)}, bf16[2,256,1024]{2,1,0:T(8,128)(2,1)S(1)}, u32[]{:S(2)}, u32[]{:S(2)}) %collective-permute-start) | collective-permute-done | bytes 1048608 | tf_op jit(solution)/shard_map/ppermute | solution.py:244
  30.0 0.7 stage_crossed.1
  30.8 5.4 %collective-permute-start.1 = (bf16[2,256,1024]{2,1,0:T(8,128)(2,1)S(1)}, bf16[2,256,1024]{2,1,0:T(8,128)(2,1)S(1)}, u32[]{:S(2)}, u32[]{:S(2)}) collective-permute-start(bf16[2,256,1024]{2,1,0:T(8,128)(2,1)S(1)} %stage_crossed.1), channel_id=1, source_target_pairs={{0,8},{12,4},{1,9},{13,5},{2,10},{14,6},{3,11},{15,7},{16,24},{28,... | collective-permute-start | bytes 3145736 | tf_op jit(solution)/shard_map/ppermute | solution.py:244
  36.2 0.0 collective-permute-done.2.listed
  36.2 1.3 %collective-permute-start.3 = (bf16[2,256,1024]{2,1,0:T(8,128)(2,1)S(1)}, bf16[2,256,1024]{2,1,0:T(8,128)(2,1)S(1)}, u32[]{:S(2)}, u32[]{:S(2)}) collective-permute-start(bf16[2,256,1024]{2,1,0:T(8,128)(2,1)S(1)} %collective-permute-done.2.listed), channel_id=1, source_target_pairs={{8,12},{4,0},{9,13},{5,1},{10,14},{6,2},{11,15},{7,3},{24,28},{20,... | collective-permute-start | bytes 3145736 | tf_op jit(solution)/shard_map/ppermute | solution.py:244
  37.5 0.0 collective-permute-done.5.after.outward
  37.5 0.7 stage_direct.1
  38.2 0.0 copy-start.2
  38.2 3.4 %collective-permute-start.6 = (bf16[2,128,1024]{2,1,0:T(8,128)(2,1)S(1)}, bf16[2,128,1024]{2,1,0:T(8,128)(2,1)S(1)}, u32[]{:S(2)}, u32[]{:S(2)}) collective-permute-start(bf16[2,128,1024]{2,1,0:T(8,128)(2,1)S(1)} %stage_direct.1), channel_id=1, source_target_pairs={{0,12},{12,0},{1,13},{13,1},{2,14},{14,2},{3,15},{15,3},{16,28},{2... | collective-permute-start | bytes 1572872 | tf_op jit(solution)/shard_map/ppermute | solution.py:244
  41.6 18.1 %collective-permute-done.1.after.crossed = bf16[2,256,1024]{2,1,0:T(8,128)(2,1)S(1)} collective-permute-done((bf16[2,256,1024]{2,1,0:T(8,128)(2,1)S(1)}, bf16[2,256,1024]{2,1,0:T(8,128)(2,1)S(1)}, u32[]{:S(2)}, u32[]{:S(2)}) %collective-permute-start.1) | collective-permute-done | bytes 1048608 | tf_op jit(solution)/shard_map/ppermute | solution.py:244
  59.7 19.0 %collective-permute-done.3.after_too.relayed = bf16[2,256,1024]{2,1,0:T(8,128)(2,1)S(1)} collective-permute-done((bf16[2,256,1024]{2,1,0:T(8,128)(2,1)S(1)}, bf16[2,256,1024]{2,1,0:T(8,128)(2,1)S(1)}, u32[]{:S(2)}, u32[]{:S(2)}) %collective-permute-start.3) | collective-permute-done | bytes 1048608 | tf_op jit(solution)/shard_map/ppermute | solution.py:244
  78.7 0.7 stage_closing.1
  79.4 1.4 %collective-permute-start.7 = (bf16[2,128,768]{2,1,0:T(8,128)(2,1)S(1)}, bf16[2,128,768]{2,1,0:T(8,128)(2,1)S(1)}, u32[]{:S(2)}, u32[]{:S(2)}) collective-permute-start(bf16[2,128,768]{2,1,0:T(8,128)(2,1)S(1)} %get-tuple-element.14), channel_id=1, source_target_pairs={{4,8},{8,4},{0,12},{12,0},{5,9},{9,5},{1,13},{13,1},{6,10},{10,6},... | collective-permute-start | bytes 1179656 | tf_op jit(solution)/shard_map/ppermute | solution.py:244
  80.8 2.5 %collective-permute-start.4 = (bf16[2,128,256]{2,1,0:T(8,128)(2,1)S(1)}, bf16[2,128,256]{2,1,0:T(8,128)(2,1)S(1)}, u32[]{:S(2)}, u32[]{:S(2)}) collective-permute-start(bf16[2,128,256]{2,1,0:T(8,128)(2,1)S(1)} %get-tuple-element.10), channel_id=1, source_target_pairs={{4,8},{8,4},{0,12},{12,0},{5,9},{9,5},{1,13},{13,1},{6,10},{10,6},... | collective-permute-start | bytes 393224 | tf_op jit(solution)/shard_map/ppermute | solution.py:244
  83.3 0.0 collective-permute-done.6.direct
  83.3 0.0 copy-done.2
  83.3 8.8 %attend.1 = (f32[8,512,128]{2,1,0:T(8,128)S(1)}, f32[8,512,128]{2,1,0:T(8,128)S(1)}, f32[8,512,128]{2,1,0:T(8,128)S(1)}) custom-call(bf16[512,1024]{1,0:T(8,128)(2,1)S(1)} %copy-done.2, bf16[512,1024]{1,0:T(8,128)(2,1)S(1)} %copy-done, bf16[512,1024]{1,0:T(8,128)(2,1)S(1)} %copy-done.1, bf16[2,256,1024]{2,1,0:T(8,128)(2,1)S(1)} %collective-permute-done.after.inward, ...), custom_call_target="tpu_custom_call" | custom-call | tf_op jit(solution)/shard_map/attend/pallas_call | solution.py:299
  92.1 0.0 collective-permute-done.7.closing
  92.1 2.0 %close.2.rest_0_ = bf16[512,1024]{1,0:T(8,128)(2,1)} custom-call(bf16[512,1024]{1,0:T(8,128)(2,1)S(1)} %copy-done.2, bf16[2,128,768]{2,1,0:T(8,128)(2,1)S(1)} %collective-permute-done.7.closing, f32[8,512,128]{2,1,0:T(8,128)S(1)} %get-tuple-element.11.mixed, f32[8,512,128]{2,1,0:T(8,128)S(1)} %get-tuple-element.12.tops, ...), custom_call_target="tpu_custom_call" | custom-call | tf_op jit(solution)/shard_map/close/pallas_call | solution.py:316
  94.1 0.0 collective-permute-done.4.closing
  94.1 1.4 %close.3 = bf16[512,1024]{1,0:T(8,128)(2,1)} custom-call(bf16[512,1024]{1,0:T(8,128)(2,1)S(1)} %copy-done.2, bf16[2,128,256]{2,1,0:T(8,128)(2,1)S(1)} %collective-permute-done.4.closing, f32[8,512,128]{2,1,0:T(8,128)S(1)} %get-tuple-element.11.mixed, f32[8,512,128]{2,1,0:T(8,128)S(1)} %get-tuple-element.12.tops, ...), custom_call_target="tpu_custom_call", output_to_operand_aliasing={{}: (5, {})} | custom-call | tf_op jit(solution)/shard_map/close/pallas_call | solution.py:316
  (1 shorter events, 0.0 us)
Async XLA Ops:
  0.0 8.4 %copy-start = (bf16[512,1024]{1,0:T(8,128)(2,1)S(1)}, bf16[512,1024]{1,0:T(8,128)(2,1)}, u32[]{:S(2)}) copy-start(bf16[512,1024]{1,0:T(8,128)(2,1)} %keys.11) | copy-start | bytes 3145732
  0.0 8.4 %copy-start.1 = (bf16[512,1024]{1,0:T(8,128)(2,1)S(1)}, bf16[512,1024]{1,0:T(8,128)(2,1)}, u32[]{:S(2)}) copy-start(bf16[512,1024]{1,0:T(8,128)(2,1)} %values.11) | copy-start | bytes 3145732
  0.0 0.8 copy-start.3
  2.7 27.3 %collective-permute-start = (bf16[2,256,1024]{2,1,0:T(8,128)(2,1)S(1)}, bf16[2,256,1024]{2,1,0:T(8,128)(2,1)S(1)}, u32[]{:S(2)}, u32[]{:S(2)}) collective-permute-start(bf16[2,256,1024]{2,1,0:T(8,128)(2,1)S(1)} %stage_first.1), channel_id=1, source_target_pairs={{0,4},{12,8},{1,5},{13,9},{2,6},{14,10},{3,7},{15,11},{16,20},{28,... | collective-permute-start | bytes 3145736 | tf_op jit(solution)/shard_map/ppermute | solution.py:244
  7.7 28.5 %collective-permute-start.2 = (bf16[2,256,1024]{2,1,0:T(8,128)(2,1)S(1)}, bf16[2,256,1024]{2,1,0:T(8,128)(2,1)S(1)}, u32[]{:S(2)}, u32[]{:S(2)}) collective-permute-start(bf16[2,256,1024]{2,1,0:T(8,128)(2,1)S(1)} %stage_first.1), channel_id=1, source_target_pairs={{4,8},{8,4},{5,9},{9,5},{6,10},{10,6},{7,11},{11,7},{20,24},{24,20... | collective-permute-start | bytes 3145736 | tf_op jit(solution)/shard_map/ppermute | solution.py:244
  8.5 29.0 %collective-permute-start.5 = (bf16[2,256,1024]{2,1,0:T(8,128)(2,1)S(1)}, bf16[2,256,1024]{2,1,0:T(8,128)(2,1)S(1)}, u32[]{:S(2)}, u32[]{:S(2)}) collective-permute-start(bf16[2,256,1024]{2,1,0:T(8,128)(2,1)S(1)} %stage_outward.1), channel_id=1, source_target_pairs={{4,0},{8,12},{5,1},{9,13},{6,2},{10,14},{7,3},{11,15},{20,16},{24,... | collective-permute-start | bytes 3145736 | tf_op jit(solution)/shard_map/ppermute | solution.py:244
  30.8 28.9 %collective-permute-start.1 = (bf16[2,256,1024]{2,1,0:T(8,128)(2,1)S(1)}, bf16[2,256,1024]{2,1,0:T(8,128)(2,1)S(1)}, u32[]{:S(2)}, u32[]{:S(2)}) collective-permute-start(bf16[2,256,1024]{2,1,0:T(8,128)(2,1)S(1)} %stage_crossed.1), channel_id=1, source_target_pairs={{0,8},{12,4},{1,9},{13,5},{2,10},{14,6},{3,11},{15,7},{16,24},{28,... | collective-permute-start | bytes 3145736 | tf_op jit(solution)/shard_map/ppermute | solution.py:244
  36.2 42.5 %collective-permute-start.3 = (bf16[2,256,1024]{2,1,0:T(8,128)(2,1)S(1)}, bf16[2,256,1024]{2,1,0:T(8,128)(2,1)S(1)}, u32[]{:S(2)}, u32[]{:S(2)}) collective-permute-start(bf16[2,256,1024]{2,1,0:T(8,128)(2,1)S(1)} %collective-permute-done.2.listed), channel_id=1, source_target_pairs={{8,12},{4,0},{9,13},{5,1},{10,14},{6,2},{11,15},{7,3},{24,28},{20,... | collective-permute-start | bytes 3145736 | tf_op jit(solution)/shard_map/ppermute | solution.py:244
  38.2 45.1 %copy-start.2 = (bf16[512,1024]{1,0:T(8,128)(2,1)S(1)}, bf16[512,1024]{1,0:T(8,128)(2,1)}, u32[]{:S(2)}) copy-start(bf16[512,1024]{1,0:T(8,128)(2,1)} %queries.5) | copy-start | bytes 3145732
  38.2 45.1 %collective-permute-start.6 = (bf16[2,128,1024]{2,1,0:T(8,128)(2,1)S(1)}, bf16[2,128,1024]{2,1,0:T(8,128)(2,1)S(1)}, u32[]{:S(2)}, u32[]{:S(2)}) collective-permute-start(bf16[2,128,1024]{2,1,0:T(8,128)(2,1)S(1)} %stage_direct.1), channel_id=1, source_target_pairs={{0,12},{12,0},{1,13},{13,1},{2,14},{14,2},{3,15},{15,3},{16,28},{2... | collective-permute-start | bytes 1572872 | tf_op jit(solution)/shard_map/ppermute | solution.py:244
  79.4 12.7 %collective-permute-start.7 = (bf16[2,128,768]{2,1,0:T(8,128)(2,1)S(1)}, bf16[2,128,768]{2,1,0:T(8,128)(2,1)S(1)}, u32[]{:S(2)}, u32[]{:S(2)}) collective-permute-start(bf16[2,128,768]{2,1,0:T(8,128)(2,1)S(1)} %get-tuple-element.14), channel_id=1, source_target_pairs={{4,8},{8,4},{0,12},{12,0},{5,9},{9,5},{1,13},{13,1},{6,10},{10,6},... | collective-permute-start | bytes 1179656 | tf_op jit(solution)/shard_map/ppermute | solution.py:244
  80.8 13.2 %collective-permute-start.4 = (bf16[2,128,256]{2,1,0:T(8,128)(2,1)S(1)}, bf16[2,128,256]{2,1,0:T(8,128)(2,1)S(1)}, u32[]{:S(2)}, u32[]{:S(2)}) collective-permute-start(bf16[2,128,256]{2,1,0:T(8,128)(2,1)S(1)} %get-tuple-element.10), channel_id=1, source_target_pairs={{4,8},{8,4},{0,12},{12,0},{5,9},{9,5},{1,13},{13,1},{6,10},{10,6},... | collective-permute-start | bytes 393224 | tf_op jit(solution)/shard_map/ppermute | solution.py:244

commit v10 on v9

--- a/solution.py
+++ b/solution.py
@@ -97,27 +97,27 @@
     return pl.ds(pl.multiple_of(block * BLOCK, BLOCK), BLOCK)
 
 
-def stage_first_kernel(bands, keys, values, first, sems):
-    frame = lax.axis_index("tm")
-    inner = (frame == 1) | (frame == 2)
-    reader = jnp.where(frame == 1, 3, 0)
-    pairs = []
-    for place in range(2):
-        slot = jnp.where(frame == 1, place, 1 - place)
-        facing = jnp.where(frame == 0, 2 + place, place)
-        rows = rows_of(jnp.where(inner, bands[reader, slot, frame], facing))
-        for kv, source in enumerate((keys, values)):
-            pairs.append((source.at[rows], first.at[kv, pl.ds(place * BLOCK, BLOCK)]))
-    run_copies(pairs, sems)
-
-
-def stage_outward_kernel(half, keys, values, outward, sems):
-    frame = lax.axis_index("tm")
+def stage_listed_kernel(bands, keys, values, listed, token, sems):
+    frame = lax.axis_index("tm")
+    token[...] = jnp.zeros_like(token)
 
     @pl.when((frame == 1) | (frame == 2))
     def _():
-        rows = pl.ds(pl.multiple_of((frame - 1) * half, half), half)
-        run_copies([(keys.at[rows], outward.at[0]), (values.at[rows], outward.at[1])], sems)
+        reader = jnp.where(frame == 1, 3, 0)
+        pairs = []
+        for place in range(2):
+            slot = jnp.where(frame == 1, place, 1 - place)
+            rows = rows_of(bands[reader, slot, frame])
+            for kv, source in enumerate((keys, values)):
+                pairs.append((source.at[rows], listed.at[kv, pl.ds(place * BLOCK, BLOCK)]))
+        run_copies(pairs, sems)
+
+
+def stage_beside_kernel(half, after, keys, values, beside, token, sems):
+    frame = lax.axis_index("tm")
+    token[...] = jnp.zeros_like(token)
+    rows = pl.ds(pl.multiple_of(lax.rem(frame + 1, 2) * half, half), half)
+    run_copies([(keys.at[rows], beside.at[0]), (values.at[rows], beside.at[1])], sems)
 
 
 def stage_crossed_kernel(after, bands, keys, values, crossed, sems):
@@ -143,7 +143,7 @@
         run_copies([(keys.at[rows], direct.at[0]), (values.at[rows], direct.at[1])], sems)
 
 
-def stage_closing_kernel(cuts, after, after_too, bands, keys, values, *rest):
+def stage_closing_kernel(cuts, after, bands, keys, values, *rest):
     closing, sems = rest[:-1], rest[-1]
     frame = lax.axis_index("tm")
     inner = (frame == 1) | (frame == 2)
@@ -169,8 +169,7 @@
 
 
 def attend_kernel(
-    chunk, queries, keys, values, inward, outward, listed, crossed, relayed, direct,
-    mixed, tops, sums
+    chunk, queries, keys, values, beside, listed, crossed, relayed, direct, mixed, tops, sums
 ):
     frame = lax.axis_index("tm")
     edge = (frame == 0) | (frame == 3)
@@ -180,7 +179,7 @@
         cols = pl.ds(head * HD, HD)
         return [
             own[:, cols],
-            jnp.where(edge, outward[kv, :, cols], inward[kv, :, cols]),
+            beside[kv, :, cols],
             jnp.where(edge, relayed[kv, :, cols], crossed[kv, :, cols]),
             jnp.where(edge, direct[kv, :, cols], listed[kv, pl.ds(BLOCK, BLOCK), cols]),
         ]
@@ -258,27 +257,27 @@
             name=name,
         )(*operands)
 
-    (first,) = stage(
-        stage_first_kernel, [two], 4, [bands, keys, values], "stage_first", 52
-    )
-    inward = send(first, [(0, 1), (3, 2)])
-    listed = send(first, [(1, 2), (2, 1)])
-    (outward,) = stage(
-        functools.partial(stage_outward_kernel, half),
-        [two],
+    token = jax.ShapeDtypeStruct((8, HD), jnp.int32)
+    listed, after = stage(
+        stage_listed_kernel, [two, token], 4, [bands, keys, values], "stage_listed", 52
+    )
+    beside, after = stage(
+        functools.partial(stage_beside_kernel, half),
+        [two, token],
         2,
-        [keys, values],
-        "stage_outward",
-        32,
-    )
-    outward = send(outward, [(1, 0), (2, 3)])
+        [after, keys, values],
+        "stage_beside",
+        52,
+    )
     (crossed,) = stage(
-        stage_crossed_kernel, [two], 4, [inward, bands, keys, values], "stage_crossed", 32
-    )
+        stage_crossed_kernel, [two], 4, [after, bands, keys, values], "stage_crossed", 32
+    )
+    beside = send(beside, [(0, 1), (1, 0), (2, 3), (3, 2)])
+    listed = send(listed, [(1, 2), (2, 1)])
     crossed = send(crossed, [(0, 2), (3, 1)])
     relayed = send(listed, [(2, 3), (1, 0)])
     (direct,) = stage(
-        stage_direct_kernel, [one], 2, [outward, bands, keys, values], "stage_direct", 32
+        stage_direct_kernel, [one], 2, [beside, bands, keys, values], "stage_direct", 32
     )
     direct = send(direct, [(0, 3), (3, 0)])
     last = heads // 4
@@ -288,7 +287,7 @@
         functools.partial(stage_closing_kernel, cuts),
         [jax.ShapeDtypeStruct((2, BLOCK, size), jnp.bfloat16) for _, size in cuts],
         2 * len(cuts),
-        [crossed, relayed, bands, keys, values],
+        [crossed, bands, keys, values],
         "stage_closing",
         32,
     )
@@ -299,11 +298,11 @@
     mixed, tops, sums = pl.pallas_call(
         functools.partial(attend_kernel, rows // 2),
         out_shape=[state] * 3,
-        in_specs=[local] * 9,
+        in_specs=[local] * 8,
         out_specs=[local] * 3,
         compiler_params=roomy,
         name="attend",
-    )(queries, keys, values, inward, outward, listed, crossed, relayed, direct)
+    )(queries, keys, values, beside, listed, crossed, relayed, direct)
     result = None
     for part, (start, size) in zip(closing, cuts):
         operands = [queries, part, mixed, tops, sums]

time: 95.7 us -> 89.8 us (0.938)
  the two profiles are of different devices: /device:TPU:0 before, /device:TPU:21 now
where the time goes in v10:
time: 89.8 us; the launch traced here: 89.6 us
  waiting for transfers between devices  64.9 us (72%)
  Pallas kernels  16.7 us (19%)
  starting transfers between devices  7.14 us (8%)
    ppermute x7, waiting for transfers between devices, send(): return lax.ppermute(array, 'tm', pairs)  64.9 us
    pallas_call x1, Pallas kernels, four_frames(): pl.pallas_call(functools.partial(attend_kernel, rows // 2), out_shape=[st...  8.28 us
    ppermute x7, starting transfers between devices, send(): return lax.ppermute(array, 'tm', pairs)  7.14 us
    pallas_call x5, Pallas kernels, stage(): pl.pallas_call(kernel, out_shape=shapes, in_specs=[scalars if operand is...  5.12 us
    pallas_call x2, Pallas kernels, four_frames(): pl.pallas_call(functools.partial(close_kernel, start), out_shape=jax.Shap...  3.33 us
  transfers between devices with their start and end apart: 7, of which 4 were waited for; matrix products, arithmetic and copies ran while one was open for 0% of the time, Pallas kernels for 15%

profile of v10, /device:TPU:21, one launch (start us, length us, event | category | flops | bytes accessed | tf_op | source)
XLA Modules:
  0.0 89.6 jit_solution(15395954328090751550)
XLA Ops:
  0.0 0.0 copy-start.3
  0.0 0.7 copy-done.3
  0.7 0.0 copy-start
  0.7 0.0 copy-start.1
  0.7 0.0 copy-start.4
  0.7 1.9 %stage_listed.1 = (bf16[2,256,1024]{2,1,0:T(8,128)(2,1)S(1)}, s32[8,128]{1,0:T(8,128)S(1)}) custom-call(s32[4,2,4]{2,1,0:T(2,128)S(1)} %bitcast.1, bf16[512,1024]{1,0:T(8,128)(2,1)} %keys.11, bf16[512,1024]{1,0:T(8,128)(2,1)} %values.11), custom_call_target="tpu_custom_call" | custom-call | tf_op jit(solution)/shard_map/stage_listed/pallas_call | solution.py:250
  2.6 2.1 %collective-permute-start.3 = (bf16[2,256,1024]{2,1,0:T(8,128)(2,1)S(1)}, bf16[2,256,1024]{2,1,0:T(8,128)(2,1)S(1)}, u32[]{:S(2)}, u32[]{:S(2)}) collective-permute-start(bf16[2,256,1024]{2,1,0:T(8,128)(2,1)S(1)} %get-tuple-element.18), channel_id=1, source_target_pairs={{4,8},{8,4},{5,9},{9,5},{6,10},{10,6},{7,11},{11,7},{20,24},{24,20... | collective-permute-start | bytes 3145736 | tf_op jit(solution)/shard_map/ppermute | solution.py:243
  4.7 1.2 %stage_beside.1 = (bf16[2,256,1024]{2,1,0:T(8,128)(2,1)S(1)}, s32[8,128]{1,0:T(8,128)S(1)}) custom-call(s32[8,128]{1,0:T(8,128)S(1)} %get-tuple-element.14.after, bf16[512,1024]{1,0:T(8,128)(2,1)} %keys.11, bf16[512,1024]{1,0:T(8,128)(2,1)} %values.11), custom_call_target="tpu_custom_call" | custom-call | tf_op jit(solution)/shard_map/stage_beside/pallas_call | solution.py:250
  5.9 0.1 collective-permute-start.2
  6.0 0.0 copy-done
  6.0 0.0 copy-done.1
  6.0 0.0 copy-done.4
  6.0 0.7 stage_crossed.1
  6.7 1.3 %collective-permute-start = (bf16[2,256,1024]{2,1,0:T(8,128)(2,1)S(1)}, bf16[2,256,1024]{2,1,0:T(8,128)(2,1)S(1)}, u32[]{:S(2)}, u32[]{:S(2)}) collective-permute-start(bf16[2,256,1024]{2,1,0:T(8,128)(2,1)S(1)} %stage_crossed.1), channel_id=1, source_target_pairs={{0,8},{12,4},{1,9},{13,5},{2,10},{14,6},{3,11},{15,7},{16,24},{28,... | collective-permute-start | bytes 3145736 | tf_op jit(solution)/shard_map/ppermute | solution.py:243
  8.0 20.5 %collective-permute-done.3.listed = bf16[2,256,1024]{2,1,0:T(8,128)(2,1)S(1)} collective-permute-done((bf16[2,256,1024]{2,1,0:T(8,128)(2,1)S(1)}, bf16[2,256,1024]{2,1,0:T(8,128)(2,1)S(1)}, u32[]{:S(2)}, u32[]{:S(2)}) %collective-permute-start.3) | collective-permute-done | bytes 1048608 | tf_op jit(solution)/shard_map/ppermute | solution.py:243
  28.5 1.3 %collective-permute-start.4 = (bf16[2,256,1024]{2,1,0:T(8,128)(2,1)S(1)}, bf16[2,256,1024]{2,1,0:T(8,128)(2,1)S(1)}, u32[]{:S(2)}, u32[]{:S(2)}) collective-permute-start(bf16[2,256,1024]{2,1,0:T(8,128)(2,1)S(1)} %collective-permute-done.3.listed), channel_id=1, source_target_pairs={{8,12},{4,0},{9,13},{5,1},{10,14},{6,2},{11,15},{7,3},{24,28},{20,... | collective-permute-start | bytes 3145736 | tf_op jit(solution)/shard_map/ppermute | solution.py:243
  29.8 0.0 collective-permute-done.2.after.beside
  29.9 0.6 stage_direct.1
  30.5 0.0 copy-start.2
  30.5 0.8 collective-permute-start.5
  31.3 21.8 %collective-permute-done.after.crossed = bf16[2,256,1024]{2,1,0:T(8,128)(2,1)S(1)} collective-permute-done((bf16[2,256,1024]{2,1,0:T(8,128)(2,1)S(1)}, bf16[2,256,1024]{2,1,0:T(8,128)(2,1)S(1)}, u32[]{:S(2)}, u32[]{:S(2)}) %collective-permute-start) | collective-permute-done | bytes 1048608 | tf_op jit(solution)/shard_map/ppermute | solution.py:243
  53.2 0.7 stage_closing.1
  53.9 0.2 collective-permute-start.6
  54.1 1.3 %collective-permute-start.1 = (bf16[2,128,256]{2,1,0:T(8,128)(2,1)S(1)}, bf16[2,128,256]{2,1,0:T(8,128)(2,1)S(1)}, u32[]{:S(2)}, u32[]{:S(2)}) collective-permute-start(bf16[2,128,256]{2,1,0:T(8,128)(2,1)S(1)} %get-tuple-element.16), channel_id=1, source_target_pairs={{4,8},{8,4},{0,12},{12,0},{5,9},{9,5},{1,13},{13,1},{6,10},{10,6},... | collective-permute-start | bytes 393224 | tf_op jit(solution)/shard_map/ppermute | solution.py:243
  55.4 0.0 collective-permute-done.5.direct
  55.4 0.0 collective-permute-done.4.relayed
  55.4 0.0 copy-done.2
  55.4 8.3 %attend.1 = (f32[8,512,128]{2,1,0:T(8,128)S(1)}, f32[8,512,128]{2,1,0:T(8,128)S(1)}, f32[8,512,128]{2,1,0:T(8,128)S(1)}) custom-call(bf16[512,1024]{1,0:T(8,128)(2,1)S(1)} %copy-done.2, bf16[512,1024]{1,0:T(8,128)(2,1)S(1)} %copy-done, bf16[512,1024]{1,0:T(8,128)(2,1)S(1)} %copy-done.1, bf16[2,256,1024]{2,1,0:T(8,128)(2,1)S(1)} %collective-permute-done.2.after.beside, ...), custom_call_target="tpu_custom_call" | custom-call | tf_op jit(solution)/shard_map/attend/pallas_call | solution.py:298
  63.7 21.7 %collective-permute-done.6.closing = bf16[2,128,768]{2,1,0:T(8,128)(2,1)S(1)} collective-permute-done((bf16[2,128,768]{2,1,0:T(8,128)(2,1)S(1)}, bf16[2,128,768]{2,1,0:T(8,128)(2,1)S(1)}, u32[]{:S(2)}, u32[]{:S(2)}) %collective-permute-start.6) | collective-permute-done | bytes 393248 | tf_op jit(solution)/shard_map/ppermute | solution.py:243
  85.4 2.0 %close.2.rest_0_ = bf16[512,1024]{1,0:T(8,128)(2,1)} custom-call(bf16[512,1024]{1,0:T(8,128)(2,1)S(1)} %copy-done.2, bf16[2,128,768]{2,1,0:T(8,128)(2,1)S(1)} %collective-permute-done.6.closing, f32[8,512,128]{2,1,0:T(8,128)S(1)} %get-tuple-element.19.mixed, f32[8,512,128]{2,1,0:T(8,128)S(1)} %get-tuple-element.20.tops, ...), custom_call_target="tpu_custom_call" | custom-call | tf_op jit(solution)/shard_map/close/pallas_call | solution.py:315
  87.4 0.8 collective-permute-done.1.closing
  88.2 1.4 %close.3 = bf16[512,1024]{1,0:T(8,128)(2,1)} custom-call(bf16[512,1024]{1,0:T(8,128)(2,1)S(1)} %copy-done.2, bf16[2,128,256]{2,1,0:T(8,128)(2,1)S(1)} %collective-permute-done.1.closing, f32[8,512,128]{2,1,0:T(8,128)S(1)} %get-tuple-element.19.mixed, f32[8,512,128]{2,1,0:T(8,128)S(1)} %get-tuple-element.20.tops, ...), custom_call_target="tpu_custom_call", output_to_operand_aliasing={{}: (5, {})} | custom-call | tf_op jit(solution)/shard_map/close/pallas_call | solution.py:315
Async XLA Ops:
  0.0 0.7 copy-start.3
  0.7 5.3 %copy-start = (bf16[512,1024]{1,0:T(8,128)(2,1)S(1)}, bf16[512,1024]{1,0:T(8,128)(2,1)}, u32[]{:S(2)}) copy-start(bf16[512,1024]{1,0:T(8,128)(2,1)} %keys.11) | copy-start | bytes 3145732
  0.7 5.3 %copy-start.1 = (bf16[512,1024]{1,0:T(8,128)(2,1)S(1)}, bf16[512,1024]{1,0:T(8,128)(2,1)}, u32[]{:S(2)}) copy-start(bf16[512,1024]{1,0:T(8,128)(2,1)} %values.11) | copy-start | bytes 3145732
  0.7 5.3 %copy-start.4 = (s32[4,4,2]{1,2,0:T(2,128)S(1)}, s32[4,4,2]{1,2,0:T(2,128)}, u32[]{:S(2)}) copy-start(s32[4,4,2]{1,2,0:T(2,128)} %param.7) | copy-start | bytes 388
  2.6 25.9 %collective-permute-start.3 = (bf16[2,256,1024]{2,1,0:T(8,128)(2,1)S(1)}, bf16[2,256,1024]{2,1,0:T(8,128)(2,1)S(1)}, u32[]{:S(2)}, u32[]{:S(2)}) collective-permute-start(bf16[2,256,1024]{2,1,0:T(8,128)(2,1)S(1)} %get-tuple-element.18), channel_id=1, source_target_pairs={{4,8},{8,4},{5,9},{9,5},{6,10},{10,6},{7,11},{11,7},{20,24},{24,20... | collective-permute-start | bytes 3145736 | tf_op jit(solution)/shard_map/ppermute | solution.py:243
  5.9 24.0 %collective-permute-start.2 = (bf16[2,256,1024]{2,1,0:T(8,128)(2,1)S(1)}, bf16[2,256,1024]{2,1,0:T(8,128)(2,1)S(1)}, u32[]{:S(2)}, u32[]{:S(2)}) collective-permute-start(bf16[2,256,1024]{2,1,0:T(8,128)(2,1)S(1)} %get-tuple-element.17), channel_id=1, source_target_pairs={{0,4},{4,0},{8,12},{12,8},{1,5},{5,1},{9,13},{13,9},{2,6},{6,2},{1... | collective-permute-start | bytes 3145736 | tf_op jit(solution)/shard_map/ppermute | solution.py:243
  6.7 46.5 %collective-permute-start = (bf16[2,256,1024]{2,1,0:T(8,128)(2,1)S(1)}, bf16[2,256,1024]{2,1,0:T(8,128)(2,1)S(1)}, u32[]{:S(2)}, u32[]{:S(2)}) collective-permute-start(bf16[2,256,1024]{2,1,0:T(8,128)(2,1)S(1)} %stage_crossed.1), channel_id=1, source_target_pairs={{0,8},{12,4},{1,9},{13,5},{2,10},{14,6},{3,11},{15,7},{16,24},{28,... | collective-permute-start | bytes 3145736 | tf_op jit(solution)/shard_map/ppermute | solution.py:243
  28.5 26.9 %collective-permute-start.4 = (bf16[2,256,1024]{2,1,0:T(8,128)(2,1)S(1)}, bf16[2,256,1024]{2,1,0:T(8,128)(2,1)S(1)}, u32[]{:S(2)}, u32[]{:S(2)}) collective-permute-start(bf16[2,256,1024]{2,1,0:T(8,128)(2,1)S(1)} %collective-permute-done.3.listed), channel_id=1, source_target_pairs={{8,12},{4,0},{9,13},{5,1},{10,14},{6,2},{11,15},{7,3},{24,28},{20,... | collective-permute-start | bytes 3145736 | tf_op jit(solution)/shard_map/ppermute | solution.py:243
  30.5 24.9 %copy-start.2 = (bf16[512,1024]{1,0:T(8,128)(2,1)S(1)}, bf16[512,1024]{1,0:T(8,128)(2,1)}, u32[]{:S(2)}) copy-start(bf16[512,1024]{1,0:T(8,128)(2,1)} %queries.5) | copy-start | bytes 3145732
  30.5 24.9 %collective-permute-start.5 = (bf16[2,128,1024]{2,1,0:T(8,128)(2,1)S(1)}, bf16[2,128,1024]{2,1,0:T(8,128)(2,1)S(1)}, u32[]{:S(2)}, u32[]{:S(2)}) collective-permute-start(bf16[2,128,1024]{2,1,0:T(8,128)(2,1)S(1)} %stage_direct.1), channel_id=1, source_target_pairs={{0,12},{12,0},{1,13},{13,1},{2,14},{14,2},{3,15},{15,3},{16,28},{2... | collective-permute-start | bytes 1572872 | tf_op jit(solution)/shard_map/ppermute | solution.py:243
  53.9 31.5 %collective-permute-start.6 = (bf16[2,128,768]{2,1,0:T(8,128)(2,1)S(1)}, bf16[2,128,768]{2,1,0:T(8,128)(2,1)S(1)}, u32[]{:S(2)}, u32[]{:S(2)}) collective-permute-start(bf16[2,128,768]{2,1,0:T(8,128)(2,1)S(1)} %get-tuple-element.22), channel_id=1, source_target_pairs={{4,8},{8,4},{0,12},{12,0},{5,9},{9,5},{1,13},{13,1},{6,10},{10,6},... | collective-permute-start | bytes 1179656 | tf_op jit(solution)/shard_map/ppermute | solution.py:243
  54.1 34.1 %collective-permute-start.1 = (bf16[2,128,256]{2,1,0:T(8,128)(2,1)S(1)}, bf16[2,128,256]{2,1,0:T(8,128)(2,1)S(1)}, u32[]{:S(2)}, u32[]{:S(2)}) collective-permute-start(bf16[2,128,256]{2,1,0:T(8,128)(2,1)S(1)} %get-tuple-element.16), channel_id=1, source_target_pairs={{4,8},{8,4},{0,12},{12,0},{5,9},{9,5},{1,13},{13,1},{6,10},{10,6},... | collective-permute-start | bytes 393224 | tf_op jit(solution)/shard_map/ppermute | solution.py:243

commit v11 on v10

--- a/solution.py
+++ b/solution.py
@@ -97,9 +97,13 @@
     return pl.ds(pl.multiple_of(block * BLOCK, BLOCK), BLOCK)
 
 
-def stage_listed_kernel(bands, keys, values, listed, token, sems):
-    frame = lax.axis_index("tm")
-    token[...] = jnp.zeros_like(token)
+def stage_near_kernel(half, bands, keys, values, listed, beside, token, sems):
+    frame = lax.axis_index("tm")
+    rows = pl.ds(pl.multiple_of(lax.rem(frame + 1, 2) * half, half), half)
+    near = [
+        pltpu.make_async_copy(source.at[rows], beside.at[kv], sems.at[kv])
+        for kv, source in enumerate((keys, values))
+    ]
 
     @pl.when((frame == 1) | (frame == 2))
     def _():
@@ -110,14 +114,18 @@
             rows = rows_of(bands[reader, slot, frame])
             for kv, source in enumerate((keys, values)):
                 pairs.append((source.at[rows], listed.at[kv, pl.ds(place * BLOCK, BLOCK)]))
-        run_copies(pairs, sems)
-
-
-def stage_beside_kernel(half, after, keys, values, beside, token, sems):
-    frame = lax.axis_index("tm")
+        for copy in near:
+            copy.start()
+        run_copies(pairs, sems.at[pl.ds(2, 4)])
+
+    @pl.when((frame == 0) | (frame == 3))
+    def _():
+        for copy in near:
+            copy.start()
+
     token[...] = jnp.zeros_like(token)
-    rows = pl.ds(pl.multiple_of(lax.rem(frame + 1, 2) * half, half), half)
-    run_copies([(keys.at[rows], beside.at[0]), (values.at[rows], beside.at[1])], sems)
+    for copy in near:
+        copy.wait()
 
 
 def stage_crossed_kernel(after, bands, keys, values, crossed, sems):
@@ -258,16 +266,13 @@
         )(*operands)
 
     token = jax.ShapeDtypeStruct((8, HD), jnp.int32)
-    listed, after = stage(
-        stage_listed_kernel, [two, token], 4, [bands, keys, values], "stage_listed", 52
-    )
-    beside, after = stage(
-        functools.partial(stage_beside_kernel, half),
-        [two, token],
-        2,
-        [after, keys, values],
-        "stage_beside",
-        52,
+    listed, beside, after = stage(
+        functools.partial(stage_near_kernel, half),
+        [two, two, token],
+        6,
+        [bands, keys, values],
+        "stage_near",
+        51,
     )
     (crossed,) = stage(
         stage_crossed_kernel, [two], 4, [after, bands, keys, values], "stage_crossed", 32

time: 89.8 us -> 90.7 us (1.010)
  the two profiles are of different devices: /device:TPU:21 before, /device:TPU:0 now
where the time goes in v11:
time: 90.7 us; the launch traced here: 90.5 us
  waiting for transfers between devices  56.6 us (62%)
  starting transfers between devices  17.3 us (19%)
  Pallas kernels  15.6 us (17%)
    ppermute x7, waiting for transfers between devices, send(): return lax.ppermute(array, 'tm', pairs)  56.6 us
    ppermute x7, starting transfers between devices, send(): return lax.ppermute(array, 'tm', pairs)  17.3 us
    pallas_call x1, Pallas kernels, four_frames(): pl.pallas_call(functools.partial(attend_kernel, rows // 2), out_shape=[st...  8.2 us
    pallas_call x4, Pallas kernels, stage(): pl.pallas_call(kernel, out_shape=shapes, in_specs=[scalars if operand is...  4.04 us
    pallas_call x2, Pallas kernels, four_frames(): pl.pallas_call(functools.partial(close_kernel, start), out_shape=jax.Shap...  3.33 us
  transfers between devices with their start and end apart: 7, of which 4 were waited for; matrix products, arithmetic and copies ran while one was open for 0% of the time, Pallas kernels for 14%

profile of v11, /device:TPU:0, one launch (start us, length us, event | category | flops | bytes accessed | tf_op | source)
XLA Modules:
  0.0 90.5 jit_solution(4231308081401709016)
XLA Ops:
  0.0 0.0 copy-start
  0.0 0.0 copy-start.1
  0.0 0.0 copy-start.3
  0.0 0.8 copy-done.3
  0.8 1.9 %stage_near.1 = (bf16[2,256,1024]{2,1,0:T(8,128)(2,1)S(1)}, bf16[2,256,1024]{2,1,0:T(8,128)(2,1)S(1)}, s32[8,128]{1,0:T(8,128)S(1)}) custom-call(s32[4,2,4]{2,1,0:T(2,128)S(1)} %bitcast.1, bf16[512,1024]{1,0:T(8,128)(2,1)} %keys.9, bf16[512,1024]{1,0:T(8,128)(2,1)} %values.9), custom_call_target="tpu_custom_call" | custom-call | tf_op jit(solution)/shard_map/stage_near/pallas_call | solution.py:258
  2.7 0.7 collective-permute-start.3
  3.5 6.1 %collective-permute-start.2 = (bf16[2,256,1024]{2,1,0:T(8,128)(2,1)S(1)}, bf16[2,256,1024]{2,1,0:T(8,128)(2,1)S(1)}, u32[]{:S(2)}, u32[]{:S(2)}) collective-permute-start(bf16[2,256,1024]{2,1,0:T(8,128)(2,1)S(1)} %get-tuple-element.15), channel_id=1, source_target_pairs={{0,4},{4,0},{8,12},{12,8},{1,5},{5,1},{9,13},{13,9},{2,6},{6,2},{1... | collective-permute-start | bytes 3145736 | tf_op jit(solution)/shard_map/ppermute | solution.py:251
  9.6 0.0 copy-done
  9.6 0.0 copy-done.1
  9.6 0.7 stage_crossed.1
  10.4 1.8 %collective-permute-start = (bf16[2,256,1024]{2,1,0:T(8,128)(2,1)S(1)}, bf16[2,256,1024]{2,1,0:T(8,128)(2,1)S(1)}, u32[]{:S(2)}, u32[]{:S(2)}) collective-permute-start(bf16[2,256,1024]{2,1,0:T(8,128)(2,1)S(1)} %stage_crossed.1), channel_id=1, source_target_pairs={{0,8},{12,4},{1,9},{13,5},{2,10},{14,6},{3,11},{15,7},{16,24},{28,... | collective-permute-start | bytes 3145736 | tf_op jit(solution)/shard_map/ppermute | solution.py:251
  12.2 0.0 collective-permute-done.3.listed
  12.2 1.3 %collective-permute-start.4 = (bf16[2,256,1024]{2,1,0:T(8,128)(2,1)S(1)}, bf16[2,256,1024]{2,1,0:T(8,128)(2,1)S(1)}, u32[]{:S(2)}, u32[]{:S(2)}) collective-permute-start(bf16[2,256,1024]{2,1,0:T(8,128)(2,1)S(1)} %collective-permute-done.3.listed), channel_id=1, source_target_pairs={{8,12},{4,0},{9,13},{5,1},{10,14},{6,2},{11,15},{7,3},{24,28},{20,... | collective-permute-start | bytes 3145736 | tf_op jit(solution)/shard_map/ppermute | solution.py:251
  13.5 19.7 %collective-permute-done.2.after.beside = bf16[2,256,1024]{2,1,0:T(8,128)(2,1)S(1)} collective-permute-done((bf16[2,256,1024]{2,1,0:T(8,128)(2,1)S(1)}, bf16[2,256,1024]{2,1,0:T(8,128)(2,1)S(1)}, u32[]{:S(2)}, u32[]{:S(2)}) %collective-permute-start.2) | collective-permute-done | bytes 1048608 | tf_op jit(solution)/shard_map/ppermute | solution.py:251
  33.2 0.7 stage_direct.1
  33.9 0.0 copy-start.2
  33.9 3.4 %collective-permute-start.5 = (bf16[2,128,1024]{2,1,0:T(8,128)(2,1)S(1)}, bf16[2,128,1024]{2,1,0:T(8,128)(2,1)S(1)}, u32[]{:S(2)}, u32[]{:S(2)}) collective-permute-start(bf16[2,128,1024]{2,1,0:T(8,128)(2,1)S(1)} %stage_direct.1), channel_id=1, source_target_pairs={{0,12},{12,0},{1,13},{13,1},{2,14},{14,2},{3,15},{15,3},{16,28},{2... | collective-permute-start | bytes 1572872 | tf_op jit(solution)/shard_map/ppermute | solution.py:251
  37.3 18.4 %collective-permute-done.after.crossed = bf16[2,256,1024]{2,1,0:T(8,128)(2,1)S(1)} collective-permute-done((bf16[2,256,1024]{2,1,0:T(8,128)(2,1)S(1)}, bf16[2,256,1024]{2,1,0:T(8,128)(2,1)S(1)}, u32[]{:S(2)}, u32[]{:S(2)}) %collective-permute-start) | collective-permute-done | bytes 1048608 | tf_op jit(solution)/shard_map/ppermute | solution.py:251
  55.7 0.7 stage_closing.1
  56.4 1.4 %collective-permute-start.6 = (bf16[2,128,768]{2,1,0:T(8,128)(2,1)S(1)}, bf16[2,128,768]{2,1,0:T(8,128)(2,1)S(1)}, u32[]{:S(2)}, u32[]{:S(2)}) collective-permute-start(bf16[2,128,768]{2,1,0:T(8,128)(2,1)S(1)} %get-tuple-element.20), channel_id=1, source_target_pairs={{4,8},{8,4},{0,12},{12,0},{5,9},{9,5},{1,13},{13,1},{6,10},{10,6},... | collective-permute-start | bytes 1179656 | tf_op jit(solution)/shard_map/ppermute | solution.py:251
  57.9 2.5 %collective-permute-start.1 = (bf16[2,128,256]{2,1,0:T(8,128)(2,1)S(1)}, bf16[2,128,256]{2,1,0:T(8,128)(2,1)S(1)}, u32[]{:S(2)}, u32[]{:S(2)}) collective-permute-start(bf16[2,128,256]{2,1,0:T(8,128)(2,1)S(1)} %get-tuple-element.14), channel_id=1, source_target_pairs={{4,8},{8,4},{0,12},{12,0},{5,9},{9,5},{1,13},{13,1},{6,10},{10,6},... | collective-permute-start | bytes 393224 | tf_op jit(solution)/shard_map/ppermute | solution.py:251
  60.3 8.6 %collective-permute-done.5.direct = bf16[2,128,1024]{2,1,0:T(8,128)(2,1)S(1)} collective-permute-done((bf16[2,128,1024]{2,1,0:T(8,128)(2,1)S(1)}, bf16[2,128,1024]{2,1,0:T(8,128)(2,1)S(1)}, u32[]{:S(2)}, u32[]{:S(2)}) %collective-permute-start.5) | collective-permute-done | bytes 524320 | tf_op jit(solution)/shard_map/ppermute | solution.py:251
  68.9 10.0 %collective-permute-done.4.relayed = bf16[2,256,1024]{2,1,0:T(8,128)(2,1)S(1)} collective-permute-done((bf16[2,256,1024]{2,1,0:T(8,128)(2,1)S(1)}, bf16[2,256,1024]{2,1,0:T(8,128)(2,1)S(1)}, u32[]{:S(2)}, u32[]{:S(2)}) %collective-permute-start.4) | collective-permute-done | bytes 1048608 | tf_op jit(solution)/shard_map/ppermute | solution.py:251
  78.9 0.0 copy-done.2
  78.9 8.2 %attend.1 = (f32[8,512,128]{2,1,0:T(8,128)S(1)}, f32[8,512,128]{2,1,0:T(8,128)S(1)}, f32[8,512,128]{2,1,0:T(8,128)S(1)}) custom-call(bf16[512,1024]{1,0:T(8,128)(2,1)S(1)} %copy-done.2, bf16[512,1024]{1,0:T(8,128)(2,1)S(1)} %copy-done, bf16[512,1024]{1,0:T(8,128)(2,1)S(1)} %copy-done.1, bf16[2,256,1024]{2,1,0:T(8,128)(2,1)S(1)} %collective-permute-done.2.after.beside, ...), custom_call_target="tpu_custom_call" | custom-call | tf_op jit(solution)/shard_map/attend/pallas_call | solution.py:303
  87.1 0.0 collective-permute-done.6.closing
  87.1 2.0 %close.2.rest_0_ = bf16[512,1024]{1,0:T(8,128)(2,1)} custom-call(bf16[512,1024]{1,0:T(8,128)(2,1)S(1)} %copy-done.2, bf16[2,128,768]{2,1,0:T(8,128)(2,1)S(1)} %collective-permute-done.6.closing, f32[8,512,128]{2,1,0:T(8,128)S(1)} %get-tuple-element.17.mixed, f32[8,512,128]{2,1,0:T(8,128)S(1)} %get-tuple-element.18.tops, ...), custom_call_target="tpu_custom_call" | custom-call | tf_op jit(solution)/shard_map/close/pallas_call | solution.py:320
  89.1 0.0 collective-permute-done.1.closing
  89.1 1.4 %close.3 = bf16[512,1024]{1,0:T(8,128)(2,1)} custom-call(bf16[512,1024]{1,0:T(8,128)(2,1)S(1)} %copy-done.2, bf16[2,128,256]{2,1,0:T(8,128)(2,1)S(1)} %collective-permute-done.1.closing, f32[8,512,128]{2,1,0:T(8,128)S(1)} %get-tuple-element.17.mixed, f32[8,512,128]{2,1,0:T(8,128)S(1)} %get-tuple-element.18.tops, ...), custom_call_target="tpu_custom_call", output_to_operand_aliasing={{}: (5, {})} | custom-call | tf_op jit(solution)/shard_map/close/pallas_call | solution.py:320
Async XLA Ops:
  0.0 9.6 %copy-start = (bf16[512,1024]{1,0:T(8,128)(2,1)S(1)}, bf16[512,1024]{1,0:T(8,128)(2,1)}, u32[]{:S(2)}) copy-start(bf16[512,1024]{1,0:T(8,128)(2,1)} %keys.9) | copy-start | bytes 3145732
  0.0 9.6 %copy-start.1 = (bf16[512,1024]{1,0:T(8,128)(2,1)S(1)}, bf16[512,1024]{1,0:T(8,128)(2,1)}, u32[]{:S(2)}) copy-start(bf16[512,1024]{1,0:T(8,128)(2,1)} %values.9) | copy-start | bytes 3145732
  0.0 0.8 copy-start.3
  2.7 9.4 %collective-permute-start.3 = (bf16[2,256,1024]{2,1,0:T(8,128)(2,1)S(1)}, bf16[2,256,1024]{2,1,0:T(8,128)(2,1)S(1)}, u32[]{:S(2)}, u32[]{:S(2)}) collective-permute-start(bf16[2,256,1024]{2,1,0:T(8,128)(2,1)S(1)} %get-tuple-element.16), channel_id=1, source_target_pairs={{4,8},{8,4},{5,9},{9,5},{6,10},{10,6},{7,11},{11,7},{20,24},{24,20... | collective-permute-start | bytes 3145736 | tf_op jit(solution)/shard_map/ppermute | solution.py:251
  3.5 29.7 %collective-permute-start.2 = (bf16[2,256,1024]{2,1,0:T(8,128)(2,1)S(1)}, bf16[2,256,1024]{2,1,0:T(8,128)(2,1)S(1)}, u32[]{:S(2)}, u32[]{:S(2)}) collective-permute-start(bf16[2,256,1024]{2,1,0:T(8,128)(2,1)S(1)} %get-tuple-element.15), channel_id=1, source_target_pairs={{0,4},{4,0},{8,12},{12,8},{1,5},{5,1},{9,13},{13,9},{2,6},{6,2},{1... | collective-permute-start | bytes 3145736 | tf_op jit(solution)/shard_map/ppermute | solution.py:251
  10.4 45.3 %collective-permute-start = (bf16[2,256,1024]{2,1,0:T(8,128)(2,1)S(1)}, bf16[2,256,1024]{2,1,0:T(8,128)(2,1)S(1)}, u32[]{:S(2)}, u32[]{:S(2)}) collective-permute-start(bf16[2,256,1024]{2,1,0:T(8,128)(2,1)S(1)} %stage_crossed.1), channel_id=1, source_target_pairs={{0,8},{12,4},{1,9},{13,5},{2,10},{14,6},{3,11},{15,7},{16,24},{28,... | collective-permute-start | bytes 3145736 | tf_op jit(solution)/shard_map/ppermute | solution.py:251
  12.2 66.7 %collective-permute-start.4 = (bf16[2,256,1024]{2,1,0:T(8,128)(2,1)S(1)}, bf16[2,256,1024]{2,1,0:T(8,128)(2,1)S(1)}, u32[]{:S(2)}, u32[]{:S(2)}) collective-permute-start(bf16[2,256,1024]{2,1,0:T(8,128)(2,1)S(1)} %collective-permute-done.3.listed), channel_id=1, source_target_pairs={{8,12},{4,0},{9,13},{5,1},{10,14},{6,2},{11,15},{7,3},{24,28},{20,... | collective-permute-start | bytes 3145736 | tf_op jit(solution)/shard_map/ppermute | solution.py:251
  33.9 45.0 %copy-start.2 = (bf16[512,1024]{1,0:T(8,128)(2,1)S(1)}, bf16[512,1024]{1,0:T(8,128)(2,1)}, u32[]{:S(2)}) copy-start(bf16[512,1024]{1,0:T(8,128)(2,1)} %queries.5) | copy-start | bytes 3145732
  33.9 35.0 %collective-permute-start.5 = (bf16[2,128,1024]{2,1,0:T(8,128)(2,1)S(1)}, bf16[2,128,1024]{2,1,0:T(8,128)(2,1)S(1)}, u32[]{:S(2)}, u32[]{:S(2)}) collective-permute-start(bf16[2,128,1024]{2,1,0:T(8,128)(2,1)S(1)} %stage_direct.1), channel_id=1, source_target_pairs={{0,12},{12,0},{1,13},{13,1},{2,14},{14,2},{3,15},{15,3},{16,28},{2... | collective-permute-start | bytes 1572872 | tf_op jit(solution)/shard_map/ppermute | solution.py:251
  56.4 30.7 %collective-permute-start.6 = (bf16[2,128,768]{2,1,0:T(8,128)(2,1)S(1)}, bf16[2,128,768]{2,1,0:T(8,128)(2,1)S(1)}, u32[]{:S(2)}, u32[]{:S(2)}) collective-permute-start(bf16[2,128,768]{2,1,0:T(8,128)(2,1)S(1)} %get-tuple-element.20), channel_id=1, source_target_pairs={{4,8},{8,4},{0,12},{12,0},{5,9},{9,5},{1,13},{13,1},{6,10},{10,6},... | collective-permute-start | bytes 1179656 | tf_op jit(solution)/shard_map/ppermute | solution.py:251
  57.9 31.2 %collective-permute-start.1 = (bf16[2,128,256]{2,1,0:T(8,128)(2,1)S(1)}, bf16[2,128,256]{2,1,0:T(8,128)(2,1)S(1)}, u32[]{:S(2)}, u32[]{:S(2)}) collective-permute-start(bf16[2,128,256]{2,1,0:T(8,128)(2,1)S(1)} %get-tuple-element.14), channel_id=1, source_target_pairs={{4,8},{8,4},{0,12},{12,0},{5,9},{9,5},{1,13},{13,1},{6,10},{10,6},... | collective-permute-start | bytes 393224 | tf_op jit(solution)/shard_map/ppermute | solution.py:251

commit v12 on v11

--- a/solution.py
+++ b/solution.py
@@ -142,29 +142,33 @@
         run_copies(pairs, sems)
 
 
-def stage_direct_kernel(after, bands, keys, values, direct, sems):
-    frame = lax.axis_index("tm")
-
-    @pl.when((frame == 0) | (frame == 3))
-    def _():
-        rows = rows_of(bands[3 - frame, 0, frame])
-        run_copies([(keys.at[rows], direct.at[0]), (values.at[rows], direct.at[1])], sems)
-
-
-def stage_closing_kernel(cuts, after, bands, keys, values, *rest):
-    closing, sems = rest[:-1], rest[-1]
+def stage_last_kernel(cuts, after, bands, keys, values, *rest):
+    direct, closing, sems = rest[: len(cuts)], rest[len(cuts) : -1], rest[-1]
     frame = lax.axis_index("tm")
     inner = (frame == 1) | (frame == 2)
-    other = jnp.where(frame == 1, 5 - bands[3, 1, 1], 1 - bands[0, 0, 2])
-    rows = rows_of(jnp.where(inner, other, bands[3 - frame, 1, frame]))
-    run_copies(
-        [
-            (source.at[rows, pl.ds(first, size)], part.at[kv])
-            for part, (first, size) in zip(closing, cuts)
-            for kv, source in enumerate((keys, values))
-        ],
-        sems,
-    )
+
+    @pl.when(inner)
+    def _():
+        rows = rows_of(jnp.where(frame == 1, 5 - bands[3, 1, 1], 1 - bands[0, 0, 2]))
+        run_copies(
+            [
+                (source.at[rows, pl.ds(*cut)], part.at[kv])
+                for part, cut in zip(closing, cuts)
+                for kv, source in enumerate((keys, values))
+            ],
+            sems,
+        )
+
+    @pl.when(jnp.logical_not(inner))
+    def _():
+        pairs = []
+        for slot in range(2):
+            rows = rows_of(bands[3 - frame, slot, frame])
+            to = pl.ds(slot * BLOCK, BLOCK)
+            for part, cut in zip(direct, cuts):
+                for kv, source in enumerate((keys, values)):
+                    pairs.append((source.at[rows, pl.ds(*cut)], part.at[kv, to]))
+        run_copies(pairs, sems)
 
 
 RATE = LOG2E * HD ** (-0.5)
@@ -176,67 +180,84 @@
     )
 
 
-def attend_kernel(
-    chunk, queries, keys, values, beside, listed, crossed, relayed, direct, mixed, tops, sums
-):
-    frame = lax.axis_index("tm")
-    edge = (frame == 0) | (frame == 3)
+def attend_kernel(chunk, queries, keys, values, beside, crossed, mixed, tops, sums):
+    frame = lax.axis_index("tm")
+    inner = (frame == 1) | (frame == 2)
     rows, columns = queries.shape
-
-    def pieces(head, own, kv):
-        cols = pl.ds(head * HD, HD)
-        return [
-            own[:, cols],
-            beside[kv, :, cols],
-            jnp.where(edge, relayed[kv, :, cols], crossed[kv, :, cols]),
-            jnp.where(edge, direct[kv, :, cols], listed[kv, pl.ds(BLOCK, BLOCK), cols]),
-        ]
-
-    def score(head, start):
-        rows_q = queries[pl.ds(start, chunk), pl.ds(head * HD, HD)]
-        return [scores_of(rows_q, piece) for piece in pieces(head, keys, 0)]
-
-    def finish(head, start, scores):
-        at = pl.ds(start, chunk)
-        row_max = functools.reduce(
-            jnp.maximum, [jnp.max(part, axis=1, keepdims=True) for part in scores]
-        )
-        powers = [jnp.exp2((part - row_max) * RATE) for part in scores]
-        row_sum = sum(jnp.sum(part, axis=1, keepdims=True) for part in powers)
-        mixed[head, at] = sum(
-            jnp.dot(part.astype(jnp.bfloat16), piece, preferred_element_type=jnp.float32)
-            for part, piece in zip(powers, pieces(head, values, 1))
-        )
-        tops[head, at] = jnp.broadcast_to(row_max, (chunk, HD))
-        sums[head, at] = jnp.broadcast_to(row_sum, (chunk, HD))
-
     units = [(head, start) for head in range(columns // HD) for start in range(0, rows, chunk)]
-    scores = score(*units[0])
-    for unit, following in zip(units, units[1:] + [None]):
-        ahead = score(*following) if following else None
-        finish(*unit, scores)
-        scores = ahead
-
-
-def close_kernel(first, queries, closing, mixed, tops, sums, *rest):
+
+    def attend(received):
+        def pieces(head, kv):
+            cols = pl.ds(head * HD, HD)
+            own = values if kv else keys
+            return [own[:, cols]] + [part[kv, :, cols] for part in received]
+
+        def score(head, start):
+            rows_q = queries[pl.ds(start, chunk), pl.ds(head * HD, HD)]
+            return [scores_of(rows_q, piece) for piece in pieces(head, 0)]
+
+        def finish(head, start, scores):
+            at = pl.ds(start, chunk)
+            row_max = functools.reduce(
+                jnp.maximum, [jnp.max(part, axis=1, keepdims=True) for part in scores]
+            )
+            powers = [jnp.exp2((part - row_max) * RATE) for part in scores]
+            row_sum = sum(jnp.sum(part, axis=1, keepdims=True) for part in powers)
+            mixed[head, at] = sum(
+                jnp.dot(part.astype(jnp.bfloat16), piece, preferred_element_type=jnp.float32)
+                for part, piece in zip(powers, pieces(head, 1))
+            )
+            tops[head, at] = jnp.broadcast_to(row_max, (chunk, HD))
+            sums[head, at] = jnp.broadcast_to(row_sum, (chunk, HD))
+
+        scores = score(*units[0])
+        for unit, following in zip(units, units[1:] + [None]):
+            ahead = score(*following) if following else None
+            finish(*unit, scores)
+            scores = ahead
+
+    pl.when(inner)(lambda: attend([beside, crossed]))
+    pl.when(jnp.logical_not(inner))(lambda: attend([beside]))
+
+
+def close_kernel(first, queries, listed, closing, relayed, direct, mixed, tops, sums, *rest):
     out, ready, sems = rest[-3:]
-    copies = []
-    for at in range(ready.shape[0]):
-        head = first // HD + at
-        here, there = pl.ds(first + at * HD, HD), pl.ds(at * HD, HD)
-        scores = scores_of(queries[:, here], closing[0, :, there])
-        top = jnp.maximum(tops[head], jnp.max(scores, axis=1, keepdims=True))
-        shrink = jnp.exp2((tops[head] - top) * RATE)
-        powers = jnp.exp2((scores - top) * RATE)
-        total = sums[head] * shrink + jnp.sum(powers, axis=1, keepdims=True)
-        more = jnp.dot(
-            powers.astype(jnp.bfloat16), closing[1, :, there], preferred_element_type=jnp.float32
-        )
-        ready[at] = ((mixed[head] * shrink + more) / total).astype(jnp.bfloat16)
-        copies.append(pltpu.make_async_copy(ready.at[at], out.at[:, here], sems.at[at]))
-        copies[-1].start()
-    for copy in copies:
-        copy.wait()
+    frame = lax.axis_index("tm")
+    inner = (frame == 1) | (frame == 2)
+
+    def close(pieces):
+        copies = []
+        for at in range(ready.shape[0]):
+            head = first // HD + at
+            here, there = pl.ds(first + at * HD, HD), pl.ds(at * HD, HD)
+            scores = [scores_of(queries[:, here], piece) for piece in pieces(0, here, there)]
+            top = functools.reduce(
+                jnp.maximum, [jnp.max(part, axis=1, keepdims=True) for part in scores], tops[head]
+            )
+            shrink = jnp.exp2((tops[head] - top) * RATE)
+            powers = [jnp.exp2((part - top[:, :1]) * RATE) for part in scores]
+            total = sums[head] * shrink + sum(
+                jnp.sum(part, axis=1, keepdims=True) for part in powers
+            )
+            more = sum(
+                jnp.dot(part.astype(jnp.bfloat16), piece, preferred_element_type=jnp.float32)
+                for part, piece in zip(powers, pieces(1, here, there))
+            )
+            ready[at] = ((mixed[head] * shrink + more) / total).astype(jnp.bfloat16)
+            copies.append(pltpu.make_async_copy(ready.at[at], out.at[:, here], sems.at[at]))
+            copies[-1].start()
+        for copy in copies:
+            copy.wait()
+
+    def of_inner(kv, here, there):
+        facing = [listed[kv, pl.ds(BLOCK, BLOCK), here], closing[kv, :, there]]
+        return [jnp.concatenate(facing, 0)]
+
+    def of_edge(kv, here, there):
+        return [relayed[kv, :, here], direct[kv, :, there]]
+
+    pl.when(inner)(lambda: close(of_inner))
+    pl.when(jnp.logical_not(inner))(lambda: close(of_edge))
 
 
 def four_frames(queries, keys, values, band_blocks):
@@ -251,7 +272,6 @@
         return lax.ppermute(array, "tm", pairs)
 
     bands = jnp.transpose(band_blocks, (0, 2, 1))
-    one = jax.ShapeDtypeStruct((2, BLOCK, columns), jnp.bfloat16)
     two = jax.ShapeDtypeStruct((2, 2 * BLOCK, columns), jnp.bfloat16)
 
     def stage(kernel, shapes, copies, operands, name, room):
@@ -281,36 +301,38 @@
     listed = send(listed, [(1, 2), (2, 1)])
     crossed = send(crossed, [(0, 2), (3, 1)])
     relayed = send(listed, [(2, 3), (1, 0)])
-    (direct,) = stage(
-        stage_direct_kernel, [one], 2, [beside, bands, keys, values], "stage_direct", 32
-    )
-    direct = send(direct, [(0, 3), (3, 0)])
     last = heads // 4
     cuts = [(0, heads - last), (heads - last, last)] if last else [(0, heads)]
     cuts = [(start * HD, size * HD) for start, size in cuts]
-    closing = stage(
-        functools.partial(stage_closing_kernel, cuts),
-        [jax.ShapeDtypeStruct((2, BLOCK, size), jnp.bfloat16) for _, size in cuts],
-        2 * len(cuts),
-        [crossed, bands, keys, values],
-        "stage_closing",
+    last_parts = stage(
+        functools.partial(stage_last_kernel, cuts),
+        [
+            jax.ShapeDtypeStruct((2, count * BLOCK, size), jnp.bfloat16)
+            for count in (2, 1)
+            for _, size in cuts
+        ],
+        4 * len(cuts),
+        [beside, bands, keys, values],
+        "stage_last",
         32,
     )
-    closing = [send(part, [(1, 2), (2, 1), (0, 3), (3, 0)]) for part in closing]
+    direct, closing = last_parts[: len(cuts)], last_parts[len(cuts) :]
+    direct = [send(part, [(0, 3), (3, 0)]) for part in direct]
+    closing = [send(part, [(1, 2), (2, 1)]) for part in closing]
 
     state = jax.ShapeDtypeStruct((heads, rows, HD), jnp.float32)
     roomy = pltpu.CompilerParams(vmem_limit_bytes=32 << 20)
     mixed, tops, sums = pl.pallas_call(
         functools.partial(attend_kernel, rows // 2),
         out_shape=[state] * 3,
-        in_specs=[local] * 8,
+        in_specs=[local] * 5,
         out_specs=[local] * 3,
         compiler_params=roomy,
         name="attend",
-    )(queries, keys, values, beside, listed, crossed, relayed, direct)
+    )(queries, keys, values, beside, crossed)
     result = None
-    for part, (start, size) in zip(closing, cuts):
-        operands = [queries, part, mixed, tops, sums]
+    for near, far, (start, size) in zip(closing, direct, cuts):
+        operands = [queries, listed, near, relayed, far, mixed, tops, sums]
         in_specs = [local] * len(operands)
         aliases = {}
         if result is not None:

time: 90.7 us -> 91.6 us (level); the launches traced: 90.5 us -> 90 us
  waiting for transfers between devices: 56.6 us -> 50.5 us
  Pallas kernels: 15.6 us -> 19.2 us
  starting transfers between devices: 17.3 us -> 19.1 us
    pallas_call x2, Pallas kernels: 3.33 us -> 10.9 us  [four_frames(): pl.pallas_call(functools.partial(close_kernel, start), out_shape=jax.Shap...]
    ppermute x7 -> x8, waiting for transfers between devices: 56.6 us -> 50.5 us  [send(): return lax.ppermute(array, 'tm', pairs)]
    pallas_call x1, Pallas kernels: 8.2 us -> 4.84 us  [four_frames(): pl.pallas_call(functools.partial(attend_kernel, rows // 2), out_shape=[st...]
    ppermute x7 -> x8, starting transfers between devices: 17.3 us -> 19.1 us  [send(): return lax.ppermute(array, 'tm', pairs)]
    pallas_call x4 -> x3, Pallas kernels: 4.04 us -> 3.48 us  [stage(): pl.pallas_call(kernel, out_shape=shapes, in_specs=[scalars if operand is...]
  transfers between devices with their start and end apart: 7 -> 8, of which waited for: 4 -> 4; matrix products, arithmetic and copies ran while one was open for 0% -> 0% of each run, Pallas kernels for 14% -> 16%
where the time goes in v12:
time: 91.6 us; the launch traced here: 90 us
  waiting for transfers between devices  50.5 us (55%)
  Pallas kernels  19.2 us (21%)
  starting transfers between devices  19.1 us (21%)
    ppermute x8, waiting for transfers between devices, send(): return lax.ppermute(array, 'tm', pairs)  50.5 us
    ppermute x8, starting transfers between devices, send(): return lax.ppermute(array, 'tm', pairs)  19.1 us
    pallas_call x2, Pallas kernels, four_frames(): pl.pallas_call(functools.partial(close_kernel, start), out_shape=jax.Shap...  10.9 us
    pallas_call x1, Pallas kernels, four_frames(): pl.pallas_call(functools.partial(attend_kernel, rows // 2), out_shape=[st...  4.84 us
    pallas_call x3, Pallas kernels, stage(): pl.pallas_call(kernel, out_shape=shapes, in_specs=[scalars if operand is...  3.48 us
  transfers between devices with their start and end apart: 8, of which 4 were waited for; matrix products, arithmetic and copies ran while one was open for 0% of the time, Pallas kernels for 16%

profile of v12, /device:TPU:0, one launch (start us, length us, event | category | flops | bytes accessed | tf_op | source)
XLA Modules:
  0.0 90.0 jit_solution(12889479090484307158)
XLA Ops:
  0.0 0.0 copy-start
  0.0 0.0 copy-start.1
  0.0 0.0 copy-start.3
  0.0 0.8 copy-done.3
  0.8 1.9 %stage_near.1 = (bf16[2,256,1024]{2,1,0:T(8,128)(2,1)S(1)}, bf16[2,256,1024]{2,1,0:T(8,128)(2,1)S(1)}, s32[8,128]{1,0:T(8,128)S(1)}) custom-call(s32[4,2,4]{2,1,0:T(2,128)S(1)} %bitcast.1, bf16[512,1024]{1,0:T(8,128)(2,1)} %keys.7, bf16[512,1024]{1,0:T(8,128)(2,1)} %values.7), custom_call_target="tpu_custom_call" | custom-call | tf_op jit(solution)/shard_map/stage_near/pallas_call | solution.py:278
  2.7 0.7 collective-permute-start
  3.5 6.1 %collective-permute-start.1 = (bf16[2,256,1024]{2,1,0:T(8,128)(2,1)S(1)}, bf16[2,256,1024]{2,1,0:T(8,128)(2,1)S(1)}, u32[]{:S(2)}, u32[]{:S(2)}) collective-permute-start(bf16[2,256,1024]{2,1,0:T(8,128)(2,1)S(1)} %get-tuple-element.16), channel_id=1, source_target_pairs={{0,4},{4,0},{8,12},{12,8},{1,5},{5,1},{9,13},{13,9},{2,6},{6,2},{1... | collective-permute-start | bytes 3145736 | tf_op jit(solution)/shard_map/ppermute | solution.py:272
  9.6 0.0 copy-done
  9.6 0.0 copy-done.1
  9.6 0.7 stage_crossed.1
  10.4 0.0 copy-start.2
  10.4 1.9 %collective-permute-start.5 = (bf16[2,256,1024]{2,1,0:T(8,128)(2,1)S(1)}, bf16[2,256,1024]{2,1,0:T(8,128)(2,1)S(1)}, u32[]{:S(2)}, u32[]{:S(2)}) collective-permute-start(bf16[2,256,1024]{2,1,0:T(8,128)(2,1)S(1)} %stage_crossed.1), channel_id=1, source_target_pairs={{0,8},{12,4},{1,9},{13,5},{2,10},{14,6},{3,11},{15,7},{16,24},{28,... | collective-permute-start | bytes 3145736 | tf_op jit(solution)/shard_map/ppermute | solution.py:272
  12.3 0.0 collective-permute-done.listed
  12.3 1.3 %collective-permute-start.3 = (bf16[2,256,1024]{2,1,0:T(8,128)(2,1)S(1)}, bf16[2,256,1024]{2,1,0:T(8,128)(2,1)S(1)}, u32[]{:S(2)}, u32[]{:S(2)}) collective-permute-start(bf16[2,256,1024]{2,1,0:T(8,128)(2,1)S(1)} %collective-permute-done.listed), channel_id=1, source_target_pairs={{8,12},{4,0},{9,13},{5,1},{10,14},{6,2},{11,15},{7,3},{24,28},{20,... | collective-permute-start | bytes 3145736 | tf_op jit(solution)/shard_map/ppermute | solution.py:272
  13.6 19.6 %collective-permute-done.1.after.beside = bf16[2,256,1024]{2,1,0:T(8,128)(2,1)S(1)} collective-permute-done((bf16[2,256,1024]{2,1,0:T(8,128)(2,1)S(1)}, bf16[2,256,1024]{2,1,0:T(8,128)(2,1)S(1)}, u32[]{:S(2)}, u32[]{:S(2)}) %collective-permute-start.1) | collective-permute-done | bytes 1048608 | tf_op jit(solution)/shard_map/ppermute | solution.py:272
  33.2 0.9 stage_last.1
  34.1 3.3 %collective-permute-start.7 = (bf16[2,256,768]{2,1,0:T(8,128)(2,1)S(1)}, bf16[2,256,768]{2,1,0:T(8,128)(2,1)S(1)}, u32[]{:S(2)}, u32[]{:S(2)}) collective-permute-start(bf16[2,256,768]{2,1,0:T(8,128)(2,1)S(1)} %get-tuple-element.24), channel_id=1, source_target_pairs={{0,12},{12,0},{1,13},{13,1},{2,14},{14,2},{3,15},{15,3},{16,28},{2... | collective-permute-start | bytes 2359304 | tf_op jit(solution)/shard_map/ppermute | solution.py:272
  37.3 0.7 collective-permute-start.6
  38.0 4.4 %collective-permute-start.4 = (bf16[2,256,256]{2,1,0:T(8,128)(2,1)S(1)}, bf16[2,256,256]{2,1,0:T(8,128)(2,1)S(1)}, u32[]{:S(2)}, u32[]{:S(2)}) collective-permute-start(bf16[2,256,256]{2,1,0:T(8,128)(2,1)S(1)} %get-tuple-element.18), channel_id=1, source_target_pairs={{0,12},{12,0},{1,13},{13,1},{2,14},{14,2},{3,15},{15,3},{16,28},{2... | collective-permute-start | bytes 786440 | tf_op jit(solution)/shard_map/ppermute | solution.py:272
  42.4 13.3 %collective-permute-done.5.crossed = bf16[2,256,1024]{2,1,0:T(8,128)(2,1)S(1)} collective-permute-done((bf16[2,256,1024]{2,1,0:T(8,128)(2,1)S(1)}, bf16[2,256,1024]{2,1,0:T(8,128)(2,1)S(1)}, u32[]{:S(2)}, u32[]{:S(2)}) %collective-permute-start.5) | collective-permute-done | bytes 1048608 | tf_op jit(solution)/shard_map/ppermute | solution.py:272
  55.7 0.7 collective-permute-start.2
  56.4 0.0 copy-done.2
  56.4 4.8 %attend.1 = (f32[8,512,128]{2,1,0:T(8,128)S(1)}, f32[8,512,128]{2,1,0:T(8,128)S(1)}, f32[8,512,128]{2,1,0:T(8,128)S(1)}) custom-call(bf16[512,1024]{1,0:T(8,128)(2,1)S(1)} %copy-done.2, bf16[512,1024]{1,0:T(8,128)(2,1)S(1)} %copy-done, bf16[512,1024]{1,0:T(8,128)(2,1)S(1)} %copy-done.1, bf16[2,256,1024]{2,1,0:T(8,128)(2,1)S(1)} %collective-permute-done.1.after.beside, ...), custom_call_target="tpu_custom_call" | custom-call | tf_op jit(solution)/shard_map/attend/pallas_call | solution.py:325
  61.2 0.0 collective-permute-done.6.closing
  61.3 13.3 %collective-permute-done.7.direct = bf16[2,256,768]{2,1,0:T(8,128)(2,1)S(1)} collective-permute-done((bf16[2,256,768]{2,1,0:T(8,128)(2,1)S(1)}, bf16[2,256,768]{2,1,0:T(8,128)(2,1)S(1)}, u32[]{:S(2)}, u32[]{:S(2)}) %collective-permute-start.7) | collective-permute-done | bytes 786464 | tf_op jit(solution)/shard_map/ppermute | solution.py:272
  74.5 4.3 %collective-permute-done.3.relayed = bf16[2,256,1024]{2,1,0:T(8,128)(2,1)S(1)} collective-permute-done((bf16[2,256,1024]{2,1,0:T(8,128)(2,1)S(1)}, bf16[2,256,1024]{2,1,0:T(8,128)(2,1)S(1)}, u32[]{:S(2)}, u32[]{:S(2)}) %collective-permute-start.3) | collective-permute-done | bytes 1048608 | tf_op jit(solution)/shard_map/ppermute | solution.py:272
  78.9 7.8 %close.2.rest_0_ = bf16[512,1024]{1,0:T(8,128)(2,1)} custom-call(bf16[512,1024]{1,0:T(8,128)(2,1)S(1)} %copy-done.2, bf16[2,256,1024]{2,1,0:T(8,128)(2,1)S(1)} %collective-permute-done.listed, bf16[2,128,768]{2,1,0:T(8,128)(2,1)S(1)} %collective-permute-done.6.closing, bf16[2,256,1024]{2,1,0:T(8,128)(2,1)S(1)} %collective-permute-done.3.relayed, ...), custom_call_target="tpu_custom_call" | custom-call | tf_op jit(solution)/shard_map/close/pallas_call | solution.py:342
  86.6 0.0 collective-permute-done.2.closing
  86.7 0.0 collective-permute-done.4.direct
  86.7 3.1 %close.3 = bf16[512,1024]{1,0:T(8,128)(2,1)} custom-call(bf16[512,1024]{1,0:T(8,128)(2,1)S(1)} %copy-done.2, bf16[2,256,1024]{2,1,0:T(8,128)(2,1)S(1)} %collective-permute-done.listed, bf16[2,128,256]{2,1,0:T(8,128)(2,1)S(1)} %collective-permute-done.2.closing, ...), custom_call_target="tpu_custom_call", output_to_operand_aliasing={{}: (8, {})} | custom-call | tf_op jit(solution)/shard_map/close/pallas_call | solution.py:342
Async XLA Ops:
  0.0 9.6 %copy-start = (bf16[512,1024]{1,0:T(8,128)(2,1)S(1)}, bf16[512,1024]{1,0:T(8,128)(2,1)}, u32[]{:S(2)}) copy-start(bf16[512,1024]{1,0:T(8,128)(2,1)} %keys.7) | copy-start | bytes 3145732
  0.0 9.6 %copy-start.1 = (bf16[512,1024]{1,0:T(8,128)(2,1)S(1)}, bf16[512,1024]{1,0:T(8,128)(2,1)}, u32[]{:S(2)}) copy-start(bf16[512,1024]{1,0:T(8,128)(2,1)} %values.7) | copy-start | bytes 3145732
  0.0 0.8 copy-start.3
  2.7 9.6 %collective-permute-start = (bf16[2,256,1024]{2,1,0:T(8,128)(2,1)S(1)}, bf16[2,256,1024]{2,1,0:T(8,128)(2,1)S(1)}, u32[]{:S(2)}, u32[]{:S(2)}) collective-permute-start(bf16[2,256,1024]{2,1,0:T(8,128)(2,1)S(1)} %get-tuple-element.15), channel_id=1, source_target_pairs={{4,8},{8,4},{5,9},{9,5},{6,10},{10,6},{7,11},{11,7},{20,24},{24,20... | collective-permute-start | bytes 3145736 | tf_op jit(solution)/shard_map/ppermute | solution.py:272
  3.5 29.7 %collective-permute-start.1 = (bf16[2,256,1024]{2,1,0:T(8,128)(2,1)S(1)}, bf16[2,256,1024]{2,1,0:T(8,128)(2,1)S(1)}, u32[]{:S(2)}, u32[]{:S(2)}) collective-permute-start(bf16[2,256,1024]{2,1,0:T(8,128)(2,1)S(1)} %get-tuple-element.16), channel_id=1, source_target_pairs={{0,4},{4,0},{8,12},{12,8},{1,5},{5,1},{9,13},{13,9},{2,6},{6,2},{1... | collective-permute-start | bytes 3145736 | tf_op jit(solution)/shard_map/ppermute | solution.py:272
  10.4 46.0 %copy-start.2 = (bf16[512,1024]{1,0:T(8,128)(2,1)S(1)}, bf16[512,1024]{1,0:T(8,128)(2,1)}, u32[]{:S(2)}) copy-start(bf16[512,1024]{1,0:T(8,128)(2,1)} %queries.5) | copy-start | bytes 3145732
  10.4 45.4 %collective-permute-start.5 = (bf16[2,256,1024]{2,1,0:T(8,128)(2,1)S(1)}, bf16[2,256,1024]{2,1,0:T(8,128)(2,1)S(1)}, u32[]{:S(2)}, u32[]{:S(2)}) collective-permute-start(bf16[2,256,1024]{2,1,0:T(8,128)(2,1)S(1)} %stage_crossed.1), channel_id=1, source_target_pairs={{0,8},{12,4},{1,9},{13,5},{2,10},{14,6},{3,11},{15,7},{16,24},{28,... | collective-permute-start | bytes 3145736 | tf_op jit(solution)/shard_map/ppermute | solution.py:272
  12.3 66.5 %collective-permute-start.3 = (bf16[2,256,1024]{2,1,0:T(8,128)(2,1)S(1)}, bf16[2,256,1024]{2,1,0:T(8,128)(2,1)S(1)}, u32[]{:S(2)}, u32[]{:S(2)}) collective-permute-start(bf16[2,256,1024]{2,1,0:T(8,128)(2,1)S(1)} %collective-permute-done.listed), channel_id=1, source_target_pairs={{8,12},{4,0},{9,13},{5,1},{10,14},{6,2},{11,15},{7,3},{24,28},{20,... | collective-permute-start | bytes 3145736 | tf_op jit(solution)/shard_map/ppermute | solution.py:272
  34.1 40.5 %collective-permute-start.7 = (bf16[2,256,768]{2,1,0:T(8,128)(2,1)S(1)}, bf16[2,256,768]{2,1,0:T(8,128)(2,1)S(1)}, u32[]{:S(2)}, u32[]{:S(2)}) collective-permute-start(bf16[2,256,768]{2,1,0:T(8,128)(2,1)S(1)} %get-tuple-element.24), channel_id=1, source_target_pairs={{0,12},{12,0},{1,13},{13,1},{2,14},{14,2},{3,15},{15,3},{16,28},{2... | collective-permute-start | bytes 2359304 | tf_op jit(solution)/shard_map/ppermute | solution.py:272
  37.3 23.9 %collective-permute-start.6 = (bf16[2,128,768]{2,1,0:T(8,128)(2,1)S(1)}, bf16[2,128,768]{2,1,0:T(8,128)(2,1)S(1)}, u32[]{:S(2)}, u32[]{:S(2)}) collective-permute-start(bf16[2,128,768]{2,1,0:T(8,128)(2,1)S(1)} %get-tuple-element.23), channel_id=1, source_target_pairs={{4,8},{8,4},{5,9},{9,5},{6,10},{10,6},{7,11},{11,7},{20,24},{24,20... | collective-permute-start | bytes 1179656 | tf_op jit(solution)/shard_map/ppermute | solution.py:272
  38.0 48.6 %collective-permute-start.4 = (bf16[2,256,256]{2,1,0:T(8,128)(2,1)S(1)}, bf16[2,256,256]{2,1,0:T(8,128)(2,1)S(1)}, u32[]{:S(2)}, u32[]{:S(2)}) collective-permute-start(bf16[2,256,256]{2,1,0:T(8,128)(2,1)S(1)} %get-tuple-element.18), channel_id=1, source_target_pairs={{0,12},{12,0},{1,13},{13,1},{2,14},{14,2},{3,15},{15,3},{16,28},{2... | collective-permute-start | bytes 786440 | tf_op jit(solution)/shard_map/ppermute | solution.py:272
  55.7 30.9 %collective-permute-start.2 = (bf16[2,128,256]{2,1,0:T(8,128)(2,1)S(1)}, bf16[2,128,256]{2,1,0:T(8,128)(2,1)S(1)}, u32[]{:S(2)}, u32[]{:S(2)}) collective-permute-start(bf16[2,128,256]{2,1,0:T(8,128)(2,1)S(1)} %get-tuple-element.17), channel_id=1, source_target_pairs={{4,8},{8,4},{5,9},{9,5},{6,10},{10,6},{7,11},{11,7},{20,24},{24,20... | collective-permute-start | bytes 393224 | tf_op jit(solution)/shard_map/ppermute | solution.py:272

commit v13 on v12

--- a/solution.py
+++ b/solution.py
@@ -180,17 +180,19 @@
     )
 
 
-def attend_kernel(chunk, queries, keys, values, beside, crossed, mixed, tops, sums):
+def attend_kernel(
+    chunk, queries, keys, values, beside, listed, crossed, mixed, tops, sums
+):
     frame = lax.axis_index("tm")
     inner = (frame == 1) | (frame == 2)
     rows, columns = queries.shape
     units = [(head, start) for head in range(columns // HD) for start in range(0, rows, chunk)]
 
-    def attend(received):
+    def attend(pieces_of):
         def pieces(head, kv):
             cols = pl.ds(head * HD, HD)
             own = values if kv else keys
-            return [own[:, cols]] + [part[kv, :, cols] for part in received]
+            return [own[:, cols], beside[kv, :, cols]] + pieces_of(kv, cols)
 
         def score(head, start):
             rows_q = queries[pl.ds(start, chunk), pl.ds(head * HD, HD)]
@@ -216,42 +218,62 @@
             finish(*unit, scores)
             scores = ahead
 
-    pl.when(inner)(lambda: attend([beside, crossed]))
-    pl.when(jnp.logical_not(inner))(lambda: attend([beside]))
-
-
-def close_kernel(first, queries, listed, closing, relayed, direct, mixed, tops, sums, *rest):
+    def of_inner(kv, cols):
+        return [crossed[kv, :, cols], listed[kv, pl.ds(BLOCK, BLOCK), cols]]
+
+    pl.when(inner)(lambda: attend(of_inner))
+    pl.when(jnp.logical_not(inner))(lambda: attend(lambda kv, cols: []))
+
+
+def close_kernel(chunk, first, queries, closing, relayed, direct, mixed, tops, sums, *rest):
     out, ready, sems = rest[-3:]
     frame = lax.axis_index("tm")
     inner = (frame == 1) | (frame == 2)
-
-    def close(pieces):
-        copies = []
-        for at in range(ready.shape[0]):
-            head = first // HD + at
-            here, there = pl.ds(first + at * HD, HD), pl.ds(at * HD, HD)
-            scores = [scores_of(queries[:, here], piece) for piece in pieces(0, here, there)]
+    heads, rows, _ = ready.shape
+    units = [(at, start) for at in range(heads) for start in range(0, rows, chunk)]
+
+    def close(pieces_of):
+        def pieces(at, kv):
+            return pieces_of(kv, pl.ds(first + at * HD, HD), pl.ds(at * HD, HD))
+
+        def score(at, start):
+            rows_q = queries[pl.ds(start, chunk), pl.ds(first + at * HD, HD)]
+            return [scores_of(rows_q, piece) for piece in pieces(at, 0)]
+
+        def finish(at, start, scores):
+            head, span = first // HD + at, pl.ds(start, chunk)
+            old_top = tops[head, span]
             top = functools.reduce(
-                jnp.maximum, [jnp.max(part, axis=1, keepdims=True) for part in scores], tops[head]
-            )
-            shrink = jnp.exp2((tops[head] - top) * RATE)
+                jnp.maximum, [jnp.max(part, axis=1, keepdims=True) for part in scores], old_top
+            )
+            shrink = jnp.exp2((old_top - top) * RATE)
             powers = [jnp.exp2((part - top[:, :1]) * RATE) for part in scores]
-            total = sums[head] * shrink + sum(
+            total = sums[head, span] * shrink + sum(
                 jnp.sum(part, axis=1, keepdims=True) for part in powers
             )
             more = sum(
                 jnp.dot(part.astype(jnp.bfloat16), piece, preferred_element_type=jnp.float32)
-                for part, piece in zip(powers, pieces(1, here, there))
-            )
-            ready[at] = ((mixed[head] * shrink + more) / total).astype(jnp.bfloat16)
-            copies.append(pltpu.make_async_copy(ready.at[at], out.at[:, here], sems.at[at]))
-            copies[-1].start()
+                for part, piece in zip(powers, pieces(at, 1))
+            )
+            whole = mixed[head, span] * shrink + more
+            ready[at, span] = (whole / total).astype(jnp.bfloat16)
+
+        copies = []
+        scores = score(*units[0])
+        for unit, following in zip(units, units[1:] + [None]):
+            ahead = score(*following) if following else None
+            finish(*unit, scores)
+            scores = ahead
+            at, start = unit
+            if start + chunk == rows:
+                here = pl.ds(first + at * HD, HD)
+                copies.append(pltpu.make_async_copy(ready.at[at], out.at[:, here], sems.at[at]))
+                copies[-1].start()
         for copy in copies:
             copy.wait()
 
     def of_inner(kv, here, there):
-        facing = [listed[kv, pl.ds(BLOCK, BLOCK), here], closing[kv, :, there]]
-        return [jnp.concatenate(facing, 0)]
+        return [closing[kv, :, there]]
 
     def of_edge(kv, here, there):
         return [relayed[kv, :, here], direct[kv, :, there]]
@@ -325,14 +347,14 @@
     mixed, tops, sums = pl.pallas_call(
         functools.partial(attend_kernel, rows // 2),
         out_shape=[state] * 3,
-        in_specs=[local] * 5,
+        in_specs=[local] * 6,
         out_specs=[local] * 3,
         compiler_params=roomy,
         name="attend",
-    )(queries, keys, values, beside, crossed)
+    )(queries, keys, values, beside, listed, crossed)
     result = None
     for near, far, (start, size) in zip(closing, direct, cuts):
-        operands = [queries, listed, near, relayed, far, mixed, tops, sums]
+        operands = [queries, near, relayed, far, mixed, tops, sums]
         in_specs = [local] * len(operands)
         aliases = {}
         if result is not None:
@@ -340,7 +362,7 @@
             in_specs.append(anywhere)
             operands.append(result)
         result = pl.pallas_call(
-            functools.partial(close_kernel, start),
+            functools.partial(close_kernel, rows // 2, start),
             out_shape=jax.ShapeDtypeStruct(queries.shape, queries.dtype),
             in_specs=in_specs,
             out_specs=anywhere,

time: 91.6 us -> 89.7 us (0.979)
  the two profiles are of different devices: /device:TPU:0 before, /device:TPU:19 now
where the time goes in v13:
time: 89.7 us; the launch traced here: 89.4 us
  waiting for transfers between devices  61.9 us (69%)
  Pallas kernels  16 us (18%)
  starting transfers between devices  10.4 us (12%)
    ppermute x8, waiting for transfers between devices, send(): return lax.ppermute(array, 'tm', pairs)  61.9 us
    ppermute x8, starting transfers between devices, send(): return lax.ppermute(array, 'tm', pairs)  10.4 us
    pallas_call x1, Pallas kernels, four_frames(): pl.pallas_call(functools.partial(attend_kernel, rows // 2), out_shape=[st...  7.75 us
    pallas_call x2, Pallas kernels, four_frames(): pl.pallas_call(functools.partial(close_kernel, rows // 2, start), out_sha...  4.62 us
    pallas_call x3, Pallas kernels, stage(): pl.pallas_call(kernel, out_shape=shapes, in_specs=[scalars if operand is...  3.6 us
  transfers between devices with their start and end apart: 8, of which 3 were waited for; matrix products, arithmetic and copies ran while one was open for 0% of the time, Pallas kernels for 14%

profile of v13, /device:TPU:19, one launch (start us, length us, event | category | flops | bytes accessed | tf_op | source)
XLA Modules:
  0.0 89.4 jit_solution(13971182673153414844)
XLA Ops:
  0.0 0.0 copy-start
  0.0 0.0 copy-start.1
  0.0 0.0 copy-start.3
  0.0 0.8 copy-done.3
  0.8 2.2 %stage_near.1 = (bf16[2,256,1024]{2,1,0:T(8,128)(2,1)S(1)}, bf16[2,256,1024]{2,1,0:T(8,128)(2,1)S(1)}, s32[8,128]{1,0:T(8,128)S(1)}) custom-call(s32[4,2,4]{2,1,0:T(2,128)S(1)} %bitcast.1, bf16[512,1024]{1,0:T(8,128)(2,1)} %keys.7, bf16[512,1024]{1,0:T(8,128)(2,1)} %values.7), custom_call_target="tpu_custom_call" | custom-call | tf_op jit(solution)/shard_map/stage_near/pallas_call | solution.py:300
  3.0 2.1 %collective-permute-start.2 = (bf16[2,256,1024]{2,1,0:T(8,128)(2,1)S(1)}, bf16[2,256,1024]{2,1,0:T(8,128)(2,1)S(1)}, u32[]{:S(2)}, u32[]{:S(2)}) collective-permute-start(bf16[2,256,1024]{2,1,0:T(8,128)(2,1)S(1)} %get-tuple-element.17), channel_id=1, source_target_pairs={{4,8},{8,4},{5,9},{9,5},{6,10},{10,6},{7,11},{11,7},{20,24},{24,20... | collective-permute-start | bytes 3145736 | tf_op jit(solution)/shard_map/ppermute | solution.py:294
  5.1 0.1 collective-permute-start
  5.2 0.0 copy-done
  5.2 0.0 copy-done.1
  5.2 0.7 stage_crossed.1
  5.9 0.0 copy-start.2
  5.9 1.4 %collective-permute-start.5 = (bf16[2,256,1024]{2,1,0:T(8,128)(2,1)S(1)}, bf16[2,256,1024]{2,1,0:T(8,128)(2,1)S(1)}, u32[]{:S(2)}, u32[]{:S(2)}) collective-permute-start(bf16[2,256,1024]{2,1,0:T(8,128)(2,1)S(1)} %stage_crossed.1), channel_id=1, source_target_pairs={{0,8},{12,4},{1,9},{13,5},{2,10},{14,6},{3,11},{15,7},{16,24},{28,... | collective-permute-start | bytes 3145736 | tf_op jit(solution)/shard_map/ppermute | solution.py:294
  7.3 21.6 %collective-permute-done.2.listed = bf16[2,256,1024]{2,1,0:T(8,128)(2,1)S(1)} collective-permute-done((bf16[2,256,1024]{2,1,0:T(8,128)(2,1)S(1)}, bf16[2,256,1024]{2,1,0:T(8,128)(2,1)S(1)}, u32[]{:S(2)}, u32[]{:S(2)}) %collective-permute-start.2) | collective-permute-done | bytes 1048608 | tf_op jit(solution)/shard_map/ppermute | solution.py:294
  28.9 1.3 %collective-permute-start.3 = (bf16[2,256,1024]{2,1,0:T(8,128)(2,1)S(1)}, bf16[2,256,1024]{2,1,0:T(8,128)(2,1)S(1)}, u32[]{:S(2)}, u32[]{:S(2)}) collective-permute-start(bf16[2,256,1024]{2,1,0:T(8,128)(2,1)S(1)} %collective-permute-done.2.listed), channel_id=1, source_target_pairs={{8,12},{4,0},{9,13},{5,1},{10,14},{6,2},{11,15},{7,3},{24,28},{20,... | collective-permute-start | bytes 3145736 | tf_op jit(solution)/shard_map/ppermute | solution.py:294
  30.3 0.0 collective-permute-done.after.beside
  30.3 0.8 stage_last.1
  31.1 0.7 collective-permute-start.7
  31.8 2.1 %collective-permute-start.6 = (bf16[2,128,768]{2,1,0:T(8,128)(2,1)S(1)}, bf16[2,128,768]{2,1,0:T(8,128)(2,1)S(1)}, u32[]{:S(2)}, u32[]{:S(2)}) collective-permute-start(bf16[2,128,768]{2,1,0:T(8,128)(2,1)S(1)} %get-tuple-element.23), channel_id=1, source_target_pairs={{4,8},{8,4},{5,9},{9,5},{6,10},{10,6},{7,11},{11,7},{20,24},{24,20... | collective-permute-start | bytes 1179656 | tf_op jit(solution)/shard_map/ppermute | solution.py:294
  33.9 0.7 collective-permute-start.4
  34.6 17.8 %collective-permute-done.5.crossed = bf16[2,256,1024]{2,1,0:T(8,128)(2,1)S(1)} collective-permute-done((bf16[2,256,1024]{2,1,0:T(8,128)(2,1)S(1)}, bf16[2,256,1024]{2,1,0:T(8,128)(2,1)S(1)}, u32[]{:S(2)}, u32[]{:S(2)}) %collective-permute-start.5) | collective-permute-done | bytes 1048608 | tf_op jit(solution)/shard_map/ppermute | solution.py:294
  52.4 2.1 %collective-permute-start.1 = (bf16[2,128,256]{2,1,0:T(8,128)(2,1)S(1)}, bf16[2,128,256]{2,1,0:T(8,128)(2,1)S(1)}, u32[]{:S(2)}, u32[]{:S(2)}) collective-permute-start(bf16[2,128,256]{2,1,0:T(8,128)(2,1)S(1)} %get-tuple-element.16), channel_id=1, source_target_pairs={{4,8},{8,4},{5,9},{9,5},{6,10},{10,6},{7,11},{11,7},{20,24},{24,20... | collective-permute-start | bytes 393224 | tf_op jit(solution)/shard_map/ppermute | solution.py:294
  54.5 0.0 copy-done.2
  54.5 7.7 %attend.1 = (f32[8,512,128]{2,1,0:T(8,128)S(1)}, f32[8,512,128]{2,1,0:T(8,128)S(1)}, f32[8,512,128]{2,1,0:T(8,128)S(1)}) custom-call(bf16[512,1024]{1,0:T(8,128)(2,1)S(1)} %copy-done.2, bf16[512,1024]{1,0:T(8,128)(2,1)S(1)} %copy-done, bf16[512,1024]{1,0:T(8,128)(2,1)S(1)} %copy-done.1, bf16[2,256,1024]{2,1,0:T(8,128)(2,1)S(1)} %collective-permute-done.after.beside, ...), custom_call_target="tpu_custom_call" | custom-call | tf_op jit(solution)/shard_map/attend/pallas_call | solution.py:347
  62.2 22.4 %collective-permute-done.6.closing = bf16[2,128,768]{2,1,0:T(8,128)(2,1)S(1)} collective-permute-done((bf16[2,128,768]{2,1,0:T(8,128)(2,1)S(1)}, bf16[2,128,768]{2,1,0:T(8,128)(2,1)S(1)}, u32[]{:S(2)}, u32[]{:S(2)}) %collective-permute-start.6) | collective-permute-done | bytes 393248 | tf_op jit(solution)/shard_map/ppermute | solution.py:294
  84.6 0.0 collective-permute-done.7.direct
  84.6 0.0 collective-permute-done.3.relayed
  84.6 3.0 %close.2.rest_0_ = bf16[512,1024]{1,0:T(8,128)(2,1)} custom-call(bf16[512,1024]{1,0:T(8,128)(2,1)S(1)} %copy-done.2, bf16[2,128,768]{2,1,0:T(8,128)(2,1)S(1)} %collective-permute-done.6.closing, bf16[2,256,1024]{2,1,0:T(8,128)(2,1)S(1)} %collective-permute-done.3.relayed, bf16[2,256,768]{2,1,0:T(8,128)(2,1)S(1)} %collective-permute-done.7.direct, ...), custom_call_target="tpu_custom_call" | custom-call | tf_op jit(solution)/shard_map/close/pallas_call | solution.py:364
  87.6 0.0 collective-permute-done.1.closing
  87.6 0.0 collective-permute-done.4.direct
  87.7 1.6 %close.3 = bf16[512,1024]{1,0:T(8,128)(2,1)} custom-call(bf16[512,1024]{1,0:T(8,128)(2,1)S(1)} %copy-done.2, bf16[2,128,256]{2,1,0:T(8,128)(2,1)S(1)} %collective-permute-done.1.closing, bf16[2,256,1024]{2,1,0:T(8,128)(2,1)S(1)} %collective-permute-done.3.relayed, ...), custom_call_target="tpu_custom_call", output_to_operand_aliasing={{}: (7, {})} | custom-call | tf_op jit(solution)/shard_map/close/pallas_call | solution.py:364
Async XLA Ops:
  0.0 5.2 %copy-start = (bf16[512,1024]{1,0:T(8,128)(2,1)S(1)}, bf16[512,1024]{1,0:T(8,128)(2,1)}, u32[]{:S(2)}) copy-start(bf16[512,1024]{1,0:T(8,128)(2,1)} %keys.7) | copy-start | bytes 3145732
  0.0 5.2 %copy-start.1 = (bf16[512,1024]{1,0:T(8,128)(2,1)S(1)}, bf16[512,1024]{1,0:T(8,128)(2,1)}, u32[]{:S(2)}) copy-start(bf16[512,1024]{1,0:T(8,128)(2,1)} %values.7) | copy-start | bytes 3145732
  0.0 0.8 copy-start.3
  3.0 25.9 %collective-permute-start.2 = (bf16[2,256,1024]{2,1,0:T(8,128)(2,1)S(1)}, bf16[2,256,1024]{2,1,0:T(8,128)(2,1)S(1)}, u32[]{:S(2)}, u32[]{:S(2)}) collective-permute-start(bf16[2,256,1024]{2,1,0:T(8,128)(2,1)S(1)} %get-tuple-element.17), channel_id=1, source_target_pairs={{4,8},{8,4},{5,9},{9,5},{6,10},{10,6},{7,11},{11,7},{20,24},{24,20... | collective-permute-start | bytes 3145736 | tf_op jit(solution)/shard_map/ppermute | solution.py:294
  5.1 25.2 %collective-permute-start = (bf16[2,256,1024]{2,1,0:T(8,128)(2,1)S(1)}, bf16[2,256,1024]{2,1,0:T(8,128)(2,1)S(1)}, u32[]{:S(2)}, u32[]{:S(2)}) collective-permute-start(bf16[2,256,1024]{2,1,0:T(8,128)(2,1)S(1)} %get-tuple-element.15), channel_id=1, source_target_pairs={{0,4},{4,0},{8,12},{12,8},{1,5},{5,1},{9,13},{13,9},{2,6},{6,2},{1... | collective-permute-start | bytes 3145736 | tf_op jit(solution)/shard_map/ppermute | solution.py:294
  5.9 48.6 %copy-start.2 = (bf16[512,1024]{1,0:T(8,128)(2,1)S(1)}, bf16[512,1024]{1,0:T(8,128)(2,1)}, u32[]{:S(2)}) copy-start(bf16[512,1024]{1,0:T(8,128)(2,1)} %queries.5) | copy-start | bytes 3145732
  5.9 46.5 %collective-permute-start.5 = (bf16[2,256,1024]{2,1,0:T(8,128)(2,1)S(1)}, bf16[2,256,1024]{2,1,0:T(8,128)(2,1)S(1)}, u32[]{:S(2)}, u32[]{:S(2)}) collective-permute-start(bf16[2,256,1024]{2,1,0:T(8,128)(2,1)S(1)} %stage_crossed.1), channel_id=1, source_target_pairs={{0,8},{12,4},{1,9},{13,5},{2,10},{14,6},{3,11},{15,7},{16,24},{28,... | collective-permute-start | bytes 3145736 | tf_op jit(solution)/shard_map/ppermute | solution.py:294
  28.9 55.7 %collective-permute-start.3 = (bf16[2,256,1024]{2,1,0:T(8,128)(2,1)S(1)}, bf16[2,256,1024]{2,1,0:T(8,128)(2,1)S(1)}, u32[]{:S(2)}, u32[]{:S(2)}) collective-permute-start(bf16[2,256,1024]{2,1,0:T(8,128)(2,1)S(1)} %collective-permute-done.2.listed), channel_id=1, source_target_pairs={{8,12},{4,0},{9,13},{5,1},{10,14},{6,2},{11,15},{7,3},{24,28},{20,... | collective-permute-start | bytes 3145736 | tf_op jit(solution)/shard_map/ppermute | solution.py:294
  31.1 53.5 %collective-permute-start.7 = (bf16[2,256,768]{2,1,0:T(8,128)(2,1)S(1)}, bf16[2,256,768]{2,1,0:T(8,128)(2,1)S(1)}, u32[]{:S(2)}, u32[]{:S(2)}) collective-permute-start(bf16[2,256,768]{2,1,0:T(8,128)(2,1)S(1)} %get-tuple-element.24), channel_id=1, source_target_pairs={{0,12},{12,0},{1,13},{13,1},{2,14},{14,2},{3,15},{15,3},{16,28},{2... | collective-permute-start | bytes 2359304 | tf_op jit(solution)/shard_map/ppermute | solution.py:294
  31.8 52.8 %collective-permute-start.6 = (bf16[2,128,768]{2,1,0:T(8,128)(2,1)S(1)}, bf16[2,128,768]{2,1,0:T(8,128)(2,1)S(1)}, u32[]{:S(2)}, u32[]{:S(2)}) collective-permute-start(bf16[2,128,768]{2,1,0:T(8,128)(2,1)S(1)} %get-tuple-element.23), channel_id=1, source_target_pairs={{4,8},{8,4},{5,9},{9,5},{6,10},{10,6},{7,11},{11,7},{20,24},{24,20... | collective-permute-start | bytes 1179656 | tf_op jit(solution)/shard_map/ppermute | solution.py:294
  33.9 53.8 %collective-permute-start.4 = (bf16[2,256,256]{2,1,0:T(8,128)(2,1)S(1)}, bf16[2,256,256]{2,1,0:T(8,128)(2,1)S(1)}, u32[]{:S(2)}, u32[]{:S(2)}) collective-permute-start(bf16[2,256,256]{2,1,0:T(8,128)(2,1)S(1)} %get-tuple-element.18), channel_id=1, source_target_pairs={{0,12},{12,0},{1,13},{13,1},{2,14},{14,2},{3,15},{15,3},{16,28},{2... | collective-permute-start | bytes 786440 | tf_op jit(solution)/shard_map/ppermute | solution.py:294
  52.4 35.2 %collective-permute-start.1 = (bf16[2,128,256]{2,1,0:T(8,128)(2,1)S(1)}, bf16[2,128,256]{2,1,0:T(8,128)(2,1)S(1)}, u32[]{:S(2)}, u32[]{:S(2)}) collective-permute-start(bf16[2,128,256]{2,1,0:T(8,128)(2,1)S(1)} %get-tuple-element.16), channel_id=1, source_target_pairs={{4,8},{8,4},{5,9},{9,5},{6,10},{10,6},{7,11},{11,7},{20,24},{24,20... | collective-permute-start | bytes 393224 | tf_op jit(solution)/shard_map/ppermute | solution.py:294

commit v14 on v13

--- a/solution.py
+++ b/solution.py
@@ -225,14 +225,15 @@
     pl.when(jnp.logical_not(inner))(lambda: attend(lambda kv, cols: []))
 
 
-def close_kernel(chunk, first, queries, closing, relayed, direct, mixed, tops, sums, *rest):
+def close_kernel(first, queries, closing, relayed, direct, mixed, tops, sums, *rest):
     out, ready, sems = rest[-3:]
     frame = lax.axis_index("tm")
     inner = (frame == 1) | (frame == 2)
     heads, rows, _ = ready.shape
-    units = [(at, start) for at in range(heads) for start in range(0, rows, chunk)]
-
-    def close(pieces_of):
+
+    def close(pieces_of, chunk):
+        units = [(at, start) for at in range(heads) for start in range(0, rows, chunk)]
+
         def pieces(at, kv):
             return pieces_of(kv, pl.ds(first + at * HD, HD), pl.ds(at * HD, HD))
 
@@ -278,8 +279,8 @@
     def of_edge(kv, here, there):
         return [relayed[kv, :, here], direct[kv, :, there]]
 
-    pl.when(inner)(lambda: close(of_inner))
-    pl.when(jnp.logical_not(inner))(lambda: close(of_edge))
+    pl.when(inner)(lambda: close(of_inner, rows))
+    pl.when(jnp.logical_not(inner))(lambda: close(of_edge, rows // 2))
 
 
 def four_frames(queries, keys, values, band_blocks):
@@ -362,7 +363,7 @@
             in_specs.append(anywhere)
             operands.append(result)
         result = pl.pallas_call(
-            functools.partial(close_kernel, rows // 2, start),
+            functools.partial(close_kernel, start),
             out_shape=jax.ShapeDtypeStruct(queries.shape, queries.dtype),
             in_specs=in_specs,
             out_specs=anywhere,

time: 89.7 us -> 89.3 us (level)
  the two profiles are of different devices: /device:TPU:19 before, /device:TPU:17 now
where the time goes in v14:
time: 89.3 us; the launch traced here: 89.1 us
  waiting for transfers between devices  62.2 us (70%)
  Pallas kernels  15.2 us (17%)
  starting transfers between devices  10.4 us (12%)
    ppermute x8, waiting for transfers between devices, send(): return lax.ppermute(array, 'tm', pairs)  62.2 us
    ppermute x8, starting transfers between devices, send(): return lax.ppermute(array, 'tm', pairs)  10.4 us
    pallas_call x1, Pallas kernels, four_frames(): pl.pallas_call(functools.partial(attend_kernel, rows // 2), out_shape=[st...  7.74 us
    pallas_call x2, Pallas kernels, four_frames(): pl.pallas_call(functools.partial(close_kernel, start), out_shape=jax.Shap...  3.9 us
    pallas_call x3, Pallas kernels, stage(): pl.pallas_call(kernel, out_shape=shapes, in_specs=[scalars if operand is...  3.6 us
  transfers between devices with their start and end apart: 8, of which 4 were waited for; matrix products, arithmetic and copies ran while one was open for 0% of the time, Pallas kernels for 13%

profile of v14, /device:TPU:17, one launch (start us, length us, event | category | flops | bytes accessed | tf_op | source)
XLA Modules:
  0.0 89.1 jit_solution(14361906328943422305)
XLA Ops:
  0.0 0.0 copy-start
  0.0 0.0 copy-start.1
  0.0 0.0 copy-start.3
  0.0 0.8 copy-done.3
  0.8 2.2 %stage_near.1 = (bf16[2,256,1024]{2,1,0:T(8,128)(2,1)S(1)}, bf16[2,256,1024]{2,1,0:T(8,128)(2,1)S(1)}, s32[8,128]{1,0:T(8,128)S(1)}) custom-call(s32[4,2,4]{2,1,0:T(2,128)S(1)} %bitcast.1, bf16[512,1024]{1,0:T(8,128)(2,1)} %keys.7, bf16[512,1024]{1,0:T(8,128)(2,1)} %values.7), custom_call_target="tpu_custom_call" | custom-call | tf_op jit(solution)/shard_map/stage_near/pallas_call | solution.py:301
  3.0 2.1 %collective-permute-start.2 = (bf16[2,256,1024]{2,1,0:T(8,128)(2,1)S(1)}, bf16[2,256,1024]{2,1,0:T(8,128)(2,1)S(1)}, u32[]{:S(2)}, u32[]{:S(2)}) collective-permute-start(bf16[2,256,1024]{2,1,0:T(8,128)(2,1)S(1)} %get-tuple-element.17), channel_id=1, source_target_pairs={{4,8},{8,4},{5,9},{9,5},{6,10},{10,6},{7,11},{11,7},{20,24},{24,20... | collective-permute-start | bytes 3145736 | tf_op jit(solution)/shard_map/ppermute | solution.py:295
  5.1 0.1 collective-permute-start
  5.2 0.0 copy-done
  5.2 0.0 copy-done.1
  5.2 0.7 stage_crossed.1
  5.9 0.0 copy-start.2
  5.9 1.4 %collective-permute-start.5 = (bf16[2,256,1024]{2,1,0:T(8,128)(2,1)S(1)}, bf16[2,256,1024]{2,1,0:T(8,128)(2,1)S(1)}, u32[]{:S(2)}, u32[]{:S(2)}) collective-permute-start(bf16[2,256,1024]{2,1,0:T(8,128)(2,1)S(1)} %stage_crossed.1), channel_id=1, source_target_pairs={{0,8},{12,4},{1,9},{13,5},{2,10},{14,6},{3,11},{15,7},{16,24},{28,... | collective-permute-start | bytes 3145736 | tf_op jit(solution)/shard_map/ppermute | solution.py:295
  7.3 21.6 %collective-permute-done.2.listed = bf16[2,256,1024]{2,1,0:T(8,128)(2,1)S(1)} collective-permute-done((bf16[2,256,1024]{2,1,0:T(8,128)(2,1)S(1)}, bf16[2,256,1024]{2,1,0:T(8,128)(2,1)S(1)}, u32[]{:S(2)}, u32[]{:S(2)}) %collective-permute-start.2) | collective-permute-done | bytes 1048608 | tf_op jit(solution)/shard_map/ppermute | solution.py:295
  28.9 1.3 %collective-permute-start.3 = (bf16[2,256,1024]{2,1,0:T(8,128)(2,1)S(1)}, bf16[2,256,1024]{2,1,0:T(8,128)(2,1)S(1)}, u32[]{:S(2)}, u32[]{:S(2)}) collective-permute-start(bf16[2,256,1024]{2,1,0:T(8,128)(2,1)S(1)} %collective-permute-done.2.listed), channel_id=1, source_target_pairs={{8,12},{4,0},{9,13},{5,1},{10,14},{6,2},{11,15},{7,3},{24,28},{20,... | collective-permute-start | bytes 3145736 | tf_op jit(solution)/shard_map/ppermute | solution.py:295
  30.3 0.0 collective-permute-done.after.beside
  30.3 0.8 stage_last.1
  31.1 0.7 collective-permute-start.7
  31.8 2.1 %collective-permute-start.6 = (bf16[2,128,768]{2,1,0:T(8,128)(2,1)S(1)}, bf16[2,128,768]{2,1,0:T(8,128)(2,1)S(1)}, u32[]{:S(2)}, u32[]{:S(2)}) collective-permute-start(bf16[2,128,768]{2,1,0:T(8,128)(2,1)S(1)} %get-tuple-element.23), channel_id=1, source_target_pairs={{4,8},{8,4},{5,9},{9,5},{6,10},{10,6},{7,11},{11,7},{20,24},{24,20... | collective-permute-start | bytes 1179656 | tf_op jit(solution)/shard_map/ppermute | solution.py:295
  33.9 0.7 collective-permute-start.4
  34.6 17.8 %collective-permute-done.5.crossed = bf16[2,256,1024]{2,1,0:T(8,128)(2,1)S(1)} collective-permute-done((bf16[2,256,1024]{2,1,0:T(8,128)(2,1)S(1)}, bf16[2,256,1024]{2,1,0:T(8,128)(2,1)S(1)}, u32[]{:S(2)}, u32[]{:S(2)}) %collective-permute-start.5) | collective-permute-done | bytes 1048608 | tf_op jit(solution)/shard_map/ppermute | solution.py:295
  52.4 2.1 %collective-permute-start.1 = (bf16[2,128,256]{2,1,0:T(8,128)(2,1)S(1)}, bf16[2,128,256]{2,1,0:T(8,128)(2,1)S(1)}, u32[]{:S(2)}, u32[]{:S(2)}) collective-permute-start(bf16[2,128,256]{2,1,0:T(8,128)(2,1)S(1)} %get-tuple-element.16), channel_id=1, source_target_pairs={{4,8},{8,4},{5,9},{9,5},{6,10},{10,6},{7,11},{11,7},{20,24},{24,20... | collective-permute-start | bytes 393224 | tf_op jit(solution)/shard_map/ppermute | solution.py:295
  54.5 0.0 copy-done.2
  54.5 7.7 %attend.1 = (f32[8,512,128]{2,1,0:T(8,128)S(1)}, f32[8,512,128]{2,1,0:T(8,128)S(1)}, f32[8,512,128]{2,1,0:T(8,128)S(1)}) custom-call(bf16[512,1024]{1,0:T(8,128)(2,1)S(1)} %copy-done.2, bf16[512,1024]{1,0:T(8,128)(2,1)S(1)} %copy-done, bf16[512,1024]{1,0:T(8,128)(2,1)S(1)} %copy-done.1, bf16[2,256,1024]{2,1,0:T(8,128)(2,1)S(1)} %collective-permute-done.after.beside, ...), custom_call_target="tpu_custom_call" | custom-call | tf_op jit(solution)/shard_map/attend/pallas_call | solution.py:348
  62.2 22.4 %collective-permute-done.6.closing = bf16[2,128,768]{2,1,0:T(8,128)(2,1)S(1)} collective-permute-done((bf16[2,128,768]{2,1,0:T(8,128)(2,1)S(1)}, bf16[2,128,768]{2,1,0:T(8,128)(2,1)S(1)}, u32[]{:S(2)}, u32[]{:S(2)}) %collective-permute-start.6) | collective-permute-done | bytes 393248 | tf_op jit(solution)/shard_map/ppermute | solution.py:295
  84.6 0.0 collective-permute-done.7.direct
  84.6 0.0 collective-permute-done.3.relayed
  84.6 2.5 %close.2.rest_0_ = bf16[512,1024]{1,0:T(8,128)(2,1)} custom-call(bf16[512,1024]{1,0:T(8,128)(2,1)S(1)} %copy-done.2, bf16[2,128,768]{2,1,0:T(8,128)(2,1)S(1)} %collective-permute-done.6.closing, bf16[2,256,1024]{2,1,0:T(8,128)(2,1)S(1)} %collective-permute-done.3.relayed, bf16[2,256,768]{2,1,0:T(8,128)(2,1)S(1)} %collective-permute-done.7.direct, ...), custom_call_target="tpu_custom_call" | custom-call | tf_op jit(solution)/shard_map/close/pallas_call | solution.py:365
  87.1 0.3 collective-permute-done.1.closing
  87.4 0.0 collective-permute-done.4.direct
  87.4 1.4 %close.3 = bf16[512,1024]{1,0:T(8,128)(2,1)} custom-call(bf16[512,1024]{1,0:T(8,128)(2,1)S(1)} %copy-done.2, bf16[2,128,256]{2,1,0:T(8,128)(2,1)S(1)} %collective-permute-done.1.closing, bf16[2,256,1024]{2,1,0:T(8,128)(2,1)S(1)} %collective-permute-done.3.relayed, ...), custom_call_target="tpu_custom_call", output_to_operand_aliasing={{}: (7, {})} | custom-call | tf_op jit(solution)/shard_map/close/pallas_call | solution.py:365
Async XLA Ops:
  0.0 5.2 %copy-start = (bf16[512,1024]{1,0:T(8,128)(2,1)S(1)}, bf16[512,1024]{1,0:T(8,128)(2,1)}, u32[]{:S(2)}) copy-start(bf16[512,1024]{1,0:T(8,128)(2,1)} %keys.7) | copy-start | bytes 3145732
  0.0 5.2 %copy-start.1 = (bf16[512,1024]{1,0:T(8,128)(2,1)S(1)}, bf16[512,1024]{1,0:T(8,128)(2,1)}, u32[]{:S(2)}) copy-start(bf16[512,1024]{1,0:T(8,128)(2,1)} %values.7) | copy-start | bytes 3145732
  0.0 0.8 copy-start.3
  3.0 25.9 %collective-permute-start.2 = (bf16[2,256,1024]{2,1,0:T(8,128)(2,1)S(1)}, bf16[2,256,1024]{2,1,0:T(8,128)(2,1)S(1)}, u32[]{:S(2)}, u32[]{:S(2)}) collective-permute-start(bf16[2,256,1024]{2,1,0:T(8,128)(2,1)S(1)} %get-tuple-element.17), channel_id=1, source_target_pairs={{4,8},{8,4},{5,9},{9,5},{6,10},{10,6},{7,11},{11,7},{20,24},{24,20... | collective-permute-start | bytes 3145736 | tf_op jit(solution)/shard_map/ppermute | solution.py:295
  5.1 25.2 %collective-permute-start = (bf16[2,256,1024]{2,1,0:T(8,128)(2,1)S(1)}, bf16[2,256,1024]{2,1,0:T(8,128)(2,1)S(1)}, u32[]{:S(2)}, u32[]{:S(2)}) collective-permute-start(bf16[2,256,1024]{2,1,0:T(8,128)(2,1)S(1)} %get-tuple-element.15), channel_id=1, source_target_pairs={{0,4},{4,0},{8,12},{12,8},{1,5},{5,1},{9,13},{13,9},{2,6},{6,2},{1... | collective-permute-start | bytes 3145736 | tf_op jit(solution)/shard_map/ppermute | solution.py:295
  5.9 48.6 %copy-start.2 = (bf16[512,1024]{1,0:T(8,128)(2,1)S(1)}, bf16[512,1024]{1,0:T(8,128)(2,1)}, u32[]{:S(2)}) copy-start(bf16[512,1024]{1,0:T(8,128)(2,1)} %queries.5) | copy-start | bytes 3145732
  5.9 46.5 %collective-permute-start.5 = (bf16[2,256,1024]{2,1,0:T(8,128)(2,1)S(1)}, bf16[2,256,1024]{2,1,0:T(8,128)(2,1)S(1)}, u32[]{:S(2)}, u32[]{:S(2)}) collective-permute-start(bf16[2,256,1024]{2,1,0:T(8,128)(2,1)S(1)} %stage_crossed.1), channel_id=1, source_target_pairs={{0,8},{12,4},{1,9},{13,5},{2,10},{14,6},{3,11},{15,7},{16,24},{28,... | collective-permute-start | bytes 3145736 | tf_op jit(solution)/shard_map/ppermute | solution.py:295
  28.9 55.7 %collective-permute-start.3 = (bf16[2,256,1024]{2,1,0:T(8,128)(2,1)S(1)}, bf16[2,256,1024]{2,1,0:T(8,128)(2,1)S(1)}, u32[]{:S(2)}, u32[]{:S(2)}) collective-permute-start(bf16[2,256,1024]{2,1,0:T(8,128)(2,1)S(1)} %collective-permute-done.2.listed), channel_id=1, source_target_pairs={{8,12},{4,0},{9,13},{5,1},{10,14},{6,2},{11,15},{7,3},{24,28},{20,... | collective-permute-start | bytes 3145736 | tf_op jit(solution)/shard_map/ppermute | solution.py:295
  31.1 53.5 %collective-permute-start.7 = (bf16[2,256,768]{2,1,0:T(8,128)(2,1)S(1)}, bf16[2,256,768]{2,1,0:T(8,128)(2,1)S(1)}, u32[]{:S(2)}, u32[]{:S(2)}) collective-permute-start(bf16[2,256,768]{2,1,0:T(8,128)(2,1)S(1)} %get-tuple-element.24), channel_id=1, source_target_pairs={{0,12},{12,0},{1,13},{13,1},{2,14},{14,2},{3,15},{15,3},{16,28},{2... | collective-permute-start | bytes 2359304 | tf_op jit(solution)/shard_map/ppermute | solution.py:295
  31.8 52.8 %collective-permute-start.6 = (bf16[2,128,768]{2,1,0:T(8,128)(2,1)S(1)}, bf16[2,128,768]{2,1,0:T(8,128)(2,1)S(1)}, u32[]{:S(2)}, u32[]{:S(2)}) collective-permute-start(bf16[2,128,768]{2,1,0:T(8,128)(2,1)S(1)} %get-tuple-element.23), channel_id=1, source_target_pairs={{4,8},{8,4},{5,9},{9,5},{6,10},{10,6},{7,11},{11,7},{20,24},{24,20... | collective-permute-start | bytes 1179656 | tf_op jit(solution)/shard_map/ppermute | solution.py:295
  33.9 53.6 %collective-permute-start.4 = (bf16[2,256,256]{2,1,0:T(8,128)(2,1)S(1)}, bf16[2,256,256]{2,1,0:T(8,128)(2,1)S(1)}, u32[]{:S(2)}, u32[]{:S(2)}) collective-permute-start(bf16[2,256,256]{2,1,0:T(8,128)(2,1)S(1)} %get-tuple-element.18), channel_id=1, source_target_pairs={{0,12},{12,0},{1,13},{13,1},{2,14},{14,2},{3,15},{15,3},{16,28},{2... | collective-permute-start | bytes 786440 | tf_op jit(solution)/shard_map/ppermute | solution.py:295
  52.4 35.0 %collective-permute-start.1 = (bf16[2,128,256]{2,1,0:T(8,128)(2,1)S(1)}, bf16[2,128,256]{2,1,0:T(8,128)(2,1)S(1)}, u32[]{:S(2)}, u32[]{:S(2)}) collective-permute-start(bf16[2,128,256]{2,1,0:T(8,128)(2,1)S(1)} %get-tuple-element.16), channel_id=1, source_target_pairs={{4,8},{8,4},{5,9},{9,5},{6,10},{10,6},{7,11},{11,7},{20,24},{24,20... | collective-permute-start | bytes 393224 | tf_op jit(solution)/shard_map/ppermute | solution.py:295

commit v15 on v14

--- a/solution.py
+++ b/solution.py
@@ -133,21 +133,41 @@
 
     @pl.when((frame == 0) | (frame == 3))
     def _():
-        reader = jnp.where(frame == 0, 2, 1)
-        pairs = []
-        for slot in range(2):
-            rows = rows_of(bands[reader, slot, frame])
-            for kv, source in enumerate((keys, values)):
-                pairs.append((source.at[rows], crossed.at[kv, pl.ds(slot * BLOCK, BLOCK)]))
-        run_copies(pairs, sems)
-
-
-def stage_last_kernel(cuts, after, bands, keys, values, *rest):
-    direct, closing, sems = rest[: len(cuts)], rest[len(cuts) : -1], rest[-1]
+        block = jnp.where(frame == 0, bands[2, 0, 0], bands[1, 1, 3])
+        rows = rows_of(block)
+        run_copies([(keys.at[rows], crossed.at[0]), (values.at[rows], crossed.at[1])], sems)
+
+
+def relay_kernel(cuts, listed, *relayed):
+    frame = lax.axis_index("tm")
+
+    @pl.when((frame == 1) | (frame == 2))
+    def _():
+        for part, cut in zip(relayed, cuts):
+            part[...] = listed[:, :, pl.ds(*cut)]
+
+
+def stage_second_kernel(beside, bands, keys, values, traded, passed, sems):
     frame = lax.axis_index("tm")
     inner = (frame == 1) | (frame == 2)
 
     @pl.when(inner)
+    def _():
+        to_inner = rows_of(jnp.where(frame == 1, bands[2, 1, 0] - 2, bands[1, 0, 3]))
+        to_edge = rows_of(jnp.where(frame == 1, bands[3, 1, 0] - 2, bands[0, 0, 3]))
+        run_copies([(beside.at[:, to_inner], traded), (beside.at[:, to_edge], passed)], sems)
+
+    @pl.when(jnp.logical_not(inner))
+    def _():
+        rows = rows_of(jnp.where(frame == 0, bands[3, 0, 0], bands[0, 1, 3]))
+        run_copies([(keys.at[rows], traded.at[0]), (values.at[rows], traded.at[1])], sems)
+
+
+def stage_closing_kernel(cuts, after, bands, keys, values, *rest):
+    closing, sems = rest[:-1], rest[-1]
+    frame = lax.axis_index("tm")
+
+    @pl.when((frame == 1) | (frame == 2))
     def _():
         rows = rows_of(jnp.where(frame == 1, 5 - bands[3, 1, 1], 1 - bands[0, 0, 2]))
         run_copies(
@@ -159,17 +179,6 @@
             sems,
         )
 
-    @pl.when(jnp.logical_not(inner))
-    def _():
-        pairs = []
-        for slot in range(2):
-            rows = rows_of(bands[3 - frame, slot, frame])
-            to = pl.ds(slot * BLOCK, BLOCK)
-            for part, cut in zip(direct, cuts):
-                for kv, source in enumerate((keys, values)):
-                    pairs.append((source.at[rows, pl.ds(*cut)], part.at[kv, to]))
-        run_copies(pairs, sems)
-
 
 RATE = LOG2E * HD ** (-0.5)
 
@@ -181,7 +190,7 @@
 
 
 def attend_kernel(
-    chunk, queries, keys, values, beside, listed, crossed, mixed, tops, sums
+    chunk, queries, keys, values, beside, listed, crossed, traded, mixed, tops, sums
 ):
     frame = lax.axis_index("tm")
     inner = (frame == 1) | (frame == 2)
@@ -219,13 +228,17 @@
             scores = ahead
 
     def of_inner(kv, cols):
-        return [crossed[kv, :, cols], listed[kv, pl.ds(BLOCK, BLOCK), cols]]
+        listed_there = jnp.concatenate([crossed[kv, :, cols], traded[kv, :, cols]], 0)
+        return [listed_there, listed[kv, pl.ds(BLOCK, BLOCK), cols]]
+
+    def of_edge(kv, cols):
+        return [traded[kv, :, cols]]
 
     pl.when(inner)(lambda: attend(of_inner))
-    pl.when(jnp.logical_not(inner))(lambda: attend(lambda kv, cols: []))
-
-
-def close_kernel(first, queries, closing, relayed, direct, mixed, tops, sums, *rest):
+    pl.when(jnp.logical_not(inner))(lambda: attend(of_edge))
+
+
+def close_kernel(first, queries, closing, relayed, passed, mixed, tops, sums, *rest):
     out, ready, sems = rest[-3:]
     frame = lax.axis_index("tm")
     inner = (frame == 1) | (frame == 2)
@@ -277,7 +290,7 @@
         return [closing[kv, :, there]]
 
     def of_edge(kv, here, there):
-        return [relayed[kv, :, here], direct[kv, :, there]]
+        return [relayed[kv, :, there], passed[kv, :, here]]
 
     pl.when(inner)(lambda: close(of_inner, rows))
     pl.when(jnp.logical_not(inner))(lambda: close(of_edge, rows // 2))
@@ -295,6 +308,7 @@
         return lax.ppermute(array, "tm", pairs)
 
     bands = jnp.transpose(band_blocks, (0, 2, 1))
+    one = jax.ShapeDtypeStruct((2, BLOCK, columns), jnp.bfloat16)
     two = jax.ShapeDtypeStruct((2, 2 * BLOCK, columns), jnp.bfloat16)
 
     def stage(kernel, shapes, copies, operands, name, room):
@@ -318,29 +332,40 @@
         51,
     )
     (crossed,) = stage(
-        stage_crossed_kernel, [two], 4, [after, bands, keys, values], "stage_crossed", 32
-    )
+        stage_crossed_kernel, [one], 2, [after, bands, keys, values], "stage_crossed", 32
+    )
+    listed = send(listed, [(1, 2), (2, 1)])
     beside = send(beside, [(0, 1), (1, 0), (2, 3), (3, 2)])
-    listed = send(listed, [(1, 2), (2, 1)])
     crossed = send(crossed, [(0, 2), (3, 1)])
-    relayed = send(listed, [(2, 3), (1, 0)])
     last = heads // 4
     cuts = [(0, heads - last), (heads - last, last)] if last else [(0, heads)]
     cuts = [(start * HD, size * HD) for start, size in cuts]
-    last_parts = stage(
-        functools.partial(stage_last_kernel, cuts),
-        [
-            jax.ShapeDtypeStruct((2, count * BLOCK, size), jnp.bfloat16)
-            for count in (2, 1)
-            for _, size in cuts
-        ],
-        4 * len(cuts),
-        [beside, bands, keys, values],
-        "stage_last",
+
+    def by_heads(blocks):
+        return [jax.ShapeDtypeStruct((2, blocks * BLOCK, size), jnp.bfloat16) for _, size in cuts]
+
+    relayed = pl.pallas_call(
+        functools.partial(relay_kernel, cuts),
+        out_shape=by_heads(2),
+        in_specs=[local],
+        out_specs=[local] * len(cuts),
+        compiler_params=pltpu.CompilerParams(vmem_limit_bytes=32 << 20),
+        name="relay",
+    )(listed)
+    relayed = [send(part, [(2, 3), (1, 0)]) for part in relayed]
+    traded, passed = stage(
+        stage_second_kernel, [one, one], 2, [beside, bands, keys, values], "stage_second", 32
+    )
+    traded = send(traded, [(0, 3), (3, 0), (1, 2), (2, 1)])
+    passed = send(passed, [(1, 3), (2, 0)])
+    closing = stage(
+        functools.partial(stage_closing_kernel, cuts),
+        by_heads(1),
+        2 * len(cuts),
+        [crossed, bands, keys, values],
+        "stage_closing",
         32,
     )
-    direct, closing = last_parts[: len(cuts)], last_parts[len(cuts) :]
-    direct = [send(part, [(0, 3), (3, 0)]) for part in direct]
     closing = [send(part, [(1, 2), (2, 1)]) for part in closing]
 
     state = jax.ShapeDtypeStruct((heads, rows, HD), jnp.float32)
@@ -348,14 +373,14 @@
     mixed, tops, sums = pl.pallas_call(
         functools.partial(attend_kernel, rows // 2),
         out_shape=[state] * 3,
-        in_specs=[local] * 6,
+        in_specs=[local] * 7,
         out_specs=[local] * 3,
         compiler_params=roomy,
         name="attend",
-    )(queries, keys, values, beside, listed, crossed)
+    )(queries, keys, values, beside, listed, crossed, traded)
     result = None
-    for near, far, (start, size) in zip(closing, direct, cuts):
-        operands = [queries, near, relayed, far, mixed, tops, sums]
+    for near, far, (start, size) in zip(closing, relayed, cuts):
+        operands = [queries, near, far, passed, mixed, tops, sums]
         in_specs = [local] * len(operands)
         aliases = {}
         if result is not None:

time: 89.3 us -> 89.4 us (level)
  waiting for transfers between devices: 62.2 us -> 58.9 us
  starting transfers between devices: 10.4 us -> 13.1 us
    ppermute x8 -> x9, waiting for transfers between devices: 62.2 us -> 58.9 us  [send(): return lax.ppermute(array, 'tm', pairs)]
    ppermute x8 -> x9, starting transfers between devices: 10.4 us -> 13.1 us  [send(): return lax.ppermute(array, 'tm', pairs)]
    pallas_call x3 -> x4, Pallas kernels: 3.6 us -> 4.25 us  [stage(): pl.pallas_call(kernel, out_shape=shapes, in_specs=[scalars if operand is...]
  transfers between devices with their start and end apart: 8 -> 9, of which waited for: 4 -> 5; matrix products, arithmetic and copies ran while one was open for 0% -> 0% of each run, Pallas kernels for 13% -> 14%
where the time goes in v15:
time: 89.4 us; the launch traced here: 89.1 us
  waiting for transfers between devices  58.9 us (66%)
  Pallas kernels  16 us (18%)
  starting transfers between devices  13.1 us (15%)
    ppermute x9, waiting for transfers between devices, send(): return lax.ppermute(array, 'tm', pairs)  58.9 us
    ppermute x9, starting transfers between devices, send(): return lax.ppermute(array, 'tm', pairs)  13.1 us
    pallas_call x1, Pallas kernels, four_frames(): pl.pallas_call(functools.partial(attend_kernel, rows // 2), out_shape=[st...  7.73 us
    pallas_call x4, Pallas kernels, stage(): pl.pallas_call(kernel, out_shape=shapes, in_specs=[scalars if operand is...  4.25 us
    pallas_call x2, Pallas kernels, four_frames(): pl.pallas_call(functools.partial(close_kernel, start), out_shape=jax.Shap...  3.88 us
  transfers between devices with their start and end apart: 9, of which 5 were waited for; matrix products, arithmetic and copies ran while one was open for 0% of the time, Pallas kernels for 14%

profile of v15, /device:TPU:17, one launch (start us, length us, event | category | flops | bytes accessed | tf_op | source)
XLA Modules:
  0.0 89.1 jit_solution(1847492687998355941)
XLA Ops:
  0.0 0.0 copy-start
  0.0 0.8 copy-done.3
  0.8 2.2 %stage_near.1 = (bf16[2,256,1024]{2,1,0:T(8,128)(2,1)S(1)}, bf16[2,256,1024]{2,1,0:T(8,128)(2,1)S(1)}, s32[8,128]{1,0:T(8,128)S(1)}) custom-call(s32[4,2,4]{2,1,0:T(2,128)S(1)} %bitcast.1, bf16[512,1024]{1,0:T(8,128)(2,1)} %keys.9, bf16[512,1024]{1,0:T(8,128)(2,1)} %values.9), custom_call_target="tpu_custom_call" | custom-call | tf_op jit(solution)/shard_map/stage_near/pallas_call | solution.py:315
  3.0 2.1 %collective-permute-start.2 = (bf16[2,256,1024]{2,1,0:T(8,128)(2,1)S(1)}, bf16[2,256,1024]{2,1,0:T(8,128)(2,1)S(1)}, u32[]{:S(2)}, u32[]{:S(2)}) collective-permute-start(bf16[2,256,1024]{2,1,0:T(8,128)(2,1)S(1)} %get-tuple-element.19), channel_id=1, source_target_pairs={{4,8},{8,4},{5,9},{9,5},{6,10},{10,6},{7,11},{11,7},{20,24},{24,20... | collective-permute-start | bytes 3145736 | tf_op jit(solution)/shard_map/ppermute | solution.py:308
  5.1 0.1 collective-permute-start.4
  5.2 0.0 copy-done
  5.2 0.0 copy-done.1
  5.2 0.6 stage_crossed.1
  5.8 1.3 %collective-permute-start = (bf16[2,128,1024]{2,1,0:T(8,128)(2,1)S(1)}, bf16[2,128,1024]{2,1,0:T(8,128)(2,1)S(1)}, u32[]{:S(2)}, u32[]{:S(2)}) collective-permute-start(bf16[2,128,1024]{2,1,0:T(8,128)(2,1)S(1)} %stage_crossed.1), channel_id=1, source_target_pairs={{0,8},{12,4},{1,9},{13,5},{2,10},{14,6},{3,11},{15,7},{16,24},{28,... | collective-permute-start | bytes 1572872 | tf_op jit(solution)/shard_map/ppermute | solution.py:308
  7.1 21.8 %collective-permute-done.2.listed = bf16[2,256,1024]{2,1,0:T(8,128)(2,1)S(1)} collective-permute-done((bf16[2,256,1024]{2,1,0:T(8,128)(2,1)S(1)}, bf16[2,256,1024]{2,1,0:T(8,128)(2,1)S(1)}, u32[]{:S(2)}, u32[]{:S(2)}) %collective-permute-start.2) | collective-permute-done | bytes 1048608 | tf_op jit(solution)/shard_map/ppermute | solution.py:308
  28.9 0.1 relay.1
  29.0 1.3 %collective-permute-start.8 = (bf16[2,256,768]{2,1,0:T(8,128)(2,1)S(1)}, bf16[2,256,768]{2,1,0:T(8,128)(2,1)S(1)}, u32[]{:S(2)}, u32[]{:S(2)}) collective-permute-start(bf16[2,256,768]{2,1,0:T(8,128)(2,1)S(1)} %get-tuple-element.28), channel_id=1, source_target_pairs={{8,12},{4,0},{9,13},{5,1},{10,14},{6,2},{11,15},{7,3},{24,28},{20,... | collective-permute-start | bytes 2359304 | tf_op jit(solution)/shard_map/ppermute | solution.py:308
  30.4 0.0 collective-permute-done.4.beside
  30.4 0.7 stage_second.1
  31.1 0.0 copy-start.2
  31.1 0.2 collective-permute-start.6
  31.4 2.6 %collective-permute-start.5 = (bf16[2,128,1024]{2,1,0:T(8,128)(2,1)S(1)}, bf16[2,128,1024]{2,1,0:T(8,128)(2,1)S(1)}, u32[]{:S(2)}, u32[]{:S(2)}) collective-permute-start(bf16[2,128,1024]{2,1,0:T(8,128)(2,1)S(1)} %get-tuple-element.22), channel_id=1, source_target_pairs={{4,12},{8,0},{5,13},{9,1},{6,14},{10,2},{7,15},{11,3},{20,28},{24,... | collective-permute-start | bytes 1572872 | tf_op jit(solution)/shard_map/ppermute | solution.py:308
  34.0 7.2 %collective-permute-done.after.crossed = bf16[2,128,1024]{2,1,0:T(8,128)(2,1)S(1)} collective-permute-done((bf16[2,128,1024]{2,1,0:T(8,128)(2,1)S(1)}, bf16[2,128,1024]{2,1,0:T(8,128)(2,1)S(1)}, u32[]{:S(2)}, u32[]{:S(2)}) %collective-permute-start) | collective-permute-done | bytes 524320 | tf_op jit(solution)/shard_map/ppermute | solution.py:308
  41.2 0.7 stage_closing.1
  41.9 2.1 %collective-permute-start.7 = (bf16[2,128,768]{2,1,0:T(8,128)(2,1)S(1)}, bf16[2,128,768]{2,1,0:T(8,128)(2,1)S(1)}, u32[]{:S(2)}, u32[]{:S(2)}) collective-permute-start(bf16[2,128,768]{2,1,0:T(8,128)(2,1)S(1)} %get-tuple-element.27), channel_id=1, source_target_pairs={{4,8},{8,4},{5,9},{9,5},{6,10},{10,6},{7,11},{11,7},{20,24},{24,20... | collective-permute-start | bytes 1179656 | tf_op jit(solution)/shard_map/ppermute | solution.py:308
  44.0 1.3 %collective-permute-start.3 = (bf16[2,256,256]{2,1,0:T(8,128)(2,1)S(1)}, bf16[2,256,256]{2,1,0:T(8,128)(2,1)S(1)}, u32[]{:S(2)}, u32[]{:S(2)}) collective-permute-start(bf16[2,256,256]{2,1,0:T(8,128)(2,1)S(1)} %get-tuple-element.20), channel_id=1, source_target_pairs={{8,12},{4,0},{9,13},{5,1},{10,14},{6,2},{11,15},{7,3},{24,28},{20,... | collective-permute-start | bytes 786440 | tf_op jit(solution)/shard_map/ppermute | solution.py:308
  45.3 19.7 %collective-permute-done.6.traded = bf16[2,128,1024]{2,1,0:T(8,128)(2,1)S(1)} collective-permute-done((bf16[2,128,1024]{2,1,0:T(8,128)(2,1)S(1)}, bf16[2,128,1024]{2,1,0:T(8,128)(2,1)S(1)}, u32[]{:S(2)}, u32[]{:S(2)}) %collective-permute-start.6) | collective-permute-done | bytes 524320 | tf_op jit(solution)/shard_map/ppermute | solution.py:308
  65.0 2.1 %collective-permute-start.1 = (bf16[2,128,256]{2,1,0:T(8,128)(2,1)S(1)}, bf16[2,128,256]{2,1,0:T(8,128)(2,1)S(1)}, u32[]{:S(2)}, u32[]{:S(2)}) collective-permute-start(bf16[2,128,256]{2,1,0:T(8,128)(2,1)S(1)} %get-tuple-element.18), channel_id=1, source_target_pairs={{4,8},{8,4},{5,9},{9,5},{6,10},{10,6},{7,11},{11,7},{20,24},{24,20... | collective-permute-start | bytes 393224 | tf_op jit(solution)/shard_map/ppermute | solution.py:308
  67.0 0.0 copy-done.2
  67.1 7.7 %attend.1 = (f32[8,512,128]{2,1,0:T(8,128)S(1)}, f32[8,512,128]{2,1,0:T(8,128)S(1)}, f32[8,512,128]{2,1,0:T(8,128)S(1)}) custom-call(bf16[512,1024]{1,0:T(8,128)(2,1)S(1)} %copy-done.2, bf16[512,1024]{1,0:T(8,128)(2,1)S(1)} %copy-done, bf16[512,1024]{1,0:T(8,128)(2,1)S(1)} %copy-done.1, bf16[2,256,1024]{2,1,0:T(8,128)(2,1)S(1)} %collective-permute-done.4.beside, ...), custom_call_target="tpu_custom_call" | custom-call | tf_op jit(solution)/shard_map/attend/pallas_call | solution.py:373
  74.8 9.9 %collective-permute-done.7.closing = bf16[2,128,768]{2,1,0:T(8,128)(2,1)S(1)} collective-permute-done((bf16[2,128,768]{2,1,0:T(8,128)(2,1)S(1)}, bf16[2,128,768]{2,1,0:T(8,128)(2,1)S(1)}, u32[]{:S(2)}, u32[]{:S(2)}) %collective-permute-start.7) | collective-permute-done | bytes 393248 | tf_op jit(solution)/shard_map/ppermute | solution.py:308
  84.7 0.0 collective-permute-done.5.passed
  84.7 0.0 collective-permute-done.8.relayed
  84.7 2.4 %close.2.rest_0_ = bf16[512,1024]{1,0:T(8,128)(2,1)} custom-call(bf16[512,1024]{1,0:T(8,128)(2,1)S(1)} %copy-done.2, bf16[2,128,768]{2,1,0:T(8,128)(2,1)S(1)} %collective-permute-done.7.closing, bf16[2,256,768]{2,1,0:T(8,128)(2,1)S(1)} %collective-permute-done.8.relayed, bf16[2,128,1024]{2,1,0:T(8,128)(2,1)S(1)} %collective-permute-done.5.passed, ...), custom_call_target="tpu_custom_call" | custom-call | tf_op jit(solution)/shard_map/close/pallas_call | solution.py:390
  87.1 0.4 collective-permute-done.1.closing
  87.5 0.0 collective-permute-done.3.relayed
  87.5 1.4 %close.3 = bf16[512,1024]{1,0:T(8,128)(2,1)} custom-call(bf16[512,1024]{1,0:T(8,128)(2,1)S(1)} %copy-done.2, bf16[2,128,256]{2,1,0:T(8,128)(2,1)S(1)} %collective-permute-done.1.closing, bf16[2,256,256]{2,1,0:T(8,128)(2,1)S(1)} %collective-permute-done.3.relayed, ...), custom_call_target="tpu_custom_call", output_to_operand_aliasing={{}: (7, {})} | custom-call | tf_op jit(solution)/shard_map/close/pallas_call | solution.py:390
  (2 shorter events, 0.0 us)
Async XLA Ops:
  0.0 5.2 %copy-start = (bf16[512,1024]{1,0:T(8,128)(2,1)S(1)}, bf16[512,1024]{1,0:T(8,128)(2,1)}, u32[]{:S(2)}) copy-start(bf16[512,1024]{1,0:T(8,128)(2,1)} %keys.9) | copy-start | bytes 3145732
  0.0 5.2 %copy-start.1 = (bf16[512,1024]{1,0:T(8,128)(2,1)S(1)}, bf16[512,1024]{1,0:T(8,128)(2,1)}, u32[]{:S(2)}) copy-start(bf16[512,1024]{1,0:T(8,128)(2,1)} %values.9) | copy-start | bytes 3145732
  0.0 0.8 copy-start.3
  3.0 25.9 %collective-permute-start.2 = (bf16[2,256,1024]{2,1,0:T(8,128)(2,1)S(1)}, bf16[2,256,1024]{2,1,0:T(8,128)(2,1)S(1)}, u32[]{:S(2)}, u32[]{:S(2)}) collective-permute-start(bf16[2,256,1024]{2,1,0:T(8,128)(2,1)S(1)} %get-tuple-element.19), channel_id=1, source_target_pairs={{4,8},{8,4},{5,9},{9,5},{6,10},{10,6},{7,11},{11,7},{20,24},{24,20... | collective-permute-start | bytes 3145736 | tf_op jit(solution)/shard_map/ppermute | solution.py:308
  5.1 25.3 %collective-permute-start.4 = (bf16[2,256,1024]{2,1,0:T(8,128)(2,1)S(1)}, bf16[2,256,1024]{2,1,0:T(8,128)(2,1)S(1)}, u32[]{:S(2)}, u32[]{:S(2)}) collective-permute-start(bf16[2,256,1024]{2,1,0:T(8,128)(2,1)S(1)} %get-tuple-element.21), channel_id=1, source_target_pairs={{0,4},{4,0},{8,12},{12,8},{1,5},{5,1},{9,13},{13,9},{2,6},{6,2},{1... | collective-permute-start | bytes 3145736 | tf_op jit(solution)/shard_map/ppermute | solution.py:308
  5.8 35.3 %collective-permute-start = (bf16[2,128,1024]{2,1,0:T(8,128)(2,1)S(1)}, bf16[2,128,1024]{2,1,0:T(8,128)(2,1)S(1)}, u32[]{:S(2)}, u32[]{:S(2)}) collective-permute-start(bf16[2,128,1024]{2,1,0:T(8,128)(2,1)S(1)} %stage_crossed.1), channel_id=1, source_target_pairs={{0,8},{12,4},{1,9},{13,5},{2,10},{14,6},{3,11},{15,7},{16,24},{28,... | collective-permute-start | bytes 1572872 | tf_op jit(solution)/shard_map/ppermute | solution.py:308
  29.0 55.7 %collective-permute-start.8 = (bf16[2,256,768]{2,1,0:T(8,128)(2,1)S(1)}, bf16[2,256,768]{2,1,0:T(8,128)(2,1)S(1)}, u32[]{:S(2)}, u32[]{:S(2)}) collective-permute-start(bf16[2,256,768]{2,1,0:T(8,128)(2,1)S(1)} %get-tuple-element.28), channel_id=1, source_target_pairs={{8,12},{4,0},{9,13},{5,1},{10,14},{6,2},{11,15},{7,3},{24,28},{20,... | collective-permute-start | bytes 2359304 | tf_op jit(solution)/shard_map/ppermute | solution.py:308
  31.1 35.9 %copy-start.2 = (bf16[512,1024]{1,0:T(8,128)(2,1)S(1)}, bf16[512,1024]{1,0:T(8,128)(2,1)}, u32[]{:S(2)}) copy-start(bf16[512,1024]{1,0:T(8,128)(2,1)} %queries.5) | copy-start | bytes 3145732
  31.1 33.8 %collective-permute-start.6 = (bf16[2,128,1024]{2,1,0:T(8,128)(2,1)S(1)}, bf16[2,128,1024]{2,1,0:T(8,128)(2,1)S(1)}, u32[]{:S(2)}, u32[]{:S(2)}) collective-permute-start(bf16[2,128,1024]{2,1,0:T(8,128)(2,1)S(1)} %get-tuple-element.23), channel_id=1, source_target_pairs={{0,12},{12,0},{4,8},{8,4},{1,13},{13,1},{5,9},{9,5},{2,14},{14,2},... | collective-permute-start | bytes 1572872 | tf_op jit(solution)/shard_map/ppermute | solution.py:308
  31.4 53.3 %collective-permute-start.5 = (bf16[2,128,1024]{2,1,0:T(8,128)(2,1)S(1)}, bf16[2,128,1024]{2,1,0:T(8,128)(2,1)S(1)}, u32[]{:S(2)}, u32[]{:S(2)}) collective-permute-start(bf16[2,128,1024]{2,1,0:T(8,128)(2,1)S(1)} %get-tuple-element.22), channel_id=1, source_target_pairs={{4,12},{8,0},{5,13},{9,1},{6,14},{10,2},{7,15},{11,3},{20,28},{24,... | collective-permute-start | bytes 1572872 | tf_op jit(solution)/shard_map/ppermute | solution.py:308
  41.9 42.8 %collective-permute-start.7 = (bf16[2,128,768]{2,1,0:T(8,128)(2,1)S(1)}, bf16[2,128,768]{2,1,0:T(8,128)(2,1)S(1)}, u32[]{:S(2)}, u32[]{:S(2)}) collective-permute-start(bf16[2,128,768]{2,1,0:T(8,128)(2,1)S(1)} %get-tuple-element.27), channel_id=1, source_target_pairs={{4,8},{8,4},{5,9},{9,5},{6,10},{10,6},{7,11},{11,7},{20,24},{24,20... | collective-permute-start | bytes 1179656 | tf_op jit(solution)/shard_map/ppermute | solution.py:308
  44.0 43.5 %collective-permute-start.3 = (bf16[2,256,256]{2,1,0:T(8,128)(2,1)S(1)}, bf16[2,256,256]{2,1,0:T(8,128)(2,1)S(1)}, u32[]{:S(2)}, u32[]{:S(2)}) collective-permute-start(bf16[2,256,256]{2,1,0:T(8,128)(2,1)S(1)} %get-tuple-element.20), channel_id=1, source_target_pairs={{8,12},{4,0},{9,13},{5,1},{10,14},{6,2},{11,15},{7,3},{24,28},{20,... | collective-permute-start | bytes 786440 | tf_op jit(solution)/shard_map/ppermute | solution.py:308
  65.0 22.5 %collective-permute-start.1 = (bf16[2,128,256]{2,1,0:T(8,128)(2,1)S(1)}, bf16[2,128,256]{2,1,0:T(8,128)(2,1)S(1)}, u32[]{:S(2)}, u32[]{:S(2)}) collective-permute-start(bf16[2,128,256]{2,1,0:T(8,128)(2,1)S(1)} %get-tuple-element.18), channel_id=1, source_target_pairs={{4,8},{8,4},{5,9},{9,5},{6,10},{10,6},{7,11},{11,7},{20,24},{24,20... | collective-permute-start | bytes 393224 | tf_op jit(solution)/shard_map/ppermute | solution.py:308

commit v16 on v15

--- a/solution.py
+++ b/solution.py
@@ -128,17 +128,32 @@
         copy.wait()
 
 
-def stage_crossed_kernel(after, bands, keys, values, crossed, sems):
-    frame = lax.axis_index("tm")
-
-    @pl.when((frame == 0) | (frame == 3))
-    def _():
-        block = jnp.where(frame == 0, bands[2, 0, 0], bands[1, 1, 3])
-        rows = rows_of(block)
+def other_rows(bands, frame):
+    return rows_of(jnp.where(frame == 1, 5 - bands[3, 1, 1], 1 - bands[0, 0, 2]))
+
+
+def stage_third_kernel(cut, after, bands, keys, values, crossed, closing, sems):
+    frame = lax.axis_index("tm")
+    inner = (frame == 1) | (frame == 2)
+
+    @pl.when(inner)
+    def _():
+        rows = other_rows(bands, frame)
+        run_copies(
+            [
+                (source.at[rows, pl.ds(*cut)], closing.at[kv])
+                for kv, source in enumerate((keys, values))
+            ],
+            sems,
+        )
+
+    @pl.when(jnp.logical_not(inner))
+    def _():
+        rows = rows_of(jnp.where(frame == 0, bands[2, 0, 0], bands[1, 1, 3]))
         run_copies([(keys.at[rows], crossed.at[0]), (values.at[rows], crossed.at[1])], sems)
 
 
-def relay_kernel(cuts, listed, *relayed):
+def relay_kernel(cuts, after, listed, *relayed):
     frame = lax.axis_index("tm")
 
     @pl.when((frame == 1) | (frame == 2))
@@ -169,7 +184,7 @@
 
     @pl.when((frame == 1) | (frame == 2))
     def _():
-        rows = rows_of(jnp.where(frame == 1, 5 - bands[3, 1, 1], 1 - bands[0, 0, 2]))
+        rows = other_rows(bands, frame)
         run_copies(
             [
                 (source.at[rows, pl.ds(*cut)], part.at[kv])
@@ -238,7 +253,9 @@
     pl.when(jnp.logical_not(inner))(lambda: attend(of_edge))
 
 
-def close_kernel(first, queries, closing, relayed, passed, mixed, tops, sums, *rest):
+def close_kernel(
+    first, early, queries, closing, early_relayed, late_relayed, passed, mixed, tops, sums, *rest
+):
     out, ready, sems = rest[-3:]
     frame = lax.axis_index("tm")
     inner = (frame == 1) | (frame == 2)
@@ -290,7 +307,11 @@
         return [closing[kv, :, there]]
 
     def of_edge(kv, here, there):
-        return [relayed[kv, :, there], passed[kv, :, here]]
+        if here.start < early:
+            relayed = early_relayed[kv, :, here]
+        else:
+            relayed = late_relayed[kv, :, pl.ds(here.start - early, HD)]
+        return [relayed, passed[kv, :, here]]
 
     pl.when(inner)(lambda: close(of_inner, rows))
     pl.when(jnp.logical_not(inner))(lambda: close(of_edge, rows // 2))
@@ -331,27 +352,36 @@
         "stage_near",
         51,
     )
-    (crossed,) = stage(
-        stage_crossed_kernel, [one], 2, [after, bands, keys, values], "stage_crossed", 32
+    last = heads // 4
+    sizes = [1, heads - 2, 1]
+    few = [(sum(sizes[:g]) * HD, size * HD) for g, size in enumerate(sizes)]
+    cuts = [(0, (heads - last) * HD), ((heads - last) * HD, last * HD)]
+
+    def by_heads(groups, blocks):
+        return [
+            jax.ShapeDtypeStruct((2, blocks * BLOCK, size), jnp.bfloat16) for _, size in groups
+        ]
+
+    crossed, first_closing = stage(
+        functools.partial(stage_third_kernel, few[0]),
+        [one] + by_heads(few[:1], 1),
+        2,
+        [after, bands, keys, values],
+        "stage_third",
+        32,
     )
     listed = send(listed, [(1, 2), (2, 1)])
     beside = send(beside, [(0, 1), (1, 0), (2, 3), (3, 2)])
+    first_closing = send(first_closing, [(1, 2), (2, 1)])
     crossed = send(crossed, [(0, 2), (3, 1)])
-    last = heads // 4
-    cuts = [(0, heads - last), (heads - last, last)] if last else [(0, heads)]
-    cuts = [(start * HD, size * HD) for start, size in cuts]
-
-    def by_heads(blocks):
-        return [jax.ShapeDtypeStruct((2, blocks * BLOCK, size), jnp.bfloat16) for _, size in cuts]
-
     relayed = pl.pallas_call(
         functools.partial(relay_kernel, cuts),
-        out_shape=by_heads(2),
-        in_specs=[local],
+        out_shape=by_heads(cuts, 2),
+        in_specs=[anywhere, local],
         out_specs=[local] * len(cuts),
         compiler_params=pltpu.CompilerParams(vmem_limit_bytes=32 << 20),
         name="relay",
-    )(listed)
+    )(first_closing, listed)
     relayed = [send(part, [(2, 3), (1, 0)]) for part in relayed]
     traded, passed = stage(
         stage_second_kernel, [one, one], 2, [beside, bands, keys, values], "stage_second", 32
@@ -359,14 +389,14 @@
     traded = send(traded, [(0, 3), (3, 0), (1, 2), (2, 1)])
     passed = send(passed, [(1, 3), (2, 0)])
     closing = stage(
-        functools.partial(stage_closing_kernel, cuts),
-        by_heads(1),
-        2 * len(cuts),
+        functools.partial(stage_closing_kernel, few[1:]),
+        by_heads(few[1:], 1),
+        2 * len(few[1:]),
         [crossed, bands, keys, values],
         "stage_closing",
         32,
     )
-    closing = [send(part, [(1, 2), (2, 1)]) for part in closing]
+    closing = [first_closing] + [send(part, [(1, 2), (2, 1)]) for part in closing]
 
     state = jax.ShapeDtypeStruct((heads, rows, HD), jnp.float32)
     roomy = pltpu.CompilerParams(vmem_limit_bytes=32 << 20)
@@ -379,8 +409,9 @@
         name="attend",
     )(queries, keys, values, beside, listed, crossed, traded)
     result = None
-    for near, far, (start, size) in zip(closing, relayed, cuts):
-        operands = [queries, near, far, passed, mixed, tops, sums]
+    for part, (start, size) in zip(closing, few):
+        used = relayed if start + size > cuts[1][0] else relayed[:1] * 2
+        operands = [queries, part, *used, passed, mixed, tops, sums]
         in_specs = [local] * len(operands)
         aliases = {}
         if result is not None:
@@ -388,7 +419,7 @@
             in_specs.append(anywhere)
             operands.append(result)
         result = pl.pallas_call(
-            functools.partial(close_kernel, start),
+            functools.partial(close_kernel, start, cuts[1][0]),
             out_shape=jax.ShapeDtypeStruct(queries.shape, queries.dtype),
             in_specs=in_specs,
             out_specs=anywhere,
@@ -404,7 +435,9 @@
 
 
 def shards(queries, keys, values, band_blocks):
-    if lax.axis_size("tm") == 4 and queries.shape[0] == 4 * BLOCK and band_blocks.shape[2] == 2:
+    rows, columns = queries.shape
+    shaped = rows == 4 * BLOCK and columns >= 4 * HD and band_blocks.shape[2] == 2
+    if lax.axis_size("tm") == 4 and shaped:
         return four_frames(queries, keys, values, band_blocks)
     return any_frames(queries, keys, values, band_blocks)
 

time: 89.4 us -> 89.4 us (level)
  the two profiles are of different devices: /device:TPU:17 before, /device:TPU:0 now
where the time goes in v16:
time: 89.4 us; the launch traced here: 88.5 us
  waiting for transfers between devices  53.6 us (60%)
  Pallas kernels  17.7 us (20%)
  starting transfers between devices  16 us (18%)
    ppermute x10, waiting for transfers between devices, send(): return lax.ppermute(array, 'tm', pairs)  53.6 us
    ppermute x10, starting transfers between devices, send(): return lax.ppermute(array, 'tm', pairs)  16 us
    pallas_call x3, Pallas kernels, four_frames(): pl.pallas_call(functools.partial(close_kernel, start, cuts[1][0]), out_sh...  7.97 us
    pallas_call x1, Pallas kernels, four_frames(): pl.pallas_call(functools.partial(attend_kernel, rows // 2), out_shape=[st...  5.87 us
    pallas_call x4, Pallas kernels, stage(): pl.pallas_call(kernel, out_shape=shapes, in_specs=[scalars if operand is...  3.89 us
  transfers between devices with their start and end apart: 10, of which 4 were waited for; matrix products, arithmetic and copies ran while one was open for 0% of the time, Pallas kernels for 16%

profile of v16, /device:TPU:0, one launch (start us, length us, event | category | flops | bytes accessed | tf_op | source)
XLA Modules:
  0.0 88.5 jit_solution(14885373364116120522)
XLA Ops:
  0.0 0.8 copy-done.3
  0.8 1.9 %stage_near.1 = (bf16[2,256,1024]{2,1,0:T(8,128)(2,1)S(1)}, bf16[2,256,1024]{2,1,0:T(8,128)(2,1)S(1)}, s32[8,128]{1,0:T(8,128)S(1)}) custom-call(s32[4,2,4]{2,1,0:T(2,128)S(1)} %bitcast.1, bf16[512,1024]{1,0:T(8,128)(2,1)} %keys.9, bf16[512,1024]{1,0:T(8,128)(2,1)} %values.9), custom_call_target="tpu_custom_call" | custom-call | tf_op jit(solution)/shard_map/stage_near/pallas_call | solution.py:336
  2.7 0.7 collective-permute-start.3
  3.5 6.1 %collective-permute-start.6 = (bf16[2,256,1024]{2,1,0:T(8,128)(2,1)S(1)}, bf16[2,256,1024]{2,1,0:T(8,128)(2,1)S(1)}, u32[]{:S(2)}, u32[]{:S(2)}) collective-permute-start(bf16[2,256,1024]{2,1,0:T(8,128)(2,1)S(1)} %get-tuple-element.26), channel_id=1, source_target_pairs={{0,4},{4,0},{8,12},{12,8},{1,5},{5,1},{9,13},{13,9},{2,6},{6,2},{1... | collective-permute-start | bytes 3145736 | tf_op jit(solution)/shard_map/ppermute | solution.py:329
  9.6 0.0 copy-done
  9.6 0.0 copy-done.1
  9.6 0.7 stage_third.1
  10.3 1.8 %collective-permute-start = (bf16[2,128,1024]{2,1,0:T(8,128)(2,1)S(1)}, bf16[2,128,1024]{2,1,0:T(8,128)(2,1)S(1)}, u32[]{:S(2)}, u32[]{:S(2)}) collective-permute-start(bf16[2,128,1024]{2,1,0:T(8,128)(2,1)S(1)} %get-tuple-element.20), channel_id=1, source_target_pairs={{0,8},{12,4},{1,9},{13,5},{2,10},{14,6},{3,11},{15,7},{16,24},{28,... | collective-permute-start | bytes 1572872 | tf_op jit(solution)/shard_map/ppermute | solution.py:329
  12.1 0.7 collective-permute-start.2
  12.8 0.0 collective-permute-done.2.after.closing
  12.8 0.0 collective-permute-done.3.listed
  12.9 1.3 %collective-permute-start.4 = (bf16[2,256,768]{2,1,0:T(8,128)(2,1)S(1)}, bf16[2,256,768]{2,1,0:T(8,128)(2,1)S(1)}, u32[]{:S(2)}, u32[]{:S(2)}) collective-permute-start(bf16[2,256,768]{2,1,0:T(8,128)(2,1)S(1)} %get-tuple-element.24), channel_id=1, source_target_pairs={{8,12},{4,0},{9,13},{5,1},{10,14},{6,2},{11,15},{7,3},{24,28},{20,... | collective-permute-start | bytes 2359304 | tf_op jit(solution)/shard_map/ppermute | solution.py:329
  14.2 19.1 %collective-permute-done.6.beside = bf16[2,256,1024]{2,1,0:T(8,128)(2,1)S(1)} collective-permute-done((bf16[2,256,1024]{2,1,0:T(8,128)(2,1)S(1)}, bf16[2,256,1024]{2,1,0:T(8,128)(2,1)S(1)}, u32[]{:S(2)}, u32[]{:S(2)}) %collective-permute-start.6) | collective-permute-done | bytes 1048608 | tf_op jit(solution)/shard_map/ppermute | solution.py:329
  33.2 0.7 stage_second.1
  33.9 0.0 copy-start.2
  33.9 1.4 %collective-permute-start.8 = (bf16[2,128,1024]{2,1,0:T(8,128)(2,1)S(1)}, bf16[2,128,1024]{2,1,0:T(8,128)(2,1)S(1)}, u32[]{:S(2)}, u32[]{:S(2)}) collective-permute-start(bf16[2,128,1024]{2,1,0:T(8,128)(2,1)S(1)} %get-tuple-element.28), channel_id=1, source_target_pairs={{0,12},{12,0},{4,8},{8,4},{1,13},{13,1},{5,9},{9,5},{2,14},{14,2},... | collective-permute-start | bytes 1572872 | tf_op jit(solution)/shard_map/ppermute | solution.py:329
  35.3 1.3 %collective-permute-start.7 = (bf16[2,128,1024]{2,1,0:T(8,128)(2,1)S(1)}, bf16[2,128,1024]{2,1,0:T(8,128)(2,1)S(1)}, u32[]{:S(2)}, u32[]{:S(2)}) collective-permute-start(bf16[2,128,1024]{2,1,0:T(8,128)(2,1)S(1)} %get-tuple-element.27), channel_id=1, source_target_pairs={{4,12},{8,0},{5,13},{9,1},{6,14},{10,2},{7,15},{11,3},{20,28},{24,... | collective-permute-start | bytes 1572872 | tf_op jit(solution)/shard_map/ppermute | solution.py:329
  36.6 7.9 %collective-permute-done.after.crossed = bf16[2,128,1024]{2,1,0:T(8,128)(2,1)S(1)} collective-permute-done((bf16[2,128,1024]{2,1,0:T(8,128)(2,1)S(1)}, bf16[2,128,1024]{2,1,0:T(8,128)(2,1)S(1)}, u32[]{:S(2)}, u32[]{:S(2)}) %collective-permute-start) | collective-permute-done | bytes 524320 | tf_op jit(solution)/shard_map/ppermute | solution.py:329
  44.5 0.6 stage_closing.1
  45.1 0.7 collective-permute-start.9
  45.8 1.3 %collective-permute-start.5 = (bf16[2,256,256]{2,1,0:T(8,128)(2,1)S(1)}, bf16[2,256,256]{2,1,0:T(8,128)(2,1)S(1)}, u32[]{:S(2)}, u32[]{:S(2)}) collective-permute-start(bf16[2,256,256]{2,1,0:T(8,128)(2,1)S(1)} %get-tuple-element.25), channel_id=1, source_target_pairs={{8,12},{4,0},{9,13},{5,1},{10,14},{6,2},{11,15},{7,3},{24,28},{20,... | collective-permute-start | bytes 786440 | tf_op jit(solution)/shard_map/ppermute | solution.py:329
  47.1 9.1 %collective-permute-done.8.traded = bf16[2,128,1024]{2,1,0:T(8,128)(2,1)S(1)} collective-permute-done((bf16[2,128,1024]{2,1,0:T(8,128)(2,1)S(1)}, bf16[2,128,1024]{2,1,0:T(8,128)(2,1)S(1)}, u32[]{:S(2)}, u32[]{:S(2)}) %collective-permute-start.8) | collective-permute-done | bytes 524320 | tf_op jit(solution)/shard_map/ppermute | solution.py:329
  56.2 0.7 collective-permute-start.1
  56.9 5.9 %attend.1 = (f32[8,512,128]{2,1,0:T(8,128)S(1)}, f32[8,512,128]{2,1,0:T(8,128)S(1)}, f32[8,512,128]{2,1,0:T(8,128)S(1)}) custom-call(bf16[512,1024]{1,0:T(8,128)(2,1)S(1)} %copy-done.2, bf16[512,1024]{1,0:T(8,128)(2,1)S(1)} %copy-done, bf16[512,1024]{1,0:T(8,128)(2,1)S(1)} %copy-done.1, bf16[2,256,1024]{2,1,0:T(8,128)(2,1)S(1)} %collective-permute-done.6.beside, ...), custom_call_target="tpu_custom_call" | custom-call | tf_op jit(solution)/shard_map/attend/pallas_call | solution.py:403
  62.8 17.5 %collective-permute-done.7.passed = bf16[2,128,1024]{2,1,0:T(8,128)(2,1)S(1)} collective-permute-done((bf16[2,128,1024]{2,1,0:T(8,128)(2,1)S(1)}, bf16[2,128,1024]{2,1,0:T(8,128)(2,1)S(1)}, u32[]{:S(2)}, u32[]{:S(2)}) %collective-permute-start.7) | collective-permute-done | bytes 524320 | tf_op jit(solution)/shard_map/ppermute | solution.py:329
  80.3 0.0 collective-permute-done.4.early_relayed.late_relayed
  80.3 1.5 %close.3.rest_0_ = bf16[512,1024]{1,0:T(8,128)(2,1)} custom-call(bf16[512,1024]{1,0:T(8,128)(2,1)S(1)} %copy-done.2, bf16[2,128,128]{2,1,0:T(8,128)(2,1)S(1)} %collective-permute-done.2.after.closing, bf16[2,256,768]{2,1,0:T(8,128)(2,1)S(1)} %collective-permute-done.4.early_relayed.late_relayed, ...), custom_call_target="tpu_custom_call" | custom-call | tf_op jit(solution)/shard_map/close/pallas_call | solution.py:421
  81.8 0.0 collective-permute-done.9.closing
  81.8 0.0 collective-permute-done.5.late_relayed
  81.8 4.9 %close.4.rest_0_ = bf16[512,1024]{1,0:T(8,128)(2,1)} custom-call(bf16[512,1024]{1,0:T(8,128)(2,1)S(1)} %copy-done.2, bf16[2,128,768]{2,1,0:T(8,128)(2,1)S(1)} %collective-permute-done.9.closing, bf16[2,256,768]{2,1,0:T(8,128)(2,1)S(1)} %collective-permute-done.4.early_relayed.late_relayed, ...), custom_call_target="tpu_custom_call", output_to_operand_aliasing={{}: (8, {})} | custom-call | tf_op jit(solution)/shard_map/close/pallas_call | solution.py:421
  86.8 0.0 collective-permute-done.1.closing
  86.8 1.5 %close.5 = bf16[512,1024]{1,0:T(8,128)(2,1)} custom-call(bf16[512,1024]{1,0:T(8,128)(2,1)S(1)} %copy-done.2, bf16[2,128,128]{2,1,0:T(8,128)(2,1)S(1)} %collective-permute-done.1.closing, bf16[2,256,768]{2,1,0:T(8,128)(2,1)S(1)} %collective-permute-done.4.early_relayed.late_relayed, ...), custom_call_target="tpu_custom_call", output_to_operand_aliasing={{}: (8, {})} | custom-call | tf_op jit(solution)/shard_map/close/pallas_call | solution.py:421
  (5 shorter events, 0.0 us)
Async XLA Ops:
  0.0 9.6 %copy-start = (bf16[512,1024]{1,0:T(8,128)(2,1)S(1)}, bf16[512,1024]{1,0:T(8,128)(2,1)}, u32[]{:S(2)}) copy-start(bf16[512,1024]{1,0:T(8,128)(2,1)} %keys.9) | copy-start | bytes 3145732
  0.0 9.6 %copy-start.1 = (bf16[512,1024]{1,0:T(8,128)(2,1)S(1)}, bf16[512,1024]{1,0:T(8,128)(2,1)}, u32[]{:S(2)}) copy-start(bf16[512,1024]{1,0:T(8,128)(2,1)} %values.9) | copy-start | bytes 3145732
  0.0 0.8 copy-start.3
  2.7 10.1 %collective-permute-start.3 = (bf16[2,256,1024]{2,1,0:T(8,128)(2,1)S(1)}, bf16[2,256,1024]{2,1,0:T(8,128)(2,1)S(1)}, u32[]{:S(2)}, u32[]{:S(2)}) collective-permute-start(bf16[2,256,1024]{2,1,0:T(8,128)(2,1)S(1)} %get-tuple-element.23), channel_id=1, source_target_pairs={{4,8},{8,4},{5,9},{9,5},{6,10},{10,6},{7,11},{11,7},{20,24},{24,20... | collective-permute-start | bytes 3145736 | tf_op jit(solution)/shard_map/ppermute | solution.py:329
  3.5 29.7 %collective-permute-start.6 = (bf16[2,256,1024]{2,1,0:T(8,128)(2,1)S(1)}, bf16[2,256,1024]{2,1,0:T(8,128)(2,1)S(1)}, u32[]{:S(2)}, u32[]{:S(2)}) collective-permute-start(bf16[2,256,1024]{2,1,0:T(8,128)(2,1)S(1)} %get-tuple-element.26), channel_id=1, source_target_pairs={{0,4},{4,0},{8,12},{12,8},{1,5},{5,1},{9,13},{13,9},{2,6},{6,2},{1... | collective-permute-start | bytes 3145736 | tf_op jit(solution)/shard_map/ppermute | solution.py:329
  10.3 34.2 %collective-permute-start = (bf16[2,128,1024]{2,1,0:T(8,128)(2,1)S(1)}, bf16[2,128,1024]{2,1,0:T(8,128)(2,1)S(1)}, u32[]{:S(2)}, u32[]{:S(2)}) collective-permute-start(bf16[2,128,1024]{2,1,0:T(8,128)(2,1)S(1)} %get-tuple-element.20), channel_id=1, source_target_pairs={{0,8},{12,4},{1,9},{13,5},{2,10},{14,6},{3,11},{15,7},{16,24},{28,... | collective-permute-start | bytes 1572872 | tf_op jit(solution)/shard_map/ppermute | solution.py:329
  12.1 0.7 collective-permute-start.2
  12.9 67.4 %collective-permute-start.4 = (bf16[2,256,768]{2,1,0:T(8,128)(2,1)S(1)}, bf16[2,256,768]{2,1,0:T(8,128)(2,1)S(1)}, u32[]{:S(2)}, u32[]{:S(2)}) collective-permute-start(bf16[2,256,768]{2,1,0:T(8,128)(2,1)S(1)} %get-tuple-element.24), channel_id=1, source_target_pairs={{8,12},{4,0},{9,13},{5,1},{10,14},{6,2},{11,15},{7,3},{24,28},{20,... | collective-permute-start | bytes 2359304 | tf_op jit(solution)/shard_map/ppermute | solution.py:329
  33.9 23.0 %copy-start.2 = (bf16[512,1024]{1,0:T(8,128)(2,1)S(1)}, bf16[512,1024]{1,0:T(8,128)(2,1)}, u32[]{:S(2)}) copy-start(bf16[512,1024]{1,0:T(8,128)(2,1)} %queries.7) | copy-start | bytes 3145732
  33.9 22.3 %collective-permute-start.8 = (bf16[2,128,1024]{2,1,0:T(8,128)(2,1)S(1)}, bf16[2,128,1024]{2,1,0:T(8,128)(2,1)S(1)}, u32[]{:S(2)}, u32[]{:S(2)}) collective-permute-start(bf16[2,128,1024]{2,1,0:T(8,128)(2,1)S(1)} %get-tuple-element.28), channel_id=1, source_target_pairs={{0,12},{12,0},{4,8},{8,4},{1,13},{13,1},{5,9},{9,5},{2,14},{14,2},... | collective-permute-start | bytes 1572872 | tf_op jit(solution)/shard_map/ppermute | solution.py:329
  35.3 45.0 %collective-permute-start.7 = (bf16[2,128,1024]{2,1,0:T(8,128)(2,1)S(1)}, bf16[2,128,1024]{2,1,0:T(8,128)(2,1)S(1)}, u32[]{:S(2)}, u32[]{:S(2)}) collective-permute-start(bf16[2,128,1024]{2,1,0:T(8,128)(2,1)S(1)} %get-tuple-element.27), channel_id=1, source_target_pairs={{4,12},{8,0},{5,13},{9,1},{6,14},{10,2},{7,15},{11,3},{20,28},{24,... | collective-permute-start | bytes 1572872 | tf_op jit(solution)/shard_map/ppermute | solution.py:329
  45.1 36.7 %collective-permute-start.9 = (bf16[2,128,768]{2,1,0:T(8,128)(2,1)S(1)}, bf16[2,128,768]{2,1,0:T(8,128)(2,1)S(1)}, u32[]{:S(2)}, u32[]{:S(2)}) collective-permute-start(bf16[2,128,768]{2,1,0:T(8,128)(2,1)S(1)} %get-tuple-element.32), channel_id=1, source_target_pairs={{4,8},{8,4},{5,9},{9,5},{6,10},{10,6},{7,11},{11,7},{20,24},{24,20... | collective-permute-start | bytes 1179656 | tf_op jit(solution)/shard_map/ppermute | solution.py:329
  45.8 36.0 %collective-permute-start.5 = (bf16[2,256,256]{2,1,0:T(8,128)(2,1)S(1)}, bf16[2,256,256]{2,1,0:T(8,128)(2,1)S(1)}, u32[]{:S(2)}, u32[]{:S(2)}) collective-permute-start(bf16[2,256,256]{2,1,0:T(8,128)(2,1)S(1)} %get-tuple-element.25), channel_id=1, source_target_pairs={{8,12},{4,0},{9,13},{5,1},{10,14},{6,2},{11,15},{7,3},{24,28},{20,... | collective-permute-start | bytes 786440 | tf_op jit(solution)/shard_map/ppermute | solution.py:329
  56.2 30.6 %collective-permute-start.1 = (bf16[2,128,128]{2,1,0:T(8,128)(2,1)S(1)}, bf16[2,128,128]{2,1,0:T(8,128)(2,1)S(1)}, u32[]{:S(2)}, u32[]{:S(2)}) collective-permute-start(bf16[2,128,128]{2,1,0:T(8,128)(2,1)S(1)} %get-tuple-element.21), channel_id=1, source_target_pairs={{4,8},{8,4},{5,9},{9,5},{6,10},{10,6},{7,11},{11,7},{20,24},{24,20... | collective-permute-start | bytes 196616 | tf_op jit(solution)/shard_map/ppermute | solution.py:329

commit v17 on v15

--- a/solution.py
+++ b/solution.py
@@ -97,87 +97,73 @@
     return pl.ds(pl.multiple_of(block * BLOCK, BLOCK), BLOCK)
 
 
-def stage_near_kernel(half, bands, keys, values, listed, beside, token, sems):
-    frame = lax.axis_index("tm")
-    rows = pl.ds(pl.multiple_of(lax.rem(frame + 1, 2) * half, half), half)
-    near = [
-        pltpu.make_async_copy(source.at[rows], beside.at[kv], sems.at[kv])
-        for kv, source in enumerate((keys, values))
-    ]
+def stage_near_kernel(half, keys, values, facing, beside, token, sems):
+    frame = lax.axis_index("tm")
+    outer = pl.ds(pl.multiple_of(lax.rem(frame + 1, 2) * half, half), half)
+    inner = pl.ds(pl.multiple_of(lax.rem(frame, 2) * half, half), half)
+    token[...] = jnp.zeros_like(token)
+    run_copies(
+        [
+            (source.at[rows], target.at[kv])
+            for target, rows in ((facing, inner), (beside, outer))
+            for kv, source in enumerate((keys, values))
+        ],
+        sems,
+    )
+
+
+def stage_missing_kernel(after, bands, keys, values, missing, sems):
+    frame = lax.axis_index("tm")
 
     @pl.when((frame == 1) | (frame == 2))
     def _():
-        reader = jnp.where(frame == 1, 3, 0)
-        pairs = []
-        for place in range(2):
-            slot = jnp.where(frame == 1, place, 1 - place)
-            rows = rows_of(bands[reader, slot, frame])
-            for kv, source in enumerate((keys, values)):
-                pairs.append((source.at[rows], listed.at[kv, pl.ds(place * BLOCK, BLOCK)]))
-        for copy in near:
-            copy.start()
-        run_copies(pairs, sems.at[pl.ds(2, 4)])
+        rows = rows_of(jnp.where(frame == 1, bands[3, 0, 1], bands[0, 1, 2]))
+        run_copies([(keys.at[rows], missing.at[0]), (values.at[rows], missing.at[1])], sems)
+
+
+def stage_picked_kernel(facing, bands, picked, sems):
+    frame = lax.axis_index("tm")
+
+    @pl.when((frame == 1) | (frame == 2))
+    def _():
+        rows = rows_of(jnp.where(frame == 1, bands[0, 0, 2], bands[3, 1, 1] - 2))
+        run_copies([(facing.at[:, rows], picked)], sems)
+
+
+def stage_crossed_kernel(after, after_too, bands, keys, values, crossed, sems):
+    frame = lax.axis_index("tm")
 
     @pl.when((frame == 0) | (frame == 3))
     def _():
-        for copy in near:
-            copy.start()
-
-    token[...] = jnp.zeros_like(token)
-    for copy in near:
-        copy.wait()
-
-
-def stage_crossed_kernel(after, bands, keys, values, crossed, sems):
+        rows = rows_of(jnp.where(frame == 0, bands[2, 0, 0], bands[1, 1, 3]))
+        run_copies([(keys.at[rows], crossed.at[0]), (values.at[rows], crossed.at[1])], sems)
+
+
+def stage_passed_kernel(beside, bands, passed, sems):
+    frame = lax.axis_index("tm")
+
+    @pl.when((frame == 1) | (frame == 2))
+    def _():
+        rows = rows_of(jnp.where(frame == 1, bands[3, 1, 0] - 2, bands[0, 0, 3]))
+        run_copies([(beside.at[:, rows], passed)], sems)
+
+
+def stage_direct_kernel(after, bands, keys, values, direct, sems):
     frame = lax.axis_index("tm")
 
     @pl.when((frame == 0) | (frame == 3))
     def _():
-        block = jnp.where(frame == 0, bands[2, 0, 0], bands[1, 1, 3])
-        rows = rows_of(block)
-        run_copies([(keys.at[rows], crossed.at[0]), (values.at[rows], crossed.at[1])], sems)
-
-
-def relay_kernel(cuts, listed, *relayed):
+        rows = rows_of(jnp.where(frame == 0, bands[3, 0, 0], bands[0, 1, 3]))
+        run_copies([(keys.at[rows], direct.at[0]), (values.at[rows], direct.at[1])], sems)
+
+
+def stage_traded_kernel(cut, after, beside, bands, traded, sems):
     frame = lax.axis_index("tm")
 
     @pl.when((frame == 1) | (frame == 2))
     def _():
-        for part, cut in zip(relayed, cuts):
-            part[...] = listed[:, :, pl.ds(*cut)]
-
-
-def stage_second_kernel(beside, bands, keys, values, traded, passed, sems):
-    frame = lax.axis_index("tm")
-    inner = (frame == 1) | (frame == 2)
-
-    @pl.when(inner)
-    def _():
-        to_inner = rows_of(jnp.where(frame == 1, bands[2, 1, 0] - 2, bands[1, 0, 3]))
-        to_edge = rows_of(jnp.where(frame == 1, bands[3, 1, 0] - 2, bands[0, 0, 3]))
-        run_copies([(beside.at[:, to_inner], traded), (beside.at[:, to_edge], passed)], sems)
-
-    @pl.when(jnp.logical_not(inner))
-    def _():
-        rows = rows_of(jnp.where(frame == 0, bands[3, 0, 0], bands[0, 1, 3]))
-        run_copies([(keys.at[rows], traded.at[0]), (values.at[rows], traded.at[1])], sems)
-
-
-def stage_closing_kernel(cuts, after, bands, keys, values, *rest):
-    closing, sems = rest[:-1], rest[-1]
-    frame = lax.axis_index("tm")
-
-    @pl.when((frame == 1) | (frame == 2))
-    def _():
-        rows = rows_of(jnp.where(frame == 1, 5 - bands[3, 1, 1], 1 - bands[0, 0, 2]))
-        run_copies(
-            [
-                (source.at[rows, pl.ds(*cut)], part.at[kv])
-                for part, cut in zip(closing, cuts)
-                for kv, source in enumerate((keys, values))
-            ],
-            sems,
-        )
+        rows = rows_of(jnp.where(frame == 1, bands[2, 1, 0] - 2, bands[1, 0, 3]))
+        run_copies([(beside.at[:, rows, pl.ds(*cut)], traded)], sems)
 
 
 RATE = LOG2E * HD ** (-0.5)
@@ -190,7 +176,7 @@
 
 
 def attend_kernel(
-    chunk, queries, keys, values, beside, listed, crossed, traded, mixed, tops, sums
+    chunk, queries, keys, values, beside, facing, crossed, picked, lone, mixed, tops, sums
 ):
     frame = lax.axis_index("tm")
     inner = (frame == 1) | (frame == 2)
@@ -228,17 +214,16 @@
             scores = ahead
 
     def of_inner(kv, cols):
-        listed_there = jnp.concatenate([crossed[kv, :, cols], traded[kv, :, cols]], 0)
-        return [listed_there, listed[kv, pl.ds(BLOCK, BLOCK), cols]]
+        return [facing[kv, :, cols], crossed[kv, :, cols]]
 
     def of_edge(kv, cols):
-        return [traded[kv, :, cols]]
+        return [jnp.concatenate([picked[kv, :, cols], lone[kv, :, cols]], 0)]
 
     pl.when(inner)(lambda: attend(of_inner))
     pl.when(jnp.logical_not(inner))(lambda: attend(of_edge))
 
 
-def close_kernel(first, queries, closing, relayed, passed, mixed, tops, sums, *rest):
+def close_kernel(first, queries, traded, passed, direct, mixed, tops, sums, *rest):
     out, ready, sems = rest[-3:]
     frame = lax.axis_index("tm")
     inner = (frame == 1) | (frame == 2)
@@ -287,10 +272,10 @@
             copy.wait()
 
     def of_inner(kv, here, there):
-        return [closing[kv, :, there]]
+        return [traded[kv, :, there]]
 
     def of_edge(kv, here, there):
-        return [relayed[kv, :, there], passed[kv, :, here]]
+        return [jnp.concatenate([passed[kv, :, here], direct[kv, :, here]], 0)]
 
     pl.when(inner)(lambda: close(of_inner, rows))
     pl.when(jnp.logical_not(inner))(lambda: close(of_edge, rows // 2))
@@ -323,64 +308,66 @@
         )(*operands)
 
     token = jax.ShapeDtypeStruct((8, HD), jnp.int32)
-    listed, beside, after = stage(
+    facing, beside, after = stage(
         functools.partial(stage_near_kernel, half),
         [two, two, token],
-        6,
-        [bands, keys, values],
+        4,
+        [keys, values],
         "stage_near",
         51,
     )
+    (missing,) = stage(
+        stage_missing_kernel, [one], 2, [after, bands, keys, values], "stage_missing", 32
+    )
+    facing = send(facing, [(1, 2), (2, 1)])
+    beside = send(beside, [(0, 1), (1, 0), (2, 3), (3, 2)])
+    missing = send(missing, [(1, 2), (2, 1)])
+    (picked,) = stage(stage_picked_kernel, [one], 1, [facing, bands], "stage_picked", 32)
+    picked = send(picked, [(2, 3), (1, 0)])
+    lone = send(missing, [(2, 3), (1, 0)])
+    (passed,) = stage(stage_passed_kernel, [one], 1, [beside, bands], "stage_passed", 32)
+    passed = send(passed, [(1, 3), (2, 0)])
     (crossed,) = stage(
-        stage_crossed_kernel, [one], 2, [after, bands, keys, values], "stage_crossed", 32
-    )
-    listed = send(listed, [(1, 2), (2, 1)])
-    beside = send(beside, [(0, 1), (1, 0), (2, 3), (3, 2)])
+        stage_crossed_kernel,
+        [one],
+        2,
+        [missing, picked, bands, keys, values],
+        "stage_crossed",
+        32,
+    )
     crossed = send(crossed, [(0, 2), (3, 1)])
     last = heads // 4
     cuts = [(0, heads - last), (heads - last, last)] if last else [(0, heads)]
     cuts = [(start * HD, size * HD) for start, size in cuts]
-
-    def by_heads(blocks):
-        return [jax.ShapeDtypeStruct((2, blocks * BLOCK, size), jnp.bfloat16) for _, size in cuts]
-
-    relayed = pl.pallas_call(
-        functools.partial(relay_kernel, cuts),
-        out_shape=by_heads(2),
-        in_specs=[local],
-        out_specs=[local] * len(cuts),
-        compiler_params=pltpu.CompilerParams(vmem_limit_bytes=32 << 20),
-        name="relay",
-    )(listed)
-    relayed = [send(part, [(2, 3), (1, 0)]) for part in relayed]
-    traded, passed = stage(
-        stage_second_kernel, [one, one], 2, [beside, bands, keys, values], "stage_second", 32
-    )
-    traded = send(traded, [(0, 3), (3, 0), (1, 2), (2, 1)])
-    passed = send(passed, [(1, 3), (2, 0)])
-    closing = stage(
-        functools.partial(stage_closing_kernel, cuts),
-        by_heads(1),
-        2 * len(cuts),
-        [crossed, bands, keys, values],
-        "stage_closing",
-        32,
-    )
-    closing = [send(part, [(1, 2), (2, 1)]) for part in closing]
+    (direct,) = stage(
+        stage_direct_kernel, [one], 2, [missing, bands, keys, values], "stage_direct", 32
+    )
+    direct = send(direct, [(0, 3), (3, 0)])
+    traded = []
+    for cut, before in zip(cuts, (beside, passed)):
+        (part,) = stage(
+            functools.partial(stage_traded_kernel, cut),
+            [jax.ShapeDtypeStruct((2, BLOCK, cut[1]), jnp.bfloat16)],
+            1,
+            [before, beside, bands],
+            "stage_traded",
+            32,
+        )
+        traded.append(send(part, [(1, 2), (2, 1)]))
 
     state = jax.ShapeDtypeStruct((heads, rows, HD), jnp.float32)
     roomy = pltpu.CompilerParams(vmem_limit_bytes=32 << 20)
     mixed, tops, sums = pl.pallas_call(
         functools.partial(attend_kernel, rows // 2),
         out_shape=[state] * 3,
-        in_specs=[local] * 7,
+        in_specs=[local] * 8,
         out_specs=[local] * 3,
         compiler_params=roomy,
         name="attend",
-    )(queries, keys, values, beside, listed, crossed, traded)
+    )(queries, keys, values, beside, facing, crossed, picked, lone)
     result = None
-    for near, far, (start, size) in zip(closing, relayed, cuts):
-        operands = [queries, near, far, passed, mixed, tops, sums]
+    for part, (start, size) in zip(traded, cuts):
+        operands = [queries, part, passed, direct, mixed, tops, sums]
         in_specs = [local] * len(operands)
         aliases = {}
         if result is not None:

time: 89.4 us -> 91.4 us (1.022)
  the two profiles are of different devices: /device:TPU:17 before, /device:TPU:0 now
where the time goes in v17:
time: 91.4 us; the launch traced here: 91.1 us
  waiting for transfers between devices  53.8 us (59%)
  Pallas kernels  18.5 us (20%)
  starting transfers between devices  18.4 us (20%)
    ppermute x10, waiting for transfers between devices, send(): return lax.ppermute(array, 'tm', pairs)  53.8 us
    ppermute x10, starting transfers between devices, send(): return lax.ppermute(array, 'tm', pairs)  18.4 us
    pallas_call x1, Pallas kernels, four_frames(): pl.pallas_call(functools.partial(attend_kernel, rows // 2), out_shape=[st...  6.47 us
    pallas_call x8, Pallas kernels, stage(): pl.pallas_call(kernel, out_shape=shapes, in_specs=[scalars if operand is...  6.18 us
    pallas_call x2, Pallas kernels, four_frames(): pl.pallas_call(functools.partial(close_kernel, start), out_shape=jax.Shap...  5.88 us
  transfers between devices with their start and end apart: 10, of which 3 were waited for; matrix products, arithmetic and copies ran while one was open for 0% of the time, Pallas kernels for 16%

profile of v17, /device:TPU:0, one launch (start us, length us, event | category | flops | bytes accessed | tf_op | source)
XLA Modules:
  0.0 91.1 jit_solution(14276676484672665229)
XLA Ops:
  0.0 1.7 %stage_near.1 = (bf16[2,256,1024]{2,1,0:T(8,128)(2,1)S(1)}, bf16[2,256,1024]{2,1,0:T(8,128)(2,1)S(1)}, s32[8,128]{1,0:T(8,128)S(1)}) custom-call(bf16[512,1024]{1,0:T(8,128)(2,1)} %keys.9, bf16[512,1024]{1,0:T(8,128)(2,1)} %values.9), custom_call_target="tpu_custom_call" | custom-call | tf_op jit(solution)/shard_map/stage_near/pallas_call | solution.py:300
  1.7 0.7 collective-permute-start.5
  2.4 5.9 %collective-permute-start = (bf16[2,256,1024]{2,1,0:T(8,128)(2,1)S(1)}, bf16[2,256,1024]{2,1,0:T(8,128)(2,1)S(1)}, u32[]{:S(2)}, u32[]{:S(2)}) collective-permute-start(bf16[2,256,1024]{2,1,0:T(8,128)(2,1)S(1)} %get-tuple-element.11), channel_id=1, source_target_pairs={{0,4},{4,0},{8,12},{12,8},{1,5},{5,1},{9,13},{13,9},{2,6},{6,2},{1... | collective-permute-start | bytes 3145736 | tf_op jit(solution)/shard_map/ppermute | solution.py:293
  8.3 0.6 stage_missing.1
  9.0 0.7 collective-permute-start.3
  9.7 0.0 collective-permute-done.5.facing
  9.7 0.6 stage_picked.1
  10.3 1.3 %collective-permute-start.6 = (bf16[2,128,1024]{2,1,0:T(8,128)(2,1)S(1)}, bf16[2,128,1024]{2,1,0:T(8,128)(2,1)S(1)}, u32[]{:S(2)}, u32[]{:S(2)}) collective-permute-start(bf16[2,128,1024]{2,1,0:T(8,128)(2,1)S(1)} %stage_picked.1), channel_id=1, source_target_pairs={{8,12},{4,0},{9,13},{5,1},{10,14},{6,2},{11,15},{7,3},{24,28},{20,... | collective-permute-start | bytes 1572872 | tf_op jit(solution)/shard_map/ppermute | solution.py:293
  11.6 19.6 %collective-permute-done.beside.after = bf16[2,256,1024]{2,1,0:T(8,128)(2,1)S(1)} collective-permute-done((bf16[2,256,1024]{2,1,0:T(8,128)(2,1)S(1)}, bf16[2,256,1024]{2,1,0:T(8,128)(2,1)S(1)}, u32[]{:S(2)}, u32[]{:S(2)}) %collective-permute-start) | collective-permute-done | bytes 1048608 | tf_op jit(solution)/shard_map/ppermute | solution.py:293
  31.2 0.6 stage_passed.1
  31.8 1.3 %collective-permute-start.1 = (bf16[2,128,1024]{2,1,0:T(8,128)(2,1)S(1)}, bf16[2,128,1024]{2,1,0:T(8,128)(2,1)S(1)}, u32[]{:S(2)}, u32[]{:S(2)}) collective-permute-start(bf16[2,128,1024]{2,1,0:T(8,128)(2,1)S(1)} %stage_passed.1), channel_id=1, source_target_pairs={{4,12},{8,0},{5,13},{9,1},{6,14},{10,2},{7,15},{11,3},{20,28},{24,... | collective-permute-start | bytes 1572872 | tf_op jit(solution)/shard_map/ppermute | solution.py:293
  33.1 0.0 collective-permute-done.3.after
  33.1 1.3 %collective-permute-start.8 = (bf16[2,128,1024]{2,1,0:T(8,128)(2,1)S(1)}, bf16[2,128,1024]{2,1,0:T(8,128)(2,1)S(1)}, u32[]{:S(2)}, u32[]{:S(2)}) collective-permute-start(bf16[2,128,1024]{2,1,0:T(8,128)(2,1)S(1)} %collective-permute-done.3.after), channel_id=1, source_target_pairs={{8,12},{4,0},{9,13},{5,1},{10,14},{6,2},{11,15},{7,3},{24,28},{20,... | collective-permute-start | bytes 1572872 | tf_op jit(solution)/shard_map/ppermute | solution.py:293
  34.4 18.6 %collective-permute-done.6.after_too.picked = bf16[2,128,1024]{2,1,0:T(8,128)(2,1)S(1)} collective-permute-done((bf16[2,128,1024]{2,1,0:T(8,128)(2,1)S(1)}, bf16[2,128,1024]{2,1,0:T(8,128)(2,1)S(1)}, u32[]{:S(2)}, u32[]{:S(2)}) %collective-permute-start.6) | collective-permute-done | bytes 524320 | tf_op jit(solution)/shard_map/ppermute | solution.py:293
  53.1 0.7 stage_crossed.1
  53.8 2.5 %collective-permute-start.7 = (bf16[2,128,1024]{2,1,0:T(8,128)(2,1)S(1)}, bf16[2,128,1024]{2,1,0:T(8,128)(2,1)S(1)}, u32[]{:S(2)}, u32[]{:S(2)}) collective-permute-start(bf16[2,128,1024]{2,1,0:T(8,128)(2,1)S(1)} %stage_crossed.1), channel_id=1, source_target_pairs={{0,8},{12,4},{1,9},{13,5},{2,10},{14,6},{3,11},{15,7},{16,24},{28,... | collective-permute-start | bytes 1572872 | tf_op jit(solution)/shard_map/ppermute | solution.py:293
  56.2 0.7 stage_direct.1
  56.9 0.0 copy-start.2
  56.9 3.4 %collective-permute-start.4 = (bf16[2,128,1024]{2,1,0:T(8,128)(2,1)S(1)}, bf16[2,128,1024]{2,1,0:T(8,128)(2,1)S(1)}, u32[]{:S(2)}, u32[]{:S(2)}) collective-permute-start(bf16[2,128,1024]{2,1,0:T(8,128)(2,1)S(1)} %stage_direct.1), channel_id=1, source_target_pairs={{0,12},{12,0},{1,13},{13,1},{2,14},{14,2},{3,15},{15,3},{16,28},{2... | collective-permute-start | bytes 1572872 | tf_op jit(solution)/shard_map/ppermute | solution.py:293
  60.3 0.6 stage_traded.3
  60.9 0.7 collective-permute-start.9
  61.6 15.6 %collective-permute-done.1.after.passed = bf16[2,128,1024]{2,1,0:T(8,128)(2,1)S(1)} collective-permute-done((bf16[2,128,1024]{2,1,0:T(8,128)(2,1)S(1)}, bf16[2,128,1024]{2,1,0:T(8,128)(2,1)S(1)}, u32[]{:S(2)}, u32[]{:S(2)}) %collective-permute-start.1) | collective-permute-done | bytes 524320 | tf_op jit(solution)/shard_map/ppermute | solution.py:293
  77.2 0.6 stage_traded.2
  77.8 0.7 collective-permute-start.2
  78.5 0.0 collective-permute-done.8.lone
  78.5 0.0 collective-permute-done.7.crossed
  78.5 6.5 %attend.1 = (f32[8,512,128]{2,1,0:T(8,128)S(1)}, f32[8,512,128]{2,1,0:T(8,128)S(1)}, f32[8,512,128]{2,1,0:T(8,128)S(1)}) custom-call(bf16[512,1024]{1,0:T(8,128)(2,1)S(1)} %copy-done.2, bf16[512,1024]{1,0:T(8,128)(2,1)S(1)} %copy-done, bf16[512,1024]{1,0:T(8,128)(2,1)S(1)} %copy-done.1, bf16[2,256,1024]{2,1,0:T(8,128)(2,1)S(1)} %collective-permute-done.beside.after, ...), custom_call_target="tpu_custom_call" | custom-call | tf_op jit(solution)/shard_map/attend/pallas_call | solution.py:360
  85.0 0.0 collective-permute-done.4.direct
  85.0 0.0 collective-permute-done.9.traded
  85.0 4.0 %close.2.rest_0_ = bf16[512,1024]{1,0:T(8,128)(2,1)} custom-call(bf16[512,1024]{1,0:T(8,128)(2,1)S(1)} %copy-done.2, bf16[2,128,768]{2,1,0:T(8,128)(2,1)S(1)} %collective-permute-done.9.traded, bf16[2,128,1024]{2,1,0:T(8,128)(2,1)S(1)} %collective-permute-done.1.after.passed, bf16[2,128,1024]{2,1,0:T(8,128)(2,1)S(1)} %collective-permute-done.4.direct, ...), custom_call_target="tpu_custom_call" | custom-call | tf_op jit(solution)/shard_map/close/pallas_call | solution.py:377
  89.0 0.0 collective-permute-done.2.traded
  89.0 1.9 %close.3 = bf16[512,1024]{1,0:T(8,128)(2,1)} custom-call(bf16[512,1024]{1,0:T(8,128)(2,1)S(1)} %copy-done.2, bf16[2,128,256]{2,1,0:T(8,128)(2,1)S(1)} %collective-permute-done.2.traded, bf16[2,128,1024]{2,1,0:T(8,128)(2,1)S(1)} %collective-permute-done.1.after.passed, ...), custom_call_target="tpu_custom_call", output_to_operand_aliasing={{}: (7, {})} | custom-call | tf_op jit(solution)/shard_map/close/pallas_call | solution.py:377
  (7 shorter events, 0.0 us)
Async XLA Ops:
  0.0 8.3 %copy-start = (bf16[512,1024]{1,0:T(8,128)(2,1)S(1)}, bf16[512,1024]{1,0:T(8,128)(2,1)}, u32[]{:S(2)}) copy-start(bf16[512,1024]{1,0:T(8,128)(2,1)} %keys.9) | copy-start | bytes 3145732
  0.0 8.3 %copy-start.1 = (bf16[512,1024]{1,0:T(8,128)(2,1)S(1)}, bf16[512,1024]{1,0:T(8,128)(2,1)}, u32[]{:S(2)}) copy-start(bf16[512,1024]{1,0:T(8,128)(2,1)} %values.9) | copy-start | bytes 3145732
  0.0 8.3 %copy-start.3 = (s32[4,4,2]{1,2,0:T(2,128)S(1)}, s32[4,4,2]{1,2,0:T(2,128)}, u32[]{:S(2)}) copy-start(s32[4,4,2]{1,2,0:T(2,128)} %param.7) | copy-start | bytes 388
  1.7 8.0 %collective-permute-start.5 = (bf16[2,256,1024]{2,1,0:T(8,128)(2,1)S(1)}, bf16[2,256,1024]{2,1,0:T(8,128)(2,1)S(1)}, u32[]{:S(2)}, u32[]{:S(2)}) collective-permute-start(bf16[2,256,1024]{2,1,0:T(8,128)(2,1)S(1)} %get-tuple-element.13), channel_id=1, source_target_pairs={{4,8},{8,4},{5,9},{9,5},{6,10},{10,6},{7,11},{11,7},{20,24},{24,20... | collective-permute-start | bytes 3145736 | tf_op jit(solution)/shard_map/ppermute | solution.py:293
  2.4 28.7 %collective-permute-start = (bf16[2,256,1024]{2,1,0:T(8,128)(2,1)S(1)}, bf16[2,256,1024]{2,1,0:T(8,128)(2,1)S(1)}, u32[]{:S(2)}, u32[]{:S(2)}) collective-permute-start(bf16[2,256,1024]{2,1,0:T(8,128)(2,1)S(1)} %get-tuple-element.11), channel_id=1, source_target_pairs={{0,4},{4,0},{8,12},{12,8},{1,5},{5,1},{9,13},{13,9},{2,6},{6,2},{1... | collective-permute-start | bytes 3145736 | tf_op jit(solution)/shard_map/ppermute | solution.py:293
  9.0 24.2 %collective-permute-start.3 = (bf16[2,128,1024]{2,1,0:T(8,128)(2,1)S(1)}, bf16[2,128,1024]{2,1,0:T(8,128)(2,1)S(1)}, u32[]{:S(2)}, u32[]{:S(2)}) collective-permute-start(bf16[2,128,1024]{2,1,0:T(8,128)(2,1)S(1)} %stage_missing.1), channel_id=1, source_target_pairs={{4,8},{8,4},{5,9},{9,5},{6,10},{10,6},{7,11},{11,7},{20,24},{24,20... | collective-permute-start | bytes 1572872 | tf_op jit(solution)/shard_map/ppermute | solution.py:293
  10.3 42.8 %collective-permute-start.6 = (bf16[2,128,1024]{2,1,0:T(8,128)(2,1)S(1)}, bf16[2,128,1024]{2,1,0:T(8,128)(2,1)S(1)}, u32[]{:S(2)}, u32[]{:S(2)}) collective-permute-start(bf16[2,128,1024]{2,1,0:T(8,128)(2,1)S(1)} %stage_picked.1), channel_id=1, source_target_pairs={{8,12},{4,0},{9,13},{5,1},{10,14},{6,2},{11,15},{7,3},{24,28},{20,... | collective-permute-start | bytes 1572872 | tf_op jit(solution)/shard_map/ppermute | solution.py:293
  31.8 45.4 %collective-permute-start.1 = (bf16[2,128,1024]{2,1,0:T(8,128)(2,1)S(1)}, bf16[2,128,1024]{2,1,0:T(8,128)(2,1)S(1)}, u32[]{:S(2)}, u32[]{:S(2)}) collective-permute-start(bf16[2,128,1024]{2,1,0:T(8,128)(2,1)S(1)} %stage_passed.1), channel_id=1, source_target_pairs={{4,12},{8,0},{5,13},{9,1},{6,14},{10,2},{7,15},{11,3},{20,28},{24,... | collective-permute-start | bytes 1572872 | tf_op jit(solution)/shard_map/ppermute | solution.py:293
  33.1 45.4 %collective-permute-start.8 = (bf16[2,128,1024]{2,1,0:T(8,128)(2,1)S(1)}, bf16[2,128,1024]{2,1,0:T(8,128)(2,1)S(1)}, u32[]{:S(2)}, u32[]{:S(2)}) collective-permute-start(bf16[2,128,1024]{2,1,0:T(8,128)(2,1)S(1)} %collective-permute-done.3.after), channel_id=1, source_target_pairs={{8,12},{4,0},{9,13},{5,1},{10,14},{6,2},{11,15},{7,3},{24,28},{20,... | collective-permute-start | bytes 1572872 | tf_op jit(solution)/shard_map/ppermute | solution.py:293
  53.8 24.8 %collective-permute-start.7 = (bf16[2,128,1024]{2,1,0:T(8,128)(2,1)S(1)}, bf16[2,128,1024]{2,1,0:T(8,128)(2,1)S(1)}, u32[]{:S(2)}, u32[]{:S(2)}) collective-permute-start(bf16[2,128,1024]{2,1,0:T(8,128)(2,1)S(1)} %stage_crossed.1), channel_id=1, source_target_pairs={{0,8},{12,4},{1,9},{13,5},{2,10},{14,6},{3,11},{15,7},{16,24},{28,... | collective-permute-start | bytes 1572872 | tf_op jit(solution)/shard_map/ppermute | solution.py:293
  56.9 21.6 %copy-start.2 = (bf16[512,1024]{1,0:T(8,128)(2,1)S(1)}, bf16[512,1024]{1,0:T(8,128)(2,1)}, u32[]{:S(2)}) copy-start(bf16[512,1024]{1,0:T(8,128)(2,1)} %queries.5) | copy-start | bytes 3145732
  56.9 28.1 %collective-permute-start.4 = (bf16[2,128,1024]{2,1,0:T(8,128)(2,1)S(1)}, bf16[2,128,1024]{2,1,0:T(8,128)(2,1)S(1)}, u32[]{:S(2)}, u32[]{:S(2)}) collective-permute-start(bf16[2,128,1024]{2,1,0:T(8,128)(2,1)S(1)} %stage_direct.1), channel_id=1, source_target_pairs={{0,12},{12,0},{1,13},{13,1},{2,14},{14,2},{3,15},{15,3},{16,28},{2... | collective-permute-start | bytes 1572872 | tf_op jit(solution)/shard_map/ppermute | solution.py:293
  60.9 24.1 %collective-permute-start.9 = (bf16[2,128,768]{2,1,0:T(8,128)(2,1)S(1)}, bf16[2,128,768]{2,1,0:T(8,128)(2,1)S(1)}, u32[]{:S(2)}, u32[]{:S(2)}) collective-permute-start(bf16[2,128,768]{2,1,0:T(8,128)(2,1)S(1)} %stage_traded.3), channel_id=1, source_target_pairs={{4,8},{8,4},{5,9},{9,5},{6,10},{10,6},{7,11},{11,7},{20,24},{24,20... | collective-permute-start | bytes 1179656 | tf_op jit(solution)/shard_map/ppermute | solution.py:293
  77.8 11.2 %collective-permute-start.2 = (bf16[2,128,256]{2,1,0:T(8,128)(2,1)S(1)}, bf16[2,128,256]{2,1,0:T(8,128)(2,1)S(1)}, u32[]{:S(2)}, u32[]{:S(2)}) collective-permute-start(bf16[2,128,256]{2,1,0:T(8,128)(2,1)S(1)} %stage_traded.2), channel_id=1, source_target_pairs={{4,8},{8,4},{5,9},{9,5},{6,10},{10,6},{7,11},{11,7},{20,24},{24,20... | collective-permute-start | bytes 393224 | tf_op jit(solution)/shard_map/ppermute | solution.py:293

commit v18 on v17

--- a/solution.py
+++ b/solution.py
@@ -157,7 +157,7 @@
         run_copies([(keys.at[rows], direct.at[0]), (values.at[rows], direct.at[1])], sems)
 
 
-def stage_traded_kernel(cut, after, beside, bands, traded, sems):
+def stage_traded_kernel(cut, after, after_too, beside, bands, traded, sems):
     frame = lax.axis_index("tm")
 
     @pl.when((frame == 1) | (frame == 2))
@@ -176,7 +176,7 @@
 
 
 def attend_kernel(
-    chunk, queries, keys, values, beside, facing, crossed, picked, lone, mixed, tops, sums
+    chunk, queries, keys, values, beside, facing, mixed, tops, sums
 ):
     frame = lax.axis_index("tm")
     inner = (frame == 1) | (frame == 2)
@@ -213,17 +213,13 @@
             finish(*unit, scores)
             scores = ahead
 
-    def of_inner(kv, cols):
-        return [facing[kv, :, cols], crossed[kv, :, cols]]
-
-    def of_edge(kv, cols):
-        return [jnp.concatenate([picked[kv, :, cols], lone[kv, :, cols]], 0)]
-
-    pl.when(inner)(lambda: attend(of_inner))
-    pl.when(jnp.logical_not(inner))(lambda: attend(of_edge))
-
-
-def close_kernel(first, queries, traded, passed, direct, mixed, tops, sums, *rest):
+    pl.when(inner)(lambda: attend(lambda kv, cols: [facing[kv, :, cols]]))
+    pl.when(jnp.logical_not(inner))(lambda: attend(lambda kv, cols: []))
+
+
+def close_kernel(
+    first, queries, traded, crossed, picked, lone, passed, direct, mixed, tops, sums, *rest
+):
     out, ready, sems = rest[-3:]
     frame = lax.axis_index("tm")
     inner = (frame == 1) | (frame == 2)
@@ -272,12 +268,13 @@
             copy.wait()
 
     def of_inner(kv, here, there):
-        return [traded[kv, :, there]]
+        return [jnp.concatenate([crossed[kv, :, here], traded[kv, :, there]], 0)]
 
     def of_edge(kv, here, there):
-        return [jnp.concatenate([passed[kv, :, here], direct[kv, :, here]], 0)]
-
-    pl.when(inner)(lambda: close(of_inner, rows))
+        pairs = (picked, lone), (passed, direct)
+        return [jnp.concatenate([part[kv, :, here] for part in pair], 0) for pair in pairs]
+
+    pl.when(inner)(lambda: close(of_inner, rows // 2))
     pl.when(jnp.logical_not(inner))(lambda: close(of_edge, rows // 2))
 
 
@@ -343,31 +340,31 @@
         stage_direct_kernel, [one], 2, [missing, bands, keys, values], "stage_direct", 32
     )
     direct = send(direct, [(0, 3), (3, 0)])
-    traded = []
-    for cut, before in zip(cuts, (beside, passed)):
-        (part,) = stage(
-            functools.partial(stage_traded_kernel, cut),
-            [jax.ShapeDtypeStruct((2, BLOCK, cut[1]), jnp.bfloat16)],
-            1,
-            [before, beside, bands],
-            "stage_traded",
-            32,
-        )
-        traded.append(send(part, [(1, 2), (2, 1)]))
-
     state = jax.ShapeDtypeStruct((heads, rows, HD), jnp.float32)
     roomy = pltpu.CompilerParams(vmem_limit_bytes=32 << 20)
     mixed, tops, sums = pl.pallas_call(
         functools.partial(attend_kernel, rows // 2),
         out_shape=[state] * 3,
-        in_specs=[local] * 8,
+        in_specs=[local] * 5,
         out_specs=[local] * 3,
         compiler_params=roomy,
         name="attend",
-    )(queries, keys, values, beside, facing, crossed, picked, lone)
+    )(queries, keys, values, beside, facing)
+    traded = []
+    for cut, before in zip(cuts, ((beside, beside), (passed, sums))):
+        (part,) = stage(
+            functools.partial(stage_traded_kernel, cut),
+            [jax.ShapeDtypeStruct((2, BLOCK, cut[1]), jnp.bfloat16)],
+            1,
+            [*before, beside, bands],
+            "stage_traded",
+            32,
+        )
+        traded.append(send(part, [(1, 2), (2, 1)]))
+
     result = None
     for part, (start, size) in zip(traded, cuts):
-        operands = [queries, part, passed, direct, mixed, tops, sums]
+        operands = [queries, part, crossed, picked, lone, passed, direct, mixed, tops, sums]
         in_specs = [local] * len(operands)
         aliases = {}
         if result is not None:

time: 91.4 us -> 89.9 us (0.984)
  the two profiles are of different devices: /device:TPU:0 before, /device:TPU:12 now
where the time goes in v18:
time: 89.9 us; the launch traced here: 89.7 us
  waiting for transfers between devices  52.5 us (58%)
  Pallas kernels  18.9 us (21%)
  starting transfers between devices  17.8 us (20%)
    ppermute x10, waiting for transfers between devices, send(): return lax.ppermute(array, 'tm', pairs)  52.5 us
    ppermute x10, starting transfers between devices, send(): return lax.ppermute(array, 'tm', pairs)  17.8 us
    pallas_call x1, Pallas kernels, four_frames(): pl.pallas_call(functools.partial(attend_kernel, rows // 2), out_shape=[st...  6.47 us
    pallas_call x8, Pallas kernels, stage(): pl.pallas_call(kernel, out_shape=shapes, in_specs=[scalars if operand is...  6.29 us
    pallas_call x2, Pallas kernels, four_frames(): pl.pallas_call(functools.partial(close_kernel, start), out_shape=jax.Shap...  6.1 us
  transfers between devices with their start and end apart: 10, of which 4 were waited for; matrix products, arithmetic and copies ran while one was open for 0% of the time, Pallas kernels for 17%

profile of v18, /device:TPU:12, one launch (start us, length us, event | category | flops | bytes accessed | tf_op | source)
XLA Modules:
  0.0 89.7 jit_solution(3798864542841765864)
XLA Ops:
  0.0 1.7 %stage_near.1 = (bf16[2,256,1024]{2,1,0:T(8,128)(2,1)S(1)}, bf16[2,256,1024]{2,1,0:T(8,128)(2,1)S(1)}, s32[8,128]{1,0:T(8,128)S(1)}) custom-call(bf16[512,1024]{1,0:T(8,128)(2,1)} %keys.9, bf16[512,1024]{1,0:T(8,128)(2,1)} %values.9), custom_call_target="tpu_custom_call" | custom-call | tf_op jit(solution)/shard_map/stage_near/pallas_call | solution.py:297
  1.7 3.5 %collective-permute-start.2 = (bf16[2,256,1024]{2,1,0:T(8,128)(2,1)S(1)}, bf16[2,256,1024]{2,1,0:T(8,128)(2,1)S(1)}, u32[]{:S(2)}, u32[]{:S(2)}) collective-permute-start(bf16[2,256,1024]{2,1,0:T(8,128)(2,1)S(1)} %get-tuple-element.12), channel_id=1, source_target_pairs={{4,8},{8,4},{5,9},{9,5},{6,10},{10,6},{7,11},{11,7},{20,24},{24,20... | collective-permute-start | bytes 3145736 | tf_op jit(solution)/shard_map/ppermute | solution.py:290
  5.2 0.1 collective-permute-start
  5.3 0.7 stage_missing.1
  6.0 2.4 %collective-permute-start.4 = (bf16[2,128,1024]{2,1,0:T(8,128)(2,1)S(1)}, bf16[2,128,1024]{2,1,0:T(8,128)(2,1)S(1)}, u32[]{:S(2)}, u32[]{:S(2)}) collective-permute-start(bf16[2,128,1024]{2,1,0:T(8,128)(2,1)S(1)} %stage_missing.1), channel_id=1, source_target_pairs={{4,8},{8,4},{5,9},{9,5},{6,10},{10,6},{7,11},{11,7},{20,24},{24,20... | collective-permute-start | bytes 1572872 | tf_op jit(solution)/shard_map/ppermute | solution.py:290
  8.4 21.3 %collective-permute-done.2.facing = bf16[2,256,1024]{2,1,0:T(8,128)(2,1)S(1)} collective-permute-done((bf16[2,256,1024]{2,1,0:T(8,128)(2,1)S(1)}, bf16[2,256,1024]{2,1,0:T(8,128)(2,1)S(1)}, u32[]{:S(2)}, u32[]{:S(2)}) %collective-permute-start.2) | collective-permute-done | bytes 1048608 | tf_op jit(solution)/shard_map/ppermute | solution.py:290
  29.7 0.7 stage_picked.1
  30.3 1.3 %collective-permute-start.5 = (bf16[2,128,1024]{2,1,0:T(8,128)(2,1)S(1)}, bf16[2,128,1024]{2,1,0:T(8,128)(2,1)S(1)}, u32[]{:S(2)}, u32[]{:S(2)}) collective-permute-start(bf16[2,128,1024]{2,1,0:T(8,128)(2,1)S(1)} %stage_picked.1), channel_id=1, source_target_pairs={{8,12},{4,0},{9,13},{5,1},{10,14},{6,2},{11,15},{7,3},{24,28},{20,... | collective-permute-start | bytes 1572872 | tf_op jit(solution)/shard_map/ppermute | solution.py:290
  31.7 0.0 collective-permute-done.beside.after.after_too
  31.7 0.7 stage_passed.1
  32.4 1.3 %collective-permute-start.1 = (bf16[2,128,1024]{2,1,0:T(8,128)(2,1)S(1)}, bf16[2,128,1024]{2,1,0:T(8,128)(2,1)S(1)}, u32[]{:S(2)}, u32[]{:S(2)}) collective-permute-start(bf16[2,128,1024]{2,1,0:T(8,128)(2,1)S(1)} %stage_passed.1), channel_id=1, source_target_pairs={{4,12},{8,0},{5,13},{9,1},{6,14},{10,2},{7,15},{11,3},{20,28},{24,... | collective-permute-start | bytes 1572872 | tf_op jit(solution)/shard_map/ppermute | solution.py:290
  33.7 18.5 %collective-permute-done.4.after = bf16[2,128,1024]{2,1,0:T(8,128)(2,1)S(1)} collective-permute-done((bf16[2,128,1024]{2,1,0:T(8,128)(2,1)S(1)}, bf16[2,128,1024]{2,1,0:T(8,128)(2,1)S(1)}, u32[]{:S(2)}, u32[]{:S(2)}) %collective-permute-start.4) | collective-permute-done | bytes 524320 | tf_op jit(solution)/shard_map/ppermute | solution.py:290
  52.1 0.6 stage_direct.1
  52.8 0.7 collective-permute-start.8
  53.5 1.3 %collective-permute-start.7 = (bf16[2,128,1024]{2,1,0:T(8,128)(2,1)S(1)}, bf16[2,128,1024]{2,1,0:T(8,128)(2,1)S(1)}, u32[]{:S(2)}, u32[]{:S(2)}) collective-permute-start(bf16[2,128,1024]{2,1,0:T(8,128)(2,1)S(1)} %collective-permute-done.4.after), channel_id=1, source_target_pairs={{8,12},{4,0},{9,13},{5,1},{10,14},{6,2},{11,15},{7,3},{24,28},{20,... | collective-permute-start | bytes 1572872 | tf_op jit(solution)/shard_map/ppermute | solution.py:290
  54.8 7.5 %collective-permute-done.5.after_too.picked = bf16[2,128,1024]{2,1,0:T(8,128)(2,1)S(1)} collective-permute-done((bf16[2,128,1024]{2,1,0:T(8,128)(2,1)S(1)}, bf16[2,128,1024]{2,1,0:T(8,128)(2,1)S(1)}, u32[]{:S(2)}, u32[]{:S(2)}) %collective-permute-start.5) | collective-permute-done | bytes 524320 | tf_op jit(solution)/shard_map/ppermute | solution.py:290
  62.3 0.6 stage_crossed.1
  63.0 0.0 copy-start.2
  63.0 1.4 %collective-permute-start.6 = (bf16[2,128,1024]{2,1,0:T(8,128)(2,1)S(1)}, bf16[2,128,1024]{2,1,0:T(8,128)(2,1)S(1)}, u32[]{:S(2)}, u32[]{:S(2)}) collective-permute-start(bf16[2,128,1024]{2,1,0:T(8,128)(2,1)S(1)} %stage_crossed.1), channel_id=1, source_target_pairs={{0,8},{12,4},{1,9},{13,5},{2,10},{14,6},{3,11},{15,7},{16,24},{28,... | collective-permute-start | bytes 1572872 | tf_op jit(solution)/shard_map/ppermute | solution.py:290
  64.4 0.7 stage_traded.3
  65.1 3.5 %collective-permute-start.9 = (bf16[2,128,768]{2,1,0:T(8,128)(2,1)S(1)}, bf16[2,128,768]{2,1,0:T(8,128)(2,1)S(1)}, u32[]{:S(2)}, u32[]{:S(2)}) collective-permute-start(bf16[2,128,768]{2,1,0:T(8,128)(2,1)S(1)} %stage_traded.3), channel_id=1, source_target_pairs={{4,8},{8,4},{5,9},{9,5},{6,10},{10,6},{7,11},{11,7},{20,24},{24,20... | collective-permute-start | bytes 1179656 | tf_op jit(solution)/shard_map/ppermute | solution.py:290
  68.6 6.5 %attend.1 = (f32[8,512,128]{2,1,0:T(8,128)S(1)}, f32[8,512,128]{2,1,0:T(8,128)S(1)}, f32[8,512,128]{2,1,0:T(8,128)S(1)}) custom-call(bf16[512,1024]{1,0:T(8,128)(2,1)S(1)} %copy-done.2, bf16[512,1024]{1,0:T(8,128)(2,1)S(1)} %copy-done, bf16[512,1024]{1,0:T(8,128)(2,1)S(1)} %copy-done.1, ...), custom_call_target="tpu_custom_call" | custom-call | tf_op jit(solution)/shard_map/attend/pallas_call | solution.py:345
  75.1 0.0 collective-permute-done.1.after.passed
  75.1 0.6 stage_traded.2
  75.7 2.4 %collective-permute-start.3 = (bf16[2,128,256]{2,1,0:T(8,128)(2,1)S(1)}, bf16[2,128,256]{2,1,0:T(8,128)(2,1)S(1)}, u32[]{:S(2)}, u32[]{:S(2)}) collective-permute-start(bf16[2,128,256]{2,1,0:T(8,128)(2,1)S(1)} %stage_traded.2), channel_id=1, source_target_pairs={{4,8},{8,4},{5,9},{9,5},{6,10},{10,6},{7,11},{11,7},{20,24},{24,20... | collective-permute-start | bytes 393224 | tf_op jit(solution)/shard_map/ppermute | solution.py:290
  78.1 0.0 collective-permute-done.7.lone
  78.1 0.0 collective-permute-done.8.direct
  78.1 5.3 %collective-permute-done.9.traded = bf16[2,128,768]{2,1,0:T(8,128)(2,1)S(1)} collective-permute-done((bf16[2,128,768]{2,1,0:T(8,128)(2,1)S(1)}, bf16[2,128,768]{2,1,0:T(8,128)(2,1)S(1)}, u32[]{:S(2)}, u32[]{:S(2)}) %collective-permute-start.9) | collective-permute-done | bytes 393248 | tf_op jit(solution)/shard_map/ppermute | solution.py:290
  83.4 0.0 collective-permute-done.6.crossed
  83.4 4.0 %close.2.rest_0_ = bf16[512,1024]{1,0:T(8,128)(2,1)} custom-call(bf16[512,1024]{1,0:T(8,128)(2,1)S(1)} %copy-done.2, bf16[2,128,768]{2,1,0:T(8,128)(2,1)S(1)} %collective-permute-done.9.traded, bf16[2,128,1024]{2,1,0:T(8,128)(2,1)S(1)} %collective-permute-done.6.crossed, bf16[2,128,1024]{2,1,0:T(8,128)(2,1)S(1)} %collective-permute-done.5.after_too.picked, ...), custom_call_target="tpu_custom_call" | custom-call | tf_op jit(solution)/shard_map/close/pallas_call | solution.py:374
  87.3 0.0 collective-permute-done.3.traded
  87.4 2.1 %close.3 = bf16[512,1024]{1,0:T(8,128)(2,1)} custom-call(bf16[512,1024]{1,0:T(8,128)(2,1)S(1)} %copy-done.2, bf16[2,128,256]{2,1,0:T(8,128)(2,1)S(1)} %collective-permute-done.3.traded, bf16[2,128,1024]{2,1,0:T(8,128)(2,1)S(1)} %collective-permute-done.6.crossed, ...), custom_call_target="tpu_custom_call", output_to_operand_aliasing={{}: (10, {})} | custom-call | tf_op jit(solution)/shard_map/close/pallas_call | solution.py:374
  (7 shorter events, 0.0 us)
Async XLA Ops:
  0.0 5.3 %copy-start = (bf16[512,1024]{1,0:T(8,128)(2,1)S(1)}, bf16[512,1024]{1,0:T(8,128)(2,1)}, u32[]{:S(2)}) copy-start(bf16[512,1024]{1,0:T(8,128)(2,1)} %keys.9) | copy-start | bytes 3145732
  0.0 5.3 %copy-start.1 = (bf16[512,1024]{1,0:T(8,128)(2,1)S(1)}, bf16[512,1024]{1,0:T(8,128)(2,1)}, u32[]{:S(2)}) copy-start(bf16[512,1024]{1,0:T(8,128)(2,1)} %values.9) | copy-start | bytes 3145732
  0.0 5.3 %copy-start.3 = (s32[4,4,2]{1,2,0:T(2,128)S(1)}, s32[4,4,2]{1,2,0:T(2,128)}, u32[]{:S(2)}) copy-start(s32[4,4,2]{1,2,0:T(2,128)} %param.7) | copy-start | bytes 388
  1.7 27.9 %collective-permute-start.2 = (bf16[2,256,1024]{2,1,0:T(8,128)(2,1)S(1)}, bf16[2,256,1024]{2,1,0:T(8,128)(2,1)S(1)}, u32[]{:S(2)}, u32[]{:S(2)}) collective-permute-start(bf16[2,256,1024]{2,1,0:T(8,128)(2,1)S(1)} %get-tuple-element.12), channel_id=1, source_target_pairs={{4,8},{8,4},{5,9},{9,5},{6,10},{10,6},{7,11},{11,7},{20,24},{24,20... | collective-permute-start | bytes 3145736 | tf_op jit(solution)/shard_map/ppermute | solution.py:290
  5.2 26.5 %collective-permute-start = (bf16[2,256,1024]{2,1,0:T(8,128)(2,1)S(1)}, bf16[2,256,1024]{2,1,0:T(8,128)(2,1)S(1)}, u32[]{:S(2)}, u32[]{:S(2)}) collective-permute-start(bf16[2,256,1024]{2,1,0:T(8,128)(2,1)S(1)} %get-tuple-element.11), channel_id=1, source_target_pairs={{0,4},{4,0},{8,12},{12,8},{1,5},{5,1},{9,13},{13,9},{2,6},{6,2},{1... | collective-permute-start | bytes 3145736 | tf_op jit(solution)/shard_map/ppermute | solution.py:290
  6.0 46.1 %collective-permute-start.4 = (bf16[2,128,1024]{2,1,0:T(8,128)(2,1)S(1)}, bf16[2,128,1024]{2,1,0:T(8,128)(2,1)S(1)}, u32[]{:S(2)}, u32[]{:S(2)}) collective-permute-start(bf16[2,128,1024]{2,1,0:T(8,128)(2,1)S(1)} %stage_missing.1), channel_id=1, source_target_pairs={{4,8},{8,4},{5,9},{9,5},{6,10},{10,6},{7,11},{11,7},{20,24},{24,20... | collective-permute-start | bytes 1572872 | tf_op jit(solution)/shard_map/ppermute | solution.py:290
  30.3 32.0 %collective-permute-start.5 = (bf16[2,128,1024]{2,1,0:T(8,128)(2,1)S(1)}, bf16[2,128,1024]{2,1,0:T(8,128)(2,1)S(1)}, u32[]{:S(2)}, u32[]{:S(2)}) collective-permute-start(bf16[2,128,1024]{2,1,0:T(8,128)(2,1)S(1)} %stage_picked.1), channel_id=1, source_target_pairs={{8,12},{4,0},{9,13},{5,1},{10,14},{6,2},{11,15},{7,3},{24,28},{20,... | collective-permute-start | bytes 1572872 | tf_op jit(solution)/shard_map/ppermute | solution.py:290
  32.4 42.7 %collective-permute-start.1 = (bf16[2,128,1024]{2,1,0:T(8,128)(2,1)S(1)}, bf16[2,128,1024]{2,1,0:T(8,128)(2,1)S(1)}, u32[]{:S(2)}, u32[]{:S(2)}) collective-permute-start(bf16[2,128,1024]{2,1,0:T(8,128)(2,1)S(1)} %stage_passed.1), channel_id=1, source_target_pairs={{4,12},{8,0},{5,13},{9,1},{6,14},{10,2},{7,15},{11,3},{20,28},{24,... | collective-permute-start | bytes 1572872 | tf_op jit(solution)/shard_map/ppermute | solution.py:290
  52.8 25.3 %collective-permute-start.8 = (bf16[2,128,1024]{2,1,0:T(8,128)(2,1)S(1)}, bf16[2,128,1024]{2,1,0:T(8,128)(2,1)S(1)}, u32[]{:S(2)}, u32[]{:S(2)}) collective-permute-start(bf16[2,128,1024]{2,1,0:T(8,128)(2,1)S(1)} %stage_direct.1), channel_id=1, source_target_pairs={{0,12},{12,0},{1,13},{13,1},{2,14},{14,2},{3,15},{15,3},{16,28},{2... | collective-permute-start | bytes 1572872 | tf_op jit(solution)/shard_map/ppermute | solution.py:290
  53.5 24.6 %collective-permute-start.7 = (bf16[2,128,1024]{2,1,0:T(8,128)(2,1)S(1)}, bf16[2,128,1024]{2,1,0:T(8,128)(2,1)S(1)}, u32[]{:S(2)}, u32[]{:S(2)}) collective-permute-start(bf16[2,128,1024]{2,1,0:T(8,128)(2,1)S(1)} %collective-permute-done.4.after), channel_id=1, source_target_pairs={{8,12},{4,0},{9,13},{5,1},{10,14},{6,2},{11,15},{7,3},{24,28},{20,... | collective-permute-start | bytes 1572872 | tf_op jit(solution)/shard_map/ppermute | solution.py:290
  63.0 5.6 %copy-start.2 = (bf16[512,1024]{1,0:T(8,128)(2,1)S(1)}, bf16[512,1024]{1,0:T(8,128)(2,1)}, u32[]{:S(2)}) copy-start(bf16[512,1024]{1,0:T(8,128)(2,1)} %queries.5) | copy-start | bytes 3145732
  63.0 20.4 %collective-permute-start.6 = (bf16[2,128,1024]{2,1,0:T(8,128)(2,1)S(1)}, bf16[2,128,1024]{2,1,0:T(8,128)(2,1)S(1)}, u32[]{:S(2)}, u32[]{:S(2)}) collective-permute-start(bf16[2,128,1024]{2,1,0:T(8,128)(2,1)S(1)} %stage_crossed.1), channel_id=1, source_target_pairs={{0,8},{12,4},{1,9},{13,5},{2,10},{14,6},{3,11},{15,7},{16,24},{28,... | collective-permute-start | bytes 1572872 | tf_op jit(solution)/shard_map/ppermute | solution.py:290
  65.1 18.3 %collective-permute-start.9 = (bf16[2,128,768]{2,1,0:T(8,128)(2,1)S(1)}, bf16[2,128,768]{2,1,0:T(8,128)(2,1)S(1)}, u32[]{:S(2)}, u32[]{:S(2)}) collective-permute-start(bf16[2,128,768]{2,1,0:T(8,128)(2,1)S(1)} %stage_traded.3), channel_id=1, source_target_pairs={{4,8},{8,4},{5,9},{9,5},{6,10},{10,6},{7,11},{11,7},{20,24},{24,20... | collective-permute-start | bytes 1179656 | tf_op jit(solution)/shard_map/ppermute | solution.py:290
  75.7 11.6 %collective-permute-start.3 = (bf16[2,128,256]{2,1,0:T(8,128)(2,1)S(1)}, bf16[2,128,256]{2,1,0:T(8,128)(2,1)S(1)}, u32[]{:S(2)}, u32[]{:S(2)}) collective-permute-start(bf16[2,128,256]{2,1,0:T(8,128)(2,1)S(1)} %stage_traded.2), channel_id=1, source_target_pairs={{4,8},{8,4},{5,9},{9,5},{6,10},{10,6},{7,11},{11,7},{20,24},{24,20... | collective-permute-start | bytes 393224 | tf_op jit(solution)/shard_map/ppermute | solution.py:290

commit v19 on v18

--- a/solution.py
+++ b/solution.py
@@ -217,9 +217,40 @@
     pl.when(jnp.logical_not(inner))(lambda: attend(lambda kv, cols: []))
 
 
-def close_kernel(
-    first, queries, traded, crossed, picked, lone, passed, direct, mixed, tops, sums, *rest
-):
+def merge_kernel(chunk, queries, crossed, picked, lone, mixed, tops, sums, *state):
+    frame = lax.axis_index("tm")
+    inner = (frame == 1) | (frame == 2)
+    rows, columns = queries.shape
+    new_mixed, new_tops, new_sums = state
+
+    def merge(piece):
+        for head in range(columns // HD):
+            cols = pl.ds(head * HD, HD)
+            for start in range(0, rows, chunk):
+                at = pl.ds(start, chunk)
+                scores = scores_of(queries[at, cols], piece(0, cols))
+                old_top = tops[head, at]
+                top = jnp.maximum(old_top, jnp.max(scores, axis=1, keepdims=True))
+                shrink = jnp.exp2((old_top - top) * RATE)
+                powers = jnp.exp2((scores - top[:, :1]) * RATE)
+                row_sum = jnp.sum(powers, axis=1, keepdims=True)
+                more = jnp.dot(
+                    powers.astype(jnp.bfloat16),
+                    piece(1, cols),
+                    preferred_element_type=jnp.float32,
+                )
+                new_mixed[head, at] = mixed[head, at] * shrink + more
+                new_tops[head, at] = top
+                new_sums[head, at] = sums[head, at] * shrink + row_sum
+
+    def of_edge(kv, cols):
+        return jnp.concatenate([picked[kv, :, cols], lone[kv, :, cols]], 0)
+
+    pl.when(inner)(lambda: merge(lambda kv, cols: crossed[kv, :, cols]))
+    pl.when(jnp.logical_not(inner))(lambda: merge(of_edge))
+
+
+def close_kernel(first, queries, traded, passed, direct, mixed, tops, sums, *rest):
     out, ready, sems = rest[-3:]
     frame = lax.axis_index("tm")
     inner = (frame == 1) | (frame == 2)
@@ -268,13 +299,12 @@
             copy.wait()
 
     def of_inner(kv, here, there):
-        return [jnp.concatenate([crossed[kv, :, here], traded[kv, :, there]], 0)]
+        return [traded[kv, :, there]]
 
     def of_edge(kv, here, there):
-        pairs = (picked, lone), (passed, direct)
-        return [jnp.concatenate([part[kv, :, here] for part in pair], 0) for pair in pairs]
-
-    pl.when(inner)(lambda: close(of_inner, rows // 2))
+        return [jnp.concatenate([passed[kv, :, here], direct[kv, :, here]], 0)]
+
+    pl.when(inner)(lambda: close(of_inner, rows))
     pl.when(jnp.logical_not(inner))(lambda: close(of_edge, rows // 2))
 
 
@@ -337,7 +367,7 @@
     cuts = [(0, heads - last), (heads - last, last)] if last else [(0, heads)]
     cuts = [(start * HD, size * HD) for start, size in cuts]
     (direct,) = stage(
-        stage_direct_kernel, [one], 2, [missing, bands, keys, values], "stage_direct", 32
+        stage_direct_kernel, [one], 2, [picked, bands, keys, values], "stage_direct", 32
     )
     direct = send(direct, [(0, 3), (3, 0)])
     state = jax.ShapeDtypeStruct((heads, rows, HD), jnp.float32)
@@ -362,9 +392,17 @@
         )
         traded.append(send(part, [(1, 2), (2, 1)]))
 
+    mixed, tops, sums = pl.pallas_call(
+        functools.partial(merge_kernel, rows // 2),
+        out_shape=[state] * 3,
+        in_specs=[local] * 7,
+        out_specs=[local] * 3,
+        compiler_params=roomy,
+        name="merge",
+    )(queries, crossed, picked, lone, mixed, tops, sums)
     result = None
     for part, (start, size) in zip(traded, cuts):
-        operands = [queries, part, crossed, picked, lone, passed, direct, mixed, tops, sums]
+        operands = [queries, part, passed, direct, mixed, tops, sums]
         in_specs = [local] * len(operands)
         aliases = {}
         if result is not None:

time: 89.9 us -> 91.1 us (1.013)
  the two profiles are of different devices: /device:TPU:12 before, /device:TPU:0 now
where the time goes in v19:
time: 91.1 us; the launch traced here: 90.8 us
  waiting for transfers between devices  48.8 us (54%)
  Pallas kernels  23.2 us (25%)
  starting transfers between devices  18.4 us (20%)
    ppermute x10, waiting for transfers between devices, send(): return lax.ppermute(array, 'tm', pairs)  48.8 us
    ppermute x10, starting transfers between devices, send(): return lax.ppermute(array, 'tm', pairs)  18.4 us
    pallas_call x8, Pallas kernels, stage(): pl.pallas_call(kernel, out_shape=shapes, in_specs=[scalars if operand is...  6.18 us
    pallas_call x1, Pallas kernels, four_frames(): pl.pallas_call(functools.partial(merge_kernel, rows // 2), out_shape=[sta...  6.16 us
    pallas_call x2, Pallas kernels, four_frames(): pl.pallas_call(functools.partial(close_kernel, start), out_shape=jax.Shap...  5.89 us
    pallas_call x1, Pallas kernels, four_frames(): pl.pallas_call(functools.partial(attend_kernel, rows // 2), out_shape=[st...  4.97 us
  transfers between devices with their start and end apart: 10, of which 3 were waited for; matrix products, arithmetic and copies ran while one was open for 0% of the time, Pallas kernels for 22%

profile of v19, /device:TPU:0, one launch (start us, length us, event | category | flops | bytes accessed | tf_op | source)
XLA Modules:
  0.0 90.8 jit_solution(18437873708498299226)
XLA Ops:
  0.0 1.7 %stage_near.1 = (bf16[2,256,1024]{2,1,0:T(8,128)(2,1)S(1)}, bf16[2,256,1024]{2,1,0:T(8,128)(2,1)S(1)}, s32[8,128]{1,0:T(8,128)S(1)}) custom-call(bf16[512,1024]{1,0:T(8,128)(2,1)} %keys.9, bf16[512,1024]{1,0:T(8,128)(2,1)} %values.9), custom_call_target="tpu_custom_call" | custom-call | tf_op jit(solution)/shard_map/stage_near/pallas_call | solution.py:327
  1.7 0.7 collective-permute-start.2
  2.4 5.9 %collective-permute-start = (bf16[2,256,1024]{2,1,0:T(8,128)(2,1)S(1)}, bf16[2,256,1024]{2,1,0:T(8,128)(2,1)S(1)}, u32[]{:S(2)}, u32[]{:S(2)}) collective-permute-start(bf16[2,256,1024]{2,1,0:T(8,128)(2,1)S(1)} %get-tuple-element.14), channel_id=1, source_target_pairs={{0,4},{4,0},{8,12},{12,8},{1,5},{5,1},{9,13},{13,9},{2,6},{6,2},{1... | collective-permute-start | bytes 3145736 | tf_op jit(solution)/shard_map/ppermute | solution.py:320
  8.3 0.6 stage_missing.1
  9.0 0.7 collective-permute-start.6
  9.7 0.0 collective-permute-done.2.facing
  9.7 0.6 stage_picked.1
  10.3 1.3 %collective-permute-start.4 = (bf16[2,128,1024]{2,1,0:T(8,128)(2,1)S(1)}, bf16[2,128,1024]{2,1,0:T(8,128)(2,1)S(1)}, u32[]{:S(2)}, u32[]{:S(2)}) collective-permute-start(bf16[2,128,1024]{2,1,0:T(8,128)(2,1)S(1)} %stage_picked.1), channel_id=1, source_target_pairs={{8,12},{4,0},{9,13},{5,1},{10,14},{6,2},{11,15},{7,3},{24,28},{20,... | collective-permute-start | bytes 1572872 | tf_op jit(solution)/shard_map/ppermute | solution.py:320
  11.6 19.6 %collective-permute-done.beside.after.after_too = bf16[2,256,1024]{2,1,0:T(8,128)(2,1)S(1)} collective-permute-done((bf16[2,256,1024]{2,1,0:T(8,128)(2,1)S(1)}, bf16[2,256,1024]{2,1,0:T(8,128)(2,1)S(1)}, u32[]{:S(2)}, u32[]{:S(2)}) %collective-permute-start) | collective-permute-done | bytes 1048608 | tf_op jit(solution)/shard_map/ppermute | solution.py:320
  31.2 0.6 stage_passed.1
  31.8 1.3 %collective-permute-start.1 = (bf16[2,128,1024]{2,1,0:T(8,128)(2,1)S(1)}, bf16[2,128,1024]{2,1,0:T(8,128)(2,1)S(1)}, u32[]{:S(2)}, u32[]{:S(2)}) collective-permute-start(bf16[2,128,1024]{2,1,0:T(8,128)(2,1)S(1)} %stage_passed.1), channel_id=1, source_target_pairs={{4,12},{8,0},{5,13},{9,1},{6,14},{10,2},{7,15},{11,3},{20,28},{24,... | collective-permute-start | bytes 1572872 | tf_op jit(solution)/shard_map/ppermute | solution.py:320
  33.1 0.0 collective-permute-done.6.after
  33.1 1.3 %collective-permute-start.8 = (bf16[2,128,1024]{2,1,0:T(8,128)(2,1)S(1)}, bf16[2,128,1024]{2,1,0:T(8,128)(2,1)S(1)}, u32[]{:S(2)}, u32[]{:S(2)}) collective-permute-start(bf16[2,128,1024]{2,1,0:T(8,128)(2,1)S(1)} %collective-permute-done.6.after), channel_id=1, source_target_pairs={{8,12},{4,0},{9,13},{5,1},{10,14},{6,2},{11,15},{7,3},{24,28},{20,... | collective-permute-start | bytes 1572872 | tf_op jit(solution)/shard_map/ppermute | solution.py:320
  34.4 18.6 %collective-permute-done.4.after.after_too.picked = bf16[2,128,1024]{2,1,0:T(8,128)(2,1)S(1)} collective-permute-done((bf16[2,128,1024]{2,1,0:T(8,128)(2,1)S(1)}, bf16[2,128,1024]{2,1,0:T(8,128)(2,1)S(1)}, u32[]{:S(2)}, u32[]{:S(2)}) %collective-permute-start.4) | collective-permute-done | bytes 524320 | tf_op jit(solution)/shard_map/ppermute | solution.py:320
  53.1 0.7 stage_crossed.1
  53.8 2.5 %collective-permute-start.7 = (bf16[2,128,1024]{2,1,0:T(8,128)(2,1)S(1)}, bf16[2,128,1024]{2,1,0:T(8,128)(2,1)S(1)}, u32[]{:S(2)}, u32[]{:S(2)}) collective-permute-start(bf16[2,128,1024]{2,1,0:T(8,128)(2,1)S(1)} %stage_crossed.1), channel_id=1, source_target_pairs={{0,8},{12,4},{1,9},{13,5},{2,10},{14,6},{3,11},{15,7},{16,24},{28,... | collective-permute-start | bytes 1572872 | tf_op jit(solution)/shard_map/ppermute | solution.py:320
  56.2 0.7 stage_direct.1
  56.9 0.0 copy-start.2
  56.9 3.4 %collective-permute-start.5 = (bf16[2,128,1024]{2,1,0:T(8,128)(2,1)S(1)}, bf16[2,128,1024]{2,1,0:T(8,128)(2,1)S(1)}, u32[]{:S(2)}, u32[]{:S(2)}) collective-permute-start(bf16[2,128,1024]{2,1,0:T(8,128)(2,1)S(1)} %stage_direct.1), channel_id=1, source_target_pairs={{0,12},{12,0},{1,13},{13,1},{2,14},{14,2},{3,15},{15,3},{16,28},{2... | collective-permute-start | bytes 1572872 | tf_op jit(solution)/shard_map/ppermute | solution.py:320
  60.3 0.6 stage_traded.3
  60.9 0.7 collective-permute-start.9
  61.6 5.0 %attend.1 = (f32[8,512,128]{2,1,0:T(8,128)S(1)}, f32[8,512,128]{2,1,0:T(8,128)S(1)}, f32[8,512,128]{2,1,0:T(8,128)S(1)}) custom-call(bf16[512,1024]{1,0:T(8,128)(2,1)S(1)} %copy-done.2, bf16[512,1024]{1,0:T(8,128)(2,1)S(1)} %copy-done, bf16[512,1024]{1,0:T(8,128)(2,1)S(1)} %copy-done.1, ...), custom_call_target="tpu_custom_call" | custom-call | tf_op jit(solution)/shard_map/attend/pallas_call | solution.py:375
  66.6 10.6 %collective-permute-done.1.after.passed = bf16[2,128,1024]{2,1,0:T(8,128)(2,1)S(1)} collective-permute-done((bf16[2,128,1024]{2,1,0:T(8,128)(2,1)S(1)}, bf16[2,128,1024]{2,1,0:T(8,128)(2,1)S(1)}, u32[]{:S(2)}, u32[]{:S(2)}) %collective-permute-start.1) | collective-permute-done | bytes 524320 | tf_op jit(solution)/shard_map/ppermute | solution.py:320
  77.2 0.6 stage_traded.2
  77.8 0.7 collective-permute-start.3
  78.5 0.0 collective-permute-done.8.lone
  78.5 0.0 collective-permute-done.7.crossed
  78.5 6.2 %merge.1 = (f32[8,512,128]{2,1,0:T(8,128)S(1)}, f32[8,512,128]{2,1,0:T(8,128)S(1)}, f32[8,512,128]{2,1,0:T(8,128)S(1)}) custom-call(bf16[512,1024]{1,0:T(8,128)(2,1)S(1)} %copy-done.2, bf16[2,128,1024]{2,1,0:T(8,128)(2,1)S(1)} %collective-permute-done.7.crossed, bf16[2,128,1024]{2,1,0:T(8,128)(2,1)S(1)} %collective-permute-done.4.after.after_too.picked, ...), custom_call_target="tpu_custom_call" | custom-call | tf_op jit(solution)/shard_map/merge/pallas_call | solution.py:395
  84.7 0.0 collective-permute-done.9.traded
  84.7 0.0 collective-permute-done.5.direct
  84.7 4.0 %close.2.rest_0_ = bf16[512,1024]{1,0:T(8,128)(2,1)} custom-call(bf16[512,1024]{1,0:T(8,128)(2,1)S(1)} %copy-done.2, bf16[2,128,768]{2,1,0:T(8,128)(2,1)S(1)} %collective-permute-done.9.traded, bf16[2,128,1024]{2,1,0:T(8,128)(2,1)S(1)} %collective-permute-done.1.after.passed, bf16[2,128,1024]{2,1,0:T(8,128)(2,1)S(1)} %collective-permute-done.5.direct, ...), custom_call_target="tpu_custom_call" | custom-call | tf_op jit(solution)/shard_map/close/pallas_call | solution.py:412
  88.7 1.9 %close.3 = bf16[512,1024]{1,0:T(8,128)(2,1)} custom-call(bf16[512,1024]{1,0:T(8,128)(2,1)S(1)} %copy-done.2, bf16[2,128,256]{2,1,0:T(8,128)(2,1)S(1)} %collective-permute-done.3.traded, bf16[2,128,1024]{2,1,0:T(8,128)(2,1)S(1)} %collective-permute-done.1.after.passed, ...), custom_call_target="tpu_custom_call", output_to_operand_aliasing={{}: (7, {})} | custom-call | tf_op jit(solution)/shard_map/close/pallas_call | solution.py:412
  (8 shorter events, 0.0 us)
Async XLA Ops:
  0.0 8.3 %copy-start = (bf16[512,1024]{1,0:T(8,128)(2,1)S(1)}, bf16[512,1024]{1,0:T(8,128)(2,1)}, u32[]{:S(2)}) copy-start(bf16[512,1024]{1,0:T(8,128)(2,1)} %keys.9) | copy-start | bytes 3145732
  0.0 8.3 %copy-start.1 = (bf16[512,1024]{1,0:T(8,128)(2,1)S(1)}, bf16[512,1024]{1,0:T(8,128)(2,1)}, u32[]{:S(2)}) copy-start(bf16[512,1024]{1,0:T(8,128)(2,1)} %values.9) | copy-start | bytes 3145732
  0.0 8.3 %copy-start.3 = (s32[4,4,2]{1,2,0:T(2,128)S(1)}, s32[4,4,2]{1,2,0:T(2,128)}, u32[]{:S(2)}) copy-start(s32[4,4,2]{1,2,0:T(2,128)} %param.7) | copy-start | bytes 388
  1.7 8.0 %collective-permute-start.2 = (bf16[2,256,1024]{2,1,0:T(8,128)(2,1)S(1)}, bf16[2,256,1024]{2,1,0:T(8,128)(2,1)S(1)}, u32[]{:S(2)}, u32[]{:S(2)}) collective-permute-start(bf16[2,256,1024]{2,1,0:T(8,128)(2,1)S(1)} %get-tuple-element.15), channel_id=1, source_target_pairs={{4,8},{8,4},{5,9},{9,5},{6,10},{10,6},{7,11},{11,7},{20,24},{24,20... | collective-permute-start | bytes 3145736 | tf_op jit(solution)/shard_map/ppermute | solution.py:320
  2.4 28.7 %collective-permute-start = (bf16[2,256,1024]{2,1,0:T(8,128)(2,1)S(1)}, bf16[2,256,1024]{2,1,0:T(8,128)(2,1)S(1)}, u32[]{:S(2)}, u32[]{:S(2)}) collective-permute-start(bf16[2,256,1024]{2,1,0:T(8,128)(2,1)S(1)} %get-tuple-element.14), channel_id=1, source_target_pairs={{0,4},{4,0},{8,12},{12,8},{1,5},{5,1},{9,13},{13,9},{2,6},{6,2},{1... | collective-permute-start | bytes 3145736 | tf_op jit(solution)/shard_map/ppermute | solution.py:320
  9.0 24.2 %collective-permute-start.6 = (bf16[2,128,1024]{2,1,0:T(8,128)(2,1)S(1)}, bf16[2,128,1024]{2,1,0:T(8,128)(2,1)S(1)}, u32[]{:S(2)}, u32[]{:S(2)}) collective-permute-start(bf16[2,128,1024]{2,1,0:T(8,128)(2,1)S(1)} %stage_missing.1), channel_id=1, source_target_pairs={{4,8},{8,4},{5,9},{9,5},{6,10},{10,6},{7,11},{11,7},{20,24},{24,20... | collective-permute-start | bytes 1572872 | tf_op jit(solution)/shard_map/ppermute | solution.py:320
  10.3 42.8 %collective-permute-start.4 = (bf16[2,128,1024]{2,1,0:T(8,128)(2,1)S(1)}, bf16[2,128,1024]{2,1,0:T(8,128)(2,1)S(1)}, u32[]{:S(2)}, u32[]{:S(2)}) collective-permute-start(bf16[2,128,1024]{2,1,0:T(8,128)(2,1)S(1)} %stage_picked.1), channel_id=1, source_target_pairs={{8,12},{4,0},{9,13},{5,1},{10,14},{6,2},{11,15},{7,3},{24,28},{20,... | collective-permute-start | bytes 1572872 | tf_op jit(solution)/shard_map/ppermute | solution.py:320
  31.8 45.4 %collective-permute-start.1 = (bf16[2,128,1024]{2,1,0:T(8,128)(2,1)S(1)}, bf16[2,128,1024]{2,1,0:T(8,128)(2,1)S(1)}, u32[]{:S(2)}, u32[]{:S(2)}) collective-permute-start(bf16[2,128,1024]{2,1,0:T(8,128)(2,1)S(1)} %stage_passed.1), channel_id=1, source_target_pairs={{4,12},{8,0},{5,13},{9,1},{6,14},{10,2},{7,15},{11,3},{20,28},{24,... | collective-permute-start | bytes 1572872 | tf_op jit(solution)/shard_map/ppermute | solution.py:320
  33.1 45.4 %collective-permute-start.8 = (bf16[2,128,1024]{2,1,0:T(8,128)(2,1)S(1)}, bf16[2,128,1024]{2,1,0:T(8,128)(2,1)S(1)}, u32[]{:S(2)}, u32[]{:S(2)}) collective-permute-start(bf16[2,128,1024]{2,1,0:T(8,128)(2,1)S(1)} %collective-permute-done.6.after), channel_id=1, source_target_pairs={{8,12},{4,0},{9,13},{5,1},{10,14},{6,2},{11,15},{7,3},{24,28},{20,... | collective-permute-start | bytes 1572872 | tf_op jit(solution)/shard_map/ppermute | solution.py:320
  53.8 24.8 %collective-permute-start.7 = (bf16[2,128,1024]{2,1,0:T(8,128)(2,1)S(1)}, bf16[2,128,1024]{2,1,0:T(8,128)(2,1)S(1)}, u32[]{:S(2)}, u32[]{:S(2)}) collective-permute-start(bf16[2,128,1024]{2,1,0:T(8,128)(2,1)S(1)} %stage_crossed.1), channel_id=1, source_target_pairs={{0,8},{12,4},{1,9},{13,5},{2,10},{14,6},{3,11},{15,7},{16,24},{28,... | collective-permute-start | bytes 1572872 | tf_op jit(solution)/shard_map/ppermute | solution.py:320
  56.9 4.7 %copy-start.2 = (bf16[512,1024]{1,0:T(8,128)(2,1)S(1)}, bf16[512,1024]{1,0:T(8,128)(2,1)}, u32[]{:S(2)}) copy-start(bf16[512,1024]{1,0:T(8,128)(2,1)} %queries.7) | copy-start | bytes 3145732
  56.9 27.8 %collective-permute-start.5 = (bf16[2,128,1024]{2,1,0:T(8,128)(2,1)S(1)}, bf16[2,128,1024]{2,1,0:T(8,128)(2,1)S(1)}, u32[]{:S(2)}, u32[]{:S(2)}) collective-permute-start(bf16[2,128,1024]{2,1,0:T(8,128)(2,1)S(1)} %stage_direct.1), channel_id=1, source_target_pairs={{0,12},{12,0},{1,13},{13,1},{2,14},{14,2},{3,15},{15,3},{16,28},{2... | collective-permute-start | bytes 1572872 | tf_op jit(solution)/shard_map/ppermute | solution.py:320
  60.9 23.8 %collective-permute-start.9 = (bf16[2,128,768]{2,1,0:T(8,128)(2,1)S(1)}, bf16[2,128,768]{2,1,0:T(8,128)(2,1)S(1)}, u32[]{:S(2)}, u32[]{:S(2)}) collective-permute-start(bf16[2,128,768]{2,1,0:T(8,128)(2,1)S(1)} %stage_traded.3), channel_id=1, source_target_pairs={{4,8},{8,4},{5,9},{9,5},{6,10},{10,6},{7,11},{11,7},{20,24},{24,20... | collective-permute-start | bytes 1179656 | tf_op jit(solution)/shard_map/ppermute | solution.py:320
  77.8 10.8 %collective-permute-start.3 = (bf16[2,128,256]{2,1,0:T(8,128)(2,1)S(1)}, bf16[2,128,256]{2,1,0:T(8,128)(2,1)S(1)}, u32[]{:S(2)}, u32[]{:S(2)}) collective-permute-start(bf16[2,128,256]{2,1,0:T(8,128)(2,1)S(1)} %stage_traded.2), channel_id=1, source_target_pairs={{4,8},{8,4},{5,9},{9,5},{6,10},{10,6},{7,11},{11,7},{20,24},{24,20... | collective-permute-start | bytes 393224 | tf_op jit(solution)/shard_map/ppermute | solution.py:320

commit v20 on v19

--- a/solution.py
+++ b/solution.py
@@ -176,11 +176,12 @@
 
 
 def attend_kernel(
-    chunk, queries, keys, values, beside, facing, mixed, tops, sums
+    chunk, queries, keys, values, beside, facing, picked, mixed, tops, sums, token
 ):
     frame = lax.axis_index("tm")
     inner = (frame == 1) | (frame == 2)
     rows, columns = queries.shape
+    token[...] = jnp.zeros_like(token)
     units = [(head, start) for head in range(columns // HD) for start in range(0, rows, chunk)]
 
     def attend(pieces_of):
@@ -214,21 +215,21 @@
             scores = ahead
 
     pl.when(inner)(lambda: attend(lambda kv, cols: [facing[kv, :, cols]]))
-    pl.when(jnp.logical_not(inner))(lambda: attend(lambda kv, cols: []))
-
-
-def merge_kernel(chunk, queries, crossed, picked, lone, mixed, tops, sums, *state):
-    frame = lax.axis_index("tm")
-    inner = (frame == 1) | (frame == 2)
+    pl.when(jnp.logical_not(inner))(lambda: attend(lambda kv, cols: [picked[kv, :, cols]]))
+
+
+def merge_kernel(chunk, after, queries, crossed, mixed, tops, sums, *state):
+    frame = lax.axis_index("tm")
     rows, columns = queries.shape
     new_mixed, new_tops, new_sums = state
 
-    def merge(piece):
+    @pl.when((frame == 1) | (frame == 2))
+    def _():
         for head in range(columns // HD):
             cols = pl.ds(head * HD, HD)
             for start in range(0, rows, chunk):
                 at = pl.ds(start, chunk)
-                scores = scores_of(queries[at, cols], piece(0, cols))
+                scores = scores_of(queries[at, cols], crossed[0, :, cols])
                 old_top = tops[head, at]
                 top = jnp.maximum(old_top, jnp.max(scores, axis=1, keepdims=True))
                 shrink = jnp.exp2((old_top - top) * RATE)
@@ -236,21 +237,15 @@
                 row_sum = jnp.sum(powers, axis=1, keepdims=True)
                 more = jnp.dot(
                     powers.astype(jnp.bfloat16),
-                    piece(1, cols),
+                    crossed[1, :, cols],
                     preferred_element_type=jnp.float32,
                 )
                 new_mixed[head, at] = mixed[head, at] * shrink + more
+                new_sums[head, at] = sums[head, at] * shrink + row_sum
                 new_tops[head, at] = top
-                new_sums[head, at] = sums[head, at] * shrink + row_sum
-
-    def of_edge(kv, cols):
-        return jnp.concatenate([picked[kv, :, cols], lone[kv, :, cols]], 0)
-
-    pl.when(inner)(lambda: merge(lambda kv, cols: crossed[kv, :, cols]))
-    pl.when(jnp.logical_not(inner))(lambda: merge(of_edge))
-
-
-def close_kernel(first, queries, traded, passed, direct, mixed, tops, sums, *rest):
+
+
+def close_kernel(first, queries, traded, lone, passed, direct, mixed, tops, sums, *rest):
     out, ready, sems = rest[-3:]
     frame = lax.axis_index("tm")
     inner = (frame == 1) | (frame == 2)
@@ -302,7 +297,8 @@
         return [traded[kv, :, there]]
 
     def of_edge(kv, here, there):
-        return [jnp.concatenate([passed[kv, :, here], direct[kv, :, here]], 0)]
+        pair = jnp.concatenate([passed[kv, :, here], direct[kv, :, here]], 0)
+        return [pair, lone[kv, :, here]]
 
     pl.when(inner)(lambda: close(of_inner, rows))
     pl.when(jnp.logical_not(inner))(lambda: close(of_edge, rows // 2))
@@ -372,16 +368,16 @@
     direct = send(direct, [(0, 3), (3, 0)])
     state = jax.ShapeDtypeStruct((heads, rows, HD), jnp.float32)
     roomy = pltpu.CompilerParams(vmem_limit_bytes=32 << 20)
-    mixed, tops, sums = pl.pallas_call(
+    mixed, tops, sums, after = pl.pallas_call(
         functools.partial(attend_kernel, rows // 2),
-        out_shape=[state] * 3,
-        in_specs=[local] * 5,
-        out_specs=[local] * 3,
+        out_shape=[state] * 3 + [token],
+        in_specs=[local] * 6,
+        out_specs=[local] * 4,
         compiler_params=roomy,
         name="attend",
-    )(queries, keys, values, beside, facing)
+    )(queries, keys, values, beside, facing, picked)
     traded = []
-    for cut, before in zip(cuts, ((beside, beside), (passed, sums))):
+    for cut, before in zip(cuts, ((beside, beside), (passed, after))):
         (part,) = stage(
             functools.partial(stage_traded_kernel, cut),
             [jax.ShapeDtypeStruct((2, BLOCK, cut[1]), jnp.bfloat16)],
@@ -395,14 +391,15 @@
     mixed, tops, sums = pl.pallas_call(
         functools.partial(merge_kernel, rows // 2),
         out_shape=[state] * 3,
-        in_specs=[local] * 7,
+        in_specs=[anywhere] + [local] * 5,
         out_specs=[local] * 3,
+        input_output_aliases={3: 0, 4: 1, 5: 2},
         compiler_params=roomy,
         name="merge",
-    )(queries, crossed, picked, lone, mixed, tops, sums)
+    )(lone, queries, crossed, mixed, tops, sums)
     result = None
     for part, (start, size) in zip(traded, cuts):
-        operands = [queries, part, passed, direct, mixed, tops, sums]
+        operands = [queries, part, lone, passed, direct, mixed, tops, sums]
         in_specs = [local] * len(operands)
         aliases = {}
         if result is not None:

time: 91.1 us -> 87.7 us (0.963); the launches traced: 90.8 us -> 86.4 us
  Pallas kernels: 23.2 us -> 19.9 us
  waiting for transfers between devices: 48.8 us -> 47.7 us
    pallas_call x1, Pallas kernels: 6.16 us -> 0.02 us  [four_frames(): pl.pallas_call(functools.partial(merge_kernel, rows // 2), out_shape=[sta...]
    pallas_call x2, Pallas kernels: 5.89 us -> 7.6 us  [four_frames(): pl.pallas_call(functools.partial(close_kernel, start), out_shape=jax.Shap...]
    pallas_call x1, Pallas kernels: 4.97 us -> 6.06 us  [four_frames(): pl.pallas_call(functools.partial(attend_kernel, rows // 2), out_shape=[st...]
    ppermute x10, waiting for transfers between devices: 48.8 us -> 47.7 us  [send(): return lax.ppermute(array, 'tm', pairs)]
  transfers between devices with their start and end apart: 10 -> 10, of which waited for: 3 -> 3; matrix products, arithmetic and copies ran while one was open for 0% -> 0% of each run, Pallas kernels for 22% -> 18%
where the time goes in v20:
time: 87.7 us; the launch traced here: 86.4 us
  waiting for transfers between devices  47.7 us (54%)
  Pallas kernels  19.9 us (23%)
  starting transfers between devices  18.4 us (21%)
    ppermute x10, waiting for transfers between devices, send(): return lax.ppermute(array, 'tm', pairs)  47.7 us
    ppermute x10, starting transfers between devices, send(): return lax.ppermute(array, 'tm', pairs)  18.4 us
    pallas_call x2, Pallas kernels, four_frames(): pl.pallas_call(functools.partial(close_kernel, start), out_shape=jax.Shap...  7.6 us
    pallas_call x8, Pallas kernels, stage(): pl.pallas_call(kernel, out_shape=shapes, in_specs=[scalars if operand is...  6.18 us
    pallas_call x1, Pallas kernels, four_frames(): pl.pallas_call(functools.partial(attend_kernel, rows // 2), out_shape=[st...  6.06 us
  transfers between devices with their start and end apart: 10, of which 3 were waited for; matrix products, arithmetic and copies ran while one was open for 0% of the time, Pallas kernels for 18%

profile of v20, /device:TPU:0, one launch (start us, length us, event | category | flops | bytes accessed | tf_op | source)
XLA Modules:
  0.0 86.4 jit_solution(12780359957190263006)
XLA Ops:
  0.0 1.7 %stage_near.1 = (bf16[2,256,1024]{2,1,0:T(8,128)(2,1)S(1)}, bf16[2,256,1024]{2,1,0:T(8,128)(2,1)S(1)}, s32[8,128]{1,0:T(8,128)S(1)}) custom-call(bf16[512,1024]{1,0:T(8,128)(2,1)} %keys.9, bf16[512,1024]{1,0:T(8,128)(2,1)} %values.9), custom_call_target="tpu_custom_call" | custom-call | tf_op jit(solution)/shard_map/stage_near/pallas_call | solution.py:323
  1.7 0.7 collective-permute-start.2
  2.4 5.9 %collective-permute-start = (bf16[2,256,1024]{2,1,0:T(8,128)(2,1)S(1)}, bf16[2,256,1024]{2,1,0:T(8,128)(2,1)S(1)}, u32[]{:S(2)}, u32[]{:S(2)}) collective-permute-start(bf16[2,256,1024]{2,1,0:T(8,128)(2,1)S(1)} %get-tuple-element.15), channel_id=1, source_target_pairs={{0,4},{4,0},{8,12},{12,8},{1,5},{5,1},{9,13},{13,9},{2,6},{6,2},{1... | collective-permute-start | bytes 3145736 | tf_op jit(solution)/shard_map/ppermute | solution.py:316
  8.3 0.6 stage_missing.1
  9.0 0.7 collective-permute-start.5
  9.7 0.0 collective-permute-done.2.facing
  9.7 0.6 stage_picked.1
  10.3 1.3 %collective-permute-start.3 = (bf16[2,128,1024]{2,1,0:T(8,128)(2,1)S(1)}, bf16[2,128,1024]{2,1,0:T(8,128)(2,1)S(1)}, u32[]{:S(2)}, u32[]{:S(2)}) collective-permute-start(bf16[2,128,1024]{2,1,0:T(8,128)(2,1)S(1)} %stage_picked.1), channel_id=1, source_target_pairs={{8,12},{4,0},{9,13},{5,1},{10,14},{6,2},{11,15},{7,3},{24,28},{20,... | collective-permute-start | bytes 1572872 | tf_op jit(solution)/shard_map/ppermute | solution.py:316
  11.6 19.6 %collective-permute-done.beside.after.after_too = bf16[2,256,1024]{2,1,0:T(8,128)(2,1)S(1)} collective-permute-done((bf16[2,256,1024]{2,1,0:T(8,128)(2,1)S(1)}, bf16[2,256,1024]{2,1,0:T(8,128)(2,1)S(1)}, u32[]{:S(2)}, u32[]{:S(2)}) %collective-permute-start) | collective-permute-done | bytes 1048608 | tf_op jit(solution)/shard_map/ppermute | solution.py:316
  31.2 0.6 stage_passed.1
  31.8 1.3 %collective-permute-start.1 = (bf16[2,128,1024]{2,1,0:T(8,128)(2,1)S(1)}, bf16[2,128,1024]{2,1,0:T(8,128)(2,1)S(1)}, u32[]{:S(2)}, u32[]{:S(2)}) collective-permute-start(bf16[2,128,1024]{2,1,0:T(8,128)(2,1)S(1)} %stage_passed.1), channel_id=1, source_target_pairs={{4,12},{8,0},{5,13},{9,1},{6,14},{10,2},{7,15},{11,3},{20,28},{24,... | collective-permute-start | bytes 1572872 | tf_op jit(solution)/shard_map/ppermute | solution.py:316
  33.1 0.0 collective-permute-done.5.after
  33.1 1.3 %collective-permute-start.6 = (bf16[2,128,1024]{2,1,0:T(8,128)(2,1)S(1)}, bf16[2,128,1024]{2,1,0:T(8,128)(2,1)S(1)}, u32[]{:S(2)}, u32[]{:S(2)}) collective-permute-start(bf16[2,128,1024]{2,1,0:T(8,128)(2,1)S(1)} %collective-permute-done.5.after), channel_id=1, source_target_pairs={{8,12},{4,0},{9,13},{5,1},{10,14},{6,2},{11,15},{7,3},{24,28},{20,... | collective-permute-start | bytes 1572872 | tf_op jit(solution)/shard_map/ppermute | solution.py:316
  34.4 18.6 %collective-permute-done.3.picked.after.after_too = bf16[2,128,1024]{2,1,0:T(8,128)(2,1)S(1)} collective-permute-done((bf16[2,128,1024]{2,1,0:T(8,128)(2,1)S(1)}, bf16[2,128,1024]{2,1,0:T(8,128)(2,1)S(1)}, u32[]{:S(2)}, u32[]{:S(2)}) %collective-permute-start.3) | collective-permute-done | bytes 524320 | tf_op jit(solution)/shard_map/ppermute | solution.py:316
  53.1 0.7 stage_crossed.1
  53.8 2.5 %collective-permute-start.8 = (bf16[2,128,1024]{2,1,0:T(8,128)(2,1)S(1)}, bf16[2,128,1024]{2,1,0:T(8,128)(2,1)S(1)}, u32[]{:S(2)}, u32[]{:S(2)}) collective-permute-start(bf16[2,128,1024]{2,1,0:T(8,128)(2,1)S(1)} %stage_crossed.1), channel_id=1, source_target_pairs={{0,8},{12,4},{1,9},{13,5},{2,10},{14,6},{3,11},{15,7},{16,24},{28,... | collective-permute-start | bytes 1572872 | tf_op jit(solution)/shard_map/ppermute | solution.py:316
  56.2 0.7 stage_direct.1
  56.9 0.0 copy-start.2
  56.9 3.4 %collective-permute-start.7 = (bf16[2,128,1024]{2,1,0:T(8,128)(2,1)S(1)}, bf16[2,128,1024]{2,1,0:T(8,128)(2,1)S(1)}, u32[]{:S(2)}, u32[]{:S(2)}) collective-permute-start(bf16[2,128,1024]{2,1,0:T(8,128)(2,1)S(1)} %stage_direct.1), channel_id=1, source_target_pairs={{0,12},{12,0},{1,13},{13,1},{2,14},{14,2},{3,15},{15,3},{16,28},{2... | collective-permute-start | bytes 1572872 | tf_op jit(solution)/shard_map/ppermute | solution.py:316
  60.3 0.6 stage_traded.3
  60.9 0.7 collective-permute-start.9
  61.6 6.1 %attend.1 = (f32[8,512,128]{2,1,0:T(8,128)S(1)}, f32[8,512,128]{2,1,0:T(8,128)S(1)}, f32[8,512,128]{2,1,0:T(8,128)S(1)}, s32[8,128]{1,0:T(8,128)S(1)}) custom-call(bf16[512,1024]{1,0:T(8,128)(2,1)S(1)} %copy-done.2, bf16[512,1024]{1,0:T(8,128)(2,1)S(1)} %copy-done, bf16[512,1024]{1,0:T(8,128)(2,1)S(1)} %copy-done.1, ...), custom_call_target="tpu_custom_call" | custom-call | tf_op jit(solution)/shard_map/attend/pallas_call | solution.py:371
  67.7 9.5 %collective-permute-done.1.after.passed = bf16[2,128,1024]{2,1,0:T(8,128)(2,1)S(1)} collective-permute-done((bf16[2,128,1024]{2,1,0:T(8,128)(2,1)S(1)}, bf16[2,128,1024]{2,1,0:T(8,128)(2,1)S(1)}, u32[]{:S(2)}, u32[]{:S(2)}) %collective-permute-start.1) | collective-permute-done | bytes 524320 | tf_op jit(solution)/shard_map/ppermute | solution.py:316
  77.2 0.6 stage_traded.2
  77.8 0.7 collective-permute-start.4
  78.5 0.0 collective-permute-done.6.after.lone
  78.5 0.0 collective-permute-done.8.crossed
  78.6 0.0 collective-permute-done.9.traded
  78.6 0.0 collective-permute-done.7.direct
  78.6 5.2 %close.2.rest_0_ = bf16[512,1024]{1,0:T(8,128)(2,1)} custom-call(bf16[512,1024]{1,0:T(8,128)(2,1)S(1)} %copy-done.2, bf16[2,128,768]{2,1,0:T(8,128)(2,1)S(1)} %collective-permute-done.9.traded, bf16[2,128,1024]{2,1,0:T(8,128)(2,1)S(1)} %collective-permute-done.6.after.lone, bf16[2,128,1024]{2,1,0:T(8,128)(2,1)S(1)} %collective-permute-done.1.after.passed, ...), custom_call_target="tpu_custom_call" | custom-call | tf_op jit(solution)/shard_map/close/pallas_call | solution.py:409
  83.8 0.0 collective-permute-done.4.traded
  83.8 2.4 %close.3 = bf16[512,1024]{1,0:T(8,128)(2,1)} custom-call(bf16[512,1024]{1,0:T(8,128)(2,1)S(1)} %copy-done.2, bf16[2,128,256]{2,1,0:T(8,128)(2,1)S(1)} %collective-permute-done.4.traded, bf16[2,128,1024]{2,1,0:T(8,128)(2,1)S(1)} %collective-permute-done.6.after.lone, ...), custom_call_target="tpu_custom_call", output_to_operand_aliasing={{}: (8, {})} | custom-call | tf_op jit(solution)/shard_map/close/pallas_call | solution.py:409
  (8 shorter events, 0.0 us)
Async XLA Ops:
  0.0 8.3 %copy-start.1 = (bf16[512,1024]{1,0:T(8,128)(2,1)S(1)}, bf16[512,1024]{1,0:T(8,128)(2,1)}, u32[]{:S(2)}) copy-start(bf16[512,1024]{1,0:T(8,128)(2,1)} %values.9) | copy-start | bytes 3145732
  0.0 8.3 %copy-start = (bf16[512,1024]{1,0:T(8,128)(2,1)S(1)}, bf16[512,1024]{1,0:T(8,128)(2,1)}, u32[]{:S(2)}) copy-start(bf16[512,1024]{1,0:T(8,128)(2,1)} %keys.9) | copy-start | bytes 3145732
  0.0 8.3 %copy-start.3 = (s32[4,4,2]{1,2,0:T(2,128)S(1)}, s32[4,4,2]{1,2,0:T(2,128)}, u32[]{:S(2)}) copy-start(s32[4,4,2]{1,2,0:T(2,128)} %param.7) | copy-start | bytes 388
  1.7 8.0 %collective-permute-start.2 = (bf16[2,256,1024]{2,1,0:T(8,128)(2,1)S(1)}, bf16[2,256,1024]{2,1,0:T(8,128)(2,1)S(1)}, u32[]{:S(2)}, u32[]{:S(2)}) collective-permute-start(bf16[2,256,1024]{2,1,0:T(8,128)(2,1)S(1)} %get-tuple-element.16), channel_id=1, source_target_pairs={{4,8},{8,4},{5,9},{9,5},{6,10},{10,6},{7,11},{11,7},{20,24},{24,20... | collective-permute-start | bytes 3145736 | tf_op jit(solution)/shard_map/ppermute | solution.py:316
  2.4 28.7 %collective-permute-start = (bf16[2,256,1024]{2,1,0:T(8,128)(2,1)S(1)}, bf16[2,256,1024]{2,1,0:T(8,128)(2,1)S(1)}, u32[]{:S(2)}, u32[]{:S(2)}) collective-permute-start(bf16[2,256,1024]{2,1,0:T(8,128)(2,1)S(1)} %get-tuple-element.15), channel_id=1, source_target_pairs={{0,4},{4,0},{8,12},{12,8},{1,5},{5,1},{9,13},{13,9},{2,6},{6,2},{1... | collective-permute-start | bytes 3145736 | tf_op jit(solution)/shard_map/ppermute | solution.py:316
  9.0 24.2 %collective-permute-start.5 = (bf16[2,128,1024]{2,1,0:T(8,128)(2,1)S(1)}, bf16[2,128,1024]{2,1,0:T(8,128)(2,1)S(1)}, u32[]{:S(2)}, u32[]{:S(2)}) collective-permute-start(bf16[2,128,1024]{2,1,0:T(8,128)(2,1)S(1)} %stage_missing.1), channel_id=1, source_target_pairs={{4,8},{8,4},{5,9},{9,5},{6,10},{10,6},{7,11},{11,7},{20,24},{24,20... | collective-permute-start | bytes 1572872 | tf_op jit(solution)/shard_map/ppermute | solution.py:316
  10.3 42.8 %collective-permute-start.3 = (bf16[2,128,1024]{2,1,0:T(8,128)(2,1)S(1)}, bf16[2,128,1024]{2,1,0:T(8,128)(2,1)S(1)}, u32[]{:S(2)}, u32[]{:S(2)}) collective-permute-start(bf16[2,128,1024]{2,1,0:T(8,128)(2,1)S(1)} %stage_picked.1), channel_id=1, source_target_pairs={{8,12},{4,0},{9,13},{5,1},{10,14},{6,2},{11,15},{7,3},{24,28},{20,... | collective-permute-start | bytes 1572872 | tf_op jit(solution)/shard_map/ppermute | solution.py:316
  31.8 45.4 %collective-permute-start.1 = (bf16[2,128,1024]{2,1,0:T(8,128)(2,1)S(1)}, bf16[2,128,1024]{2,1,0:T(8,128)(2,1)S(1)}, u32[]{:S(2)}, u32[]{:S(2)}) collective-permute-start(bf16[2,128,1024]{2,1,0:T(8,128)(2,1)S(1)} %stage_passed.1), channel_id=1, source_target_pairs={{4,12},{8,0},{5,13},{9,1},{6,14},{10,2},{7,15},{11,3},{20,28},{24,... | collective-permute-start | bytes 1572872 | tf_op jit(solution)/shard_map/ppermute | solution.py:316
  33.1 45.4 %collective-permute-start.6 = (bf16[2,128,1024]{2,1,0:T(8,128)(2,1)S(1)}, bf16[2,128,1024]{2,1,0:T(8,128)(2,1)S(1)}, u32[]{:S(2)}, u32[]{:S(2)}) collective-permute-start(bf16[2,128,1024]{2,1,0:T(8,128)(2,1)S(1)} %collective-permute-done.5.after), channel_id=1, source_target_pairs={{8,12},{4,0},{9,13},{5,1},{10,14},{6,2},{11,15},{7,3},{24,28},{20,... | collective-permute-start | bytes 1572872 | tf_op jit(solution)/shard_map/ppermute | solution.py:316
  53.8 24.8 %collective-permute-start.8 = (bf16[2,128,1024]{2,1,0:T(8,128)(2,1)S(1)}, bf16[2,128,1024]{2,1,0:T(8,128)(2,1)S(1)}, u32[]{:S(2)}, u32[]{:S(2)}) collective-permute-start(bf16[2,128,1024]{2,1,0:T(8,128)(2,1)S(1)} %stage_crossed.1), channel_id=1, source_target_pairs={{0,8},{12,4},{1,9},{13,5},{2,10},{14,6},{3,11},{15,7},{16,24},{28,... | collective-permute-start | bytes 1572872 | tf_op jit(solution)/shard_map/ppermute | solution.py:316
  56.9 4.7 %copy-start.2 = (bf16[512,1024]{1,0:T(8,128)(2,1)S(1)}, bf16[512,1024]{1,0:T(8,128)(2,1)}, u32[]{:S(2)}) copy-start(bf16[512,1024]{1,0:T(8,128)(2,1)} %queries.7) | copy-start | bytes 3145732
  56.9 21.7 %collective-permute-start.7 = (bf16[2,128,1024]{2,1,0:T(8,128)(2,1)S(1)}, bf16[2,128,1024]{2,1,0:T(8,128)(2,1)S(1)}, u32[]{:S(2)}, u32[]{:S(2)}) collective-permute-start(bf16[2,128,1024]{2,1,0:T(8,128)(2,1)S(1)} %stage_direct.1), channel_id=1, source_target_pairs={{0,12},{12,0},{1,13},{13,1},{2,14},{14,2},{3,15},{15,3},{16,28},{2... | collective-permute-start | bytes 1572872 | tf_op jit(solution)/shard_map/ppermute | solution.py:316
  60.9 17.6 %collective-permute-start.9 = (bf16[2,128,768]{2,1,0:T(8,128)(2,1)S(1)}, bf16[2,128,768]{2,1,0:T(8,128)(2,1)S(1)}, u32[]{:S(2)}, u32[]{:S(2)}) collective-permute-start(bf16[2,128,768]{2,1,0:T(8,128)(2,1)S(1)} %stage_traded.3), channel_id=1, source_target_pairs={{4,8},{8,4},{5,9},{9,5},{6,10},{10,6},{7,11},{11,7},{20,24},{24,20... | collective-permute-start | bytes 1179656 | tf_op jit(solution)/shard_map/ppermute | solution.py:316
  77.8 6.0 %collective-permute-start.4 = (bf16[2,128,256]{2,1,0:T(8,128)(2,1)S(1)}, bf16[2,128,256]{2,1,0:T(8,128)(2,1)S(1)}, u32[]{:S(2)}, u32[]{:S(2)}) collective-permute-start(bf16[2,128,256]{2,1,0:T(8,128)(2,1)S(1)} %stage_traded.2), channel_id=1, source_target_pairs={{4,8},{8,4},{5,9},{9,5},{6,10},{10,6},{7,11},{11,7},{20,24},{24,20... | collective-permute-start | bytes 393224 | tf_op jit(solution)/shard_map/ppermute | solution.py:316

commit v21 on v20

--- a/solution.py
+++ b/solution.py
@@ -97,19 +97,18 @@
     return pl.ds(pl.multiple_of(block * BLOCK, BLOCK), BLOCK)
 
 
-def stage_near_kernel(half, keys, values, facing, beside, token, sems):
-    frame = lax.axis_index("tm")
-    outer = pl.ds(pl.multiple_of(lax.rem(frame + 1, 2) * half, half), half)
-    inner = pl.ds(pl.multiple_of(lax.rem(frame, 2) * half, half), half)
+def stage_facing_kernel(half, keys, values, facing, token, sems):
+    frame = lax.axis_index("tm")
+    rows = pl.ds(pl.multiple_of(lax.rem(frame, 2) * half, half), half)
     token[...] = jnp.zeros_like(token)
-    run_copies(
-        [
-            (source.at[rows], target.at[kv])
-            for target, rows in ((facing, inner), (beside, outer))
-            for kv, source in enumerate((keys, values))
-        ],
-        sems,
-    )
+    run_copies([(keys.at[rows], facing.at[0]), (values.at[rows], facing.at[1])], sems)
+
+
+def stage_beside_kernel(half, after, keys, values, beside, token, sems):
+    frame = lax.axis_index("tm")
+    rows = pl.ds(pl.multiple_of(lax.rem(frame + 1, 2) * half, half), half)
+    token[...] = jnp.zeros_like(token)
+    run_copies([(keys.at[rows], beside.at[0]), (values.at[rows], beside.at[1])], sems)
 
 
 def stage_missing_kernel(after, bands, keys, values, missing, sems):
@@ -331,13 +330,21 @@
         )(*operands)
 
     token = jax.ShapeDtypeStruct((8, HD), jnp.int32)
-    facing, beside, after = stage(
-        functools.partial(stage_near_kernel, half),
-        [two, two, token],
-        4,
+    facing, after = stage(
+        functools.partial(stage_facing_kernel, half),
+        [two, token],
+        2,
         [keys, values],
-        "stage_near",
-        51,
+        "stage_facing",
+        52,
+    )
+    beside, after = stage(
+        functools.partial(stage_beside_kernel, half),
+        [two, token],
+        2,
+        [after, keys, values],
+        "stage_beside",
+        52,
     )
     (missing,) = stage(
         stage_missing_kernel, [one], 2, [after, bands, keys, values], "stage_missing", 32
@@ -389,7 +396,7 @@
         traded.append(send(part, [(1, 2), (2, 1)]))
 
     mixed, tops, sums = pl.pallas_call(
-        functools.partial(merge_kernel, rows // 2),
+        functools.partial(merge_kernel, rows),
         out_shape=[state] * 3,
         in_specs=[anywhere] + [local] * 5,
         out_specs=[local] * 3,

time: 87.7 us -> 87.4 us (level)
  waiting for transfers between devices: 47.7 us -> 46.5 us
  Pallas kernels: 19.9 us -> 20.8 us
    ppermute x10, waiting for transfers between devices: 47.7 us -> 46.5 us  [send(): return lax.ppermute(array, 'tm', pairs)]
    pallas_call x8 -> x9, Pallas kernels: 6.18 us -> 7.08 us  [stage(): pl.pallas_call(kernel, out_shape=shapes, in_specs=[scalars if operand is...]
  transfers between devices with their start and end apart: 10 -> 10, of which waited for: 3 -> 3; matrix products, arithmetic and copies ran while one was open for 0% -> 0% of each run, Pallas kernels for 18% -> 20%
where the time goes in v21:
time: 87.4 us; the launch traced here: 86.1 us
  waiting for transfers between devices  46.5 us (53%)
  Pallas kernels  20.8 us (24%)
  starting transfers between devices  18.4 us (21%)
    ppermute x10, waiting for transfers between devices, send(): return lax.ppermute(array, 'tm', pairs)  46.5 us
    ppermute x10, starting transfers between devices, send(): return lax.ppermute(array, 'tm', pairs)  18.4 us
    pallas_call x2, Pallas kernels, four_frames(): pl.pallas_call(functools.partial(close_kernel, start), out_shape=jax.Shap...  7.62 us
    pallas_call x9, Pallas kernels, stage(): pl.pallas_call(kernel, out_shape=shapes, in_specs=[scalars if operand is...  7.08 us
    pallas_call x1, Pallas kernels, four_frames(): pl.pallas_call(functools.partial(attend_kernel, rows // 2), out_shape=[st...  6.08 us
  transfers between devices with their start and end apart: 10, of which 3 were waited for; matrix products, arithmetic and copies ran while one was open for 0% of the time, Pallas kernels for 20%

profile of v21, /device:TPU:0, one launch (start us, length us, event | category | flops | bytes accessed | tf_op | source)
XLA Modules:
  0.0 86.1 jit_solution(782806167079719331)
XLA Ops:
  0.0 1.4 %stage_facing.1 = (bf16[2,256,1024]{2,1,0:T(8,128)(2,1)S(1)}, s32[8,128]{1,0:T(8,128)S(1)}) custom-call(bf16[512,1024]{1,0:T(8,128)(2,1)} %keys.11, bf16[512,1024]{1,0:T(8,128)(2,1)} %values.11), custom_call_target="tpu_custom_call" | custom-call | tf_op jit(solution)/shard_map/stage_facing/pallas_call | solution.py:322
  1.4 0.7 collective-permute-start.2
  2.1 1.2 %stage_beside.1 = (bf16[2,256,1024]{2,1,0:T(8,128)(2,1)S(1)}, s32[8,128]{1,0:T(8,128)S(1)}) custom-call(s32[8,128]{1,0:T(8,128)S(1)} %get-tuple-element.16.after, bf16[512,1024]{1,0:T(8,128)(2,1)} %keys.11, bf16[512,1024]{1,0:T(8,128)(2,1)} %values.11), custom_call_target="tpu_custom_call" | custom-call | tf_op jit(solution)/shard_map/stage_beside/pallas_call | solution.py:322
  3.4 5.9 %collective-permute-start = (bf16[2,256,1024]{2,1,0:T(8,128)(2,1)S(1)}, bf16[2,256,1024]{2,1,0:T(8,128)(2,1)S(1)}, u32[]{:S(2)}, u32[]{:S(2)}) collective-permute-start(bf16[2,256,1024]{2,1,0:T(8,128)(2,1)S(1)} %get-tuple-element.17), channel_id=1, source_target_pairs={{0,4},{4,0},{8,12},{12,8},{1,5},{5,1},{9,13},{13,9},{2,6},{6,2},{1... | collective-permute-start | bytes 3145736 | tf_op jit(solution)/shard_map/ppermute | solution.py:315
  9.2 0.6 stage_missing.1
  9.9 0.7 collective-permute-start.5
  10.6 0.0 collective-permute-done.2.facing
  10.6 0.6 stage_picked.1
  11.2 1.3 %collective-permute-start.3 = (bf16[2,128,1024]{2,1,0:T(8,128)(2,1)S(1)}, bf16[2,128,1024]{2,1,0:T(8,128)(2,1)S(1)}, u32[]{:S(2)}, u32[]{:S(2)}) collective-permute-start(bf16[2,128,1024]{2,1,0:T(8,128)(2,1)S(1)} %stage_picked.1), channel_id=1, source_target_pairs={{8,12},{4,0},{9,13},{5,1},{10,14},{6,2},{11,15},{7,3},{24,28},{20,... | collective-permute-start | bytes 1572872 | tf_op jit(solution)/shard_map/ppermute | solution.py:315
  12.5 19.6 %collective-permute-done.beside.after.after_too = bf16[2,256,1024]{2,1,0:T(8,128)(2,1)S(1)} collective-permute-done((bf16[2,256,1024]{2,1,0:T(8,128)(2,1)S(1)}, bf16[2,256,1024]{2,1,0:T(8,128)(2,1)S(1)}, u32[]{:S(2)}, u32[]{:S(2)}) %collective-permute-start) | collective-permute-done | bytes 1048608 | tf_op jit(solution)/shard_map/ppermute | solution.py:315
  32.1 0.6 stage_passed.1
  32.7 1.3 %collective-permute-start.1 = (bf16[2,128,1024]{2,1,0:T(8,128)(2,1)S(1)}, bf16[2,128,1024]{2,1,0:T(8,128)(2,1)S(1)}, u32[]{:S(2)}, u32[]{:S(2)}) collective-permute-start(bf16[2,128,1024]{2,1,0:T(8,128)(2,1)S(1)} %stage_passed.1), channel_id=1, source_target_pairs={{4,12},{8,0},{5,13},{9,1},{6,14},{10,2},{7,15},{11,3},{20,28},{24,... | collective-permute-start | bytes 1572872 | tf_op jit(solution)/shard_map/ppermute | solution.py:315
  34.0 0.0 collective-permute-done.5.after
  34.0 1.3 %collective-permute-start.6 = (bf16[2,128,1024]{2,1,0:T(8,128)(2,1)S(1)}, bf16[2,128,1024]{2,1,0:T(8,128)(2,1)S(1)}, u32[]{:S(2)}, u32[]{:S(2)}) collective-permute-start(bf16[2,128,1024]{2,1,0:T(8,128)(2,1)S(1)} %collective-permute-done.5.after), channel_id=1, source_target_pairs={{8,12},{4,0},{9,13},{5,1},{10,14},{6,2},{11,15},{7,3},{24,28},{20,... | collective-permute-start | bytes 1572872 | tf_op jit(solution)/shard_map/ppermute | solution.py:315
  35.3 17.4 %collective-permute-done.3.picked.after.after_too = bf16[2,128,1024]{2,1,0:T(8,128)(2,1)S(1)} collective-permute-done((bf16[2,128,1024]{2,1,0:T(8,128)(2,1)S(1)}, bf16[2,128,1024]{2,1,0:T(8,128)(2,1)S(1)}, u32[]{:S(2)}, u32[]{:S(2)}) %collective-permute-start.3) | collective-permute-done | bytes 524320 | tf_op jit(solution)/shard_map/ppermute | solution.py:315
  52.7 0.7 stage_crossed.1
  53.4 2.5 %collective-permute-start.8 = (bf16[2,128,1024]{2,1,0:T(8,128)(2,1)S(1)}, bf16[2,128,1024]{2,1,0:T(8,128)(2,1)S(1)}, u32[]{:S(2)}, u32[]{:S(2)}) collective-permute-start(bf16[2,128,1024]{2,1,0:T(8,128)(2,1)S(1)} %stage_crossed.1), channel_id=1, source_target_pairs={{0,8},{12,4},{1,9},{13,5},{2,10},{14,6},{3,11},{15,7},{16,24},{28,... | collective-permute-start | bytes 1572872 | tf_op jit(solution)/shard_map/ppermute | solution.py:315
  55.9 0.7 stage_direct.1
  56.6 0.0 copy-start.2
  56.6 3.4 %collective-permute-start.7 = (bf16[2,128,1024]{2,1,0:T(8,128)(2,1)S(1)}, bf16[2,128,1024]{2,1,0:T(8,128)(2,1)S(1)}, u32[]{:S(2)}, u32[]{:S(2)}) collective-permute-start(bf16[2,128,1024]{2,1,0:T(8,128)(2,1)S(1)} %stage_direct.1), channel_id=1, source_target_pairs={{0,12},{12,0},{1,13},{13,1},{2,14},{14,2},{3,15},{15,3},{16,28},{2... | collective-permute-start | bytes 1572872 | tf_op jit(solution)/shard_map/ppermute | solution.py:315
  60.0 0.6 stage_traded.3
  60.6 0.7 collective-permute-start.9
  61.3 6.1 %attend.1 = (f32[8,512,128]{2,1,0:T(8,128)S(1)}, f32[8,512,128]{2,1,0:T(8,128)S(1)}, f32[8,512,128]{2,1,0:T(8,128)S(1)}, s32[8,128]{1,0:T(8,128)S(1)}) custom-call(bf16[512,1024]{1,0:T(8,128)(2,1)S(1)} %copy-done.2, bf16[512,1024]{1,0:T(8,128)(2,1)S(1)} %copy-done, bf16[512,1024]{1,0:T(8,128)(2,1)S(1)} %copy-done.1, ...), custom_call_target="tpu_custom_call" | custom-call | tf_op jit(solution)/shard_map/attend/pallas_call | solution.py:378
  67.4 9.5 %collective-permute-done.1.after.passed = bf16[2,128,1024]{2,1,0:T(8,128)(2,1)S(1)} collective-permute-done((bf16[2,128,1024]{2,1,0:T(8,128)(2,1)S(1)}, bf16[2,128,1024]{2,1,0:T(8,128)(2,1)S(1)}, u32[]{:S(2)}, u32[]{:S(2)}) %collective-permute-start.1) | collective-permute-done | bytes 524320 | tf_op jit(solution)/shard_map/ppermute | solution.py:315
  76.9 0.6 stage_traded.2
  77.5 0.7 collective-permute-start.4
  78.2 0.0 collective-permute-done.6.after.lone
  78.2 0.0 collective-permute-done.8.crossed
  78.2 0.0 collective-permute-done.9.traded
  78.2 0.0 collective-permute-done.7.direct
  78.2 5.3 %close.2.rest_0_ = bf16[512,1024]{1,0:T(8,128)(2,1)} custom-call(bf16[512,1024]{1,0:T(8,128)(2,1)S(1)} %copy-done.2, bf16[2,128,768]{2,1,0:T(8,128)(2,1)S(1)} %collective-permute-done.9.traded, bf16[2,128,1024]{2,1,0:T(8,128)(2,1)S(1)} %collective-permute-done.6.after.lone, bf16[2,128,1024]{2,1,0:T(8,128)(2,1)S(1)} %collective-permute-done.1.after.passed, ...), custom_call_target="tpu_custom_call" | custom-call | tf_op jit(solution)/shard_map/close/pallas_call | solution.py:416
  83.5 2.4 %close.3 = bf16[512,1024]{1,0:T(8,128)(2,1)} custom-call(bf16[512,1024]{1,0:T(8,128)(2,1)S(1)} %copy-done.2, bf16[2,128,256]{2,1,0:T(8,128)(2,1)S(1)} %collective-permute-done.4.traded, bf16[2,128,1024]{2,1,0:T(8,128)(2,1)S(1)} %collective-permute-done.6.after.lone, ...), custom_call_target="tpu_custom_call", output_to_operand_aliasing={{}: (8, {})} | custom-call | tf_op jit(solution)/shard_map/close/pallas_call | solution.py:416
  (9 shorter events, 0.0 us)
Async XLA Ops:
  0.0 9.2 %copy-start.1 = (bf16[512,1024]{1,0:T(8,128)(2,1)S(1)}, bf16[512,1024]{1,0:T(8,128)(2,1)}, u32[]{:S(2)}) copy-start(bf16[512,1024]{1,0:T(8,128)(2,1)} %values.11) | copy-start | bytes 3145732
  0.0 9.2 %copy-start = (bf16[512,1024]{1,0:T(8,128)(2,1)S(1)}, bf16[512,1024]{1,0:T(8,128)(2,1)}, u32[]{:S(2)}) copy-start(bf16[512,1024]{1,0:T(8,128)(2,1)} %keys.11) | copy-start | bytes 3145732
  0.0 9.2 %copy-start.3 = (s32[4,4,2]{1,2,0:T(2,128)S(1)}, s32[4,4,2]{1,2,0:T(2,128)}, u32[]{:S(2)}) copy-start(s32[4,4,2]{1,2,0:T(2,128)} %param.7) | copy-start | bytes 388
  1.4 9.2 %collective-permute-start.2 = (bf16[2,256,1024]{2,1,0:T(8,128)(2,1)S(1)}, bf16[2,256,1024]{2,1,0:T(8,128)(2,1)S(1)}, u32[]{:S(2)}, u32[]{:S(2)}) collective-permute-start(bf16[2,256,1024]{2,1,0:T(8,128)(2,1)S(1)} %get-tuple-element.18), channel_id=1, source_target_pairs={{4,8},{8,4},{5,9},{9,5},{6,10},{10,6},{7,11},{11,7},{20,24},{24,20... | collective-permute-start | bytes 3145736 | tf_op jit(solution)/shard_map/ppermute | solution.py:315
  3.4 28.7 %collective-permute-start = (bf16[2,256,1024]{2,1,0:T(8,128)(2,1)S(1)}, bf16[2,256,1024]{2,1,0:T(8,128)(2,1)S(1)}, u32[]{:S(2)}, u32[]{:S(2)}) collective-permute-start(bf16[2,256,1024]{2,1,0:T(8,128)(2,1)S(1)} %get-tuple-element.17), channel_id=1, source_target_pairs={{0,4},{4,0},{8,12},{12,8},{1,5},{5,1},{9,13},{13,9},{2,6},{6,2},{1... | collective-permute-start | bytes 3145736 | tf_op jit(solution)/shard_map/ppermute | solution.py:315
  9.9 24.2 %collective-permute-start.5 = (bf16[2,128,1024]{2,1,0:T(8,128)(2,1)S(1)}, bf16[2,128,1024]{2,1,0:T(8,128)(2,1)S(1)}, u32[]{:S(2)}, u32[]{:S(2)}) collective-permute-start(bf16[2,128,1024]{2,1,0:T(8,128)(2,1)S(1)} %stage_missing.1), channel_id=1, source_target_pairs={{4,8},{8,4},{5,9},{9,5},{6,10},{10,6},{7,11},{11,7},{20,24},{24,20... | collective-permute-start | bytes 1572872 | tf_op jit(solution)/shard_map/ppermute | solution.py:315
  11.2 41.5 %collective-permute-start.3 = (bf16[2,128,1024]{2,1,0:T(8,128)(2,1)S(1)}, bf16[2,128,1024]{2,1,0:T(8,128)(2,1)S(1)}, u32[]{:S(2)}, u32[]{:S(2)}) collective-permute-start(bf16[2,128,1024]{2,1,0:T(8,128)(2,1)S(1)} %stage_picked.1), channel_id=1, source_target_pairs={{8,12},{4,0},{9,13},{5,1},{10,14},{6,2},{11,15},{7,3},{24,28},{20,... | collective-permute-start | bytes 1572872 | tf_op jit(solution)/shard_map/ppermute | solution.py:315
  32.7 44.1 %collective-permute-start.1 = (bf16[2,128,1024]{2,1,0:T(8,128)(2,1)S(1)}, bf16[2,128,1024]{2,1,0:T(8,128)(2,1)S(1)}, u32[]{:S(2)}, u32[]{:S(2)}) collective-permute-start(bf16[2,128,1024]{2,1,0:T(8,128)(2,1)S(1)} %stage_passed.1), channel_id=1, source_target_pairs={{4,12},{8,0},{5,13},{9,1},{6,14},{10,2},{7,15},{11,3},{20,28},{24,... | collective-permute-start | bytes 1572872 | tf_op jit(solution)/shard_map/ppermute | solution.py:315
  34.0 44.1 %collective-permute-start.6 = (bf16[2,128,1024]{2,1,0:T(8,128)(2,1)S(1)}, bf16[2,128,1024]{2,1,0:T(8,128)(2,1)S(1)}, u32[]{:S(2)}, u32[]{:S(2)}) collective-permute-start(bf16[2,128,1024]{2,1,0:T(8,128)(2,1)S(1)} %collective-permute-done.5.after), channel_id=1, source_target_pairs={{8,12},{4,0},{9,13},{5,1},{10,14},{6,2},{11,15},{7,3},{24,28},{20,... | collective-permute-start | bytes 1572872 | tf_op jit(solution)/shard_map/ppermute | solution.py:315
  53.4 24.8 %collective-permute-start.8 = (bf16[2,128,1024]{2,1,0:T(8,128)(2,1)S(1)}, bf16[2,128,1024]{2,1,0:T(8,128)(2,1)S(1)}, u32[]{:S(2)}, u32[]{:S(2)}) collective-permute-start(bf16[2,128,1024]{2,1,0:T(8,128)(2,1)S(1)} %stage_crossed.1), channel_id=1, source_target_pairs={{0,8},{12,4},{1,9},{13,5},{2,10},{14,6},{3,11},{15,7},{16,24},{28,... | collective-permute-start | bytes 1572872 | tf_op jit(solution)/shard_map/ppermute | solution.py:315
  56.6 4.7 %copy-start.2 = (bf16[512,1024]{1,0:T(8,128)(2,1)S(1)}, bf16[512,1024]{1,0:T(8,128)(2,1)}, u32[]{:S(2)}) copy-start(bf16[512,1024]{1,0:T(8,128)(2,1)} %queries.7) | copy-start | bytes 3145732
  56.6 21.7 %collective-permute-start.7 = (bf16[2,128,1024]{2,1,0:T(8,128)(2,1)S(1)}, bf16[2,128,1024]{2,1,0:T(8,128)(2,1)S(1)}, u32[]{:S(2)}, u32[]{:S(2)}) collective-permute-start(bf16[2,128,1024]{2,1,0:T(8,128)(2,1)S(1)} %stage_direct.1), channel_id=1, source_target_pairs={{0,12},{12,0},{1,13},{13,1},{2,14},{14,2},{3,15},{15,3},{16,28},{2... | collective-permute-start | bytes 1572872 | tf_op jit(solution)/shard_map/ppermute | solution.py:315
  60.6 17.6 %collective-permute-start.9 = (bf16[2,128,768]{2,1,0:T(8,128)(2,1)S(1)}, bf16[2,128,768]{2,1,0:T(8,128)(2,1)S(1)}, u32[]{:S(2)}, u32[]{:S(2)}) collective-permute-start(bf16[2,128,768]{2,1,0:T(8,128)(2,1)S(1)} %stage_traded.3), channel_id=1, source_target_pairs={{4,8},{8,4},{5,9},{9,5},{6,10},{10,6},{7,11},{11,7},{20,24},{24,20... | collective-permute-start | bytes 1179656 | tf_op jit(solution)/shard_map/ppermute | solution.py:315
  77.5 6.0 %collective-permute-start.4 = (bf16[2,128,256]{2,1,0:T(8,128)(2,1)S(1)}, bf16[2,128,256]{2,1,0:T(8,128)(2,1)S(1)}, u32[]{:S(2)}, u32[]{:S(2)}) collective-permute-start(bf16[2,128,256]{2,1,0:T(8,128)(2,1)S(1)} %stage_traded.2), channel_id=1, source_target_pairs={{4,8},{8,4},{5,9},{9,5},{6,10},{10,6},{7,11},{11,7},{20,24},{24,20... | collective-permute-start | bytes 393224 | tf_op jit(solution)/shard_map/ppermute | solution.py:315

commit v22 on v21

--- a/solution.py
+++ b/solution.py
@@ -366,7 +366,7 @@
         32,
     )
     crossed = send(crossed, [(0, 2), (3, 1)])
-    last = heads // 4
+    last = 3 * heads // 8
     cuts = [(0, heads - last), (heads - last, last)] if last else [(0, heads)]
     cuts = [(start * HD, size * HD) for start, size in cuts]
     (direct,) = stage(

time: 87.4 us -> 86.7 us (level); the launches traced: 86.1 us -> 86.3 us
  transfers between devices with their start and end apart: 10 -> 10, of which waited for: 3 -> 3; matrix products, arithmetic and copies ran while one was open for 0% -> 0% of each run, Pallas kernels for 20% -> 19%
where the time goes in v22:
time: 86.7 us; the launch traced here: 86.3 us
  waiting for transfers between devices  46.5 us (54%)
  Pallas kernels  21 us (24%)
  starting transfers between devices  18.4 us (21%)
    ppermute x10, waiting for transfers between devices, send(): return lax.ppermute(array, 'tm', pairs)  46.5 us
    ppermute x10, starting transfers between devices, send(): return lax.ppermute(array, 'tm', pairs)  18.4 us
    pallas_call x2, Pallas kernels, four_frames(): pl.pallas_call(functools.partial(close_kernel, start), out_shape=jax.Shap...  7.8 us
    pallas_call x9, Pallas kernels, stage(): pl.pallas_call(kernel, out_shape=shapes, in_specs=[scalars if operand is...  7.08 us
    pallas_call x1, Pallas kernels, four_frames(): pl.pallas_call(functools.partial(attend_kernel, rows // 2), out_shape=[st...  6.08 us
  transfers between devices with their start and end apart: 10, of which 3 were waited for; matrix products, arithmetic and copies ran while one was open for 0% of the time, Pallas kernels for 19%

profile of v22, /device:TPU:0, one launch (start us, length us, event | category | flops | bytes accessed | tf_op | source)
XLA Modules:
  0.0 86.3 jit_solution(11138411915280435324)
XLA Ops:
  0.0 1.4 %stage_facing.1 = (bf16[2,256,1024]{2,1,0:T(8,128)(2,1)S(1)}, s32[8,128]{1,0:T(8,128)S(1)}) custom-call(bf16[512,1024]{1,0:T(8,128)(2,1)} %keys.11, bf16[512,1024]{1,0:T(8,128)(2,1)} %values.11), custom_call_target="tpu_custom_call" | custom-call | tf_op jit(solution)/shard_map/stage_facing/pallas_call | solution.py:322
  1.4 0.7 collective-permute-start.2
  2.1 1.2 %stage_beside.1 = (bf16[2,256,1024]{2,1,0:T(8,128)(2,1)S(1)}, s32[8,128]{1,0:T(8,128)S(1)}) custom-call(s32[8,128]{1,0:T(8,128)S(1)} %get-tuple-element.16.after, bf16[512,1024]{1,0:T(8,128)(2,1)} %keys.11, bf16[512,1024]{1,0:T(8,128)(2,1)} %values.11), custom_call_target="tpu_custom_call" | custom-call | tf_op jit(solution)/shard_map/stage_beside/pallas_call | solution.py:322
  3.4 5.9 %collective-permute-start = (bf16[2,256,1024]{2,1,0:T(8,128)(2,1)S(1)}, bf16[2,256,1024]{2,1,0:T(8,128)(2,1)S(1)}, u32[]{:S(2)}, u32[]{:S(2)}) collective-permute-start(bf16[2,256,1024]{2,1,0:T(8,128)(2,1)S(1)} %get-tuple-element.17), channel_id=1, source_target_pairs={{0,4},{4,0},{8,12},{12,8},{1,5},{5,1},{9,13},{13,9},{2,6},{6,2},{1... | collective-permute-start | bytes 3145736 | tf_op jit(solution)/shard_map/ppermute | solution.py:315
  9.2 0.6 stage_missing.1
  9.9 0.7 collective-permute-start.5
  10.6 0.0 collective-permute-done.2.facing
  10.6 0.6 stage_picked.1
  11.2 1.3 %collective-permute-start.3 = (bf16[2,128,1024]{2,1,0:T(8,128)(2,1)S(1)}, bf16[2,128,1024]{2,1,0:T(8,128)(2,1)S(1)}, u32[]{:S(2)}, u32[]{:S(2)}) collective-permute-start(bf16[2,128,1024]{2,1,0:T(8,128)(2,1)S(1)} %stage_picked.1), channel_id=1, source_target_pairs={{8,12},{4,0},{9,13},{5,1},{10,14},{6,2},{11,15},{7,3},{24,28},{20,... | collective-permute-start | bytes 1572872 | tf_op jit(solution)/shard_map/ppermute | solution.py:315
  12.5 19.6 %collective-permute-done.beside.after.after_too = bf16[2,256,1024]{2,1,0:T(8,128)(2,1)S(1)} collective-permute-done((bf16[2,256,1024]{2,1,0:T(8,128)(2,1)S(1)}, bf16[2,256,1024]{2,1,0:T(8,128)(2,1)S(1)}, u32[]{:S(2)}, u32[]{:S(2)}) %collective-permute-start) | collective-permute-done | bytes 1048608 | tf_op jit(solution)/shard_map/ppermute | solution.py:315
  32.1 0.6 stage_passed.1
  32.7 1.3 %collective-permute-start.1 = (bf16[2,128,1024]{2,1,0:T(8,128)(2,1)S(1)}, bf16[2,128,1024]{2,1,0:T(8,128)(2,1)S(1)}, u32[]{:S(2)}, u32[]{:S(2)}) collective-permute-start(bf16[2,128,1024]{2,1,0:T(8,128)(2,1)S(1)} %stage_passed.1), channel_id=1, source_target_pairs={{4,12},{8,0},{5,13},{9,1},{6,14},{10,2},{7,15},{11,3},{20,28},{24,... | collective-permute-start | bytes 1572872 | tf_op jit(solution)/shard_map/ppermute | solution.py:315
  34.0 0.0 collective-permute-done.5.after
  34.0 1.3 %collective-permute-start.6 = (bf16[2,128,1024]{2,1,0:T(8,128)(2,1)S(1)}, bf16[2,128,1024]{2,1,0:T(8,128)(2,1)S(1)}, u32[]{:S(2)}, u32[]{:S(2)}) collective-permute-start(bf16[2,128,1024]{2,1,0:T(8,128)(2,1)S(1)} %collective-permute-done.5.after), channel_id=1, source_target_pairs={{8,12},{4,0},{9,13},{5,1},{10,14},{6,2},{11,15},{7,3},{24,28},{20,... | collective-permute-start | bytes 1572872 | tf_op jit(solution)/shard_map/ppermute | solution.py:315
  35.3 17.4 %collective-permute-done.3.picked.after.after_too = bf16[2,128,1024]{2,1,0:T(8,128)(2,1)S(1)} collective-permute-done((bf16[2,128,1024]{2,1,0:T(8,128)(2,1)S(1)}, bf16[2,128,1024]{2,1,0:T(8,128)(2,1)S(1)}, u32[]{:S(2)}, u32[]{:S(2)}) %collective-permute-start.3) | collective-permute-done | bytes 524320 | tf_op jit(solution)/shard_map/ppermute | solution.py:315
  52.7 0.7 stage_crossed.1
  53.4 2.5 %collective-permute-start.8 = (bf16[2,128,1024]{2,1,0:T(8,128)(2,1)S(1)}, bf16[2,128,1024]{2,1,0:T(8,128)(2,1)S(1)}, u32[]{:S(2)}, u32[]{:S(2)}) collective-permute-start(bf16[2,128,1024]{2,1,0:T(8,128)(2,1)S(1)} %stage_crossed.1), channel_id=1, source_target_pairs={{0,8},{12,4},{1,9},{13,5},{2,10},{14,6},{3,11},{15,7},{16,24},{28,... | collective-permute-start | bytes 1572872 | tf_op jit(solution)/shard_map/ppermute | solution.py:315
  55.9 0.7 stage_direct.1
  56.6 0.0 copy-start.2
  56.6 3.4 %collective-permute-start.7 = (bf16[2,128,1024]{2,1,0:T(8,128)(2,1)S(1)}, bf16[2,128,1024]{2,1,0:T(8,128)(2,1)S(1)}, u32[]{:S(2)}, u32[]{:S(2)}) collective-permute-start(bf16[2,128,1024]{2,1,0:T(8,128)(2,1)S(1)} %stage_direct.1), channel_id=1, source_target_pairs={{0,12},{12,0},{1,13},{13,1},{2,14},{14,2},{3,15},{15,3},{16,28},{2... | collective-permute-start | bytes 1572872 | tf_op jit(solution)/shard_map/ppermute | solution.py:315
  60.0 0.6 stage_traded.3
  60.6 0.7 collective-permute-start.9
  61.3 6.1 %attend.1 = (f32[8,512,128]{2,1,0:T(8,128)S(1)}, f32[8,512,128]{2,1,0:T(8,128)S(1)}, f32[8,512,128]{2,1,0:T(8,128)S(1)}, s32[8,128]{1,0:T(8,128)S(1)}) custom-call(bf16[512,1024]{1,0:T(8,128)(2,1)S(1)} %copy-done.2, bf16[512,1024]{1,0:T(8,128)(2,1)S(1)} %copy-done, bf16[512,1024]{1,0:T(8,128)(2,1)S(1)} %copy-done.1, ...), custom_call_target="tpu_custom_call" | custom-call | tf_op jit(solution)/shard_map/attend/pallas_call | solution.py:378
  67.4 9.5 %collective-permute-done.1.after.passed = bf16[2,128,1024]{2,1,0:T(8,128)(2,1)S(1)} collective-permute-done((bf16[2,128,1024]{2,1,0:T(8,128)(2,1)S(1)}, bf16[2,128,1024]{2,1,0:T(8,128)(2,1)S(1)}, u32[]{:S(2)}, u32[]{:S(2)}) %collective-permute-start.1) | collective-permute-done | bytes 524320 | tf_op jit(solution)/shard_map/ppermute | solution.py:315
  76.9 0.6 stage_traded.2
  77.5 0.7 collective-permute-start.4
  78.2 0.0 collective-permute-done.6.after.lone
  78.2 0.0 collective-permute-done.8.crossed
  78.2 0.0 collective-permute-done.9.traded
  78.3 4.6 %close.2.rest_0_ = bf16[512,1024]{1,0:T(8,128)(2,1)} custom-call(bf16[512,1024]{1,0:T(8,128)(2,1)S(1)} %copy-done.2, bf16[2,128,640]{2,1,0:T(8,128)(2,1)S(1)} %collective-permute-done.9.traded, bf16[2,128,1024]{2,1,0:T(8,128)(2,1)S(1)} %collective-permute-done.6.after.lone, bf16[2,128,1024]{2,1,0:T(8,128)(2,1)S(1)} %collective-permute-done.1.after.passed, ...), custom_call_target="tpu_custom_call" | custom-call | tf_op jit(solution)/shard_map/close/pallas_call | solution.py:416
  82.9 0.0 collective-permute-done.4.traded
  82.9 3.2 %close.3 = bf16[512,1024]{1,0:T(8,128)(2,1)} custom-call(bf16[512,1024]{1,0:T(8,128)(2,1)S(1)} %copy-done.2, bf16[2,128,384]{2,1,0:T(8,128)(2,1)S(1)} %collective-permute-done.4.traded, bf16[2,128,1024]{2,1,0:T(8,128)(2,1)S(1)} %collective-permute-done.6.after.lone, ...), custom_call_target="tpu_custom_call", output_to_operand_aliasing={{}: (8, {})} | custom-call | tf_op jit(solution)/shard_map/close/pallas_call | solution.py:416
  (9 shorter events, 0.0 us)
Async XLA Ops:
  0.0 9.2 %copy-start.1 = (bf16[512,1024]{1,0:T(8,128)(2,1)S(1)}, bf16[512,1024]{1,0:T(8,128)(2,1)}, u32[]{:S(2)}) copy-start(bf16[512,1024]{1,0:T(8,128)(2,1)} %values.11) | copy-start | bytes 3145732
  0.0 9.2 %copy-start = (bf16[512,1024]{1,0:T(8,128)(2,1)S(1)}, bf16[512,1024]{1,0:T(8,128)(2,1)}, u32[]{:S(2)}) copy-start(bf16[512,1024]{1,0:T(8,128)(2,1)} %keys.11) | copy-start | bytes 3145732
  0.0 9.2 %copy-start.3 = (s32[4,4,2]{1,2,0:T(2,128)S(1)}, s32[4,4,2]{1,2,0:T(2,128)}, u32[]{:S(2)}) copy-start(s32[4,4,2]{1,2,0:T(2,128)} %param.7) | copy-start | bytes 388
  1.4 9.2 %collective-permute-start.2 = (bf16[2,256,1024]{2,1,0:T(8,128)(2,1)S(1)}, bf16[2,256,1024]{2,1,0:T(8,128)(2,1)S(1)}, u32[]{:S(2)}, u32[]{:S(2)}) collective-permute-start(bf16[2,256,1024]{2,1,0:T(8,128)(2,1)S(1)} %get-tuple-element.18), channel_id=1, source_target_pairs={{4,8},{8,4},{5,9},{9,5},{6,10},{10,6},{7,11},{11,7},{20,24},{24,20... | collective-permute-start | bytes 3145736 | tf_op jit(solution)/shard_map/ppermute | solution.py:315
  3.4 28.7 %collective-permute-start = (bf16[2,256,1024]{2,1,0:T(8,128)(2,1)S(1)}, bf16[2,256,1024]{2,1,0:T(8,128)(2,1)S(1)}, u32[]{:S(2)}, u32[]{:S(2)}) collective-permute-start(bf16[2,256,1024]{2,1,0:T(8,128)(2,1)S(1)} %get-tuple-element.17), channel_id=1, source_target_pairs={{0,4},{4,0},{8,12},{12,8},{1,5},{5,1},{9,13},{13,9},{2,6},{6,2},{1... | collective-permute-start | bytes 3145736 | tf_op jit(solution)/shard_map/ppermute | solution.py:315
  9.9 24.2 %collective-permute-start.5 = (bf16[2,128,1024]{2,1,0:T(8,128)(2,1)S(1)}, bf16[2,128,1024]{2,1,0:T(8,128)(2,1)S(1)}, u32[]{:S(2)}, u32[]{:S(2)}) collective-permute-start(bf16[2,128,1024]{2,1,0:T(8,128)(2,1)S(1)} %stage_missing.1), channel_id=1, source_target_pairs={{4,8},{8,4},{5,9},{9,5},{6,10},{10,6},{7,11},{11,7},{20,24},{24,20... | collective-permute-start | bytes 1572872 | tf_op jit(solution)/shard_map/ppermute | solution.py:315
  11.2 41.5 %collective-permute-start.3 = (bf16[2,128,1024]{2,1,0:T(8,128)(2,1)S(1)}, bf16[2,128,1024]{2,1,0:T(8,128)(2,1)S(1)}, u32[]{:S(2)}, u32[]{:S(2)}) collective-permute-start(bf16[2,128,1024]{2,1,0:T(8,128)(2,1)S(1)} %stage_picked.1), channel_id=1, source_target_pairs={{8,12},{4,0},{9,13},{5,1},{10,14},{6,2},{11,15},{7,3},{24,28},{20,... | collective-permute-start | bytes 1572872 | tf_op jit(solution)/shard_map/ppermute | solution.py:315
  32.7 44.1 %collective-permute-start.1 = (bf16[2,128,1024]{2,1,0:T(8,128)(2,1)S(1)}, bf16[2,128,1024]{2,1,0:T(8,128)(2,1)S(1)}, u32[]{:S(2)}, u32[]{:S(2)}) collective-permute-start(bf16[2,128,1024]{2,1,0:T(8,128)(2,1)S(1)} %stage_passed.1), channel_id=1, source_target_pairs={{4,12},{8,0},{5,13},{9,1},{6,14},{10,2},{7,15},{11,3},{20,28},{24,... | collective-permute-start | bytes 1572872 | tf_op jit(solution)/shard_map/ppermute | solution.py:315
  34.0 44.1 %collective-permute-start.6 = (bf16[2,128,1024]{2,1,0:T(8,128)(2,1)S(1)}, bf16[2,128,1024]{2,1,0:T(8,128)(2,1)S(1)}, u32[]{:S(2)}, u32[]{:S(2)}) collective-permute-start(bf16[2,128,1024]{2,1,0:T(8,128)(2,1)S(1)} %collective-permute-done.5.after), channel_id=1, source_target_pairs={{8,12},{4,0},{9,13},{5,1},{10,14},{6,2},{11,15},{7,3},{24,28},{20,... | collective-permute-start | bytes 1572872 | tf_op jit(solution)/shard_map/ppermute | solution.py:315
  53.4 24.8 %collective-permute-start.8 = (bf16[2,128,1024]{2,1,0:T(8,128)(2,1)S(1)}, bf16[2,128,1024]{2,1,0:T(8,128)(2,1)S(1)}, u32[]{:S(2)}, u32[]{:S(2)}) collective-permute-start(bf16[2,128,1024]{2,1,0:T(8,128)(2,1)S(1)} %stage_crossed.1), channel_id=1, source_target_pairs={{0,8},{12,4},{1,9},{13,5},{2,10},{14,6},{3,11},{15,7},{16,24},{28,... | collective-permute-start | bytes 1572872 | tf_op jit(solution)/shard_map/ppermute | solution.py:315
  56.6 4.7 %copy-start.2 = (bf16[512,1024]{1,0:T(8,128)(2,1)S(1)}, bf16[512,1024]{1,0:T(8,128)(2,1)}, u32[]{:S(2)}) copy-start(bf16[512,1024]{1,0:T(8,128)(2,1)} %queries.7) | copy-start | bytes 3145732
  56.6 21.7 %collective-permute-start.7 = (bf16[2,128,1024]{2,1,0:T(8,128)(2,1)S(1)}, bf16[2,128,1024]{2,1,0:T(8,128)(2,1)S(1)}, u32[]{:S(2)}, u32[]{:S(2)}) collective-permute-start(bf16[2,128,1024]{2,1,0:T(8,128)(2,1)S(1)} %stage_direct.1), channel_id=1, source_target_pairs={{0,12},{12,0},{1,13},{13,1},{2,14},{14,2},{3,15},{15,3},{16,28},{2... | collective-permute-start | bytes 1572872 | tf_op jit(solution)/shard_map/ppermute | solution.py:315
  60.6 17.6 %collective-permute-start.9 = (bf16[2,128,640]{2,1,0:T(8,128)(2,1)S(1)}, bf16[2,128,640]{2,1,0:T(8,128)(2,1)S(1)}, u32[]{:S(2)}, u32[]{:S(2)}) collective-permute-start(bf16[2,128,640]{2,1,0:T(8,128)(2,1)S(1)} %stage_traded.3), channel_id=1, source_target_pairs={{4,8},{8,4},{5,9},{9,5},{6,10},{10,6},{7,11},{11,7},{20,24},{24,20... | collective-permute-start | bytes 983048 | tf_op jit(solution)/shard_map/ppermute | solution.py:315
  77.5 5.4 %collective-permute-start.4 = (bf16[2,128,384]{2,1,0:T(8,128)(2,1)S(1)}, bf16[2,128,384]{2,1,0:T(8,128)(2,1)S(1)}, u32[]{:S(2)}, u32[]{:S(2)}) collective-permute-start(bf16[2,128,384]{2,1,0:T(8,128)(2,1)S(1)} %stage_traded.2), channel_id=1, source_target_pairs={{4,8},{8,4},{5,9},{9,5},{6,10},{10,6},{7,11},{11,7},{20,24},{24,20... | collective-permute-start | bytes 589832 | tf_op jit(solution)/shard_map/ppermute | solution.py:315
